TPU v7x, 128 devices: a whole 4x4x4 slice. The times are simulated.
128 devices in a mesh: row: 8 (over y, x_hi), col: 16 (over x_lo, z, core).
Axes of the slice: x: 4 (x_hi: 2, x_lo: 2; x = x_hi * 2 + x_lo), y: 4, z: 4, core: 2. Of those that a mesh axis runs over, the one named last changes fastest.
Arguments:
- tokens: bfloat16 [1024, 6144], P('row', 'col'), may hold values from -6 to 6
- cotangent: bfloat16 [1024, 6144], P('row', 'col'), may hold values from -6 to 6
- w_in: bfloat16 [6144, 24576], P('col', 'row'), may hold values from -0.078125 to 0.078125
- w_out: bfloat16 [24576, 6144], P('row', 'col'), may hold values from -0.0390625 to 0.0390625
Outputs:
- input_grad: bfloat16 [1024, 6144], P('row', 'col')
- w_in_grad: bfloat16 [6144, 24576], P('col', 'row')
- w_out_grad: bfloat16 [24576, 6144], P('row', 'col')
All inputs are finite; a program needn't handle non-finite values.
Results may differ from a plain program's by a relative error of at most 0.0049.
Values may be sent and summed in bfloat16 or wider, within the bound.
No kernel may reach another device: no remote copies, remote signals or barrier semaphores. Data moves between devices by JAX's collectives and lax.ppermute only.
A program may use at most 128 MiB of HBM per device.

v0:
```python
import jax
import jax.numpy as jnp
from jax import lax
from jax.sharding import PartitionSpec as P


def gelu_parts(pre):
    cdf = 0.5 * (1.0 + lax.erf(pre * 0.7071067811865476))
    pdf = jnp.exp(-0.5 * pre * pre) * 0.3989422804014327
    return (cdf, pdf)


def local(tokens, cotangent, w_in, w_out):
    tok_all, cot_all = (
        lax.all_gather(tokens, "row", axis=0, tiled=True),
        lax.all_gather(cotangent, "row", axis=0, tiled=True),
    )
    piece = cot_all
    act_grad = lax.psum_scatter(
        lax.dot_general(piece, w_out, (((1,), (1,)), ((), ())), preferred_element_type=jnp.float32),
        "col",
        scatter_dimension=0,
        tiled=True,
    )
    piece = tok_all
    pre = lax.psum_scatter(
        jnp.dot(piece, w_in, preferred_element_type=jnp.float32),
        "col",
        scatter_dimension=0,
        tiled=True,
    )
    cdf, pdf = gelu_parts(pre)
    act = (pre * cdf).astype(jnp.bfloat16)
    pre_grad = (act_grad * (cdf + pre * pdf)).astype(jnp.bfloat16)
    act_all, grad_all = (
        lax.all_gather(act, "col", axis=0, tiled=True),
        lax.all_gather(pre_grad, "col", axis=0, tiled=True),
    )
    w_in_grad = lax.dot_general(
        tok_all, grad_all, (((0,), (0,)), ((), ())), preferred_element_type=jnp.float32
    ).astype(jnp.bfloat16)
    w_out_grad = lax.dot_general(
        act_all, cot_all, (((0,), (0,)), ((), ())), preferred_element_type=jnp.float32
    ).astype(jnp.bfloat16)
    piece = grad_all
    input_grad = lax.psum_scatter(
        lax.dot_general(piece, w_in, (((1,), (1,)), ((), ())), preferred_element_type=jnp.float32),
        "row",
        scatter_dimension=0,
        tiled=True,
    ).astype(jnp.bfloat16)
    return (input_grad, w_in_grad, w_out_grad)


def solution(mesh):
    placed = (P("row", "col"), P("row", "col"), P("col", "row"), P("row", "col"))
    return jax.shard_map(
        local,
        mesh=mesh,
        in_specs=placed,
        out_specs=(P("row", "col"), P("col", "row"), P("row", "col")),
        check_vma=False,
    )
```

profile of v0, /device:TPU:0, one launch (start us, length us, event | category | flops | bytes accessed | tf_op | source)
XLA Modules:
  0.0 406.8 jit_solution(1029882341992234221)
XLA Ops:
  7.2 0.0 copy-start
  7.2 0.0 reduce-scatter.4.cloned.1.call-start
  7.2 37.4 %all_gather.12 = bf16[1024,384]{1,0:T(8,128)(2,1)S(1)} all-gather(bf16[128,384]{1,0:T(8,128)(2,1)} %param.5), channel_id=1, replica_groups=mesh['row'=8,'col'=16] {'row'}, dimensions={0}, use_global_device_ids=true | all-gather | bytes 884736 | tf_op jit(solution)/shard_map/all_gather | solution.py:16
  44.6 0.0 copy-start.1
  44.6 1.0 copy-done.1
  45.5 8.0 %fusion.7 = f32[1024,3072]{1,0:T(8,128)} fusion(bf16[1024,384]{1,0:T(8,128)(2,1)S(1)} %all_gather.12, bf16[3072,384]{1,0:T(8,128)(2,1)} %param.7), kind=kOutput, calls=%fused_computation.12 | convolution fusion | flops 2415919104 | bytes 15728640 | tf_op jit(solution)/shard_map/dot_general | solution.py:20
  53.6 0.0 copy-start.3
  53.6 0.0 reduce-scatter.4.cloned.1.call-update
  53.6 0.0 reduce-scatter.6.cloned.1.call-start
  53.6 0.8 copy-done.3
  54.5 39.2 %all_gather.13 = bf16[1024,384]{1,0:T(8,128)(2,1)S(1)} all-gather(bf16[128,384]{1,0:T(8,128)(2,1)S(1)} %copy-done.3), channel_id=1, replica_groups=mesh['row'=8,'col'=16] {'row'}, dimensions={0}, use_global_device_ids=true | all-gather | bytes 884736 | tf_op jit(solution)/shard_map/all_gather | solution.py:15
  93.7 0.0 copy-done
  93.7 6.5 %fusion.8 = f32[1024,3072]{1,0:T(8,128)} fusion(bf16[1024,384]{1,0:T(8,128)(2,1)S(1)} %all_gather.13, bf16[384,3072]{1,0:T(8,128)(2,1)S(1)} %copy-done), kind=kOutput, calls=%fused_computation.13 | convolution fusion | flops 2415919104 | bytes 15728640 | tf_op jit(solution)/shard_map/dot_general | solution.py:27
  100.2 0.0 reduce-scatter.6.cloned.1.call-update
  100.2 0.0 all-gather.3.cloned.1.call-start
  100.3 47.5 %reduce-scatter.4.cloned.1.call-done = f32[64,3072]{1,0:T(8,128)} async-done(((f32[1024,3072]{1,0:T(8,128)}), f32[64,3072]{1,0:T(8,128)}) %reduce-scatter.4.cloned.1.call-update) | async-done | bytes 786448 | tf_op jit(solution)/shard_map/reduce_scatter | solution.py:19
  147.7 84.4 %reduce-scatter.6.cloned.1.call-done = f32[64,3072]{1,0:T(8,128)} async-done(((f32[1024,3072]{1,0:T(8,128)}), f32[64,3072]{1,0:T(8,128)}) %reduce-scatter.6.cloned.1.call-update) | async-done | bytes 786448 | tf_op jit(solution)/shard_map/reduce_scatter | solution.py:26
  232.2 2.6 multiply_convert_fusion
  234.8 0.0 all-gather.3.cloned.1.call-update
  234.8 0.0 all-gather.5.cloned.1.call-start
  234.9 0.5 all-gather.5.cloned.1.call-update
  235.4 0.2 reduce-scatter.8.cloned.1.call-start
  235.6 40.8 %all-gather.3.cloned.1.call-done = bf16[1024,3072]{1,0:T(8,128)(2,1)} async-done(((bf16[64,3072]{1,0:T(8,128)(2,1)}), bf16[1024,3072]{1,0:T(8,128)(2,1)}) %all-gather.3.cloned.1.call-update) | async-done | bytes 6291472 | tf_op jit(solution)/shard_map/all_gather | solution.py:37
  276.4 6.7 %fusion.9 = f32[1024,384]{1,0:T(8,128)} fusion(bf16[1024,3072]{1,0:T(8,128)(2,1)} %all-gather.3.cloned.1.call-done, bf16[384,3072]{1,0:T(8,128)(2,1)S(1)} %copy-done), kind=kOutput, calls=%fused_computation.14 | convolution fusion | flops 2415919104 | bytes 10223616 | tf_op jit(solution)/shard_map/dot_general | solution.py:47
  283.1 0.0 reduce-scatter.8.cloned.1.call-update
  283.1 7.7 %fusion = bf16[384,3072]{0,1:T(8,128)(2,1)} fusion(bf16[1024,3072]{1,0:T(8,128)(2,1)} %all-gather.3.cloned.1.call-done, bf16[1024,384]{1,0:T(8,128)(2,1)S(1)} %all_gather.13), kind=kOutput, calls=%fused_computation.2 | convolution fusion | flops 2417098752 | bytes 9437184 | tf_op jit(solution)/shard_map/dot_general | solution.py:39
  290.8 0.0 copy-start.2
  290.8 4.3 %copy.7 = bf16[384,3072]{1,0:T(8,128)(2,1)} copy(bf16[384,3072]{0,1:T(8,128)(2,1)} %fusion) | data formatting | bytes 4718592
  295.2 26.1 %all-gather.5.cloned.1.call-done = bf16[1024,3072]{1,0:T(8,128)(2,1)} async-done(((bf16[64,3072]{1,0:T(8,128)(2,1)}), bf16[1024,3072]{1,0:T(8,128)(2,1)}) %all-gather.5.cloned.1.call-update) | async-done | bytes 6291472 | tf_op jit(solution)/shard_map/all_gather | solution.py:36
  321.3 0.0 copy-done.2
  321.3 7.7 %convolution_convert_fusion = bf16[3072,384]{1,0:T(8,128)(2,1)} fusion(bf16[1024,3072]{1,0:T(8,128)(2,1)} %all-gather.5.cloned.1.call-done, bf16[1024,384]{1,0:T(8,128)(2,1)S(1)} %copy-done.2), kind=kOutput, calls=%fused_computation | convolution fusion | flops 2417098752 | bytes 9437184 | tf_op jit(solution)/shard_map/dot_general | solution.py:42
  328.9 69.7 %reduce-scatter.8.cloned.1.call-done = f32[128,384]{1,0:T(8,128)} async-done(((f32[1024,384]{1,0:T(8,128)}), f32[128,384]{1,0:T(8,128)}) %reduce-scatter.8.cloned.1.call-update) | async-done | bytes 196624 | tf_op jit(solution)/shard_map/reduce_scatter | solution.py:46
  398.7 1.6 convert_element_type.19
Async XLA Ops:
  7.2 86.5 %copy-start = (bf16[384,3072]{1,0:T(8,128)(2,1)S(1)}, bf16[384,3072]{1,0:T(8,128)(2,1)}, u32[]{:S(2)}) copy-start(bf16[384,3072]{1,0:T(8,128)(2,1)} %param.6) | copy-start | bytes 7077892
  7.2 140.6 %reduce-scatter.4.cloned.1.call-start = ((), (), s32[]{:S(2)}) async-start(), calls=%async_computation.3 | async-start | bytes 13369344 | tf_op jit(solution)/shard_map/reduce_scatter | solution.py:19
  44.6 1.0 copy-start.1
  53.6 0.9 copy-start.3
  53.6 178.6 %reduce-scatter.6.cloned.1.call-start = ((), (), s32[]{:S(2)}) async-start(), calls=%async_computation.4 | async-start | bytes 13369344 | tf_op jit(solution)/shard_map/reduce_scatter | solution.py:26
  100.2 176.2 %all-gather.3.cloned.1.call-start = ((), (), s32[]{:S(2)}) async-start(), calls=%async_computation.5 | async-start | bytes 6684672 | tf_op jit(solution)/shard_map/all_gather | solution.py:37
  234.8 86.5 %all-gather.5.cloned.1.call-start = ((), (), s32[]{:S(2)}) async-start(), calls=%async_computation.7 | async-start | bytes 6684672 | tf_op jit(solution)/shard_map/all_gather | solution.py:36
  235.4 163.3 %reduce-scatter.8.cloned.1.call-start = ((), (), s32[]{:S(2)}) async-start(), calls=%async_computation.6 | async-start | bytes 1769472 | tf_op jit(solution)/shard_map/reduce_scatter | solution.py:46
  290.8 30.5 %copy-start.2 = (bf16[1024,384]{1,0:T(8,128)(2,1)S(1)}, bf16[1024,384]{1,0:T(8,128)(2,1)}, u32[]{:S(2)}) copy-start(bf16[1024,384]{1,0:T(8,128)(2,1)} %copy-done.1) | copy-start | bytes 2359300
Sparse Core Ops, SparseCore 0:
  53.7 93.9 reduce-scatter.3
  150.2 81.9 reduce-scatter.5
  234.9 41.4 all-gather.2
  278.0 43.2 all-gather.4
  324.8 73.8 reduce-scatter.7
where the time goes:
time: 407 us
  waiting for transfers between devices  269 us (66%)
  blocking collectives  76.6 us (19%)
  matrix products  36.5 us (9%)
  between operations  13.8 us (3%)
  local copies, waits for them, and re-layouts  6.13 us (2%)
  other arithmetic  4.18 us (1%)
    reduce_scatter x1, waiting for transfers between devices, local(): lax.psum_scatter(jnp.dot(piece, w_in, preferred_element_type=jnp.float32)...  84.4 us
    reduce_scatter x1, waiting for transfers between devices, local(): lax.psum_scatter(lax.dot_general(piece, w_in, (((1,), (1,)), ((), ())), p...  69.7 us
    reduce_scatter x1, waiting for transfers between devices, local(): lax.psum_scatter(lax.dot_general(piece, w_out, (((1,), (1,)), ((), ())),...  47.5 us
    all_gather x1, waiting for transfers between devices, local(): lax.all_gather(pre_grad, 'col', axis=0, tiled=True)  40.8 us
    all_gather x1, blocking collectives, local(): lax.all_gather(tokens, 'row', axis=0, tiled=True)  39.2 us
    all_gather x1, blocking collectives, local(): lax.all_gather(cotangent, 'row', axis=0, tiled=True)  37.4 us
    all_gather x1, waiting for transfers between devices, local(): lax.all_gather(act, 'col', axis=0, tiled=True)  26.1 us
  transfers between devices with their start and end apart: 5, of which 5 were waited for; matrix products, arithmetic and copies ran while one was open for 8% of the time, Pallas kernels for 0%

commit v1 on v0

v1 whole, which is shorter than its diff:
```python
import jax
import jax.numpy as jnp
from jax import lax
from jax.sharding import Mesh
from jax.sharding import PartitionSpec as P

AXES = ("y", "xh", "xl", "z", "core")
SIZES = (4, 2, 2, 4, 2)
ROWS = ("y", "xh")
COLS = ("xl", "z", "core")
F32 = jnp.float32
BF16 = jnp.bfloat16


def gelu_parts(pre):
    cdf = 0.5 * (1.0 + lax.erf(pre * 0.7071067811865476))
    pdf = jnp.exp(-0.5 * pre * pre) * 0.3989422804014327
    return (cdf, pdf)


def shift(x, axis, by):
    n = SIZES[AXES.index(axis)]
    return lax.ppermute(x, axis, [(i, (i + by) % n) for i in range(n)])


def dot(a, b, da, db):
    return lax.dot_general(a, b, (((da,), (db,)), ((), ())), preferred_element_type=F32)


def swap_halves(first, second, flag, axis):
    return jnp.concatenate([jnp.where(flag == 0, first, second), jnp.where(flag == 0, second, first)], axis)


def local(tokens, cotangent, w_in, w_out):
    z, xl, core = lax.axis_index("z"), lax.axis_index("xl"), lax.axis_index("core")
    rows, feat = tokens.shape
    hid = w_in.shape[1] // 2
    piece = rows // 8

    def relative(a, sign):
        a = a.reshape(4, 2, piece, a.shape[-1])
        return jnp.roll(jnp.roll(a, sign * z, 0), sign * xl, 1)

    own = relative(jnp.concatenate([tokens, cotangent], 1), -1)

    near = jnp.stack([own, shift(own, "y", -1), shift(own, "y", -2), shift(own, "y", -3)])
    near = near.transpose(1, 2, 0, 3, 4).reshape(rows * 4, 2 * feat)
    far = shift(near, "xh", 1)

    def core_weights(w, axis):
        keep = lax.dynamic_slice_in_dim(w, core * hid, hid, axis)
        send = lax.dynamic_slice_in_dim(w, (1 - core) * hid, hid, axis)
        return jnp.concatenate([keep, shift(send, "core", 1)], 1 - axis)

    wi = core_weights(w_in, 1)
    wo = core_weights(w_out, 0)

    def chip_features(a):
        b = shift(a, "core", 1)
        return (
            jnp.concatenate([a[:, :feat], b[:, :feat]], 1),
            jnp.concatenate([a[:, feat:], b[:, feat:]], 1),
        )

    def hidden(tok, cot):
        tok4, cot4 = tok.reshape(4, rows, -1), cot.reshape(4, rows, -1)
        pre = lambda k: dot(tok4[k], wi, 1, 0)
        grad = lambda k: dot(cot4[k], wo, 1, 1)
        cat = lambda p, g: jnp.concatenate([p.astype(BF16), g.astype(BF16)], 1)
        up = shift(pre(2).astype(BF16), "z", 1)
        down = shift(grad(2).astype(BF16), "z", -1)
        up = shift(cat(pre(1) + up.astype(F32), grad(1)), "z", 1)
        down = shift(cat(pre(3), grad(3) + down.astype(F32)), "z", -1)
        p = pre(0) + up[:, :hid].astype(F32) + down[:, :hid].astype(F32)
        g = grad(0) + up[:, hid:].astype(F32) + down[:, hid:].astype(F32)
        half = rows // 2
        other = shift(cat(p[half:], g[half:]), "xl", 1)
        p = p[:half] + other[:, :hid].astype(F32)
        g = g[:half] + other[:, hid:].astype(F32)
        cdf, pdf = gelu_parts(p)
        act = (p * cdf).astype(BF16)
        pre_grad = (g * (cdf + p * pdf)).astype(BF16)
        return jnp.concatenate([act, pre_grad], 1)

    def spread(mine):
        mine = jnp.concatenate([mine, shift(mine, "xl", 1)], 0)
        above = shift(mine, "z", -1)
        below = shift(mine, "z", 1)
        act2 = shift(above[:, :hid], "z", -1)
        grad2 = shift(below[:, hid:], "z", 1)
        act = jnp.concatenate([mine[:, :hid], above[:, :hid], act2, below[:, :hid]], 0)
        grad = jnp.concatenate([mine[:, hid:], above[:, hid:], grad2, below[:, hid:]], 0)
        return act, grad

    def input_part(grad):
        part = dot(grad, wi, 1, 1)
        return part[:, :feat] + shift(part[:, feat:], "core", 1)

    tok_a, cot_a = chip_features(near)
    tok_b, cot_b = chip_features(far)
    mine_a = hidden(tok_a, cot_a)
    mine_b = hidden(tok_b, cot_b)
    act_b, grad_b = spread(mine_b)
    act_a, grad_a = spread(mine_a)
    in_b = shift(input_part(grad_b).astype(BF16), "xh", 1)
    in_a = input_part(grad_a) + in_b.astype(F32)
    in_a = in_a.reshape(4, 2, 4, piece, feat).transpose(2, 0, 1, 3, 4)
    total = in_a[0]
    for d in (1, 2, 3):
        total = total + shift(in_a[d].astype(BF16), "y", d).astype(F32)
    input_grad = relative(total, 1).reshape(rows, feat).astype(BF16)

    wi_grad = (dot(tok_b, grad_b, 0, 0) + dot(tok_a, grad_a, 0, 0)).astype(BF16)
    wo_grad = (dot(act_b, cot_b, 0, 0) + dot(act_a, cot_a, 0, 0)).astype(BF16)
    w_in_grad = swap_halves(wi_grad[:feat], shift(wi_grad[feat:], "core", 1), core, 1)
    w_out_grad = swap_halves(wo_grad[:, :feat], shift(wo_grad[:, feat:], "core", 1), core, 0)
    return (input_grad, w_in_grad, w_out_grad)


def solution(mesh):
    fine = Mesh(mesh.devices.reshape(SIZES), AXES)
    return jax.shard_map(
        local,
        mesh=fine,
        in_specs=(P(ROWS, COLS), P(ROWS, COLS), P(COLS, ROWS), P(ROWS, COLS)),
        out_specs=(P(ROWS, COLS), P(COLS, ROWS), P(ROWS, COLS)),
        check_vma=False,
    )
```

time: 407 us -> 198 us (0.49)
  waiting for transfers between devices: 269 us -> 120 us
  blocking collectives: 76.6 us -> 0 us
  starting transfers between devices: 0.38 us -> 43.2 us
  matrix products: 36.5 us -> 19.7 us
  between operations: 13.8 us -> 1.5 us
  other arithmetic: 4.18 us -> 9.91 us
    reduce_scatter x3 -> x0, waiting for transfers between devices: 202 us -> none  [the longest x1 84.4 us: local(): lax.psum_scatter(jnp.dot(piece, w_in, preferred_element_type=jnp.float32)...]
    ppermute x0 -> x36, waiting for transfers between devices: none -> 120 us  [shift(): return lax.ppermute(x, axis, [(i, (i + by) % n) for i in range(n)])]
    all_gather x2 -> x0, blocking collectives: 76.6 us -> none  [the longest x1 39.2 us: local(): lax.all_gather(tokens, 'row', axis=0, tiled=True)]
    all_gather x2 -> x0, waiting for transfers between devices: 66.9 us -> none  [the longest x1 40.8 us: local(): lax.all_gather(pre_grad, 'col', axis=0, tiled=True)]
    ppermute x0 -> x36, starting transfers between devices: none -> 43.2 us  [shift(): return lax.ppermute(x, axis, [(i, (i + by) % n) for i in range(n)])]
    dot_general x5 -> x22, matrix products: 36.5 us -> 19.7 us  [dot(): lax.dot_general(a, b, (((da,), (db,)), ((), ())), preferred_element_type=...]
    concatenate x0 -> x16, other arithmetic: none -> 6.86 us  [the longest x2 3.38 us: swap_halves(): jnp.concatenate([jnp.where(flag == 0, first, second), jnp.where(flag == 0...]
    unnamed x9 -> x38, local copies, waits for them, and re-layouts: 6.13 us -> 0.08 us
  transfers between devices with their start and end apart: 5 -> 36, of which waited for: 5 -> 19; matrix products, arithmetic and copies ran while one was open for 8% -> 16% of each run, Pallas kernels for 0% -> 0%
where the time goes in v1:
time: 198 us
  waiting for transfers between devices  120 us (61%)
  starting transfers between devices  43.2 us (22%)
  matrix products  19.7 us (10%)
  other arithmetic  9.91 us (5%)
  local copies, waits for them, and re-layouts  3.34 us (2%)
    ppermute x36, waiting for transfers between devices, shift(): return lax.ppermute(x, axis, [(i, (i + by) % n) for i in range(n)])  120 us
    ppermute x36, starting transfers between devices, shift(): return lax.ppermute(x, axis, [(i, (i + by) % n) for i in range(n)])  43.2 us
    dot_general x22, matrix products, dot(): lax.dot_general(a, b, (((da,), (db,)), ((), ())), preferred_element_type=...  19.7 us
  transfers between devices with their start and end apart: 36, of which 19 were waited for; matrix products, arithmetic and copies ran while one was open for 16% of the time, Pallas kernels for 0%

profile of v1, /device:TPU:0, one launch (start us, length us, event | category | flops | bytes accessed | tf_op | source)
XLA Modules:
  0.0 198.2 jit_solution(5970695969356293371)
XLA Ops:
  0.7 1.0 pad_maximum_fusion.29
  1.8 3.2 %collective-permute-start = (bf16[4,2,16,768]{3,2,1,0:T(8,128)(2,1)S(1)}, bf16[4,2,16,768]{3,2,1,0:T(8,128)(2,1)S(1)}, u32[]{:S(2)}, u32[]{:S(2)}) collective-permute-start(bf16[4,2,16,768]{3,2,1,0:T(8,128)(2,1)S(1)} %fusion.43), channel_id=1, source_target_pairs={{0,96},{32,0},{64,32},{96,64},{1,97},{33,1},{65,33},{97,65},{2,98}... | collective-permute-start | bytes 589832 | tf_op jit(solution)/shard_map/ppermute | solution.py:23
  5.0 0.6 collective-permute-start.1
  5.6 1.0 collective-permute-start.2
  6.6 2.0 %constant_dynamic-slice_fusion.1 = (bf16[1536,384]{1,0:T(8,128)(2,1)S(1)}, bf16[1536,384]{1,0:T(8,128)(2,1)S(1)}) fusion(bf16[3072,384]{1,0:T(8,128)(2,1)} %param.7, s32[]{:T(128)S(6)} %select_n.79, s32[]{:T(128)S(6)} %select_n.80), kind=kLoop, calls=%fused_computation.169 | loop fusion | bytes 4718600 | tf_op jit(solution)/shard_map/dynamic_slice | solution.py:51
  8.8 4.6 %collective-permute-done = bf16[4,2,16,768]{3,2,1,0:T(8,128)(2,1)S(1)} collective-permute-done((bf16[4,2,16,768]{3,2,1,0:T(8,128)(2,1)S(1)}, bf16[4,2,16,768]{3,2,1,0:T(8,128)(2,1)S(1)}, u32[]{:S(2)}, u32[]{:S(2)}) %collective-permute-start) | collective-permute-done | bytes 196640 | tf_op jit(solution)/shard_map/ppermute | solution.py:23
  13.4 1.0 collective-permute-done.1
  14.4 2.7 %collective-permute-done.2 = bf16[4,2,16,768]{3,2,1,0:T(8,128)(2,1)S(1)} collective-permute-done((bf16[4,2,16,768]{3,2,1,0:T(8,128)(2,1)S(1)}, bf16[4,2,16,768]{3,2,1,0:T(8,128)(2,1)S(1)}, u32[]{:S(2)}, u32[]{:S(2)}) %collective-permute-start.2) | collective-permute-done | bytes 196640 | tf_op jit(solution)/shard_map/ppermute | solution.py:23
  17.5 0.6 collective-permute-start.4
  18.0 3.0 %collective-permute-start.16 = (bf16[512,768]{1,0:T(8,128)(2,1)S(1)}, bf16[512,768]{1,0:T(8,128)(2,1)S(1)}, u32[]{:S(2)}, u32[]{:S(2)}) collective-permute-start(bf16[512,768]{1,0:T(8,128)(2,1)S(1)} %bitcast.40), channel_id=1, source_target_pairs={{0,16},{16,0},{1,17},{17,1},{2,18},{18,2},{3,19},{19,3},{4,20},{20... | collective-permute-start | bytes 2359304 | tf_op jit(solution)/shard_map/ppermute | solution.py:23
  21.3 0.9 convolution_convert_fusion.4
  22.2 4.1 %collective-permute-start.8 = (bf16[128,1536]{1,0:T(8,128)(2,1)S(1)}, bf16[128,1536]{1,0:T(8,128)(2,1)S(1)}, u32[]{:S(2)}, u32[]{:S(2)}) collective-permute-start(bf16[128,1536]{1,0:T(8,128)(2,1)S(1)} %convolution_convert_fusion.4), channel_id=1, source_target_pairs={{0,6},{2,0},{4,2},{6,4},{1,7},{3,1},{5,3},{7,5},{8,14},{10,8},{12,... | collective-permute-start | bytes 1179656 | tf_op jit(solution)/shard_map/ppermute | solution.py:23
  26.3 12.8 %collective-permute-done.16 = bf16[512,768]{1,0:T(8,128)(2,1)S(1)} collective-permute-done((bf16[512,768]{1,0:T(8,128)(2,1)S(1)}, bf16[512,768]{1,0:T(8,128)(2,1)S(1)}, u32[]{:S(2)}, u32[]{:S(2)}) %collective-permute-start.16) | collective-permute-done | bytes 786464 | tf_op jit(solution)/shard_map/ppermute | solution.py:23
  39.3 0.5 convolution_convert_fusion.7
  39.8 2.0 %collective-permute-start.5 = (bf16[128,1536]{1,0:T(8,128)(2,1)S(1)}, bf16[128,1536]{1,0:T(8,128)(2,1)S(1)}, u32[]{:S(2)}, u32[]{:S(2)}) collective-permute-start(bf16[128,1536]{1,0:T(8,128)(2,1)S(1)} %convolution_convert_fusion.7), channel_id=1, source_target_pairs={{0,2},{2,4},{4,6},{6,0},{1,3},{3,5},{5,7},{7,1},{8,10},{10,12},{12... | collective-permute-start | bytes 1179656 | tf_op jit(solution)/shard_map/ppermute | solution.py:23
  42.2 0.9 convolution_convert_fusion.6
  43.2 0.9 fusion.5
  44.2 2.2 %collective-permute-start.9 = (bf16[128,3072]{1,0:T(8,128)(2,1)S(1)}, bf16[128,3072]{1,0:T(8,128)(2,1)S(1)}, u32[]{:S(2)}, u32[]{:S(2)}) collective-permute-start(bf16[128,3072]{1,0:T(8,128)(2,1)S(1)} %pad_maximum_fusion.16), channel_id=1, source_target_pairs={{0,6},{2,0},{4,2},{6,4},{1,7},{3,1},{5,3},{7,5},{8,14},{10,8},{12,... | collective-permute-start | bytes 2359304 | tf_op jit(solution)/shard_map/ppermute | solution.py:23
  46.4 7.3 %collective-permute-done.5 = bf16[128,1536]{1,0:T(8,128)(2,1)S(1)} collective-permute-done((bf16[128,1536]{1,0:T(8,128)(2,1)S(1)}, bf16[128,1536]{1,0:T(8,128)(2,1)S(1)}, u32[]{:S(2)}, u32[]{:S(2)}) %collective-permute-start.5) | collective-permute-done | bytes 393248 | tf_op jit(solution)/shard_map/ppermute | solution.py:23
  53.7 0.5 fusion.4
  54.3 0.9 convolution_convert_fusion
  55.2 1.8 collective-permute-start.20
  58.5 0.9 convolution_convert_fusion.2
  59.4 13.1 %collective-permute-done.20 = bf16[128,1536]{1,0:T(8,128)(2,1)S(1)} collective-permute-done((bf16[128,1536]{1,0:T(8,128)(2,1)S(1)}, bf16[128,1536]{1,0:T(8,128)(2,1)S(1)}, u32[]{:S(2)}, u32[]{:S(2)}) %collective-permute-start.20) | collective-permute-done | bytes 393248 | tf_op jit(solution)/shard_map/ppermute | solution.py:23
  72.5 0.9 fusion.7
  73.5 3.5 %collective-permute-start.21 = (bf16[128,3072]{1,0:T(8,128)(2,1)S(1)}, bf16[128,3072]{1,0:T(8,128)(2,1)S(1)}, u32[]{:S(2)}, u32[]{:S(2)}) collective-permute-start(bf16[128,3072]{1,0:T(8,128)(2,1)S(1)} %pad_maximum_fusion.19), channel_id=1, source_target_pairs={{0,6},{2,0},{4,2},{6,4},{1,7},{3,1},{5,3},{7,5},{8,14},{10,8},{12,... | collective-permute-start | bytes 2359304 | tf_op jit(solution)/shard_map/ppermute | solution.py:23
  77.0 1.8 collective-permute-done.7
  78.8 0.9 fusion.2
  79.7 0.5 fusion.3
  80.3 1.7 collective-permute-start.10
  82.1 3.5 %collective-permute-done.18 = bf16[128,1536]{1,0:T(8,128)(2,1)S(1)} collective-permute-done((bf16[128,1536]{1,0:T(8,128)(2,1)S(1)}, bf16[128,1536]{1,0:T(8,128)(2,1)S(1)}, u32[]{:S(2)}, u32[]{:S(2)}) %collective-permute-start.18) | collective-permute-done | bytes 393248 | tf_op jit(solution)/shard_map/ppermute | solution.py:23
  86.3 3.3 %collective-permute-done.10 = bf16[64,3072]{1,0:T(8,128)(2,1)S(1)} collective-permute-done((bf16[64,3072]{1,0:T(8,128)(2,1)S(1)}, bf16[64,3072]{1,0:T(8,128)(2,1)S(1)}, u32[]{:S(2)}, u32[]{:S(2)}) %collective-permute-start.10) | collective-permute-done | bytes 393248 | tf_op jit(solution)/shard_map/ppermute | solution.py:23
  89.8 1.6 collective-permute-start.11
  91.4 2.3 %collective-permute-done.21 = bf16[128,3072]{1,0:T(8,128)(2,1)S(1)} collective-permute-done((bf16[128,3072]{1,0:T(8,128)(2,1)S(1)}, bf16[128,3072]{1,0:T(8,128)(2,1)S(1)}, u32[]{:S(2)}, u32[]{:S(2)}) %collective-permute-start.21) | collective-permute-done | bytes 786464 | tf_op jit(solution)/shard_map/ppermute | solution.py:23
  93.7 11.7 %collective-permute-done.19 = bf16[128,3072]{1,0:T(8,128)(2,1)S(1)} collective-permute-done((bf16[128,3072]{1,0:T(8,128)(2,1)S(1)}, bf16[128,3072]{1,0:T(8,128)(2,1)S(1)}, u32[]{:S(2)}, u32[]{:S(2)}) %collective-permute-start.19) | collective-permute-done | bytes 786464 | tf_op jit(solution)/shard_map/ppermute | solution.py:23
  105.4 0.9 fusion
  106.4 0.5 fusion.1
  106.9 0.8 pad_maximum_fusion.23
  107.7 1.5 collective-permute-start.22
  109.2 1.1 pad_maximum_fusion.17
  110.3 3.2 %collective-permute-start.12 = (bf16[128,3072]{1,0:T(8,128)(2,1)S(1)}, bf16[128,3072]{1,0:T(8,128)(2,1)S(1)}, u32[]{:S(2)}, u32[]{:S(2)}) collective-permute-start(bf16[128,3072]{1,0:T(8,128)(2,1)S(1)} %pad_maximum_fusion.17), channel_id=1, source_target_pairs={{0,6},{2,0},{4,2},{6,4},{1,7},{3,1},{5,3},{7,5},{8,14},{10,8},{12,... | collective-permute-start | bytes 2359304 | tf_op jit(solution)/shard_map/ppermute | solution.py:23
  113.5 3.1 %collective-permute-done.22 = bf16[64,3072]{1,0:T(8,128)(2,1)} collective-permute-done((bf16[64,3072]{1,0:T(8,128)(2,1)}, bf16[64,3072]{1,0:T(8,128)(2,1)}, u32[]{:S(2)}, u32[]{:S(2)}) %collective-permute-start.22) | collective-permute-done | bytes 393248 | tf_op jit(solution)/shard_map/ppermute | solution.py:23
  116.6 1.3 multiply_convert_fusion
  117.9 1.6 collective-permute-start.23
  119.5 6.2 %collective-permute-done.23 = bf16[64,3072]{1,0:T(8,128)(2,1)S(1)} collective-permute-done((bf16[64,3072]{1,0:T(8,128)(2,1)S(1)}, bf16[64,3072]{1,0:T(8,128)(2,1)S(1)}, u32[]{:S(2)}, u32[]{:S(2)}) %collective-permute-start.23) | collective-permute-done | bytes 393248 | tf_op jit(solution)/shard_map/ppermute | solution.py:23
  125.9 5.0 %collective-permute-done.13 = bf16[128,3072]{1,0:T(8,128)(2,1)S(1)} collective-permute-done((bf16[128,3072]{1,0:T(8,128)(2,1)S(1)}, bf16[128,3072]{1,0:T(8,128)(2,1)S(1)}, u32[]{:S(2)}, u32[]{:S(2)}) %collective-permute-start.13) | collective-permute-done | bytes 786464 | tf_op jit(solution)/shard_map/ppermute | solution.py:23
  131.1 3.3 %collective-permute-start.34 = (bf16[128,1536]{1,0:T(8,128)(2,1)S(1)}, bf16[128,1536]{1,0:T(8,128)(2,1)S(1)}, u32[]{:S(2)}, u32[]{:S(2)}) collective-permute-start(bf16[128,1536]{1,0:T(8,128)(2,1)S(1)} %get-tuple-element.23), channel_id=1, source_target_pairs={{0,6},{2,0},{4,2},{6,4},{1,7},{3,1},{5,3},{7,5},{8,14},{10,8},{12,... | collective-permute-start | bytes 1179656 | tf_op jit(solution)/shard_map/ppermute | solution.py:23
  134.6 19.0 %collective-permute-done.14 = bf16[128,1536]{1,0:T(8,128)(2,1)S(1)} collective-permute-done((bf16[128,1536]{1,0:T(8,128)(2,1)S(1)}, bf16[128,1536]{1,0:T(8,128)(2,1)S(1)}, u32[]{:S(2)}, u32[]{:S(2)}) %collective-permute-start.14) | collective-permute-done | bytes 393248 | tf_op jit(solution)/shard_map/ppermute | solution.py:23
  153.6 1.4 fusion.39
  155.1 1.4 fusion.15
  156.8 12.6 %collective-permute-done.26 = bf16[128,1536]{1,0:T(8,128)(2,1)S(1)} collective-permute-done((bf16[128,1536]{1,0:T(8,128)(2,1)S(1)}, bf16[128,1536]{1,0:T(8,128)(2,1)S(1)}, u32[]{:S(2)}, u32[]{:S(2)}) %collective-permute-start.26) | collective-permute-done | bytes 393248 | tf_op jit(solution)/shard_map/ppermute | solution.py:23
  169.4 1.4 fusion.38
  171.1 1.4 fusion.23
  172.8 1.5 add_convert_fusion.1
  174.4 0.6 collective-permute-start.32
  175.1 2.8 %collective-permute-start.28 = (bf16[512,384]{1,0:T(8,128)(2,1)S(1)}, bf16[512,384]{1,0:T(8,128)(2,1)S(1)}, u32[]{:S(2)}, u32[]{:S(2)}) collective-permute-start(bf16[512,384]{1,0:T(8,128)(2,1)S(1)} %fusion.24), channel_id=1, source_target_pairs={{0,16},{16,0},{1,17},{17,1},{2,18},{18,2},{3,19},{19,3},{4,20},{20... | collective-permute-start | bytes 1179656 | tf_op jit(solution)/shard_map/ppermute | solution.py:23
  177.8 6.4 %collective-permute-done.33 = bf16[128,1536]{1,0:T(8,128)(2,1)S(1)} collective-permute-done((bf16[128,1536]{1,0:T(8,128)(2,1)S(1)}, bf16[128,1536]{1,0:T(8,128)(2,1)S(1)}, u32[]{:S(2)}, u32[]{:S(2)}) %collective-permute-start.33) | collective-permute-done | bytes 393248 | tf_op jit(solution)/shard_map/ppermute | solution.py:23
  184.3 1.5 add_convert_fusion
  186.0 1.7 collective-permute-done.28
  188.0 3.2 %collective-permute-start.31 = (bf16[4,2,16,384]{3,2,1,0:T(8,128)(2,1)S(1)}, bf16[4,2,16,384]{3,2,1,0:T(8,128)(2,1)S(1)}, u32[]{:S(2)}, u32[]{:S(2)}) collective-permute-start(bf16[4,2,16,384]{3,2,1,0:T(8,128)(2,1)S(1)} %get-tuple-element.36), channel_id=1, source_target_pairs={{0,96},{32,0},{64,32},{96,64},{1,97},{33,1},{65,33},{97,65},{2,98}... | collective-permute-start | bytes 294920 | tf_op jit(solution)/shard_map/ppermute | solution.py:23
  191.4 1.7 pad_maximum_fusion.2
  193.3 1.6 pad_maximum_fusion.3
  195.0 2.3 %collective-permute-done.30 = bf16[4,2,16,384]{3,2,1,0:T(8,128)(2,1)S(1)} collective-permute-done((bf16[4,2,16,384]{3,2,1,0:T(8,128)(2,1)S(1)}, bf16[4,2,16,384]{3,2,1,0:T(8,128)(2,1)S(1)}, u32[]{:S(2)}, u32[]{:S(2)}) %collective-permute-start.30) | collective-permute-done | bytes 98336 | tf_op jit(solution)/shard_map/ppermute | solution.py:23
  197.5 0.7 fusion.41
  (116 shorter events, 6.9 us)
Async XLA Ops:
  1.8 11.5 %collective-permute-start = (bf16[4,2,16,768]{3,2,1,0:T(8,128)(2,1)S(1)}, bf16[4,2,16,768]{3,2,1,0:T(8,128)(2,1)S(1)}, u32[]{:S(2)}, u32[]{:S(2)}) collective-permute-start(bf16[4,2,16,768]{3,2,1,0:T(8,128)(2,1)S(1)} %fusion.43), channel_id=1, source_target_pairs={{0,96},{32,0},{64,32},{96,64},{1,97},{33,1},{65,33},{97,65},{2,98}... | collective-permute-start | bytes 589832 | tf_op jit(solution)/shard_map/ppermute | solution.py:23
  5.0 9.4 %collective-permute-start.1 = (bf16[4,2,16,768]{3,2,1,0:T(8,128)(2,1)S(1)}, bf16[4,2,16,768]{3,2,1,0:T(8,128)(2,1)S(1)}, u32[]{:S(2)}, u32[]{:S(2)}) collective-permute-start(bf16[4,2,16,768]{3,2,1,0:T(8,128)(2,1)S(1)} %fusion.43), channel_id=1, source_target_pairs={{0,64},{32,96},{64,0},{96,32},{1,65},{33,97},{65,1},{97,33},{2,66}... | collective-permute-start | bytes 589832 | tf_op jit(solution)/shard_map/ppermute | solution.py:23
  5.6 11.4 %collective-permute-start.2 = (bf16[4,2,16,768]{3,2,1,0:T(8,128)(2,1)S(1)}, bf16[4,2,16,768]{3,2,1,0:T(8,128)(2,1)S(1)}, u32[]{:S(2)}, u32[]{:S(2)}) collective-permute-start(bf16[4,2,16,768]{3,2,1,0:T(8,128)(2,1)S(1)} %fusion.43), channel_id=1, source_target_pairs={{0,32},{32,64},{64,96},{96,0},{1,33},{33,65},{65,97},{97,1},{2,34}... | collective-permute-start | bytes 589832 | tf_op jit(solution)/shard_map/ppermute | solution.py:23
  6.6 10.7 %copy-start = (bf16[384,3072]{1,0:T(8,128)(2,1)S(1)}, bf16[384,3072]{1,0:T(8,128)(2,1)}, u32[]{:S(2)}) copy-start(bf16[384,3072]{1,0:T(8,128)(2,1)} %param.6) | copy-start | bytes 7077892
  8.6 12.7 %collective-permute-start.6 = (bf16[1536,384]{1,0:T(8,128)(2,1)S(1)}, bf16[1536,384]{1,0:T(8,128)(2,1)S(1)}, u32[]{:S(2)}, u32[]{:S(2)}) collective-permute-start(bf16[1536,384]{1,0:T(8,128)(2,1)S(1)} %get-tuple-element.10), channel_id=1, source_target_pairs={{0,1},{1,0},{2,3},{3,2},{4,5},{5,4},{6,7},{7,6},{8,9},{9,8},{10,11... | collective-permute-start | bytes 3538952 | tf_op jit(solution)/shard_map/ppermute | solution.py:23
  17.2 4.0 %collective-permute-start.3 = (bf16[512,768]{1,0:T(8,128)(2,1)S(1)}, bf16[512,768]{1,0:T(8,128)(2,1)S(1)}, u32[]{:S(2)}, u32[]{:S(2)}) collective-permute-start(bf16[512,768]{1,0:T(8,128)(2,1)S(1)} %bitcast.39), channel_id=1, source_target_pairs={{0,1},{1,0},{2,3},{3,2},{4,5},{5,4},{6,7},{7,6},{8,9},{9,8},{10,11... | collective-permute-start | bytes 2359304 | tf_op jit(solution)/shard_map/ppermute | solution.py:23
  17.5 21.8 %collective-permute-start.4 = (bf16[384,1536]{1,0:T(8,128)(2,1)S(1)}, bf16[384,1536]{1,0:T(8,128)(2,1)S(1)}, u32[]{:S(2)}, u32[]{:S(2)}) collective-permute-start(bf16[384,1536]{1,0:T(8,128)(2,1)S(1)} %get-tuple-element.8), channel_id=1, source_target_pairs={{0,1},{1,0},{2,3},{3,2},{4,5},{5,4},{6,7},{7,6},{8,9},{9,8},{10,11... | collective-permute-start | bytes 3538952 | tf_op jit(solution)/shard_map/ppermute | solution.py:23
  18.0 21.0 %collective-permute-start.16 = (bf16[512,768]{1,0:T(8,128)(2,1)S(1)}, bf16[512,768]{1,0:T(8,128)(2,1)S(1)}, u32[]{:S(2)}, u32[]{:S(2)}) collective-permute-start(bf16[512,768]{1,0:T(8,128)(2,1)S(1)} %bitcast.40), channel_id=1, source_target_pairs={{0,16},{16,0},{1,17},{17,1},{2,18},{18,2},{3,19},{19,3},{4,20},{20... | collective-permute-start | bytes 2359304 | tf_op jit(solution)/shard_map/ppermute | solution.py:23
  21.1 57.7 %copy-start.11 = (bf16[512,384]{1,0:T(8,128)(2,1)}, bf16[512,384]{1,0:T(8,128)(2,1)S(1)}, u32[]{:S(2)}) copy-start(bf16[512,384]{1,0:T(8,128)(2,1)S(1)} %get-tuple-element.34) | copy-start | bytes 1179652
  21.1 58.6 %copy-start.3 = (bf16[512,384]{1,0:T(8,128)(2,1)}, bf16[512,384]{1,0:T(8,128)(2,1)S(1)}, u32[]{:S(2)}) copy-start(bf16[512,384]{1,0:T(8,128)(2,1)S(1)} %get-tuple-element.33) | copy-start | bytes 1179652
  21.3 57.5 %copy-start.13 = (bf16[512,384]{1,0:T(8,128)(2,1)}, bf16[512,384]{1,0:T(8,128)(2,1)S(1)}, u32[]{:S(2)}) copy-start(bf16[512,384]{1,0:T(8,128)(2,1)S(1)} %get-tuple-element.32) | copy-start | bytes 1179652
  21.3 58.5 %copy-start.5 = (bf16[512,384]{1,0:T(8,128)(2,1)}, bf16[512,384]{1,0:T(8,128)(2,1)S(1)}, u32[]{:S(2)}) copy-start(bf16[512,384]{1,0:T(8,128)(2,1)S(1)} %get-tuple-element.31) | copy-start | bytes 1179652
  22.2 21.0 %collective-permute-start.8 = (bf16[128,1536]{1,0:T(8,128)(2,1)S(1)}, bf16[128,1536]{1,0:T(8,128)(2,1)S(1)}, u32[]{:S(2)}, u32[]{:S(2)}) collective-permute-start(bf16[128,1536]{1,0:T(8,128)(2,1)S(1)} %convolution_convert_fusion.4), channel_id=1, source_target_pairs={{0,6},{2,0},{4,2},{6,4},{1,7},{3,1},{5,3},{7,5},{8,14},{10,8},{12,... | collective-permute-start | bytes 1179656 | tf_op jit(solution)/shard_map/ppermute | solution.py:23
  39.2 66.3 %copy-start.1 = (bf16[512,384]{1,0:T(8,128)(2,1)}, bf16[512,384]{1,0:T(8,128)(2,1)S(1)}, u32[]{:S(2)}) copy-start(bf16[512,384]{1,0:T(8,128)(2,1)S(1)} %get-tuple-element.30) | copy-start | bytes 1179652
  39.2 67.2 %copy-start.7 = (bf16[512,384]{1,0:T(8,128)(2,1)}, bf16[512,384]{1,0:T(8,128)(2,1)S(1)}, u32[]{:S(2)}) copy-start(bf16[512,384]{1,0:T(8,128)(2,1)S(1)} %get-tuple-element.29) | copy-start | bytes 1179652
  39.2 15.0 %collective-permute-start.17 = (bf16[512,768]{1,0:T(8,128)(2,1)S(1)}, bf16[512,768]{1,0:T(8,128)(2,1)S(1)}, u32[]{:S(2)}, u32[]{:S(2)}) collective-permute-start(bf16[512,768]{1,0:T(8,128)(2,1)S(1)} %collective-permute-done.16), channel_id=1, source_target_pairs={{0,1},{1,0},{2,3},{3,2},{4,5},{5,4},{6,7},{7,6},{8,9},{9,8},{10,11... | collective-permute-start | bytes 2359304 | tf_op jit(solution)/shard_map/ppermute | solution.py:23
  39.3 67.1 %copy-start.17 = (bf16[384,1536]{1,0:T(8,128)(2,1)}, bf16[384,1536]{1,0:T(8,128)(2,1)S(1)}, u32[]{:S(2)}) copy-start(bf16[384,1536]{1,0:T(8,128)(2,1)S(1)} %collective-permute-done.4) | copy-start | bytes 3538948
  39.8 13.9 %collective-permute-start.5 = (bf16[128,1536]{1,0:T(8,128)(2,1)S(1)}, bf16[128,1536]{1,0:T(8,128)(2,1)S(1)}, u32[]{:S(2)}, u32[]{:S(2)}) collective-permute-start(bf16[128,1536]{1,0:T(8,128)(2,1)S(1)} %convolution_convert_fusion.7), channel_id=1, source_target_pairs={{0,2},{2,4},{4,6},{6,0},{1,3},{3,5},{5,7},{7,1},{8,10},{10,12},{12... | collective-permute-start | bytes 1179656 | tf_op jit(solution)/shard_map/ppermute | solution.py:23
  44.2 32.8 %collective-permute-start.9 = (bf16[128,3072]{1,0:T(8,128)(2,1)S(1)}, bf16[128,3072]{1,0:T(8,128)(2,1)S(1)}, u32[]{:S(2)}, u32[]{:S(2)}) collective-permute-start(bf16[128,3072]{1,0:T(8,128)(2,1)S(1)} %pad_maximum_fusion.16), channel_id=1, source_target_pairs={{0,6},{2,0},{4,2},{6,4},{1,7},{3,1},{5,3},{7,5},{8,14},{10,8},{12,... | collective-permute-start | bytes 2359304 | tf_op jit(solution)/shard_map/ppermute | solution.py:23
  54.2 51.2 %copy-start.9 = (bf16[512,384]{1,0:T(8,128)(2,1)}, bf16[512,384]{1,0:T(8,128)(2,1)S(1)}, u32[]{:S(2)}) copy-start(bf16[512,384]{1,0:T(8,128)(2,1)S(1)} %get-tuple-element.28) | copy-start | bytes 1179652
  54.2 52.1 %copy-start.15 = (bf16[512,384]{1,0:T(8,128)(2,1)}, bf16[512,384]{1,0:T(8,128)(2,1)S(1)}, u32[]{:S(2)}) copy-start(bf16[512,384]{1,0:T(8,128)(2,1)S(1)} %get-tuple-element.27) | copy-start | bytes 1179652
  55.2 17.3 %collective-permute-start.20 = (bf16[128,1536]{1,0:T(8,128)(2,1)S(1)}, bf16[128,1536]{1,0:T(8,128)(2,1)S(1)}, u32[]{:S(2)}, u32[]{:S(2)}) collective-permute-start(bf16[128,1536]{1,0:T(8,128)(2,1)S(1)} %convolution_convert_fusion), channel_id=1, source_target_pairs={{0,6},{2,0},{4,2},{6,4},{1,7},{3,1},{5,3},{7,5},{8,14},{10,8},{12,... | collective-permute-start | bytes 1179656 | tf_op jit(solution)/shard_map/ppermute | solution.py:23
  57.0 21.8 %collective-permute-start.7 = (bf16[128,3072]{1,0:T(8,128)(2,1)S(1)}, bf16[128,3072]{1,0:T(8,128)(2,1)S(1)}, u32[]{:S(2)}, u32[]{:S(2)}) collective-permute-start(bf16[128,3072]{1,0:T(8,128)(2,1)S(1)} %pad_maximum_fusion.15), channel_id=1, source_target_pairs={{0,2},{2,4},{4,6},{6,0},{1,3},{3,5},{5,7},{7,1},{8,10},{10,12},{12... | collective-permute-start | bytes 2359304 | tf_op jit(solution)/shard_map/ppermute | solution.py:23
  57.9 27.7 %collective-permute-start.18 = (bf16[128,1536]{1,0:T(8,128)(2,1)S(1)}, bf16[128,1536]{1,0:T(8,128)(2,1)S(1)}, u32[]{:S(2)}, u32[]{:S(2)}) collective-permute-start(bf16[128,1536]{1,0:T(8,128)(2,1)S(1)} %convolution_convert_fusion.3), channel_id=1, source_target_pairs={{0,2},{2,4},{4,6},{6,0},{1,3},{3,5},{5,7},{7,1},{8,10},{10,12},{12... | collective-permute-start | bytes 1179656 | tf_op jit(solution)/shard_map/ppermute | solution.py:23
  73.5 20.2 %collective-permute-start.21 = (bf16[128,3072]{1,0:T(8,128)(2,1)S(1)}, bf16[128,3072]{1,0:T(8,128)(2,1)S(1)}, u32[]{:S(2)}, u32[]{:S(2)}) collective-permute-start(bf16[128,3072]{1,0:T(8,128)(2,1)S(1)} %pad_maximum_fusion.19), channel_id=1, source_target_pairs={{0,6},{2,0},{4,2},{6,4},{1,7},{3,1},{5,3},{7,5},{8,14},{10,8},{12,... | collective-permute-start | bytes 2359304 | tf_op jit(solution)/shard_map/ppermute | solution.py:23
  80.3 9.2 %collective-permute-start.10 = (bf16[64,3072]{1,0:T(8,128)(2,1)S(1)}, bf16[64,3072]{1,0:T(8,128)(2,1)S(1)}, u32[]{:S(2)}, u32[]{:S(2)}) collective-permute-start(bf16[64,3072]{1,0:T(8,128)(2,1)S(1)} %pad_maximum_fusion.21), channel_id=1, source_target_pairs={{0,8},{8,0},{1,9},{9,1},{2,10},{10,2},{3,11},{11,3},{4,12},{12,4},... | collective-permute-start | bytes 1179656 | tf_op jit(solution)/shard_map/ppermute | solution.py:23
  86.2 19.2 %collective-permute-start.19 = (bf16[128,3072]{1,0:T(8,128)(2,1)S(1)}, bf16[128,3072]{1,0:T(8,128)(2,1)S(1)}, u32[]{:S(2)}, u32[]{:S(2)}) collective-permute-start(bf16[128,3072]{1,0:T(8,128)(2,1)S(1)} %pad_maximum_fusion.18), channel_id=1, source_target_pairs={{0,2},{2,4},{4,6},{6,0},{1,3},{3,5},{5,7},{7,1},{8,10},{10,12},{12... | collective-permute-start | bytes 2359304 | tf_op jit(solution)/shard_map/ppermute | solution.py:23
  89.8 19.4 %collective-permute-start.11 = (bf16[64,3072]{1,0:T(8,128)(2,1)S(1)}, bf16[64,3072]{1,0:T(8,128)(2,1)}, u32[]{:S(2)}, u32[]{:S(2)}) collective-permute-start(bf16[64,3072]{1,0:T(8,128)(2,1)S(1)} %pad_maximum_fusion.22), channel_id=1, source_target_pairs={{0,8},{8,0},{1,9},{9,1},{2,10},{10,2},{3,11},{11,3},{4,12},{12,4},... | collective-permute-start | bytes 1179656 | tf_op jit(solution)/shard_map/ppermute | solution.py:23
  107.7 8.9 %collective-permute-start.22 = (bf16[64,3072]{1,0:T(8,128)(2,1)}, bf16[64,3072]{1,0:T(8,128)(2,1)}, u32[]{:S(2)}, u32[]{:S(2)}) collective-permute-start(bf16[64,3072]{1,0:T(8,128)(2,1)} %pad_maximum_fusion.23), channel_id=1, source_target_pairs={{0,8},{8,0},{1,9},{9,1},{2,10},{10,2},{3,11},{11,3},{4,12},{12,4},... | collective-permute-start | bytes 1179656 | tf_op jit(solution)/shard_map/ppermute | solution.py:23
  110.2 20.7 %collective-permute-start.13 = (bf16[128,3072]{1,0:T(8,128)(2,1)S(1)}, bf16[128,3072]{1,0:T(8,128)(2,1)S(1)}, u32[]{:S(2)}, u32[]{:S(2)}) collective-permute-start(bf16[128,3072]{1,0:T(8,128)(2,1)S(1)} %pad_maximum_fusion.17), channel_id=1, source_target_pairs={{0,2},{2,4},{4,6},{6,0},{1,3},{3,5},{5,7},{7,1},{8,10},{10,12},{12... | collective-permute-start | bytes 2359304 | tf_op jit(solution)/shard_map/ppermute | solution.py:23
  110.3 20.8 %collective-permute-start.12 = (bf16[128,3072]{1,0:T(8,128)(2,1)S(1)}, bf16[128,3072]{1,0:T(8,128)(2,1)S(1)}, u32[]{:S(2)}, u32[]{:S(2)}) collective-permute-start(bf16[128,3072]{1,0:T(8,128)(2,1)S(1)} %pad_maximum_fusion.17), channel_id=1, source_target_pairs={{0,6},{2,0},{4,2},{6,4},{1,7},{3,1},{5,3},{7,5},{8,14},{10,8},{12,... | collective-permute-start | bytes 2359304 | tf_op jit(solution)/shard_map/ppermute | solution.py:23
  117.9 7.9 %collective-permute-start.23 = (bf16[64,3072]{1,0:T(8,128)(2,1)S(1)}, bf16[64,3072]{1,0:T(8,128)(2,1)S(1)}, u32[]{:S(2)}, u32[]{:S(2)}) collective-permute-start(bf16[64,3072]{1,0:T(8,128)(2,1)S(1)} %pad_maximum_fusion.24), channel_id=1, source_target_pairs={{0,8},{8,0},{1,9},{9,1},{2,10},{10,2},{3,11},{11,3},{4,12},{12,4},... | collective-permute-start | bytes 1179656 | tf_op jit(solution)/shard_map/ppermute | solution.py:23
  125.9 27.7 %copy-start.18 = (bf16[384,1536]{1,0:T(8,128)(2,1)S(1)}, bf16[384,1536]{1,0:T(8,128)(2,1)}, u32[]{:S(2)}) copy-start(bf16[384,1536]{1,0:T(8,128)(2,1)} %copy-done.17) | copy-start | bytes 3538948
  125.9 30.7 %collective-permute-start.25 = (bf16[128,3072]{1,0:T(8,128)(2,1)S(1)}, bf16[128,3072]{1,0:T(8,128)(2,1)S(1)}, u32[]{:S(2)}, u32[]{:S(2)}) collective-permute-start(bf16[128,3072]{1,0:T(8,128)(2,1)S(1)} %pad_maximum_fusion.20), channel_id=1, source_target_pairs={{0,2},{2,4},{4,6},{6,0},{1,3},{3,5},{5,7},{7,1},{8,10},{10,12},{12... | collective-permute-start | bytes 2359304 | tf_op jit(solution)/shard_map/ppermute | solution.py:23
  131.0 22.6 %collective-permute-start.14 = (bf16[128,1536]{1,0:T(8,128)(2,1)S(1)}, bf16[128,1536]{1,0:T(8,128)(2,1)S(1)}, u32[]{:S(2)}, u32[]{:S(2)}) collective-permute-start(bf16[128,1536]{1,0:T(8,128)(2,1)S(1)} %get-tuple-element.26), channel_id=1, source_target_pairs={{0,2},{2,4},{4,6},{6,0},{1,3},{3,5},{5,7},{7,1},{8,10},{10,12},{12... | collective-permute-start | bytes 1179656 | tf_op jit(solution)/shard_map/ppermute | solution.py:23
  131.1 24.0 %collective-permute-start.34 = (bf16[128,1536]{1,0:T(8,128)(2,1)S(1)}, bf16[128,1536]{1,0:T(8,128)(2,1)S(1)}, u32[]{:S(2)}, u32[]{:S(2)}) collective-permute-start(bf16[128,1536]{1,0:T(8,128)(2,1)S(1)} %get-tuple-element.23), channel_id=1, source_target_pairs={{0,6},{2,0},{4,2},{6,4},{1,7},{3,1},{5,3},{7,5},{8,14},{10,8},{12,... | collective-permute-start | bytes 1179656 | tf_op jit(solution)/shard_map/ppermute | solution.py:23
  134.5 22.3 %collective-permute-start.24 = (bf16[128,3072]{1,0:T(8,128)(2,1)S(1)}, bf16[128,3072]{1,0:T(8,128)(2,1)S(1)}, u32[]{:S(2)}, u32[]{:S(2)}) collective-permute-start(bf16[128,3072]{1,0:T(8,128)(2,1)S(1)} %pad_maximum_fusion.20), channel_id=1, source_target_pairs={{0,6},{2,0},{4,2},{6,4},{1,7},{3,1},{5,3},{7,5},{8,14},{10,8},{12,... | collective-permute-start | bytes 2359304 | tf_op jit(solution)/shard_map/ppermute | solution.py:23
  153.5 1.6 copy-start.12
  153.6 1.6 copy-start.14
  155.0 31.0 %collective-permute-start.15 = (f32[512,384]{1,0:T(8,128)S(1)}, f32[512,384]{1,0:T(8,128)S(1)}, u32[]{:S(2)}, u32[]{:S(2)}) collective-permute-start(f32[512,384]{1,0:T(8,128)S(1)} %slice.333), channel_id=1, source_target_pairs={{0,1},{1,0},{2,3},{3,2},{4,5},{5,4},{6,7},{7,6},{8,9},{9,8},{10,11... | collective-permute-start | bytes 2359304 | tf_op jit(solution)/shard_map/ppermute | solution.py:23
  156.7 12.8 %collective-permute-start.26 = (bf16[128,1536]{1,0:T(8,128)(2,1)S(1)}, bf16[128,1536]{1,0:T(8,128)(2,1)S(1)}, u32[]{:S(2)}, u32[]{:S(2)}) collective-permute-start(bf16[128,1536]{1,0:T(8,128)(2,1)S(1)} %get-tuple-element.20), channel_id=1, source_target_pairs={{0,2},{2,4},{4,6},{6,0},{1,3},{3,5},{5,7},{7,1},{8,10},{10,12},{12... | collective-permute-start | bytes 1179656 | tf_op jit(solution)/shard_map/ppermute | solution.py:23
  169.4 1.6 copy-start.4
  169.4 1.6 copy-start.6
  170.9 1.9 copy-start.8
  170.9 1.9 copy-start.16
  170.9 4.0 %collective-permute-start.27 = (f32[512,384]{1,0:T(8,128)S(1)}, f32[512,384]{1,0:T(8,128)S(1)}, u32[]{:S(2)}, u32[]{:S(2)}) collective-permute-start(f32[512,384]{1,0:T(8,128)S(1)} %slice.368), channel_id=1, source_target_pairs={{0,1},{1,0},{2,3},{3,2},{4,5},{5,4},{6,7},{7,6},{8,9},{9,8},{10,11... | collective-permute-start | bytes 2359304 | tf_op jit(solution)/shard_map/ppermute | solution.py:23
  172.5 11.8 %collective-permute-start.33 = (bf16[128,1536]{1,0:T(8,128)(2,1)S(1)}, bf16[128,1536]{1,0:T(8,128)(2,1)S(1)}, u32[]{:S(2)}, u32[]{:S(2)}) collective-permute-start(bf16[128,1536]{1,0:T(8,128)(2,1)S(1)} %get-tuple-element.17), channel_id=1, source_target_pairs={{0,6},{2,0},{4,2},{6,4},{1,7},{3,1},{5,3},{7,5},{8,14},{10,8},{12,... | collective-permute-start | bytes 1179656 | tf_op jit(solution)/shard_map/ppermute | solution.py:23
  174.3 10.0 %copy-start.2 = (bf16[512,384]{1,0:T(8,128)(2,1)S(1)}, bf16[512,384]{1,0:T(8,128)(2,1)}, u32[]{:S(2)}) copy-start(bf16[512,384]{1,0:T(8,128)(2,1)} %copy-done.1) | copy-start | bytes 1179652
  174.3 10.0 %copy-start.10 = (bf16[512,384]{1,0:T(8,128)(2,1)S(1)}, bf16[512,384]{1,0:T(8,128)(2,1)}, u32[]{:S(2)}) copy-start(bf16[512,384]{1,0:T(8,128)(2,1)} %copy-done.9) | copy-start | bytes 1179652
  174.4 16.8 %collective-permute-start.32 = (bf16[384,1536]{1,0:T(8,128)(2,1)S(1)}, bf16[384,1536]{1,0:T(8,128)(2,1)S(1)}, u32[]{:S(2)}, u32[]{:S(2)}) collective-permute-start(bf16[384,1536]{1,0:T(8,128)(2,1)S(1)} %slice.374), channel_id=1, source_target_pairs={{0,1},{1,0},{2,3},{3,2},{4,5},{5,4},{6,7},{7,6},{8,9},{9,8},{10,11... | collective-permute-start | bytes 3538952 | tf_op jit(solution)/shard_map/ppermute | solution.py:23
  175.1 12.6 %collective-permute-start.28 = (bf16[512,384]{1,0:T(8,128)(2,1)S(1)}, bf16[512,384]{1,0:T(8,128)(2,1)S(1)}, u32[]{:S(2)}, u32[]{:S(2)}) collective-permute-start(bf16[512,384]{1,0:T(8,128)(2,1)S(1)} %fusion.24), channel_id=1, source_target_pairs={{0,16},{16,0},{1,17},{17,1},{2,18},{18,2},{3,19},{19,3},{4,20},{20... | collective-permute-start | bytes 1179656 | tf_op jit(solution)/shard_map/ppermute | solution.py:23
  185.9 7.2 %collective-permute-start.35 = (bf16[1536,384]{1,0:T(8,128)(2,1)S(1)}, bf16[1536,384]{1,0:T(8,128)(2,1)S(1)}, u32[]{:S(2)}, u32[]{:S(2)}) collective-permute-start(bf16[1536,384]{1,0:T(8,128)(2,1)S(1)} %slice.382), channel_id=1, source_target_pairs={{0,1},{1,0},{2,3},{3,2},{4,5},{5,4},{6,7},{7,6},{8,9},{9,8},{10,11... | collective-permute-start | bytes 3538952 | tf_op jit(solution)/shard_map/ppermute | solution.py:23
  187.9 7.1 %collective-permute-start.29 = (bf16[4,2,16,384]{3,2,1,0:T(8,128)(2,1)S(1)}, bf16[4,2,16,384]{3,2,1,0:T(8,128)(2,1)S(1)}, u32[]{:S(2)}, u32[]{:S(2)}) collective-permute-start(bf16[4,2,16,384]{3,2,1,0:T(8,128)(2,1)S(1)} %get-tuple-element.35), channel_id=1, source_target_pairs={{0,32},{32,64},{64,96},{96,0},{1,33},{33,65},{65,97},{97,1},{2,34}... | collective-permute-start | bytes 294920 | tf_op jit(solution)/shard_map/ppermute | solution.py:23
  188.0 7.0 %collective-permute-start.31 = (bf16[4,2,16,384]{3,2,1,0:T(8,128)(2,1)S(1)}, bf16[4,2,16,384]{3,2,1,0:T(8,128)(2,1)S(1)}, u32[]{:S(2)}, u32[]{:S(2)}) collective-permute-start(bf16[4,2,16,384]{3,2,1,0:T(8,128)(2,1)S(1)} %get-tuple-element.36), channel_id=1, source_target_pairs={{0,96},{32,0},{64,32},{96,64},{1,97},{33,1},{65,33},{97,65},{2,98}... | collective-permute-start | bytes 294920 | tf_op jit(solution)/shard_map/ppermute | solution.py:23
  191.2 6.1 %collective-permute-start.30 = (bf16[4,2,16,384]{3,2,1,0:T(8,128)(2,1)S(1)}, bf16[4,2,16,384]{3,2,1,0:T(8,128)(2,1)S(1)}, u32[]{:S(2)}, u32[]{:S(2)}) collective-permute-start(bf16[4,2,16,384]{3,2,1,0:T(8,128)(2,1)S(1)} %get-tuple-element.37), channel_id=1, source_target_pairs={{0,64},{32,96},{64,0},{96,32},{1,65},{33,97},{65,1},{97,33},{2,66}... | collective-permute-start | bytes 294920 | tf_op jit(solution)/shard_map/ppermute | solution.py:23

commit v2 on v0

v2 whole, which is shorter than its diff:
```python
import jax
import jax.numpy as jnp
from jax import lax
from jax.experimental import pallas as pl
from jax.experimental.pallas import tpu as pltpu
from jax.sharding import Mesh
from jax.sharding import PartitionSpec as P

AXES = ("y", "xh", "xl", "z", "core")
SIZES = (4, 2, 2, 4, 2)
ROWS = ("y", "xh")
COLS = ("xl", "z", "core")
F32 = jnp.float32
BF16 = jnp.bfloat16
STEPS = 3


def gelu_parts(pre):
    cdf = 0.5 * (1.0 + lax.erf(pre * 0.7071067811865476))
    pdf = jnp.exp(-0.5 * pre * pre) * 0.3989422804014327
    return (cdf, pdf)


def shift(x, axis, by):
    n = SIZES[AXES.index(axis)]
    return lax.ppermute(x, axis, [(i, (i + by) % n) for i in range(n)])


def dot(a, b, da, db):
    return lax.dot_general(a, b, (((da,), (db,)), ((), ())), preferred_element_type=F32)


def gate(value, *after):
    return lax.optimization_barrier((value, after))[0]


COST = dict(pack=1, weights=1, join=0.1, products=0.1, ring_add=0.1, own_sum=0.1, hidden=0.1, pass_on=0.1, input_part=0.1, return_pieces=0.1, return_far=10, weight_grads=0.1, all_grads=10)


def kernel(name, body, grid, ins, outs, scratch=(), scalar=None):
    def spec(block, index):
        def at(i, *refs):
            return tuple(i if k == "i" else k(i, refs[0][0]) if callable(k) else k for k in index)

        return pl.BlockSpec(block, at)

    def run(*refs):
        body(*(refs if scalar is None else refs[1:]))

    return pl.pallas_call(
        run,
        name=name,
        grid_spec=pltpu.PrefetchScalarGridSpec(
            num_scalar_prefetch=0 if scalar is None else 1,
            grid=(grid,),
            in_specs=[spec(block, index) for _, block, index in ins],
            out_specs=[spec(block, index) for _, _, block, index in outs],
            scratch_shapes=list(scratch),
        ),
        out_shape=[jax.ShapeDtypeStruct(shape, dtype) for shape, dtype, _, _ in outs],
        cost_estimate=pl.CostEstimate(flops=0, bytes_accessed=int(COST[name] * 3.69e6), transcendentals=0),
        compiler_params=pltpu.CompilerParams(vmem_limit_bytes=24 * 2**20),
    )(*([] if scalar is None else [scalar]), *[a for a, _, _ in ins])


def pack(w_in, w_out, core):
    feat = w_in.shape[0]
    half = w_out.shape[0] // feat // 2

    def body(wi, wo, out):
        out[0, 0] = wi[...]
        out[1, 0] = wo[...]

    block = (feat, feat)
    place = lambda i, c: (1 - c) * half + i
    return kernel(
        "pack",
        body,
        half,
        [(w_in, block, (0, place)), (w_out, block, (place, 0))],
        [((2, half, feat, feat), BF16, (2, 1, feat, feat), (0, "i", 0, 0))],
        scalar=core,
    )[0]


def weights(w_in, w_out, got, core):
    feat = w_in.shape[0]
    half = w_out.shape[0] // feat // 2

    def body(wi, wo, got, wi_out, wo_out):
        wi_out[:feat] = wi[...]
        wi_out[feat:] = got[0, 0]
        wo_out[:, :feat] = wo[...]
        wo_out[:, feat:] = got[1, 0]

    block = (feat, feat)
    place = lambda i, c: c * half + i
    return kernel(
        "weights",
        body,
        half,
        [(w_in, block, (0, place)), (w_out, block, (place, 0)), (got, (2, 1, feat, feat), (0, "i", 0, 0))],
        [
            ((2 * feat, half * feat), BF16, (2 * feat, feat), (0, "i")),
            ((half * feat, 2 * feat), BF16, (feat, 2 * feat), ("i", 0)),
        ],
        scalar=core,
    )


def join(pieces, others):
    zs, piece, width = pieces[0].shape
    count = len(pieces)
    per = count * piece

    def body(*refs):
        for out, side in zip(refs[-2:], (refs[:count], refs[count:])):
            for k in range(zs):
                for j in range(count):
                    out[pl.ds(k * per + j * piece, piece), :] = side[j][k]

    return kernel(
        "join",
        body,
        1,
        [(a, (zs, piece, width), (0, 0, 0)) for a in (*pieces, *others)],
        [((zs * per, width), BF16, (zs * per, width), (0, 0))] * 2,
    )


def pass_on(above, below):
    _, per, hid = above.shape

    def body(above, below, act, grad):
        act[...] = above[0]
        grad[...] = below[0]

    return kernel(
        "pass_on",
        body,
        1,
        [(above, (1, per, hid), (0, 0, 0)), (below, (1, per, hid), (1, 0, 0))],
        [((per, hid), BF16, (per, hid), (0, 0))] * 2,
    )


def products(own, other, wi, wo):
    rows, width = own.shape
    feat, hid = wi.shape
    half, per, block = width // 2, rows // 4, hid // STEPS

    def body(own, other, wi, wo, pg, up, down, tok, cot):
        @pl.when(pl.program_id(0) == 0)
        def _():
            for side, ref in enumerate((own, other)):
                tok[:, side * half : (side + 1) * half] = ref[:, :half]
                cot[:, side * half : (side + 1) * half] = ref[:, half:]

        p = jnp.dot(tok[...], wi[...], preferred_element_type=F32)
        g = dot(cot[...], wo[...], 1, 1)
        pg[0] = p
        pg[1] = g
        up[...] = p[2 * per : 3 * per].astype(BF16)
        down[...] = g[2 * per : 3 * per].astype(BF16)

    whole = (rows, width)
    return kernel(
        "products",
        body,
        STEPS,
        [(own, whole, (0, 0)), (other, whole, (0, 0)), (wi, (feat, block), (0, "i")), (wo, (block, feat), ("i", 0))],
        [
            ((2, rows, hid), F32, (2, rows, block), (0, 0, "i")),
            ((per, hid), BF16, (per, block), (0, "i")),
            ((per, hid), BF16, (per, block), (0, "i")),
            ((rows, feat), BF16, (rows, feat), (0, 0)),
            ((rows, feat), BF16, (rows, feat), (0, 0)),
        ],
    )


def ring_add(pg, up, down):
    per, hid = up.shape
    block = hid // STEPS

    def body(one, three, up, down, up_out, down_out):
        up_out[0] = (one[0] + up[...].astype(F32)).astype(BF16)
        up_out[1] = one[1].astype(BF16)
        down_out[0] = three[0].astype(BF16)
        down_out[1] = (three[1] + down[...].astype(F32)).astype(BF16)

    part = (2, per, block)
    return kernel(
        "ring_add",
        body,
        STEPS,
        [(pg, part, (0, 1, "i")), (pg, part, (0, 3, "i")), (up, (per, block), (0, "i")), (down, (per, block), (0, "i"))],
        [((2, per, hid), BF16, part, (0, 0, "i"))] * 2,
    )


def own_sum(pg, up, down):
    _, per, hid = up.shape
    part = (2, per, hid // STEPS)

    def body(zero, up, down, out, sent):
        total = zero[...] + up[...].astype(F32) + down[...].astype(F32)
        out[...] = total
        sent[...] = total.astype(BF16)

    return kernel(
        "own_sum",
        body,
        STEPS,
        [(pg, part, (0, 0, "i")), (up, part, (0, 0, "i")), (down, part, (0, 0, "i"))],
        [((2, per, hid), F32, part, (0, 0, "i")), ((2, per, hid), BF16, part, (0, 0, "i"))],
    )


def hidden(total, other):
    _, per, hid = total.shape
    part = (2, per, hid // STEPS)

    def body(total, other, out):
        pre = total[0] + other[0].astype(F32)
        act_grad = total[1] + other[1].astype(F32)
        cdf, pdf = gelu_parts(pre)
        out[0] = (pre * cdf).astype(BF16)
        out[1] = (act_grad * (cdf + pre * pdf)).astype(BF16)

    return kernel(
        "hidden",
        body,
        STEPS,
        [(total, part, (0, 0, "i")), (other, part, (0, 0, "i"))],
        [((2, per, hid), BF16, part, (0, 0, "i"))],
    )[0]


def input_part(mine, above, grad2, below, wi):
    _, per, hid = mine.shape
    feat = wi.shape[0]
    half = feat // 2

    def body(mine, above, grad2, below, wi, own, other):
        for k, grad in enumerate((mine.at[0], above.at[0], grad2, below.at[0])):
            part = dot(grad[...], wi[...], 1, 1)
            own[k * per : (k + 1) * per] = part[:, :half]
            other[k * per : (k + 1) * per] = part[:, half:]

    second, whole = (1, per, hid), (4 * per, half)
    return kernel(
        "input_part",
        body,
        1,
        [
            (mine, second, (1, 0, 0)),
            (above, second, (1, 0, 0)),
            (grad2, (per, hid), (0, 0)),
            (below, second, (1, 0, 0)),
            (wi, (feat, hid), (0, 0)),
        ],
        [(whole, F32, whole, (0, 0))] * 2,
    )


def return_pieces(name, mine, other, pieces, kinds):
    rows, feat = mine.shape
    piece = rows // 4 // pieces

    def body(mine, other, *outs):
        for k in range(4):
            for j, out in enumerate(outs):
                at = pl.ds((k * pieces + j) * piece, piece)
                out[k] = (mine[at, :] + other[at, :]).astype(out.dtype)

    return kernel(
        name,
        body,
        1,
        [(mine, (rows, feat), (0, 0)), (other, (rows, feat), (0, 0))],
        [((4, piece, feat), kind, (4, piece, feat), (0, 0, 0)) for kind in kinds],
    )


def weight_grads(toks, cots, blocks, side, other=None, core=None):
    rows, feat = toks[0].shape
    _, per, hid = blocks[0][0].shape
    half, block, chunks = feat // 2, hid // STEPS, len(toks)
    both = other is not None

    def body(*refs):
        toks, cots = refs[:chunks], refs[chunks : 2 * chunks]
        parts = refs[2 * chunks : -6]
        wi_out, wo_out, tok, cot, act, grad = refs[-6:]
        step = pl.program_id(0)

        @pl.when(step == 0)
        def _():
            for c in range(chunks):
                tok[c * rows : (c + 1) * rows] = toks[c][...]
                cot[c * rows : (c + 1) * rows] = cots[c][...]

        @pl.when(step < STEPS)
        def _():
            for k in range(4 * chunks):
                a, g = parts[2 * k : 2 * k + 2]
                at = pl.ds(k * per, per)
                act[at, :] = a[0] if len(a.shape) == 3 else a[...]
                grad[at, :] = g[0] if len(g.shape) == 3 else g[...]
            wi_out[...] = dot(tok[...], grad[...], 0, 0).astype(BF16)
            wo_out[...] = dot(act[...], cot[...], 0, 0).astype(BF16)

        if both:

            @pl.when(step >= STEPS)
            def _():
                wi_out[...] = parts[-2][...]
                wo_out[...] = parts[-1][...]

    if both:
        at = lambda i, c: jnp.minimum(i, STEPS - 1)
        late = lambda i, c: jnp.maximum(i - STEPS, 0)
        out = lambda i, c: jnp.where(i < STEPS, c * STEPS + i, (1 - c) * STEPS + i - STEPS)
    else:
        at = out = "i"
    ins = [(a, (rows, half), (0, side)) for a in (*toks, *cots)]
    for mine, above, act2, grad2, below in blocks:
        for pair in (mine, above, (act2, grad2), below):
            if isinstance(pair, tuple):
                ins += [(a, (per, block), (0, at)) for a in pair]
            else:
                ins += [(pair, (1, per, block), (k, 0, at)) for k in (0, 1)]
    if both:
        ins += [(other[0], (half, block), (0, late)), (other[1], (block, half), (late, 0))]
    cols = 2 * hid if both else hid
    return kernel(
        "all_grads" if both else "weight_grads",
        body,
        2 * STEPS if both else STEPS,
        ins,
        [((half, cols), BF16, (half, block), (0, out)), ((cols, half), BF16, (block, half), (out, 0))],
        [pltpu.VMEM((chunks * rows, half), BF16)] * 2 + [pltpu.VMEM((chunks * rows, block), BF16)] * 2,
        core,
    )


def local(tokens, cotangent, w_in, w_out):
    z, core = lax.axis_index("z"), lax.axis_index("core")
    rows, feat = tokens.shape
    hid = w_in.shape[1] // 2
    piece = rows // 4

    def relative(a, sign):
        return jnp.roll(a.reshape(4, piece, a.shape[-1]), sign * z, 0)

    def to_core(parts):
        return [shift(a, "core", 1) for a in parts]

    def up_down(up, down):
        return shift(up, "z", 1), shift(down, "z", -1)

    def send_mine(mine):
        return shift(mine, "z", -1), shift(mine, "z", 1)

    def send_on(above, below):
        act, grad = pass_on(above, below)
        return shift(act, "z", -1), shift(grad, "z", 1)

    place = jnp.reshape(core, (1,)).astype(jnp.int32)
    packed = pack(w_in, w_out, place)
    got = shift(packed, "core", 1)
    own = relative(jnp.concatenate([tokens, cotangent], 1), -1)
    across = shift(own, "xh", 1)
    near = [shift(own, "y", -d) for d in (1, 2, 3)]
    across = gate(across, packed)
    far = [shift(across, "y", -d) for d in (1, 2, 3)]
    near = [own, *gate(near, across)]
    near = join(near, to_core(near))
    wi, wo = weights(w_in, w_out, got, place)

    pg_a, up_a, down_a, tok_a, cot_a = products(*near, wi, wo)
    r_a = up_down(up_a, down_a)

    far = [across, *gate(far, up_a)]
    far = join(far, to_core(far))
    pg_b, up_b, down_b, tok_b, cot_b = products(*far, wi, wo)
    r_b = up_down(up_b, down_b)

    m_a = ring_add(pg_a, *gate(r_a, up_b))
    r_a = up_down(*m_a)
    m_b = ring_add(pg_b, *gate(r_b, m_a))
    r_b = up_down(*m_b)

    t_a, m_a = own_sum(pg_a, *gate(r_a, m_b))
    x_a = shift(m_a, "xl", 1)
    t_b, m_b = own_sum(pg_b, *gate(r_b, m_a))
    x_b = shift(m_b, "xl", 1)

    mine_a = hidden(t_a, gate(x_a, m_b))
    s_a = send_mine(mine_a)
    mine_b = hidden(t_b, gate(x_b, mine_a))
    s_b = send_mine(mine_b)

    s_a = gate(s_a, mine_b)
    f_a = send_on(*s_a)
    s_b = gate(s_b, s_a)
    f_b = send_on(*s_b)

    f_a = gate(f_a, s_b)
    in_a, in_a_other = input_part(mine_a, s_a[0], f_a[1], s_a[1], wi)
    in_a_got = shift(in_a_other, "core", 1)
    kept, *back = return_pieces("return_pieces", in_a, in_a_got, 4, (F32, BF16, BF16, BF16))
    back = [shift(a, "y", d) for d, a in zip((1, 2, 3), back)]

    f_b, back = gate((f_b, back), kept)
    in_b, in_b_other = input_part(mine_b, s_b[0], f_b[1], s_b[1], wi)
    in_b_got = shift(in_b_other, "core", 1)

    blocks = [(mine_a, s_a[0], *f_a, s_a[1]), (mine_b, s_b[0], *f_b, s_b[1])]
    blocks = gate(blocks, in_b_other)
    grads_other = weight_grads([tok_a, tok_b], [cot_a, cot_b], blocks, 1)
    got_other = to_core(grads_other)

    back_far = return_pieces("return_far", in_b, gate(in_b_got, grads_other), 4, (BF16,) * 4)
    got_other = gate(got_other, back_far)
    back_far = [
        lax.ppermute(a, ROWS, [(i, ((i // 2 + d) % 4) * 2 + (i + 1) % 2) for i in range(8)])
        for d, a in enumerate(back_far)
    ]
    w_in_grad, w_out_grad = weight_grads([tok_a, tok_b], [cot_a, cot_b], blocks, 0, got_other, place)

    total = kept
    for part in back + gate(back_far, w_in_grad, w_out_grad):
        total = total + part.astype(F32)
    input_grad = relative(total, 1).reshape(rows, feat).astype(BF16)
    return (input_grad, w_in_grad, w_out_grad)


def solution(mesh):
    fine = Mesh(mesh.devices.reshape(SIZES), AXES)
    return jax.shard_map(
        local,
        mesh=fine,
        in_specs=(P(ROWS, COLS), P(ROWS, COLS), P(COLS, ROWS), P(ROWS, COLS)),
        out_specs=(P(ROWS, COLS), P(COLS, ROWS), P(ROWS, COLS)),
        check_vma=False,
    )
```

time: 407 us -> 210 us (0.52)
  waiting for transfers between devices: 269 us -> 97.2 us
  blocking collectives: 76.6 us -> 0 us
  starting transfers between devices: 0.38 us -> 54 us
  Pallas kernels: 0 us -> 37.5 us
  matrix products: 36.5 us -> 0 us
  between operations: 13.8 us -> 1.14 us
  local copies, waits for them, and re-layouts: 6.13 us -> 17.1 us
    reduce_scatter x3 -> x0, waiting for transfers between devices: 202 us -> none  [the longest x1 84.4 us: local(): lax.psum_scatter(jnp.dot(piece, w_in, preferred_element_type=jnp.float32)...]
    ppermute x0 -> x45, waiting for transfers between devices: none -> 97.2 us  [the longest x41 97.2 us: shift(): return lax.ppermute(x, axis, [(i, (i + by) % n) for i in range(n)])]
    all_gather x2 -> x0, blocking collectives: 76.6 us -> none  [the longest x1 39.2 us: local(): lax.all_gather(tokens, 'row', axis=0, tiled=True)]
    all_gather x2 -> x0, waiting for transfers between devices: 66.9 us -> none  [the longest x1 40.8 us: local(): lax.all_gather(pre_grad, 'col', axis=0, tiled=True)]
    ppermute x0 -> x45, starting transfers between devices: none -> 54 us  [the longest x41 42.2 us: shift(): return lax.ppermute(x, axis, [(i, (i + by) % n) for i in range(n)])]
    pallas_call x0 -> x20, Pallas kernels: none -> 37.5 us  [kernel(): pl.pallas_call(run, name=name, grid_spec=pltpu.PrefetchScalarGridSpec(num...]
    dot_general x5 -> x0, matrix products: 36.5 us -> none  [the longest x1 8.02 us: local(): lax.dot_general(piece, w_out, (((1,), (1,)), ((), ())), preferred_element...]
    unnamed x9 -> x68, local copies, waits for them, and re-layouts: 6.13 us -> 17.1 us
  transfers between devices with their start and end apart: 5 -> 45, of which waited for: 5 -> 23; matrix products, arithmetic and copies ran while one was open for 8% -> 0% of each run, Pallas kernels for 0% -> 11%
where the time goes in v2:
time: 210 us; the launch traced here: 209 us
  waiting for transfers between devices  97.2 us (46%)
  starting transfers between devices  54 us (26%)
  Pallas kernels  37.5 us (18%)
  local copies, waits for them, and re-layouts  17.1 us (8%)
    ppermute x41, waiting for transfers between devices, shift(): return lax.ppermute(x, axis, [(i, (i + by) % n) for i in range(n)])  97.2 us
    ppermute x41, starting transfers between devices, shift(): return lax.ppermute(x, axis, [(i, (i + by) % n) for i in range(n)])  42.2 us
    pallas_call x20, Pallas kernels, kernel(): pl.pallas_call(run, name=name, grid_spec=pltpu.PrefetchScalarGridSpec(num...  37.5 us
    unnamed x68, local copies, waits for them, and re-layouts  17.1 us
    ppermute x4, starting transfers between devices, local(): lax.ppermute(a, ROWS, [(i, (i // 2 + d) % 4 * 2 + (i + 1) % 2) for i in r...  11.8 us
  transfers between devices with their start and end apart: 45, of which 23 were waited for; matrix products, arithmetic and copies ran while one was open for 0% of the time, Pallas kernels for 11%

profile of v2, /device:TPU:0, one launch (start us, length us, event | category | flops | bytes accessed | tf_op | source)
XLA Modules:
  0.0 208.9 jit_solution(6034418665728084532)
XLA Ops:
  0.6 1.7 copy-done.4
  2.3 1.7 copy-done.6
  4.0 2.0 pack.1
  6.2 3.2 %collective-permute-start.3 = (bf16[4,32,768]{2,1,0:T(8,128)(2,1)S(1)}, bf16[4,32,768]{2,1,0:T(8,128)(2,1)S(1)}, u32[]{:S(2)}, u32[]{:S(2)}) collective-permute-start(bf16[4,32,768]{2,1,0:T(8,128)(2,1)S(1)} %fusion.2.refs_0_), channel_id=1, source_target_pairs={{0,16},{16,0},{1,17},{17,1},{2,18},{18,2},{3,19},{19,3},{4,20},{20... | collective-permute-start | bytes 589832 | tf_op jit(solution)/shard_map/ppermute | solution.py:26
  9.3 3.0 %collective-permute-start = (bf16[4,32,768]{2,1,0:T(8,128)(2,1)S(1)}, bf16[4,32,768]{2,1,0:T(8,128)(2,1)S(1)}, u32[]{:S(2)}, u32[]{:S(2)}) collective-permute-start(bf16[4,32,768]{2,1,0:T(8,128)(2,1)S(1)} %fusion.2.refs_0_), channel_id=1, source_target_pairs={{0,96},{32,0},{64,32},{96,64},{1,97},{33,1},{65,33},{97,65},{2,98}... | collective-permute-start | bytes 589832 | tf_op jit(solution)/shard_map/ppermute | solution.py:26
  13.0 1.0 collective-permute-start.2
  14.0 1.1 collective-permute-done.3.refs_0_
  15.0 6.1 %collective-permute-done.refs_1_ = bf16[4,32,768]{2,1,0:T(8,128)(2,1)S(1)} collective-permute-done((bf16[4,32,768]{2,1,0:T(8,128)(2,1)S(1)}, bf16[4,32,768]{2,1,0:T(8,128)(2,1)S(1)}, u32[]{:S(2)}, u32[]{:S(2)}) %collective-permute-start) | collective-permute-done | bytes 196640 | tf_op jit(solution)/shard_map/ppermute | solution.py:26
  21.7 3.1 %collective-permute-done.2.refs_3_ = bf16[4,32,768]{2,1,0:T(8,128)(2,1)S(1)} collective-permute-done((bf16[4,32,768]{2,1,0:T(8,128)(2,1)S(1)}, bf16[4,32,768]{2,1,0:T(8,128)(2,1)S(1)}, u32[]{:S(2)}, u32[]{:S(2)}) %collective-permute-start.2) | collective-permute-done | bytes 196640 | tf_op jit(solution)/shard_map/ppermute | solution.py:26
  26.9 0.8 collective-permute-start.13
  27.9 1.7 copy-done.7
  29.5 2.8 %weights.1 = (bf16[768,1536]{1,0:T(8,128)(2,1)S(1)}, bf16[1536,768]{1,0:T(8,128)(2,1)S(1)}) custom-call(s32[1]{0:T(128)} %bitcast.1.refs_0_, bf16[384,3072]{1,0:T(8,128)(2,1)S(1)} %copy-done.5, bf16[3072,384]{1,0:T(8,128)(2,1)S(1)} %copy-done.7, bf16[2,4,384,384]{3,2,1,0:T(8,128)(2,1)} %collective-permute-done.8.refs_3_), custom_call_target="tpu_custom_call" | custom-call | bytes 3690000 | tf_op jit(solution)/shard_map/weights/pallas_call | solution.py:50
  32.4 3.7 %products.2 = (f32[2,512,1536]{2,1,0:T(8,128)S(1)}, bf16[128,1536]{1,0:T(8,128)(2,1)S(1)}, bf16[128,1536]{1,0:T(8,128)(2,1)S(1)}, bf16[512,768]{1,0:T(8,128)(2,1)S(1)}, bf16[512,768]{1,0:T(8,128)(2,1)S(1)}) custom-call(bf16[512,768]{1,0:T(8,128)(2,1)S(1)} %get-tuple-element.96.refs_0_, bf16[512,768]{1,0:T(8,128)(2,1)S(1)} %get-tuple-element.97.refs_1_, ...), custom_call_target="tpu_custom_call" | custom-call | bytes 369000 | tf_op jit(solution)/shard_map/products/pallas_call | solution.py:50
  36.1 4.1 %collective-permute-start.10 = (bf16[128,1536]{1,0:T(8,128)(2,1)S(1)}, bf16[128,1536]{1,0:T(8,128)(2,1)S(1)}, u32[]{:S(2)}, u32[]{:S(2)}) collective-permute-start(bf16[128,1536]{1,0:T(8,128)(2,1)S(1)} %get-tuple-element.102), channel_id=1, source_target_pairs={{0,6},{2,0},{4,2},{6,4},{1,7},{3,1},{5,3},{7,5},{8,14},{10,8},{12,... | collective-permute-start | bytes 1179656 | tf_op jit(solution)/shard_map/ppermute | solution.py:26
  42.4 3.7 %products.3 = (f32[2,512,1536]{2,1,0:T(8,128)S(1)}, bf16[128,1536]{1,0:T(8,128)(2,1)S(1)}, bf16[128,1536]{1,0:T(8,128)(2,1)S(1)}, bf16[512,768]{1,0:T(8,128)(2,1)S(1)}, bf16[512,768]{1,0:T(8,128)(2,1)S(1)}) custom-call(bf16[512,768]{1,0:T(8,128)(2,1)S(1)} %get-tuple-element.106.refs_0_, bf16[512,768]{1,0:T(8,128)(2,1)S(1)} %get-tuple-element.107.refs_1_, ...), custom_call_target="tpu_custom_call" | custom-call | bytes 369000 | tf_op jit(solution)/shard_map/products/pallas_call | solution.py:50
  46.8 2.7 %collective-permute-start.21 = (bf16[128,1536]{1,0:T(8,128)(2,1)S(1)}, bf16[128,1536]{1,0:T(8,128)(2,1)S(1)}, u32[]{:S(2)}, u32[]{:S(2)}) collective-permute-start(bf16[128,1536]{1,0:T(8,128)(2,1)S(1)} %get-tuple-element.114), channel_id=1, source_target_pairs={{0,6},{2,0},{4,2},{6,4},{1,7},{3,1},{5,3},{7,5},{8,14},{10,8},{12,... | collective-permute-start | bytes 1179656 | tf_op jit(solution)/shard_map/ppermute | solution.py:26
  49.5 3.9 %collective-permute-done.9.refs_2_ = bf16[128,1536]{1,0:T(8,128)(2,1)S(1)} collective-permute-done((bf16[128,1536]{1,0:T(8,128)(2,1)S(1)}, bf16[128,1536]{1,0:T(8,128)(2,1)S(1)}, u32[]{:S(2)}, u32[]{:S(2)}) %collective-permute-start.9) | collective-permute-done | bytes 393248 | tf_op jit(solution)/shard_map/ppermute | solution.py:26
  54.1 3.2 %collective-permute-start.19 = (bf16[2,128,1536]{2,1,0:T(8,128)(2,1)S(1)}, bf16[2,128,1536]{2,1,0:T(8,128)(2,1)S(1)}, u32[]{:S(2)}, u32[]{:S(2)}) collective-permute-start(bf16[2,128,1536]{2,1,0:T(8,128)(2,1)S(1)} %get-tuple-element.112), channel_id=1, source_target_pairs={{0,6},{2,0},{4,2},{6,4},{1,7},{3,1},{5,3},{7,5},{8,14},{10,8},{12,... | collective-permute-start | bytes 2359304 | tf_op jit(solution)/shard_map/ppermute | solution.py:26
  57.3 4.5 %collective-permute-done.20.refs_2_ = bf16[128,1536]{1,0:T(8,128)(2,1)S(1)} collective-permute-done((bf16[128,1536]{1,0:T(8,128)(2,1)S(1)}, bf16[128,1536]{1,0:T(8,128)(2,1)S(1)}, u32[]{:S(2)}, u32[]{:S(2)}) %collective-permute-start.20) | collective-permute-done | bytes 393248 | tf_op jit(solution)/shard_map/ppermute | solution.py:26
  62.6 3.2 %collective-permute-start.24 = (bf16[2,128,1536]{2,1,0:T(8,128)(2,1)S(1)}, bf16[2,128,1536]{2,1,0:T(8,128)(2,1)S(1)}, u32[]{:S(2)}, u32[]{:S(2)}) collective-permute-start(bf16[2,128,1536]{2,1,0:T(8,128)(2,1)S(1)} %get-tuple-element.118), channel_id=1, source_target_pairs={{0,6},{2,0},{4,2},{6,4},{1,7},{3,1},{5,3},{7,5},{8,14},{10,8},{12,... | collective-permute-start | bytes 2359304 | tf_op jit(solution)/shard_map/ppermute | solution.py:26
  65.8 12.9 %collective-permute-done.18.refs_1_ = bf16[2,128,1536]{2,1,0:T(8,128)(2,1)S(1)} collective-permute-done((bf16[2,128,1536]{2,1,0:T(8,128)(2,1)S(1)}, bf16[2,128,1536]{2,1,0:T(8,128)(2,1)S(1)}, u32[]{:S(2)}, u32[]{:S(2)}) %collective-permute-start.18) | collective-permute-done | bytes 786464 | tf_op jit(solution)/shard_map/ppermute | solution.py:26
  80.1 14.8 %collective-permute-done.23.refs_1_ = bf16[2,128,1536]{2,1,0:T(8,128)(2,1)S(1)} collective-permute-done((bf16[2,128,1536]{2,1,0:T(8,128)(2,1)S(1)}, bf16[2,128,1536]{2,1,0:T(8,128)(2,1)S(1)}, u32[]{:S(2)}, u32[]{:S(2)}) %collective-permute-start.23) | collective-permute-done | bytes 786464 | tf_op jit(solution)/shard_map/ppermute | solution.py:26
  95.5 0.9 collective-permute-start.27
  96.4 1.2 collective-permute-done.22.refs_1_
  97.6 0.7 hidden.2.refs_0_.refs_4_.refs_5_.refs_6_
  98.4 0.9 collective-permute-start.25
  99.3 1.2 collective-permute-start.26
  100.5 14.2 %collective-permute-done.27.refs_1_ = bf16[2,128,1536]{2,1,0:T(8,128)(2,1)S(1)} collective-permute-done((bf16[2,128,1536]{2,1,0:T(8,128)(2,1)S(1)}, bf16[2,128,1536]{2,1,0:T(8,128)(2,1)S(1)}, u32[]{:S(2)}, u32[]{:S(2)}) %collective-permute-start.27) | collective-permute-done | bytes 786464 | tf_op jit(solution)/shard_map/ppermute | solution.py:26
  114.7 0.7 hidden.3.refs_0_.refs_12_.refs_13_.refs_14_
  115.4 0.9 collective-permute-start.30
  116.3 1.2 collective-permute-start.31
  117.6 2.1 collective-permute-start.28
  119.7 16.2 %collective-permute-done.30.refs_0_.refs_1_.refs_14_.refs_15_.refs_16_ = bf16[2,128,1536]{2,1,0:T(8,128)(2,1)S(1)} collective-permute-done((bf16[2,128,1536]{2,1,0:T(8,128)(2,1)S(1)}, bf16[2,128,1536]{2,1,0:T(8,128)(2,1)S(1)}, u32[]{:S(2)}, u32[]{:S(2)}) %collective-permute-start.30) | collective-permute-done | bytes 786464 | tf_op jit(solution)/shard_map/ppermute | solution.py:26
  136.0 2.0 collective-permute-done.31.refs_1_.refs_3_.refs_18_.refs_19_.refs_20_
  138.0 3.8 %collective-permute-done.28.refs_8_.refs_9_ = bf16[128,1536]{1,0:T(8,128)(2,1)S(1)} collective-permute-done((bf16[128,1536]{1,0:T(8,128)(2,1)S(1)}, bf16[128,1536]{1,0:T(8,128)(2,1)S(1)}, u32[]{:S(2)}, u32[]{:S(2)}) %collective-permute-start.28) | collective-permute-done | bytes 393248 | tf_op jit(solution)/shard_map/ppermute | solution.py:26
  141.8 1.8 collective-permute-done.29.refs_2_.refs_9_.refs_10_
  143.6 3.1 %input_part.2 = (f32[512,384]{1,0:T(8,128)S(1)}, f32[512,384]{1,0:T(8,128)S(1)}) custom-call(bf16[2,128,1536]{2,1,0:T(8,128)(2,1)S(1)} %hidden.2.refs_0_.refs_4_.refs_5_.refs_6_, bf16[2,128,1536]{2,1,0:T(8,128)(2,1)S(1)} %collective-permute-done.25.refs_0_.refs_1_.refs_6_.refs_7_.refs_8_, ...), custom_call_target="tpu_custom_call" | custom-call | bytes 369000 | tf_op jit(solution)/shard_map/input_part/pallas_call | solution.py:50
  147.2 1.7 collective-permute-start.34
  149.2 2.1 collective-permute-start.35
  151.3 1.9 collective-permute-start.36
  153.1 2.5 %collective-permute-start.37 = (bf16[4,32,384]{2,1,0:T(8,128)(2,1)S(1)}, bf16[4,32,384]{2,1,0:T(8,128)(2,1)S(1)}, u32[]{:S(2)}, u32[]{:S(2)}) collective-permute-start(bf16[4,32,384]{2,1,0:T(8,128)(2,1)S(1)} %get-tuple-element.143), channel_id=1, source_target_pairs={{0,96},{32,0},{64,32},{96,64},{1,97},{33,1},{65,33},{97,65},{2,98}... | collective-permute-start | bytes 294920 | tf_op jit(solution)/shard_map/ppermute | solution.py:26
  155.7 2.8 %collective-permute-done.33.refs_16_.refs_17_ = bf16[128,1536]{1,0:T(8,128)(2,1)S(1)} collective-permute-done((bf16[128,1536]{1,0:T(8,128)(2,1)S(1)}, bf16[128,1536]{1,0:T(8,128)(2,1)S(1)}, u32[]{:S(2)}, u32[]{:S(2)}) %collective-permute-start.33) | collective-permute-done | bytes 393248 | tf_op jit(solution)/shard_map/ppermute | solution.py:26
  158.5 1.3 collective-permute-done.34.refs_2_.refs_17_.refs_18_
  159.8 3.1 %input_part.3 = (f32[512,384]{1,0:T(8,128)S(1)}, f32[512,384]{1,0:T(8,128)S(1)}) custom-call(bf16[2,128,1536]{2,1,0:T(8,128)(2,1)S(1)} %hidden.3.refs_0_.refs_12_.refs_13_.refs_14_, bf16[2,128,1536]{2,1,0:T(8,128)(2,1)S(1)} %collective-permute-done.30.refs_0_.refs_1_.refs_14_.refs_15_.refs_16_, ...), custom_call_target="tpu_custom_call" | custom-call | bytes 369000 | tf_op jit(solution)/shard_map/input_part/pallas_call | solution.py:50
  163.1 5.3 %weight_grads.1 = (bf16[384,1536]{1,0:T(8,128)(2,1)S(1)}, bf16[1536,384]{1,0:T(8,128)(2,1)}) custom-call(bf16[512,768]{1,0:T(8,128)(2,1)S(1)} %get-tuple-element.150.refs_0_.refs_1_, bf16[512,768]{1,0:T(8,128)(2,1)S(1)} %get-tuple-element.151.refs_1_.refs_2_, bf16[512,768]{1,0:T(8,128)(2,1)S(1)} %get-tuple-element.152.refs_2_.refs_3_, ...), custom_call_target="tpu_custom_call" | custom-call | bytes 369000 | tf_op jit(solution)/shard_map/weight_grads/pallas_call | solution.py:50
  168.9 5.1 %collective-permute-done.38.refs_1_ = f32[512,384]{1,0:T(8,128)S(1)} collective-permute-done((f32[512,384]{1,0:T(8,128)S(1)}, f32[512,384]{1,0:T(8,128)S(1)}, u32[]{:S(2)}, u32[]{:S(2)}) %collective-permute-start.38) | collective-permute-done | bytes 786464 | tf_op jit(solution)/shard_map/ppermute | solution.py:26
  174.1 0.8 return_far.1
  174.9 1.2 collective-permute-start.39
  176.1 3.7 %collective-permute-start.40 = (bf16[4,32,384]{2,1,0:T(8,128)(2,1)}, bf16[4,32,384]{2,1,0:T(8,128)(2,1)}, u32[]{:S(2)}, u32[]{:S(2)}) collective-permute-start(bf16[4,32,384]{2,1,0:T(8,128)(2,1)} %get-tuple-element.170), channel_id=1, source_target_pairs={{0,48},{16,32},{32,80},{48,64},{64,112},{80,96},{96,16},{112,0},{1... | collective-permute-start | bytes 294920 | tf_op jit(solution)/shard_map/ppermute | solution.py:428
  179.8 2.6 %collective-permute-start.41 = (bf16[4,32,384]{2,1,0:T(8,128)(2,1)}, bf16[4,32,384]{2,1,0:T(8,128)(2,1)}, u32[]{:S(2)}, u32[]{:S(2)}) collective-permute-start(bf16[4,32,384]{2,1,0:T(8,128)(2,1)} %get-tuple-element.171), channel_id=1, source_target_pairs={{0,80},{16,64},{32,112},{48,96},{64,16},{80,0},{96,48},{112,32},{1... | collective-permute-start | bytes 294920 | tf_op jit(solution)/shard_map/ppermute | solution.py:428
  182.4 1.0 copy-done.22
  183.4 4.2 %collective-permute-start.42 = (bf16[4,32,384]{2,1,0:T(8,128)(2,1)}, bf16[4,32,384]{2,1,0:T(8,128)(2,1)}, u32[]{:S(2)}, u32[]{:S(2)}) collective-permute-start(bf16[4,32,384]{2,1,0:T(8,128)(2,1)} %get-tuple-element.172), channel_id=1, source_target_pairs={{0,112},{16,96},{32,16},{48,0},{64,48},{80,32},{96,80},{112,64},{1... | collective-permute-start | bytes 294920 | tf_op jit(solution)/shard_map/ppermute | solution.py:428
  187.7 1.1 copy-done.1
  188.8 1.1 copy-done.3
  189.9 1.0 copy-done.9
  190.9 1.1 copy-done.11
  192.1 1.1 copy-done.13
  193.2 1.1 copy-done.15
  194.3 1.1 copy-done.17
  195.5 1.0 copy-done.19
  196.5 1.0 copy-done.21
  197.5 1.3 copy-done.23
  198.7 8.2 %all_grads.1 = (bf16[384,3072]{1,0:T(8,128)(2,1)}, bf16[3072,384]{1,0:T(8,128)(2,1)}) custom-call(s32[1]{0:T(128)} %bitcast.1.refs_0_, bf16[512,768]{1,0:T(8,128)(2,1)S(1)} %copy-done.11, bf16[512,768]{1,0:T(8,128)(2,1)S(1)} %copy-done.15, bf16[512,768]{1,0:T(8,128)(2,1)S(1)} %copy-done.13, bf16[512,768]{1,0:T(8,128)(2,1)S(1)} %copy-done.17, ...), custom_call_target="tpu_custom_call" | custom-call | bytes 36900000 | tf_op jit(solution)/shard_map/all_grads/pallas_call | solution.py:50
  207.0 1.1 convert_add_fusion
  (118 shorter events, 12.0 us)
Async XLA Ops:
  4.0 2.1 copy-start.27
  6.0 21.8 %copy-start.5 = (bf16[384,3072]{1,0:T(8,128)(2,1)S(1)}, bf16[384,3072]{1,0:T(8,128)(2,1)}, u32[]{:S(2)}) copy-start(bf16[384,3072]{1,0:T(8,128)(2,1)} %refs_1_.3) | copy-start | bytes 7077892
  6.0 21.8 %collective-permute-start.8 = (bf16[2,4,384,384]{3,2,1,0:T(8,128)(2,1)}, bf16[2,4,384,384]{3,2,1,0:T(8,128)(2,1)}, u32[]{:S(2)}, u32[]{:S(2)}) collective-permute-start(bf16[2,4,384,384]{3,2,1,0:T(8,128)(2,1)} %pack.1), channel_id=1, source_target_pairs={{0,1},{1,0},{2,3},{3,2},{4,5},{5,4},{6,7},{7,6},{8,9},{9,8},{10,11... | collective-permute-start | bytes 7077896 | tf_op jit(solution)/shard_map/ppermute | solution.py:26
  6.2 8.9 %collective-permute-start.3 = (bf16[4,32,768]{2,1,0:T(8,128)(2,1)S(1)}, bf16[4,32,768]{2,1,0:T(8,128)(2,1)S(1)}, u32[]{:S(2)}, u32[]{:S(2)}) collective-permute-start(bf16[4,32,768]{2,1,0:T(8,128)(2,1)S(1)} %fusion.2.refs_0_), channel_id=1, source_target_pairs={{0,16},{16,0},{1,17},{17,1},{2,18},{18,2},{3,19},{19,3},{4,20},{20... | collective-permute-start | bytes 589832 | tf_op jit(solution)/shard_map/ppermute | solution.py:26
  9.3 11.8 %collective-permute-start = (bf16[4,32,768]{2,1,0:T(8,128)(2,1)S(1)}, bf16[4,32,768]{2,1,0:T(8,128)(2,1)S(1)}, u32[]{:S(2)}, u32[]{:S(2)}) collective-permute-start(bf16[4,32,768]{2,1,0:T(8,128)(2,1)S(1)} %fusion.2.refs_0_), channel_id=1, source_target_pairs={{0,96},{32,0},{64,32},{96,64},{1,97},{33,1},{65,33},{97,65},{2,98}... | collective-permute-start | bytes 589832 | tf_op jit(solution)/shard_map/ppermute | solution.py:26
  12.4 9.3 %collective-permute-start.1 = (bf16[4,32,768]{2,1,0:T(8,128)(2,1)S(1)}, bf16[4,32,768]{2,1,0:T(8,128)(2,1)S(1)}, u32[]{:S(2)}, u32[]{:S(2)}) collective-permute-start(bf16[4,32,768]{2,1,0:T(8,128)(2,1)S(1)} %fusion.2.refs_0_), channel_id=1, source_target_pairs={{0,64},{32,96},{64,0},{96,32},{1,65},{33,97},{65,1},{97,33},{2,66}... | collective-permute-start | bytes 589832 | tf_op jit(solution)/shard_map/ppermute | solution.py:26
  13.0 11.8 %collective-permute-start.2 = (bf16[4,32,768]{2,1,0:T(8,128)(2,1)S(1)}, bf16[4,32,768]{2,1,0:T(8,128)(2,1)S(1)}, u32[]{:S(2)}, u32[]{:S(2)}) collective-permute-start(bf16[4,32,768]{2,1,0:T(8,128)(2,1)S(1)} %fusion.2.refs_0_), channel_id=1, source_target_pairs={{0,32},{32,64},{64,96},{96,0},{1,33},{33,65},{65,97},{97,1},{2,34}... | collective-permute-start | bytes 589832 | tf_op jit(solution)/shard_map/ppermute | solution.py:26
  15.0 10.3 %collective-permute-start.4 = (bf16[4,32,768]{2,1,0:T(8,128)(2,1)S(1)}, bf16[4,32,768]{2,1,0:T(8,128)(2,1)S(1)}, u32[]{:S(2)}, u32[]{:S(2)}) collective-permute-start(bf16[4,32,768]{2,1,0:T(8,128)(2,1)S(1)} %fusion.2.refs_0_), channel_id=1, source_target_pairs={{0,1},{1,0},{2,3},{3,2},{4,5},{5,4},{6,7},{7,6},{8,9},{9,8},{10,11... | collective-permute-start | bytes 589832 | tf_op jit(solution)/shard_map/ppermute | solution.py:26
  24.8 1.4 collective-permute-start.5
  24.8 2.1 collective-permute-start.6
  25.3 2.4 %collective-permute-start.7 = (bf16[4,32,768]{2,1,0:T(8,128)(2,1)S(1)}, bf16[4,32,768]{2,1,0:T(8,128)(2,1)S(1)}, u32[]{:S(2)}, u32[]{:S(2)}) collective-permute-start(bf16[4,32,768]{2,1,0:T(8,128)(2,1)S(1)} %collective-permute-done.2.refs_3_), channel_id=1, source_target_pairs={{0,1},{1,0},{2,3},{3,2},{4,5},{5,4},{6,7},{7,6},{8,9},{9,8},{10,11... | collective-permute-start | bytes 589832 | tf_op jit(solution)/shard_map/ppermute | solution.py:26
  25.3 14.9 %collective-permute-start.11 = (bf16[4,32,768]{2,1,0:T(8,128)(2,1)S(1)}, bf16[4,32,768]{2,1,0:T(8,128)(2,1)S(1)}, u32[]{:S(2)}, u32[]{:S(2)}) collective-permute-start(bf16[4,32,768]{2,1,0:T(8,128)(2,1)S(1)} %collective-permute-done.3.refs_0_), channel_id=1, source_target_pairs={{0,96},{32,0},{64,32},{96,64},{1,97},{33,1},{65,33},{97,65},{2,98}... | collective-permute-start | bytes 589832 | tf_op jit(solution)/shard_map/ppermute | solution.py:26
  26.3 14.0 %collective-permute-start.12 = (bf16[4,32,768]{2,1,0:T(8,128)(2,1)S(1)}, bf16[4,32,768]{2,1,0:T(8,128)(2,1)S(1)}, u32[]{:S(2)}, u32[]{:S(2)}) collective-permute-start(bf16[4,32,768]{2,1,0:T(8,128)(2,1)S(1)} %collective-permute-done.3.refs_0_), channel_id=1, source_target_pairs={{0,64},{32,96},{64,0},{96,32},{1,65},{33,97},{65,1},{97,33},{2,66}... | collective-permute-start | bytes 589832 | tf_op jit(solution)/shard_map/ppermute | solution.py:26
  26.9 13.3 %collective-permute-start.13 = (bf16[4,32,768]{2,1,0:T(8,128)(2,1)S(1)}, bf16[4,32,768]{2,1,0:T(8,128)(2,1)S(1)}, u32[]{:S(2)}, u32[]{:S(2)}) collective-permute-start(bf16[4,32,768]{2,1,0:T(8,128)(2,1)S(1)} %collective-permute-done.3.refs_0_), channel_id=1, source_target_pairs={{0,32},{32,64},{64,96},{96,0},{1,33},{33,65},{65,97},{97,1},{2,34}... | collective-permute-start | bytes 589832 | tf_op jit(solution)/shard_map/ppermute | solution.py:26
  27.7 13.1 %collective-permute-start.14 = (bf16[4,32,768]{2,1,0:T(8,128)(2,1)S(1)}, bf16[4,32,768]{2,1,0:T(8,128)(2,1)S(1)}, u32[]{:S(2)}, u32[]{:S(2)}) collective-permute-start(bf16[4,32,768]{2,1,0:T(8,128)(2,1)S(1)} %collective-permute-done.3.refs_0_), channel_id=1, source_target_pairs={{0,1},{1,0},{2,3},{3,2},{4,5},{5,4},{6,7},{7,6},{8,9},{9,8},{10,11... | collective-permute-start | bytes 589832 | tf_op jit(solution)/shard_map/ppermute | solution.py:26
  36.1 126.9 %copy-start.10 = (bf16[512,768]{1,0:T(8,128)(2,1)}, bf16[512,768]{1,0:T(8,128)(2,1)S(1)}, u32[]{:S(2)}) copy-start(bf16[512,768]{1,0:T(8,128)(2,1)S(1)} %get-tuple-element.150.refs_0_.refs_1_) | copy-start | bytes 2359300
  36.1 126.9 %copy-start.12 = (bf16[512,768]{1,0:T(8,128)(2,1)}, bf16[512,768]{1,0:T(8,128)(2,1)S(1)}, u32[]{:S(2)}) copy-start(bf16[512,768]{1,0:T(8,128)(2,1)S(1)} %get-tuple-element.152.refs_2_.refs_3_) | copy-start | bytes 2359300
  36.1 13.4 %collective-permute-start.10 = (bf16[128,1536]{1,0:T(8,128)(2,1)S(1)}, bf16[128,1536]{1,0:T(8,128)(2,1)S(1)}, u32[]{:S(2)}, u32[]{:S(2)}) collective-permute-start(bf16[128,1536]{1,0:T(8,128)(2,1)S(1)} %get-tuple-element.102), channel_id=1, source_target_pairs={{0,6},{2,0},{4,2},{6,4},{1,7},{3,1},{5,3},{7,5},{8,14},{10,8},{12,... | collective-permute-start | bytes 1179656 | tf_op jit(solution)/shard_map/ppermute | solution.py:26
  40.2 13.2 %collective-permute-start.9 = (bf16[128,1536]{1,0:T(8,128)(2,1)S(1)}, bf16[128,1536]{1,0:T(8,128)(2,1)S(1)}, u32[]{:S(2)}, u32[]{:S(2)}) collective-permute-start(bf16[128,1536]{1,0:T(8,128)(2,1)S(1)} %get-tuple-element.101), channel_id=1, source_target_pairs={{0,2},{2,4},{4,6},{6,0},{1,3},{3,5},{5,7},{7,1},{8,10},{10,12},{12... | collective-permute-start | bytes 1179656 | tf_op jit(solution)/shard_map/ppermute | solution.py:26
  40.2 1.5 collective-permute-start.15
  40.6 1.5 collective-permute-start.16
  40.8 1.5 collective-permute-start.17
  46.2 116.8 %copy-start.14 = (bf16[512,768]{1,0:T(8,128)(2,1)}, bf16[512,768]{1,0:T(8,128)(2,1)S(1)}, u32[]{:S(2)}) copy-start(bf16[512,768]{1,0:T(8,128)(2,1)S(1)} %get-tuple-element.151.refs_1_.refs_2_) | copy-start | bytes 2359300
  46.2 116.8 %copy-start.16 = (bf16[512,768]{1,0:T(8,128)(2,1)}, bf16[512,768]{1,0:T(8,128)(2,1)S(1)}, u32[]{:S(2)}) copy-start(bf16[512,768]{1,0:T(8,128)(2,1)S(1)} %get-tuple-element.153.refs_3_.refs_4_) | copy-start | bytes 2359300
  46.2 15.6 %collective-permute-start.20 = (bf16[128,1536]{1,0:T(8,128)(2,1)S(1)}, bf16[128,1536]{1,0:T(8,128)(2,1)S(1)}, u32[]{:S(2)}, u32[]{:S(2)}) collective-permute-start(bf16[128,1536]{1,0:T(8,128)(2,1)S(1)} %get-tuple-element.108), channel_id=1, source_target_pairs={{0,2},{2,4},{4,6},{6,0},{1,3},{3,5},{5,7},{7,1},{8,10},{10,12},{12... | collective-permute-start | bytes 1179656 | tf_op jit(solution)/shard_map/ppermute | solution.py:26
  46.8 15.0 %collective-permute-start.21 = (bf16[128,1536]{1,0:T(8,128)(2,1)S(1)}, bf16[128,1536]{1,0:T(8,128)(2,1)S(1)}, u32[]{:S(2)}, u32[]{:S(2)}) collective-permute-start(bf16[128,1536]{1,0:T(8,128)(2,1)S(1)} %get-tuple-element.114), channel_id=1, source_target_pairs={{0,6},{2,0},{4,2},{6,4},{1,7},{3,1},{5,3},{7,5},{8,14},{10,8},{12,... | collective-permute-start | bytes 1179656 | tf_op jit(solution)/shard_map/ppermute | solution.py:26
  54.0 24.6 %collective-permute-start.18 = (bf16[2,128,1536]{2,1,0:T(8,128)(2,1)S(1)}, bf16[2,128,1536]{2,1,0:T(8,128)(2,1)S(1)}, u32[]{:S(2)}, u32[]{:S(2)}) collective-permute-start(bf16[2,128,1536]{2,1,0:T(8,128)(2,1)S(1)} %get-tuple-element.111), channel_id=1, source_target_pairs={{0,2},{2,4},{4,6},{6,0},{1,3},{3,5},{5,7},{7,1},{8,10},{10,12},{12... | collective-permute-start | bytes 2359304 | tf_op jit(solution)/shard_map/ppermute | solution.py:26
  54.1 24.5 %collective-permute-start.19 = (bf16[2,128,1536]{2,1,0:T(8,128)(2,1)S(1)}, bf16[2,128,1536]{2,1,0:T(8,128)(2,1)S(1)}, u32[]{:S(2)}, u32[]{:S(2)}) collective-permute-start(bf16[2,128,1536]{2,1,0:T(8,128)(2,1)S(1)} %get-tuple-element.112), channel_id=1, source_target_pairs={{0,6},{2,0},{4,2},{6,4},{1,7},{3,1},{5,3},{7,5},{8,14},{10,8},{12,... | collective-permute-start | bytes 2359304 | tf_op jit(solution)/shard_map/ppermute | solution.py:26
  62.5 32.3 %collective-permute-start.23 = (bf16[2,128,1536]{2,1,0:T(8,128)(2,1)S(1)}, bf16[2,128,1536]{2,1,0:T(8,128)(2,1)S(1)}, u32[]{:S(2)}, u32[]{:S(2)}) collective-permute-start(bf16[2,128,1536]{2,1,0:T(8,128)(2,1)S(1)} %get-tuple-element.117), channel_id=1, source_target_pairs={{0,2},{2,4},{4,6},{6,0},{1,3},{3,5},{5,7},{7,1},{8,10},{10,12},{12... | collective-permute-start | bytes 2359304 | tf_op jit(solution)/shard_map/ppermute | solution.py:26
  62.6 32.3 %collective-permute-start.24 = (bf16[2,128,1536]{2,1,0:T(8,128)(2,1)S(1)}, bf16[2,128,1536]{2,1,0:T(8,128)(2,1)S(1)}, u32[]{:S(2)}, u32[]{:S(2)}) collective-permute-start(bf16[2,128,1536]{2,1,0:T(8,128)(2,1)S(1)} %get-tuple-element.118), channel_id=1, source_target_pairs={{0,6},{2,0},{4,2},{6,4},{1,7},{3,1},{5,3},{7,5},{8,14},{10,8},{12,... | collective-permute-start | bytes 2359304 | tf_op jit(solution)/shard_map/ppermute | solution.py:26
  79.4 18.2 %collective-permute-start.22 = (bf16[2,128,1536]{2,1,0:T(8,128)(2,1)S(1)}, bf16[2,128,1536]{2,1,0:T(8,128)(2,1)S(1)}, u32[]{:S(2)}, u32[]{:S(2)}) collective-permute-start(bf16[2,128,1536]{2,1,0:T(8,128)(2,1)S(1)} %get-tuple-element.122), channel_id=1, source_target_pairs={{0,8},{8,0},{1,9},{9,1},{2,10},{10,2},{3,11},{11,3},{4,12},{12,4},... | collective-permute-start | bytes 2359304 | tf_op jit(solution)/shard_map/ppermute | solution.py:26
  95.5 19.1 %collective-permute-start.27 = (bf16[2,128,1536]{2,1,0:T(8,128)(2,1)S(1)}, bf16[2,128,1536]{2,1,0:T(8,128)(2,1)S(1)}, u32[]{:S(2)}, u32[]{:S(2)}) collective-permute-start(bf16[2,128,1536]{2,1,0:T(8,128)(2,1)S(1)} %get-tuple-element.125), channel_id=1, source_target_pairs={{0,8},{8,0},{1,9},{9,1},{2,10},{10,2},{3,11},{11,3},{4,12},{12,4},... | collective-permute-start | bytes 2359304 | tf_op jit(solution)/shard_map/ppermute | solution.py:26
  98.4 64.6 %copy-start = (bf16[2,128,1536]{2,1,0:T(8,128)(2,1)}, bf16[2,128,1536]{2,1,0:T(8,128)(2,1)S(1)}, u32[]{:S(2)}) copy-start(bf16[2,128,1536]{2,1,0:T(8,128)(2,1)S(1)} %hidden.2.refs_0_.refs_4_.refs_5_.refs_6_) | copy-start | bytes 2359300
  98.4 19.1 %collective-permute-start.25 = (bf16[2,128,1536]{2,1,0:T(8,128)(2,1)S(1)}, bf16[2,128,1536]{2,1,0:T(8,128)(2,1)S(1)}, u32[]{:S(2)}, u32[]{:S(2)}) collective-permute-start(bf16[2,128,1536]{2,1,0:T(8,128)(2,1)S(1)} %hidden.2.refs_0_.refs_4_.refs_5_.refs_6_), channel_id=1, source_target_pairs={{0,6},{2,0},{4,2},{6,4},{1,7},{3,1},{5,3},{7,5},{8,14},{10,8},{12,... | collective-permute-start | bytes 2359304 | tf_op jit(solution)/shard_map/ppermute | solution.py:26
  99.3 18.3 %collective-permute-start.26 = (bf16[2,128,1536]{2,1,0:T(8,128)(2,1)S(1)}, bf16[2,128,1536]{2,1,0:T(8,128)(2,1)S(1)}, u32[]{:S(2)}, u32[]{:S(2)}) collective-permute-start(bf16[2,128,1536]{2,1,0:T(8,128)(2,1)S(1)} %hidden.2.refs_0_.refs_4_.refs_5_.refs_6_), channel_id=1, source_target_pairs={{0,2},{2,4},{4,6},{6,0},{1,3},{3,5},{5,7},{7,1},{8,10},{10,12},{12... | collective-permute-start | bytes 2359304 | tf_op jit(solution)/shard_map/ppermute | solution.py:26
  115.4 47.6 %copy-start.2 = (bf16[2,128,1536]{2,1,0:T(8,128)(2,1)}, bf16[2,128,1536]{2,1,0:T(8,128)(2,1)S(1)}, u32[]{:S(2)}) copy-start(bf16[2,128,1536]{2,1,0:T(8,128)(2,1)S(1)} %hidden.3.refs_0_.refs_12_.refs_13_.refs_14_) | copy-start | bytes 2359300
  115.4 20.5 %collective-permute-start.30 = (bf16[2,128,1536]{2,1,0:T(8,128)(2,1)S(1)}, bf16[2,128,1536]{2,1,0:T(8,128)(2,1)S(1)}, u32[]{:S(2)}, u32[]{:S(2)}) collective-permute-start(bf16[2,128,1536]{2,1,0:T(8,128)(2,1)S(1)} %hidden.3.refs_0_.refs_12_.refs_13_.refs_14_), channel_id=1, source_target_pairs={{0,6},{2,0},{4,2},{6,4},{1,7},{3,1},{5,3},{7,5},{8,14},{10,8},{12,... | collective-permute-start | bytes 2359304 | tf_op jit(solution)/shard_map/ppermute | solution.py:26
  116.3 21.7 %collective-permute-start.31 = (bf16[2,128,1536]{2,1,0:T(8,128)(2,1)S(1)}, bf16[2,128,1536]{2,1,0:T(8,128)(2,1)S(1)}, u32[]{:S(2)}, u32[]{:S(2)}) collective-permute-start(bf16[2,128,1536]{2,1,0:T(8,128)(2,1)S(1)} %hidden.3.refs_0_.refs_12_.refs_13_.refs_14_), channel_id=1, source_target_pairs={{0,2},{2,4},{4,6},{6,0},{1,3},{3,5},{5,7},{7,1},{8,10},{10,12},{12... | collective-permute-start | bytes 2359304 | tf_op jit(solution)/shard_map/ppermute | solution.py:26
  117.6 24.2 %collective-permute-start.28 = (bf16[128,1536]{1,0:T(8,128)(2,1)S(1)}, bf16[128,1536]{1,0:T(8,128)(2,1)S(1)}, u32[]{:S(2)}, u32[]{:S(2)}) collective-permute-start(bf16[128,1536]{1,0:T(8,128)(2,1)S(1)} %get-tuple-element.131), channel_id=1, source_target_pairs={{0,6},{2,0},{4,2},{6,4},{1,7},{3,1},{5,3},{7,5},{8,14},{10,8},{12,... | collective-permute-start | bytes 1179656 | tf_op jit(solution)/shard_map/ppermute | solution.py:26
  119.7 23.9 %collective-permute-start.29 = (bf16[128,1536]{1,0:T(8,128)(2,1)S(1)}, bf16[128,1536]{1,0:T(8,128)(2,1)S(1)}, u32[]{:S(2)}, u32[]{:S(2)}) collective-permute-start(bf16[128,1536]{1,0:T(8,128)(2,1)S(1)} %get-tuple-element.132), channel_id=1, source_target_pairs={{0,2},{2,4},{4,6},{6,0},{1,3},{3,5},{5,7},{7,1},{8,10},{10,12},{12... | collective-permute-start | bytes 1179656 | tf_op jit(solution)/shard_map/ppermute | solution.py:26
  141.8 21.2 %copy-start.18 = (bf16[128,1536]{1,0:T(8,128)(2,1)}, bf16[128,1536]{1,0:T(8,128)(2,1)S(1)}, u32[]{:S(2)}) copy-start(bf16[128,1536]{1,0:T(8,128)(2,1)S(1)} %collective-permute-done.28.refs_8_.refs_9_) | copy-start | bytes 1179652
  146.7 2.4 %collective-permute-start.32 = (f32[512,384]{1,0:T(8,128)S(1)}, f32[512,384]{1,0:T(8,128)S(1)}, u32[]{:S(2)}, u32[]{:S(2)}) collective-permute-start(f32[512,384]{1,0:T(8,128)S(1)} %get-tuple-element.137), channel_id=1, source_target_pairs={{0,1},{1,0},{2,3},{3,2},{4,5},{5,4},{6,7},{7,6},{8,9},{9,8},{10,11... | collective-permute-start | bytes 2359304 | tf_op jit(solution)/shard_map/ppermute | solution.py:26
  146.9 11.6 %collective-permute-start.33 = (bf16[128,1536]{1,0:T(8,128)(2,1)S(1)}, bf16[128,1536]{1,0:T(8,128)(2,1)S(1)}, u32[]{:S(2)}, u32[]{:S(2)}) collective-permute-start(bf16[128,1536]{1,0:T(8,128)(2,1)S(1)} %get-tuple-element.139), channel_id=1, source_target_pairs={{0,6},{2,0},{4,2},{6,4},{1,7},{3,1},{5,3},{7,5},{8,14},{10,8},{12,... | collective-permute-start | bytes 1179656 | tf_op jit(solution)/shard_map/ppermute | solution.py:26
  147.2 12.5 %collective-permute-start.34 = (bf16[128,1536]{1,0:T(8,128)(2,1)S(1)}, bf16[128,1536]{1,0:T(8,128)(2,1)S(1)}, u32[]{:S(2)}, u32[]{:S(2)}) collective-permute-start(bf16[128,1536]{1,0:T(8,128)(2,1)S(1)} %get-tuple-element.140), channel_id=1, source_target_pairs={{0,2},{2,4},{4,6},{6,0},{1,3},{3,5},{5,7},{7,1},{8,10},{10,12},{12... | collective-permute-start | bytes 1179656 | tf_op jit(solution)/shard_map/ppermute | solution.py:26
  149.2 13.8 %copy-start.24 = (f32[4,32,384]{2,1,0:T(8,128)}, f32[4,32,384]{2,1,0:T(8,128)S(1)}, u32[]{:S(2)}) copy-start(f32[4,32,384]{2,1,0:T(8,128)S(1)} %get-tuple-element.138) | copy-start | bytes 589828
  149.2 10.6 %collective-permute-start.35 = (bf16[4,32,384]{2,1,0:T(8,128)(2,1)S(1)}, bf16[4,32,384]{2,1,0:T(8,128)(2,1)S(1)}, u32[]{:S(2)}, u32[]{:S(2)}) collective-permute-start(bf16[4,32,384]{2,1,0:T(8,128)(2,1)S(1)} %get-tuple-element.141), channel_id=1, source_target_pairs={{0,32},{32,64},{64,96},{96,0},{1,33},{33,65},{65,97},{97,1},{2,34}... | collective-permute-start | bytes 294920 | tf_op jit(solution)/shard_map/ppermute | solution.py:26
  151.3 8.5 %collective-permute-start.36 = (bf16[4,32,384]{2,1,0:T(8,128)(2,1)S(1)}, bf16[4,32,384]{2,1,0:T(8,128)(2,1)S(1)}, u32[]{:S(2)}, u32[]{:S(2)}) collective-permute-start(bf16[4,32,384]{2,1,0:T(8,128)(2,1)S(1)} %get-tuple-element.142), channel_id=1, source_target_pairs={{0,64},{32,96},{64,0},{96,32},{1,65},{33,97},{65,1},{97,33},{2,66}... | collective-permute-start | bytes 294920 | tf_op jit(solution)/shard_map/ppermute | solution.py:26
  153.1 6.6 %collective-permute-start.37 = (bf16[4,32,384]{2,1,0:T(8,128)(2,1)S(1)}, bf16[4,32,384]{2,1,0:T(8,128)(2,1)S(1)}, u32[]{:S(2)}, u32[]{:S(2)}) collective-permute-start(bf16[4,32,384]{2,1,0:T(8,128)(2,1)S(1)} %get-tuple-element.143), channel_id=1, source_target_pairs={{0,96},{32,0},{64,32},{96,64},{1,97},{33,1},{65,33},{97,65},{2,98}... | collective-permute-start | bytes 294920 | tf_op jit(solution)/shard_map/ppermute | solution.py:26
  158.5 4.6 %copy-start.20 = (bf16[128,1536]{1,0:T(8,128)(2,1)}, bf16[128,1536]{1,0:T(8,128)(2,1)S(1)}, u32[]{:S(2)}) copy-start(bf16[128,1536]{1,0:T(8,128)(2,1)S(1)} %collective-permute-done.33.refs_16_.refs_17_) | copy-start | bytes 1179652
  159.8 3.3 %copy-start.8 = (bf16[128,1536]{1,0:T(8,128)(2,1)}, bf16[128,1536]{1,0:T(8,128)(2,1)S(1)}, u32[]{:S(2)}) copy-start(bf16[128,1536]{1,0:T(8,128)(2,1)S(1)} %collective-permute-done.34.refs_2_.refs_17_.refs_18_) | copy-start | bytes 1179652
  159.8 3.2 %copy-start.28 = (bf16[4,32,384]{2,1,0:T(8,128)(2,1)}, bf16[4,32,384]{2,1,0:T(8,128)(2,1)S(1)}, u32[]{:S(2)}) copy-start(bf16[4,32,384]{2,1,0:T(8,128)(2,1)S(1)} %collective-permute-done.35) | copy-start | bytes 294916
  159.8 3.2 %copy-start.30 = (bf16[4,32,384]{2,1,0:T(8,128)(2,1)}, bf16[4,32,384]{2,1,0:T(8,128)(2,1)S(1)}, u32[]{:S(2)}) copy-start(bf16[4,32,384]{2,1,0:T(8,128)(2,1)S(1)} %collective-permute-done.36) | copy-start | bytes 294916
  159.8 3.2 %copy-start.32 = (bf16[4,32,384]{2,1,0:T(8,128)(2,1)}, bf16[4,32,384]{2,1,0:T(8,128)(2,1)S(1)}, u32[]{:S(2)}) copy-start(bf16[4,32,384]{2,1,0:T(8,128)(2,1)S(1)} %collective-permute-done.37) | copy-start | bytes 294916
  168.4 14.0 %collective-permute-start.43 = (bf16[384,1536]{1,0:T(8,128)(2,1)S(1)}, bf16[384,1536]{1,0:T(8,128)(2,1)S(1)}, u32[]{:S(2)}, u32[]{:S(2)}) collective-permute-start(bf16[384,1536]{1,0:T(8,128)(2,1)S(1)} %get-tuple-element.166), channel_id=1, source_target_pairs={{0,1},{1,0},{2,3},{3,2},{4,5},{5,4},{6,7},{7,6},{8,9},{9,8},{10,11... | collective-permute-start | bytes 3538952 | tf_op jit(solution)/shard_map/ppermute | solution.py:26
  168.4 19.3 %collective-permute-start.44 = (bf16[1536,384]{1,0:T(8,128)(2,1)}, bf16[1536,384]{1,0:T(8,128)(2,1)}, u32[]{:S(2)}, u32[]{:S(2)}) collective-permute-start(bf16[1536,384]{1,0:T(8,128)(2,1)} %get-tuple-element.167), channel_id=1, source_target_pairs={{0,1},{1,0},{2,3},{3,2},{4,5},{5,4},{6,7},{7,6},{8,9},{9,8},{10,11... | collective-permute-start | bytes 3538952 | tf_op jit(solution)/shard_map/ppermute | solution.py:26
  168.9 5.1 %collective-permute-start.38 = (f32[512,384]{1,0:T(8,128)S(1)}, f32[512,384]{1,0:T(8,128)S(1)}, u32[]{:S(2)}, u32[]{:S(2)}) collective-permute-start(f32[512,384]{1,0:T(8,128)S(1)} %get-tuple-element.149), channel_id=1, source_target_pairs={{0,1},{1,0},{2,3},{3,2},{4,5},{5,4},{6,7},{7,6},{8,9},{9,8},{10,11... | collective-permute-start | bytes 2359304 | tf_op jit(solution)/shard_map/ppermute | solution.py:26
  174.9 32.1 %collective-permute-start.39 = (bf16[4,32,384]{2,1,0:T(8,128)(2,1)}, bf16[4,32,384]{2,1,0:T(8,128)(2,1)}, u32[]{:S(2)}, u32[]{:S(2)}) collective-permute-start(bf16[4,32,384]{2,1,0:T(8,128)(2,1)} %get-tuple-element.169), channel_id=1, source_target_pairs={{0,16},{16,0},{32,48},{48,32},{64,80},{80,64},{96,112},{112,96},{1... | collective-permute-start | bytes 294920 | tf_op jit(solution)/shard_map/ppermute | solution.py:428
  176.1 30.9 %collective-permute-start.40 = (bf16[4,32,384]{2,1,0:T(8,128)(2,1)}, bf16[4,32,384]{2,1,0:T(8,128)(2,1)}, u32[]{:S(2)}, u32[]{:S(2)}) collective-permute-start(bf16[4,32,384]{2,1,0:T(8,128)(2,1)} %get-tuple-element.170), channel_id=1, source_target_pairs={{0,48},{16,32},{32,80},{48,64},{64,112},{80,96},{96,16},{112,0},{1... | collective-permute-start | bytes 294920 | tf_op jit(solution)/shard_map/ppermute | solution.py:428
  179.8 27.1 %collective-permute-start.41 = (bf16[4,32,384]{2,1,0:T(8,128)(2,1)}, bf16[4,32,384]{2,1,0:T(8,128)(2,1)}, u32[]{:S(2)}, u32[]{:S(2)}) collective-permute-start(bf16[4,32,384]{2,1,0:T(8,128)(2,1)} %get-tuple-element.171), channel_id=1, source_target_pairs={{0,80},{16,64},{32,112},{48,96},{64,16},{80,0},{96,48},{112,32},{1... | collective-permute-start | bytes 294920 | tf_op jit(solution)/shard_map/ppermute | solution.py:428
  183.4 23.6 %collective-permute-start.42 = (bf16[4,32,384]{2,1,0:T(8,128)(2,1)}, bf16[4,32,384]{2,1,0:T(8,128)(2,1)}, u32[]{:S(2)}, u32[]{:S(2)}) collective-permute-start(bf16[4,32,384]{2,1,0:T(8,128)(2,1)} %get-tuple-element.172), channel_id=1, source_target_pairs={{0,112},{16,96},{32,16},{48,0},{64,48},{80,32},{96,80},{112,64},{1... | collective-permute-start | bytes 294920 | tf_op jit(solution)/shard_map/ppermute | solution.py:428
  198.7 8.3 %copy-start.25 = (f32[4,32,384]{2,1,0:T(8,128)S(1)}, f32[4,32,384]{2,1,0:T(8,128)}, u32[]{:S(2)}) copy-start(f32[4,32,384]{2,1,0:T(8,128)} %copy-done.24) | copy-start | bytes 589828
  198.7 8.3 %copy-start.29 = (bf16[4,32,384]{2,1,0:T(8,128)(2,1)S(1)}, bf16[4,32,384]{2,1,0:T(8,128)(2,1)}, u32[]{:S(2)}) copy-start(bf16[4,32,384]{2,1,0:T(8,128)(2,1)} %copy-done.28) | copy-start | bytes 294916
  198.7 8.3 %copy-start.31 = (bf16[4,32,384]{2,1,0:T(8,128)(2,1)S(1)}, bf16[4,32,384]{2,1,0:T(8,128)(2,1)}, u32[]{:S(2)}) copy-start(bf16[4,32,384]{2,1,0:T(8,128)(2,1)} %copy-done.30) | copy-start | bytes 294916
  198.7 8.3 %copy-start.33 = (bf16[4,32,384]{2,1,0:T(8,128)(2,1)S(1)}, bf16[4,32,384]{2,1,0:T(8,128)(2,1)}, u32[]{:S(2)}) copy-start(bf16[4,32,384]{2,1,0:T(8,128)(2,1)} %copy-done.32) | copy-start | bytes 294916
  (15 other events, 19.1 us)

commit v3 on v2

--- a/solution.py
+++ b/solution.py
@@ -34,7 +34,7 @@
     return lax.optimization_barrier((value, after))[0]
 
 
-COST = dict(pack=1, weights=1, join=0.1, products=0.1, ring_add=0.1, own_sum=0.1, hidden=0.1, pass_on=0.1, input_part=0.1, return_pieces=0.1, return_far=10, weight_grads=0.1, all_grads=10)
+COST = dict(pack=0.1, weights=0.1, join_a=0.1, join_b=0.1, products=0.1, ring_add=0.1, own_sum=0.1, hidden=0.1, pass_on=0.1, input_a=0.1, input_b=20, grads_a=0.1, grads_b=0.1, returns=0.1, place=5)
 
 
 def kernel(name, body, grid, ins, outs, scratch=(), scalar=None):
@@ -44,11 +44,8 @@
 
         return pl.BlockSpec(block, at)
 
-    def run(*refs):
-        body(*(refs if scalar is None else refs[1:]))
-
     return pl.pallas_call(
-        run,
+        body,
         name=name,
         grid_spec=pltpu.PrefetchScalarGridSpec(
             num_scalar_prefetch=0 if scalar is None else 1,
@@ -67,7 +64,7 @@
     feat = w_in.shape[0]
     half = w_out.shape[0] // feat // 2
 
-    def body(wi, wo, out):
+    def body(_, wi, wo, out):
         out[0, 0] = wi[...]
         out[1, 0] = wo[...]
 
@@ -87,7 +84,7 @@
     feat = w_in.shape[0]
     half = w_out.shape[0] // feat // 2
 
-    def body(wi, wo, got, wi_out, wo_out):
+    def body(_, wi, wo, got, wi_out, wo_out):
         wi_out[:feat] = wi[...]
         wi_out[feat:] = got[0, 0]
         wo_out[:, :feat] = wo[...]
@@ -108,7 +105,7 @@
     )
 
 
-def join(pieces, others):
+def join(name, pieces, others):
     zs, piece, width = pieces[0].shape
     count = len(pieces)
     per = count * piece
@@ -120,7 +117,7 @@
                     out[pl.ds(k * per + j * piece, piece), :] = side[j][k]
 
     return kernel(
-        "join",
+        name,
         body,
         1,
         [(a, (zs, piece, width), (0, 0, 0)) for a in (*pieces, *others)],
@@ -237,111 +234,119 @@
     )[0]
 
 
-def input_part(mine, above, grad2, below, wi):
+def input_part(name, mine, above, grad2, below, wi):
     _, per, hid = mine.shape
-    feat = wi.shape[0]
-    half = feat // 2
+    half = wi.shape[0] // 2
 
     def body(mine, above, grad2, below, wi, own, other):
-        for k, grad in enumerate((mine.at[0], above.at[0], grad2, below.at[0])):
-            part = dot(grad[...], wi[...], 1, 1)
-            own[k * per : (k + 1) * per] = part[:, :half]
-            other[k * per : (k + 1) * per] = part[:, half:]
+        for step, out in enumerate((own, other)):
+
+            @pl.when(pl.program_id(0) == step)
+            def _():
+                for k, grad in enumerate((mine.at[0], above.at[0], grad2, below.at[0])):
+                    out[k * per : (k + 1) * per] = dot(grad[...], wi[...], 1, 1)
 
     second, whole = (1, per, hid), (4 * per, half)
     return kernel(
-        "input_part",
-        body,
-        1,
+        name,
+        body,
+        2,
         [
             (mine, second, (1, 0, 0)),
             (above, second, (1, 0, 0)),
             (grad2, (per, hid), (0, 0)),
             (below, second, (1, 0, 0)),
-            (wi, (feat, hid), (0, 0)),
+            (wi, (half, hid), ("i", 0)),
         ],
         [(whole, F32, whole, (0, 0))] * 2,
     )
 
 
-def return_pieces(name, mine, other, pieces, kinds):
-    rows, feat = mine.shape
-    piece = rows // 4 // pieces
-
-    def body(mine, other, *outs):
+def returns(near, near_got, far, far_got, row):
+    rows, feat = near.shape
+    piece = rows // 16
+
+    def body(row, near, near_got, far, far_got, out):
+        here = row[0] % 2
+        for at, mine, got in ((here, near, near_got), (1 - here, far, far_got)):
+            out[at] = (mine[...] + got[...]).reshape(4 * piece, feat).astype(BF16)
+
+    split = lambda a: a.reshape(4, 4, piece, feat)
+    block = (4, 1, piece, feat)
+    return kernel(
+        "returns",
+        body,
+        4,
+        [(split(a), block, (0, "i", 0, 0)) for a in (near, near_got, far, far_got)],
+        [((8, 4 * piece, feat), BF16, (2, 4 * piece, feat), (lambda i, r: (r // 2 + i) % 4, 0, 0))],
+        scalar=row,
+    )[0]
+
+
+def weight_grads(name, tok, cot, blocks, sums=None):
+    rows, feat = tok.shape
+    _, per, hid = blocks[0].shape
+    half, block = feat // 2, hid // STEPS
+    last = sums is not None
+
+    def body(tok, cot, *refs):
+        parts, refs = refs[:8], refs[8:]
+        act, grad = refs[-2:]
         for k in range(4):
-            for j, out in enumerate(outs):
-                at = pl.ds((k * pieces + j) * piece, piece)
-                out[k] = (mine[at, :] + other[at, :]).astype(out.dtype)
-
-    return kernel(
-        name,
-        body,
-        1,
-        [(mine, (rows, feat), (0, 0)), (other, (rows, feat), (0, 0))],
-        [((4, piece, feat), kind, (4, piece, feat), (0, 0, 0)) for kind in kinds],
-    )
-
-
-def weight_grads(toks, cots, blocks, side, other=None, core=None):
-    rows, feat = toks[0].shape
-    _, per, hid = blocks[0][0].shape
-    half, block, chunks = feat // 2, hid // STEPS, len(toks)
-    both = other is not None
-
-    def body(*refs):
-        toks, cots = refs[:chunks], refs[chunks : 2 * chunks]
-        parts = refs[2 * chunks : -6]
-        wi_out, wo_out, tok, cot, act, grad = refs[-6:]
-        step = pl.program_id(0)
-
-        @pl.when(step == 0)
+            for ref, out in zip(parts[2 * k : 2 * k + 2], (act, grad)):
+                out[pl.ds(k * per, per), :] = ref[0] if len(ref.shape) == 3 else ref[...]
+        wi = dot(tok[...], grad[...], 0, 0)
+        wo = dot(act[...], cot[...], 0, 0)
+        if not last:
+            refs[0][...] = wi
+            refs[1][...] = wo
+        else:
+            wi = (wi + refs[0][...]).astype(BF16)
+            wo = (wo + refs[1][...]).astype(BF16)
+            refs[2][...], refs[3][...] = wi[:half], wi[half:]
+            refs[4][...], refs[5][...] = wo[:, :half], wo[:, half:]
+
+    mine, above, act2, grad2, below = blocks
+    ins = [(tok, (rows, feat), (0, 0)), (cot, (rows, feat), (0, 0))]
+    for pair in (mine, above, (act2, grad2), below):
+        if isinstance(pair, tuple):
+            ins += [(a, (per, block), (0, "i")) for a in pair]
+        else:
+            ins += [(pair, (1, per, block), (k, 0, "i")) for k in (0, 1)]
+    if last:
+        ins += [(sums[0], (feat, block), (0, "i")), (sums[1], (block, feat), ("i", 0))]
+        outs = [((half, hid), BF16, (half, block), (0, "i"))] * 2 + [((hid, half), BF16, (block, half), ("i", 0))] * 2
+    else:
+        outs = [((feat, hid), F32, (feat, block), (0, "i")), ((hid, feat), F32, (block, feat), ("i", 0))]
+    return kernel(name, body, STEPS, ins, outs, [pltpu.VMEM((rows, block), BF16)] * 2)
+
+
+def place(wi_own, wi_got, wo_own, wo_got, core):
+    half, hid = wi_own.shape
+
+    def body(core, wi_own, wi_got, wo_own, wo_got, wi, wo):
+        mine = pl.program_id(0) // STEPS == core[0]
+
+        @pl.when(mine)
         def _():
-            for c in range(chunks):
-                tok[c * rows : (c + 1) * rows] = toks[c][...]
-                cot[c * rows : (c + 1) * rows] = cots[c][...]
-
-        @pl.when(step < STEPS)
+            wi[...] = wi_own[...]
+            wo[...] = wo_own[...]
+
+        @pl.when(jnp.logical_not(mine))
         def _():
-            for k in range(4 * chunks):
-                a, g = parts[2 * k : 2 * k + 2]
-                at = pl.ds(k * per, per)
-                act[at, :] = a[0] if len(a.shape) == 3 else a[...]
-                grad[at, :] = g[0] if len(g.shape) == 3 else g[...]
-            wi_out[...] = dot(tok[...], grad[...], 0, 0).astype(BF16)
-            wo_out[...] = dot(act[...], cot[...], 0, 0).astype(BF16)
-
-        if both:
-
-            @pl.when(step >= STEPS)
-            def _():
-                wi_out[...] = parts[-2][...]
-                wo_out[...] = parts[-1][...]
-
-    if both:
-        at = lambda i, c: jnp.minimum(i, STEPS - 1)
-        late = lambda i, c: jnp.maximum(i - STEPS, 0)
-        out = lambda i, c: jnp.where(i < STEPS, c * STEPS + i, (1 - c) * STEPS + i - STEPS)
-    else:
-        at = out = "i"
-    ins = [(a, (rows, half), (0, side)) for a in (*toks, *cots)]
-    for mine, above, act2, grad2, below in blocks:
-        for pair in (mine, above, (act2, grad2), below):
-            if isinstance(pair, tuple):
-                ins += [(a, (per, block), (0, at)) for a in pair]
-            else:
-                ins += [(pair, (1, per, block), (k, 0, at)) for k in (0, 1)]
-    if both:
-        ins += [(other[0], (half, block), (0, late)), (other[1], (block, half), (late, 0))]
-    cols = 2 * hid if both else hid
-    return kernel(
-        "all_grads" if both else "weight_grads",
-        body,
-        2 * STEPS if both else STEPS,
-        ins,
-        [((half, cols), BF16, (half, block), (0, out)), ((cols, half), BF16, (block, half), (out, 0))],
-        [pltpu.VMEM((chunks * rows, half), BF16)] * 2 + [pltpu.VMEM((chunks * rows, block), BF16)] * 2,
-        core,
+            wi[...] = wi_got[...]
+            wo[...] = wo_got[...]
+
+    block = hid // STEPS
+    at = lambda i, c: i % STEPS
+    across, down = ((half, block), (0, at)), ((block, half), (at, 0))
+    return kernel(
+        "place",
+        body,
+        2 * STEPS,
+        [(wi_own, *across), (wi_got, *across), (wo_own, *down), (wo_got, *down)],
+        [((half, 2 * hid), BF16, (half, block), (0, "i")), ((2 * hid, half), BF16, (block, half), ("i", 0))],
+        scalar=core,
     )
 
 
@@ -365,25 +370,26 @@
 
     def send_on(above, below):
         act, grad = pass_on(above, below)
-        return shift(act, "z", -1), shift(grad, "z", 1)
-
-    place = jnp.reshape(core, (1,)).astype(jnp.int32)
-    packed = pack(w_in, w_out, place)
-    got = shift(packed, "core", 1)
+        return shift(act, "z", -1), shift(grad, "z", 1), act
+
+    at_core = jnp.reshape(core, (1,)).astype(jnp.int32)
+    at_row = jnp.reshape(lax.axis_index(ROWS), (1,)).astype(jnp.int32)
     own = relative(jnp.concatenate([tokens, cotangent], 1), -1)
     across = shift(own, "xh", 1)
     near = [shift(own, "y", -d) for d in (1, 2, 3)]
+    packed = pack(*gate((w_in, w_out), own), at_core)
+    got = shift(packed, "core", 1)
     across = gate(across, packed)
     far = [shift(across, "y", -d) for d in (1, 2, 3)]
-    near = [own, *gate(near, across)]
-    near = join(near, to_core(near))
-    wi, wo = weights(w_in, w_out, got, place)
+    wi, wo = weights(w_in, w_out, gate(got, across), at_core)
+    near = [own, *gate(near, wi)]
+    near = join("join_a", near, to_core(near))
 
     pg_a, up_a, down_a, tok_a, cot_a = products(*near, wi, wo)
     r_a = up_down(up_a, down_a)
 
-    far = [across, *gate(far, up_a)]
-    far = join(far, to_core(far))
+    far = gate([across, *far], up_a)
+    far = join("join_b", far, to_core(far))
     pg_b, up_b, down_b, tok_b, cot_b = products(*far, wi, wo)
     r_b = up_down(up_b, down_b)
 
@@ -403,37 +409,27 @@
     s_b = send_mine(mine_b)
 
     s_a = gate(s_a, mine_b)
-    f_a = send_on(*s_a)
+    f_a = send_on(*s_a)[:2]
     s_b = gate(s_b, s_a)
     f_b = send_on(*s_b)
 
-    f_a = gate(f_a, s_b)
-    in_a, in_a_other = input_part(mine_a, s_a[0], f_a[1], s_a[1], wi)
+    f_a = gate(f_a, f_b[2])
+    in_a, in_a_other = input_part("input_a", mine_a, s_a[0], f_a[1], s_a[1], wi)
     in_a_got = shift(in_a_other, "core", 1)
-    kept, *back = return_pieces("return_pieces", in_a, in_a_got, 4, (F32, BF16, BF16, BF16))
-    back = [shift(a, "y", d) for d, a in zip((1, 2, 3), back)]
-
-    f_b, back = gate((f_b, back), kept)
-    in_b, in_b_other = input_part(mine_b, s_b[0], f_b[1], s_b[1], wi)
+    sums = weight_grads("grads_a", tok_a, cot_a, gate((mine_a, s_a[0], *f_a, s_a[1]), in_a_other))
+
+    f_b = gate(f_b[:2], sums)
+    in_b, in_b_other = input_part("input_b", mine_b, s_b[0], f_b[1], s_b[1], wi)
     in_b_got = shift(in_b_other, "core", 1)
-
-    blocks = [(mine_a, s_a[0], *f_a, s_a[1]), (mine_b, s_b[0], *f_b, s_b[1])]
-    blocks = gate(blocks, in_b_other)
-    grads_other = weight_grads([tok_a, tok_b], [cot_a, cot_b], blocks, 1)
-    got_other = to_core(grads_other)
-
-    back_far = return_pieces("return_far", in_b, gate(in_b_got, grads_other), 4, (BF16,) * 4)
-    got_other = gate(got_other, back_far)
-    back_far = [
-        lax.ppermute(a, ROWS, [(i, ((i // 2 + d) % 4) * 2 + (i + 1) % 2) for i in range(8)])
-        for d, a in enumerate(back_far)
-    ]
-    w_in_grad, w_out_grad = weight_grads([tok_a, tok_b], [cot_a, cot_b], blocks, 0, got_other, place)
-
-    total = kept
-    for part in back + gate(back_far, w_in_grad, w_out_grad):
-        total = total + part.astype(F32)
-    input_grad = relative(total, 1).reshape(rows, feat).astype(BF16)
+    blocks = gate((mine_b, s_b[0], *f_b, s_b[1]), in_b_other)
+    wi_own, wi_other, wo_own, wo_other = weight_grads("grads_b", tok_b, cot_b, blocks, sums)
+    wi_got, wo_got = to_core((wi_other, wo_other))
+
+    in_a_got, in_b_got = gate((in_a_got, in_b_got), wi_own)
+    back = returns(in_a, in_a_got, in_b, in_b_got, at_row)
+    back = lax.all_to_all(back, ROWS, 0, 0, tiled=True)
+    w_in_grad, w_out_grad = place(wi_own, gate(wi_got, back), wo_own, wo_got, at_core)
+    input_grad = relative(jnp.sum(back.astype(F32), 0), 1).reshape(rows, feat).astype(BF16)
     return (input_grad, w_in_grad, w_out_grad)
 
 

time: 210 us -> 198 us (0.943)
  starting transfers between devices: 54 us -> 40.7 us
  local copies, waits for them, and re-layouts: 17.1 us -> 5.6 us
  waiting for transfers between devices: 97.2 us -> 108 us
    all_to_all x0 -> x1, waiting for transfers between devices: none -> 14.9 us  [local(): back = lax.all_to_all(back, ROWS, 0, 0, tiled=True)]
    ppermute x4 -> x0, starting transfers between devices: 11.8 us -> none  [local(): lax.ppermute(a, ROWS, [(i, (i // 2 + d) % 4 * 2 + (i + 1) % 2) for i in r...]
    unnamed x68 -> x12, local copies, waits for them, and re-layouts: 17.1 us -> 5.6 us
    ppermute x41 -> x38, starting transfers between devices: 42.2 us -> 36.5 us  [shift(): return lax.ppermute(x, axis, [(i, (i + by) % n) for i in range(n)])]
    all_to_all x0 -> x1, starting transfers between devices: none -> 4.21 us  [local(): back = lax.all_to_all(back, ROWS, 0, 0, tiled=True)]
    ppermute x41 -> x38, waiting for transfers between devices: 97.2 us -> 93.5 us  [shift(): return lax.ppermute(x, axis, [(i, (i + by) % n) for i in range(n)])]
  transfers between devices with their start and end apart: 45 -> 39, of which waited for: 23 -> 19; matrix products, arithmetic and copies ran while one was open for 0% -> 1% of each run, Pallas kernels for 11% -> 17%
where the time goes in v3:
time: 198 us
  waiting for transfers between devices  108 us (55%)
  starting transfers between devices  40.7 us (21%)
  Pallas kernels  39 us (20%)
  local copies, waits for them, and re-layouts  5.6 us (3%)
  other arithmetic  2.99 us (2%)
    ppermute x38, waiting for transfers between devices, shift(): return lax.ppermute(x, axis, [(i, (i + by) % n) for i in range(n)])  93.5 us
    pallas_call x20, Pallas kernels, kernel(): pl.pallas_call(body, name=name, grid_spec=pltpu.PrefetchScalarGridSpec(nu...  39 us
    ppermute x38, starting transfers between devices, shift(): return lax.ppermute(x, axis, [(i, (i + by) % n) for i in range(n)])  36.5 us
    all_to_all x1, waiting for transfers between devices, local(): back = lax.all_to_all(back, ROWS, 0, 0, tiled=True)  14.9 us
    unnamed x12, local copies, waits for them, and re-layouts  5.6 us
    all_to_all x1, starting transfers between devices, local(): back = lax.all_to_all(back, ROWS, 0, 0, tiled=True)  4.21 us
  transfers between devices with their start and end apart: 39, of which 19 were waited for; matrix products, arithmetic and copies ran while one was open for 1% of the time, Pallas kernels for 17%

profile of v3, /device:TPU:0, one launch (start us, length us, event | category | flops | bytes accessed | tf_op | source)
XLA Modules:
  0.0 197.6 jit_solution(12759690800241392170)
XLA Ops:
  0.7 1.0 pad_maximum_fusion
  1.7 1.7 copy-done
  3.4 1.7 copy-done.1
  5.1 0.7 pack.1
  5.8 3.2 %collective-permute-start.4 = (bf16[4,32,768]{2,1,0:T(8,128)(2,1)S(1)}, bf16[4,32,768]{2,1,0:T(8,128)(2,1)S(1)}, u32[]{:S(2)}, u32[]{:S(2)}) collective-permute-start(bf16[4,32,768]{2,1,0:T(8,128)(2,1)S(1)} %fusion.2.refs_0_), channel_id=1, source_target_pairs={{0,16},{16,0},{1,17},{17,1},{2,18},{18,2},{3,19},{19,3},{4,20},{20... | collective-permute-start | bytes 589832 | tf_op jit(solution)/shard_map/ppermute | solution.py:26
  9.0 3.0 %collective-permute-start = (bf16[4,32,768]{2,1,0:T(8,128)(2,1)S(1)}, bf16[4,32,768]{2,1,0:T(8,128)(2,1)S(1)}, u32[]{:S(2)}, u32[]{:S(2)}) collective-permute-start(bf16[4,32,768]{2,1,0:T(8,128)(2,1)S(1)} %fusion.2.refs_0_), channel_id=1, source_target_pairs={{0,96},{32,0},{64,32},{96,64},{1,97},{33,1},{65,33},{97,65},{2,98}... | collective-permute-start | bytes 589832 | tf_op jit(solution)/shard_map/ppermute | solution.py:26
  12.0 0.6 collective-permute-start.1
  12.6 1.0 collective-permute-start.2
  13.6 1.0 collective-permute-done.4.refs_0_
  14.6 1.1 weights.1
  15.8 4.9 %collective-permute-done.refs_1_ = bf16[4,32,768]{2,1,0:T(8,128)(2,1)S(1)} collective-permute-done((bf16[4,32,768]{2,1,0:T(8,128)(2,1)S(1)}, bf16[4,32,768]{2,1,0:T(8,128)(2,1)S(1)}, u32[]{:S(2)}, u32[]{:S(2)}) %collective-permute-start) | collective-permute-done | bytes 196640 | tf_op jit(solution)/shard_map/ppermute | solution.py:26
  20.7 0.6 collective-permute-done.1.refs_2_
  21.4 3.1 %collective-permute-done.2.refs_3_ = bf16[4,32,768]{2,1,0:T(8,128)(2,1)S(1)} collective-permute-done((bf16[4,32,768]{2,1,0:T(8,128)(2,1)S(1)}, bf16[4,32,768]{2,1,0:T(8,128)(2,1)S(1)}, u32[]{:S(2)}, u32[]{:S(2)}) %collective-permute-start.2) | collective-permute-done | bytes 196640 | tf_op jit(solution)/shard_map/ppermute | solution.py:26
  24.4 0.5 collective-permute-start.7
  24.9 0.6 collective-permute-start.11
  25.5 0.6 collective-permute-start.12
  26.2 0.9 collective-permute-start.13
  27.2 3.7 %products.2 = (f32[2,512,1536]{2,1,0:T(8,128)S(1)}, bf16[128,1536]{1,0:T(8,128)(2,1)S(1)}, bf16[128,1536]{1,0:T(8,128)(2,1)S(1)}, bf16[512,768]{1,0:T(8,128)(2,1)S(1)}, bf16[512,768]{1,0:T(8,128)(2,1)S(1)}) custom-call(bf16[512,768]{1,0:T(8,128)(2,1)S(1)} %get-tuple-element.93.own, bf16[512,768]{1,0:T(8,128)(2,1)S(1)} %get-tuple-element.94.other, ...), custom_call_target="tpu_custom_call" | custom-call | bytes 369000 | tf_op jit(solution)/shard_map/products/pallas_call | solution.py:47
  30.9 1.7 collective-permute-done.11.refs_1_
  32.6 2.2 %collective-permute-done.12.refs_2_ = bf16[4,32,768]{2,1,0:T(8,128)(2,1)S(1)} collective-permute-done((bf16[4,32,768]{2,1,0:T(8,128)(2,1)S(1)}, bf16[4,32,768]{2,1,0:T(8,128)(2,1)S(1)}, u32[]{:S(2)}, u32[]{:S(2)}) %collective-permute-start.12) | collective-permute-done | bytes 196640 | tf_op jit(solution)/shard_map/ppermute | solution.py:26
  34.8 3.5 %collective-permute-done.13.refs_3_ = bf16[4,32,768]{2,1,0:T(8,128)(2,1)S(1)} collective-permute-done((bf16[4,32,768]{2,1,0:T(8,128)(2,1)S(1)}, bf16[4,32,768]{2,1,0:T(8,128)(2,1)S(1)}, u32[]{:S(2)}, u32[]{:S(2)}) %collective-permute-start.13) | collective-permute-done | bytes 196640 | tf_op jit(solution)/shard_map/ppermute | solution.py:26
  39.3 4.0 %collective-permute-start.10 = (bf16[128,1536]{1,0:T(8,128)(2,1)S(1)}, bf16[128,1536]{1,0:T(8,128)(2,1)S(1)}, u32[]{:S(2)}, u32[]{:S(2)}) collective-permute-start(bf16[128,1536]{1,0:T(8,128)(2,1)S(1)} %get-tuple-element.98), channel_id=1, source_target_pairs={{0,6},{2,0},{4,2},{6,4},{1,7},{3,1},{5,3},{7,5},{8,14},{10,8},{12,... | collective-permute-start | bytes 1179656 | tf_op jit(solution)/shard_map/ppermute | solution.py:26
  43.5 3.7 %products.3 = (f32[2,512,1536]{2,1,0:T(8,128)S(1)}, bf16[128,1536]{1,0:T(8,128)(2,1)S(1)}, bf16[128,1536]{1,0:T(8,128)(2,1)S(1)}, bf16[512,768]{1,0:T(8,128)(2,1)S(1)}, bf16[512,768]{1,0:T(8,128)(2,1)S(1)}) custom-call(bf16[512,768]{1,0:T(8,128)(2,1)S(1)} %get-tuple-element.103.own, bf16[512,768]{1,0:T(8,128)(2,1)S(1)} %get-tuple-element.104.other, ...), custom_call_target="tpu_custom_call" | custom-call | bytes 369000 | tf_op jit(solution)/shard_map/products/pallas_call | solution.py:47
  47.5 3.1 %collective-permute-start.21 = (bf16[128,1536]{1,0:T(8,128)(2,1)S(1)}, bf16[128,1536]{1,0:T(8,128)(2,1)S(1)}, u32[]{:S(2)}, u32[]{:S(2)}) collective-permute-start(bf16[128,1536]{1,0:T(8,128)(2,1)S(1)} %get-tuple-element.111), channel_id=1, source_target_pairs={{0,6},{2,0},{4,2},{6,4},{1,7},{3,1},{5,3},{7,5},{8,14},{10,8},{12,... | collective-permute-start | bytes 1179656 | tf_op jit(solution)/shard_map/ppermute | solution.py:26
  50.6 2.2 %collective-permute-done.10.down = bf16[128,1536]{1,0:T(8,128)(2,1)S(1)} collective-permute-done((bf16[128,1536]{1,0:T(8,128)(2,1)S(1)}, bf16[128,1536]{1,0:T(8,128)(2,1)S(1)}, u32[]{:S(2)}, u32[]{:S(2)}) %collective-permute-start.10) | collective-permute-done | bytes 393248 | tf_op jit(solution)/shard_map/ppermute | solution.py:26
  52.8 3.7 %collective-permute-done.9.up = bf16[128,1536]{1,0:T(8,128)(2,1)S(1)} collective-permute-done((bf16[128,1536]{1,0:T(8,128)(2,1)S(1)}, bf16[128,1536]{1,0:T(8,128)(2,1)S(1)}, u32[]{:S(2)}, u32[]{:S(2)}) %collective-permute-start.9) | collective-permute-done | bytes 393248 | tf_op jit(solution)/shard_map/ppermute | solution.py:26
  56.6 0.6 ring_add.2
  57.3 3.2 %collective-permute-start.19 = (bf16[2,128,1536]{2,1,0:T(8,128)(2,1)S(1)}, bf16[2,128,1536]{2,1,0:T(8,128)(2,1)S(1)}, u32[]{:S(2)}, u32[]{:S(2)}) collective-permute-start(bf16[2,128,1536]{2,1,0:T(8,128)(2,1)S(1)} %get-tuple-element.109), channel_id=1, source_target_pairs={{0,6},{2,0},{4,2},{6,4},{1,7},{3,1},{5,3},{7,5},{8,14},{10,8},{12,... | collective-permute-start | bytes 2359304 | tf_op jit(solution)/shard_map/ppermute | solution.py:26
  60.5 4.5 %collective-permute-done.20.up = bf16[128,1536]{1,0:T(8,128)(2,1)S(1)} collective-permute-done((bf16[128,1536]{1,0:T(8,128)(2,1)S(1)}, bf16[128,1536]{1,0:T(8,128)(2,1)S(1)}, u32[]{:S(2)}, u32[]{:S(2)}) %collective-permute-start.20) | collective-permute-done | bytes 393248 | tf_op jit(solution)/shard_map/ppermute | solution.py:26
  65.0 0.6 ring_add.3
  65.7 3.2 %collective-permute-start.24 = (bf16[2,128,1536]{2,1,0:T(8,128)(2,1)S(1)}, bf16[2,128,1536]{2,1,0:T(8,128)(2,1)S(1)}, u32[]{:S(2)}, u32[]{:S(2)}) collective-permute-start(bf16[2,128,1536]{2,1,0:T(8,128)(2,1)S(1)} %get-tuple-element.115), channel_id=1, source_target_pairs={{0,6},{2,0},{4,2},{6,4},{1,7},{3,1},{5,3},{7,5},{8,14},{10,8},{12,... | collective-permute-start | bytes 2359304 | tf_op jit(solution)/shard_map/ppermute | solution.py:26
  69.0 12.9 %collective-permute-done.18.up = bf16[2,128,1536]{2,1,0:T(8,128)(2,1)S(1)} collective-permute-done((bf16[2,128,1536]{2,1,0:T(8,128)(2,1)S(1)}, bf16[2,128,1536]{2,1,0:T(8,128)(2,1)S(1)}, u32[]{:S(2)}, u32[]{:S(2)}) %collective-permute-start.18) | collective-permute-done | bytes 786464 | tf_op jit(solution)/shard_map/ppermute | solution.py:26
  81.9 0.7 own_sum.2
  82.6 0.7 collective-permute-start.22
  83.3 14.2 %collective-permute-done.23.up = bf16[2,128,1536]{2,1,0:T(8,128)(2,1)S(1)} collective-permute-done((bf16[2,128,1536]{2,1,0:T(8,128)(2,1)S(1)}, bf16[2,128,1536]{2,1,0:T(8,128)(2,1)S(1)}, u32[]{:S(2)}, u32[]{:S(2)}) %collective-permute-start.23) | collective-permute-done | bytes 786464 | tf_op jit(solution)/shard_map/ppermute | solution.py:26
  97.5 0.7 own_sum.3
  98.2 0.9 collective-permute-start.27
  99.1 0.7 collective-permute-done.22.other
  99.8 0.7 hidden.2.mine.refs_0_.refs_1_
  100.8 1.8 collective-permute-start.26
  102.6 14.2 %collective-permute-done.27.other = bf16[2,128,1536]{2,1,0:T(8,128)(2,1)S(1)} collective-permute-done((bf16[2,128,1536]{2,1,0:T(8,128)(2,1)S(1)}, bf16[2,128,1536]{2,1,0:T(8,128)(2,1)S(1)}, u32[]{:S(2)}, u32[]{:S(2)}) %collective-permute-start.27) | collective-permute-done | bytes 786464 | tf_op jit(solution)/shard_map/ppermute | solution.py:26
  116.8 0.7 hidden.3.mine.refs_0_.refs_1_
  117.8 1.8 collective-permute-start.31
  119.7 1.5 collective-permute-start.28
  121.2 0.6 collective-permute-start.29
  121.8 16.3 %collective-permute-done.30.above.refs_2_.refs_3_ = bf16[2,128,1536]{2,1,0:T(8,128)(2,1)S(1)} collective-permute-done((bf16[2,128,1536]{2,1,0:T(8,128)(2,1)S(1)}, bf16[2,128,1536]{2,1,0:T(8,128)(2,1)S(1)}, u32[]{:S(2)}, u32[]{:S(2)}) %collective-permute-start.30) | collective-permute-done | bytes 786464 | tf_op jit(solution)/shard_map/ppermute | solution.py:26
  138.1 1.4 collective-permute-done.31.below.refs_6_.refs_7_
  139.6 2.0 %collective-permute-start.34 = (bf16[128,1536]{1,0:T(8,128)(2,1)S(1)}, bf16[128,1536]{1,0:T(8,128)(2,1)S(1)}, u32[]{:S(2)}, u32[]{:S(2)}) collective-permute-start(bf16[128,1536]{1,0:T(8,128)(2,1)S(1)} %get-tuple-element.136), channel_id=1, source_target_pairs={{0,2},{2,4},{4,6},{6,0},{1,3},{3,5},{5,7},{7,1},{8,10},{10,12},{12... | collective-permute-start | bytes 1179656 | tf_op jit(solution)/shard_map/ppermute | solution.py:26
  141.6 4.9 %collective-permute-done.28.refs_4_ = bf16[128,1536]{1,0:T(8,128)(2,1)S(1)} collective-permute-done((bf16[128,1536]{1,0:T(8,128)(2,1)S(1)}, bf16[128,1536]{1,0:T(8,128)(2,1)S(1)}, u32[]{:S(2)}, u32[]{:S(2)}) %collective-permute-start.28) | collective-permute-done | bytes 393248 | tf_op jit(solution)/shard_map/ppermute | solution.py:26
  146.5 1.4 collective-permute-done.29.grad2.refs_5_
  147.9 3.9 %input_a.1 = (f32[512,384]{1,0:T(8,128)S(1)}, f32[512,384]{1,0:T(8,128)}) custom-call(bf16[2,128,1536]{2,1,0:T(8,128)(2,1)S(1)} %hidden.2.mine.refs_0_.refs_1_, bf16[2,128,1536]{2,1,0:T(8,128)(2,1)S(1)} %collective-permute-done.25.above.refs_2_.refs_3_, bf16[128,1536]{1,0:T(8,128)(2,1)S(1)} %collective-permute-done.29.grad2.refs_5_, ...), custom_call_target="tpu_custom_call" | custom-call | bytes 369000 | tf_op jit(solution)/shard_map/input_a/pallas_call | solution.py:47
  151.8 3.7 %grads_a.1 = (f32[768,1536]{1,0:T(8,128)S(1)}, f32[1536,768]{1,0:T(8,128)S(1)}) custom-call(bf16[512,768]{1,0:T(8,128)(2,1)S(1)} %get-tuple-element.137.tok, bf16[512,768]{1,0:T(8,128)(2,1)S(1)} %get-tuple-element.138.cot, bf16[2,128,1536]{2,1,0:T(8,128)(2,1)S(1)} %hidden.2.mine.refs_0_.refs_1_, bf16[2,128,1536]{2,1,0:T(8,128)(2,1)S(1)} %hidden.2.mine.refs_0_.refs_1_, ...), custom_call_target="tpu_custom_call" | custom-call | bytes 369000 | tf_op jit(solution)/shard_map/grads_a/pallas_call | solution.py:47
  155.5 3.9 %input_b.1 = (f32[512,384]{1,0:T(8,128)S(1)}, f32[512,384]{1,0:T(8,128)}) custom-call(bf16[2,128,1536]{2,1,0:T(8,128)(2,1)S(1)} %hidden.3.mine.refs_0_.refs_1_, bf16[2,128,1536]{2,1,0:T(8,128)(2,1)S(1)} %collective-permute-done.30.above.refs_2_.refs_3_, bf16[128,1536]{1,0:T(8,128)(2,1)S(1)} %collective-permute-done.34.grad2.refs_5_, ...), custom_call_target="tpu_custom_call" | custom-call | bytes 73800000 | tf_op jit(solution)/shard_map/input_b/pallas_call | solution.py:47
  159.5 0.5 collective-permute-start.35
  160.0 4.7 %grads_b.1 = (bf16[384,1536]{1,0:T(8,128)(2,1)S(1)}, bf16[384,1536]{1,0:T(8,128)(2,1)}, bf16[1536,384]{1,0:T(8,128)(2,1)S(1)}, bf16[1536,384]{1,0:T(8,128)(2,1)}) custom-call(bf16[512,768]{1,0:T(8,128)(2,1)S(1)} %get-tuple-element.149.tok, bf16[512,768]{1,0:T(8,128)(2,1)S(1)} %get-tuple-element.150.cot, ...), custom_call_target="tpu_custom_call" | custom-call | bytes 369000 | tf_op jit(solution)/shard_map/grads_b/pallas_call | solution.py:47
  164.7 0.5 collective-permute-start.37
  165.2 1.1 copy-done.3
  166.4 1.1 copy-done.5
  167.5 3.6 %returns.1 = bf16[8,128,384]{2,1,0:T(8,128)(2,1)} custom-call(s32[1]{0:T(128)} %bitcast.row, f32[4,4,32,384]{3,2,1,0:T(8,128)S(1)} %bitcast.9, f32[4,4,32,384]{3,2,1,0:T(8,128)} %bitcast.4.near_got, f32[4,4,32,384]{3,2,1,0:T(8,128)S(1)} %bitcast.10, f32[4,4,32,384]{3,2,1,0:T(8,128)} %bitcast.6.far_got), custom_call_target="tpu_custom_call" | custom-call | bytes 369000 | tf_op jit(solution)/shard_map/returns/pallas_call | solution.py:47
  171.1 4.2 %all-to-all-start = ((bf16[8,128,384]{2,1,0:T(8,128)(2,1)}), bf16[8,128,384]{2,1,0:T(8,128)(2,1)}, u32[]{:S(2)}, u32[]{:S(2)}) async-start(bf16[8,128,384]{2,1,0:T(8,128)(2,1)} %returns.1), calls=%async_computation | async-start | bytes 1572864 | tf_op jit(solution)/shard_map/all_to_all | solution.py:430
  175.3 14.9 %all-to-all-done = bf16[8,128,384]{2,1,0:T(8,128)(2,1)} async-done(((bf16[8,128,384]{2,1,0:T(8,128)(2,1)}), bf16[8,128,384]{2,1,0:T(8,128)(2,1)}, u32[]{:S(2)}, u32[]{:S(2)}) %all-to-all-start) | async-done | bytes 786464 | tf_op jit(solution)/shard_map/all_to_all | solution.py:430
  190.2 1.2 convert_reduce_fusion
  191.4 0.7 fusion.1
  192.1 5.5 %place.1 = (bf16[384,3072]{1,0:T(8,128)(2,1)}, bf16[3072,384]{1,0:T(8,128)(2,1)}) custom-call(s32[1]{0:T(128)} %bitcast.2._.core, bf16[384,1536]{1,0:T(8,128)(2,1)S(1)} %get-tuple-element.157.wi_own, bf16[384,1536]{1,0:T(8,128)(2,1)S(1)} %collective-permute-done.36.wi_got, bf16[1536,384]{1,0:T(8,128)(2,1)S(1)} %get-tuple-element.163.wo_own, ...), custom_call_target="tpu_custom_call" | custom-call | bytes 18450000 | tf_op jit(solution)/shard_map/place/pallas_call | solution.py:47
  (50 shorter events, 2.6 us)
Async XLA Ops:
  1.7 1.7 copy-start
  3.4 1.7 copy-start.1
  5.7 8.9 %collective-permute-start.3 = (bf16[2,4,384,384]{3,2,1,0:T(8,128)(2,1)S(1)}, bf16[2,4,384,384]{3,2,1,0:T(8,128)(2,1)S(1)}, u32[]{:S(2)}, u32[]{:S(2)}) collective-permute-start(bf16[2,4,384,384]{3,2,1,0:T(8,128)(2,1)S(1)} %pack.1), channel_id=1, source_target_pairs={{0,1},{1,0},{2,3},{3,2},{4,5},{5,4},{6,7},{7,6},{8,9},{9,8},{10,11... | collective-permute-start | bytes 7077896 | tf_op jit(solution)/shard_map/ppermute | solution.py:26
  5.8 8.8 %collective-permute-start.4 = (bf16[4,32,768]{2,1,0:T(8,128)(2,1)S(1)}, bf16[4,32,768]{2,1,0:T(8,128)(2,1)S(1)}, u32[]{:S(2)}, u32[]{:S(2)}) collective-permute-start(bf16[4,32,768]{2,1,0:T(8,128)(2,1)S(1)} %fusion.2.refs_0_), channel_id=1, source_target_pairs={{0,16},{16,0},{1,17},{17,1},{2,18},{18,2},{3,19},{19,3},{4,20},{20... | collective-permute-start | bytes 589832 | tf_op jit(solution)/shard_map/ppermute | solution.py:26
  9.0 11.7 %collective-permute-start = (bf16[4,32,768]{2,1,0:T(8,128)(2,1)S(1)}, bf16[4,32,768]{2,1,0:T(8,128)(2,1)S(1)}, u32[]{:S(2)}, u32[]{:S(2)}) collective-permute-start(bf16[4,32,768]{2,1,0:T(8,128)(2,1)S(1)} %fusion.2.refs_0_), channel_id=1, source_target_pairs={{0,96},{32,0},{64,32},{96,64},{1,97},{33,1},{65,33},{97,65},{2,98}... | collective-permute-start | bytes 589832 | tf_op jit(solution)/shard_map/ppermute | solution.py:26
  12.0 9.3 %collective-permute-start.1 = (bf16[4,32,768]{2,1,0:T(8,128)(2,1)S(1)}, bf16[4,32,768]{2,1,0:T(8,128)(2,1)S(1)}, u32[]{:S(2)}, u32[]{:S(2)}) collective-permute-start(bf16[4,32,768]{2,1,0:T(8,128)(2,1)S(1)} %fusion.2.refs_0_), channel_id=1, source_target_pairs={{0,64},{32,96},{64,0},{96,32},{1,65},{33,97},{65,1},{97,33},{2,66}... | collective-permute-start | bytes 589832 | tf_op jit(solution)/shard_map/ppermute | solution.py:26
  12.6 11.8 %collective-permute-start.2 = (bf16[4,32,768]{2,1,0:T(8,128)(2,1)S(1)}, bf16[4,32,768]{2,1,0:T(8,128)(2,1)S(1)}, u32[]{:S(2)}, u32[]{:S(2)}) collective-permute-start(bf16[4,32,768]{2,1,0:T(8,128)(2,1)S(1)} %fusion.2.refs_0_), channel_id=1, source_target_pairs={{0,32},{32,64},{64,96},{96,0},{1,33},{33,65},{65,97},{97,1},{2,34}... | collective-permute-start | bytes 589832 | tf_op jit(solution)/shard_map/ppermute | solution.py:26
  14.6 10.9 %collective-permute-start.5 = (bf16[4,32,768]{2,1,0:T(8,128)(2,1)S(1)}, bf16[4,32,768]{2,1,0:T(8,128)(2,1)S(1)}, u32[]{:S(2)}, u32[]{:S(2)}) collective-permute-start(bf16[4,32,768]{2,1,0:T(8,128)(2,1)S(1)} %fusion.2.refs_0_), channel_id=1, source_target_pairs={{0,1},{1,0},{2,3},{3,2},{4,5},{5,4},{6,7},{7,6},{8,9},{9,8},{10,11... | collective-permute-start | bytes 589832 | tf_op jit(solution)/shard_map/ppermute | solution.py:26
  24.4 1.8 collective-permute-start.6
  24.4 2.6 %collective-permute-start.7 = (bf16[4,32,768]{2,1,0:T(8,128)(2,1)S(1)}, bf16[4,32,768]{2,1,0:T(8,128)(2,1)S(1)}, u32[]{:S(2)}, u32[]{:S(2)}) collective-permute-start(bf16[4,32,768]{2,1,0:T(8,128)(2,1)S(1)} %collective-permute-done.1.refs_2_), channel_id=1, source_target_pairs={{0,1},{1,0},{2,3},{3,2},{4,5},{5,4},{6,7},{7,6},{8,9},{9,8},{10,11... | collective-permute-start | bytes 589832 | tf_op jit(solution)/shard_map/ppermute | solution.py:26
  24.9 2.1 %collective-permute-start.8 = (bf16[4,32,768]{2,1,0:T(8,128)(2,1)S(1)}, bf16[4,32,768]{2,1,0:T(8,128)(2,1)S(1)}, u32[]{:S(2)}, u32[]{:S(2)}) collective-permute-start(bf16[4,32,768]{2,1,0:T(8,128)(2,1)S(1)} %collective-permute-done.2.refs_3_), channel_id=1, source_target_pairs={{0,1},{1,0},{2,3},{3,2},{4,5},{5,4},{6,7},{7,6},{8,9},{9,8},{10,11... | collective-permute-start | bytes 589832 | tf_op jit(solution)/shard_map/ppermute | solution.py:26
  24.9 7.7 %collective-permute-start.11 = (bf16[4,32,768]{2,1,0:T(8,128)(2,1)S(1)}, bf16[4,32,768]{2,1,0:T(8,128)(2,1)S(1)}, u32[]{:S(2)}, u32[]{:S(2)}) collective-permute-start(bf16[4,32,768]{2,1,0:T(8,128)(2,1)S(1)} %collective-permute-done.4.refs_0_), channel_id=1, source_target_pairs={{0,96},{32,0},{64,32},{96,64},{1,97},{33,1},{65,33},{97,65},{2,98}... | collective-permute-start | bytes 589832 | tf_op jit(solution)/shard_map/ppermute | solution.py:26
  25.5 9.3 %collective-permute-start.12 = (bf16[4,32,768]{2,1,0:T(8,128)(2,1)S(1)}, bf16[4,32,768]{2,1,0:T(8,128)(2,1)S(1)}, u32[]{:S(2)}, u32[]{:S(2)}) collective-permute-start(bf16[4,32,768]{2,1,0:T(8,128)(2,1)S(1)} %collective-permute-done.4.refs_0_), channel_id=1, source_target_pairs={{0,64},{32,96},{64,0},{96,32},{1,65},{33,97},{65,1},{97,33},{2,66}... | collective-permute-start | bytes 589832 | tf_op jit(solution)/shard_map/ppermute | solution.py:26
  26.2 12.1 %collective-permute-start.13 = (bf16[4,32,768]{2,1,0:T(8,128)(2,1)S(1)}, bf16[4,32,768]{2,1,0:T(8,128)(2,1)S(1)}, u32[]{:S(2)}, u32[]{:S(2)}) collective-permute-start(bf16[4,32,768]{2,1,0:T(8,128)(2,1)S(1)} %collective-permute-done.4.refs_0_), channel_id=1, source_target_pairs={{0,32},{32,64},{64,96},{96,0},{1,33},{33,65},{65,97},{97,1},{2,34}... | collective-permute-start | bytes 589832 | tf_op jit(solution)/shard_map/ppermute | solution.py:26
  38.3 5.1 %collective-permute-start.14 = (bf16[4,32,768]{2,1,0:T(8,128)(2,1)S(1)}, bf16[4,32,768]{2,1,0:T(8,128)(2,1)S(1)}, u32[]{:S(2)}, u32[]{:S(2)}) collective-permute-start(bf16[4,32,768]{2,1,0:T(8,128)(2,1)S(1)} %collective-permute-done.4.refs_0_), channel_id=1, source_target_pairs={{0,1},{1,0},{2,3},{3,2},{4,5},{5,4},{6,7},{7,6},{8,9},{9,8},{10,11... | collective-permute-start | bytes 589832 | tf_op jit(solution)/shard_map/ppermute | solution.py:26
  38.3 5.0 %collective-permute-start.15 = (bf16[4,32,768]{2,1,0:T(8,128)(2,1)S(1)}, bf16[4,32,768]{2,1,0:T(8,128)(2,1)S(1)}, u32[]{:S(2)}, u32[]{:S(2)}) collective-permute-start(bf16[4,32,768]{2,1,0:T(8,128)(2,1)S(1)} %collective-permute-done.11.refs_1_), channel_id=1, source_target_pairs={{0,1},{1,0},{2,3},{3,2},{4,5},{5,4},{6,7},{7,6},{8,9},{9,8},{10,11... | collective-permute-start | bytes 589832 | tf_op jit(solution)/shard_map/ppermute | solution.py:26
  38.8 4.6 %collective-permute-start.16 = (bf16[4,32,768]{2,1,0:T(8,128)(2,1)S(1)}, bf16[4,32,768]{2,1,0:T(8,128)(2,1)S(1)}, u32[]{:S(2)}, u32[]{:S(2)}) collective-permute-start(bf16[4,32,768]{2,1,0:T(8,128)(2,1)S(1)} %collective-permute-done.12.refs_2_), channel_id=1, source_target_pairs={{0,1},{1,0},{2,3},{3,2},{4,5},{5,4},{6,7},{7,6},{8,9},{9,8},{10,11... | collective-permute-start | bytes 589832 | tf_op jit(solution)/shard_map/ppermute | solution.py:26
  38.8 4.5 %collective-permute-start.17 = (bf16[4,32,768]{2,1,0:T(8,128)(2,1)S(1)}, bf16[4,32,768]{2,1,0:T(8,128)(2,1)S(1)}, u32[]{:S(2)}, u32[]{:S(2)}) collective-permute-start(bf16[4,32,768]{2,1,0:T(8,128)(2,1)S(1)} %collective-permute-done.13.refs_3_), channel_id=1, source_target_pairs={{0,1},{1,0},{2,3},{3,2},{4,5},{5,4},{6,7},{7,6},{8,9},{9,8},{10,11... | collective-permute-start | bytes 589832 | tf_op jit(solution)/shard_map/ppermute | solution.py:26
  39.3 13.5 %collective-permute-start.10 = (bf16[128,1536]{1,0:T(8,128)(2,1)S(1)}, bf16[128,1536]{1,0:T(8,128)(2,1)S(1)}, u32[]{:S(2)}, u32[]{:S(2)}) collective-permute-start(bf16[128,1536]{1,0:T(8,128)(2,1)S(1)} %get-tuple-element.98), channel_id=1, source_target_pairs={{0,6},{2,0},{4,2},{6,4},{1,7},{3,1},{5,3},{7,5},{8,14},{10,8},{12,... | collective-permute-start | bytes 1179656 | tf_op jit(solution)/shard_map/ppermute | solution.py:26
  43.4 13.2 %collective-permute-start.9 = (bf16[128,1536]{1,0:T(8,128)(2,1)S(1)}, bf16[128,1536]{1,0:T(8,128)(2,1)S(1)}, u32[]{:S(2)}, u32[]{:S(2)}) collective-permute-start(bf16[128,1536]{1,0:T(8,128)(2,1)S(1)} %get-tuple-element.97), channel_id=1, source_target_pairs={{0,2},{2,4},{4,6},{6,0},{1,3},{3,5},{5,7},{7,1},{8,10},{10,12},{12... | collective-permute-start | bytes 1179656 | tf_op jit(solution)/shard_map/ppermute | solution.py:26
  47.2 17.8 %collective-permute-start.20 = (bf16[128,1536]{1,0:T(8,128)(2,1)S(1)}, bf16[128,1536]{1,0:T(8,128)(2,1)S(1)}, u32[]{:S(2)}, u32[]{:S(2)}) collective-permute-start(bf16[128,1536]{1,0:T(8,128)(2,1)S(1)} %get-tuple-element.105), channel_id=1, source_target_pairs={{0,2},{2,4},{4,6},{6,0},{1,3},{3,5},{5,7},{7,1},{8,10},{10,12},{12... | collective-permute-start | bytes 1179656 | tf_op jit(solution)/shard_map/ppermute | solution.py:26
  47.5 17.5 %collective-permute-start.21 = (bf16[128,1536]{1,0:T(8,128)(2,1)S(1)}, bf16[128,1536]{1,0:T(8,128)(2,1)S(1)}, u32[]{:S(2)}, u32[]{:S(2)}) collective-permute-start(bf16[128,1536]{1,0:T(8,128)(2,1)S(1)} %get-tuple-element.111), channel_id=1, source_target_pairs={{0,6},{2,0},{4,2},{6,4},{1,7},{3,1},{5,3},{7,5},{8,14},{10,8},{12,... | collective-permute-start | bytes 1179656 | tf_op jit(solution)/shard_map/ppermute | solution.py:26
  57.2 24.6 %collective-permute-start.18 = (bf16[2,128,1536]{2,1,0:T(8,128)(2,1)S(1)}, bf16[2,128,1536]{2,1,0:T(8,128)(2,1)S(1)}, u32[]{:S(2)}, u32[]{:S(2)}) collective-permute-start(bf16[2,128,1536]{2,1,0:T(8,128)(2,1)S(1)} %get-tuple-element.108), channel_id=1, source_target_pairs={{0,2},{2,4},{4,6},{6,0},{1,3},{3,5},{5,7},{7,1},{8,10},{10,12},{12... | collective-permute-start | bytes 2359304 | tf_op jit(solution)/shard_map/ppermute | solution.py:26
  57.3 24.5 %collective-permute-start.19 = (bf16[2,128,1536]{2,1,0:T(8,128)(2,1)S(1)}, bf16[2,128,1536]{2,1,0:T(8,128)(2,1)S(1)}, u32[]{:S(2)}, u32[]{:S(2)}) collective-permute-start(bf16[2,128,1536]{2,1,0:T(8,128)(2,1)S(1)} %get-tuple-element.109), channel_id=1, source_target_pairs={{0,6},{2,0},{4,2},{6,4},{1,7},{3,1},{5,3},{7,5},{8,14},{10,8},{12,... | collective-permute-start | bytes 2359304 | tf_op jit(solution)/shard_map/ppermute | solution.py:26
  65.7 31.8 %collective-permute-start.23 = (bf16[2,128,1536]{2,1,0:T(8,128)(2,1)S(1)}, bf16[2,128,1536]{2,1,0:T(8,128)(2,1)S(1)}, u32[]{:S(2)}, u32[]{:S(2)}) collective-permute-start(bf16[2,128,1536]{2,1,0:T(8,128)(2,1)S(1)} %get-tuple-element.114), channel_id=1, source_target_pairs={{0,2},{2,4},{4,6},{6,0},{1,3},{3,5},{5,7},{7,1},{8,10},{10,12},{12... | collective-permute-start | bytes 2359304 | tf_op jit(solution)/shard_map/ppermute | solution.py:26
  65.7 31.7 %collective-permute-start.24 = (bf16[2,128,1536]{2,1,0:T(8,128)(2,1)S(1)}, bf16[2,128,1536]{2,1,0:T(8,128)(2,1)S(1)}, u32[]{:S(2)}, u32[]{:S(2)}) collective-permute-start(bf16[2,128,1536]{2,1,0:T(8,128)(2,1)S(1)} %get-tuple-element.115), channel_id=1, source_target_pairs={{0,6},{2,0},{4,2},{6,4},{1,7},{3,1},{5,3},{7,5},{8,14},{10,8},{12,... | collective-permute-start | bytes 2359304 | tf_op jit(solution)/shard_map/ppermute | solution.py:26
  82.6 17.2 %collective-permute-start.22 = (bf16[2,128,1536]{2,1,0:T(8,128)(2,1)S(1)}, bf16[2,128,1536]{2,1,0:T(8,128)(2,1)S(1)}, u32[]{:S(2)}, u32[]{:S(2)}) collective-permute-start(bf16[2,128,1536]{2,1,0:T(8,128)(2,1)S(1)} %get-tuple-element.119), channel_id=1, source_target_pairs={{0,8},{8,0},{1,9},{9,1},{2,10},{10,2},{3,11},{11,3},{4,12},{12,4},... | collective-permute-start | bytes 2359304 | tf_op jit(solution)/shard_map/ppermute | solution.py:26
  98.2 18.6 %collective-permute-start.27 = (bf16[2,128,1536]{2,1,0:T(8,128)(2,1)S(1)}, bf16[2,128,1536]{2,1,0:T(8,128)(2,1)S(1)}, u32[]{:S(2)}, u32[]{:S(2)}) collective-permute-start(bf16[2,128,1536]{2,1,0:T(8,128)(2,1)S(1)} %get-tuple-element.122), channel_id=1, source_target_pairs={{0,8},{8,0},{1,9},{9,1},{2,10},{10,2},{3,11},{11,3},{4,12},{12,4},... | collective-permute-start | bytes 2359304 | tf_op jit(solution)/shard_map/ppermute | solution.py:26
  100.5 19.1 %collective-permute-start.25 = (bf16[2,128,1536]{2,1,0:T(8,128)(2,1)S(1)}, bf16[2,128,1536]{2,1,0:T(8,128)(2,1)S(1)}, u32[]{:S(2)}, u32[]{:S(2)}) collective-permute-start(bf16[2,128,1536]{2,1,0:T(8,128)(2,1)S(1)} %hidden.2.mine.refs_0_.refs_1_), channel_id=1, source_target_pairs={{0,6},{2,0},{4,2},{6,4},{1,7},{3,1},{5,3},{7,5},{8,14},{10,8},{12,... | collective-permute-start | bytes 2359304 | tf_op jit(solution)/shard_map/ppermute | solution.py:26
  100.8 18.9 %collective-permute-start.26 = (bf16[2,128,1536]{2,1,0:T(8,128)(2,1)S(1)}, bf16[2,128,1536]{2,1,0:T(8,128)(2,1)S(1)}, u32[]{:S(2)}, u32[]{:S(2)}) collective-permute-start(bf16[2,128,1536]{2,1,0:T(8,128)(2,1)S(1)} %hidden.2.mine.refs_0_.refs_1_), channel_id=1, source_target_pairs={{0,2},{2,4},{4,6},{6,0},{1,3},{3,5},{5,7},{7,1},{8,10},{10,12},{12... | collective-permute-start | bytes 2359304 | tf_op jit(solution)/shard_map/ppermute | solution.py:26
  117.5 20.5 %collective-permute-start.30 = (bf16[2,128,1536]{2,1,0:T(8,128)(2,1)S(1)}, bf16[2,128,1536]{2,1,0:T(8,128)(2,1)S(1)}, u32[]{:S(2)}, u32[]{:S(2)}) collective-permute-start(bf16[2,128,1536]{2,1,0:T(8,128)(2,1)S(1)} %hidden.3.mine.refs_0_.refs_1_), channel_id=1, source_target_pairs={{0,6},{2,0},{4,2},{6,4},{1,7},{3,1},{5,3},{7,5},{8,14},{10,8},{12,... | collective-permute-start | bytes 2359304 | tf_op jit(solution)/shard_map/ppermute | solution.py:26
  117.8 21.7 %collective-permute-start.31 = (bf16[2,128,1536]{2,1,0:T(8,128)(2,1)S(1)}, bf16[2,128,1536]{2,1,0:T(8,128)(2,1)S(1)}, u32[]{:S(2)}, u32[]{:S(2)}) collective-permute-start(bf16[2,128,1536]{2,1,0:T(8,128)(2,1)S(1)} %hidden.3.mine.refs_0_.refs_1_), channel_id=1, source_target_pairs={{0,2},{2,4},{4,6},{6,0},{1,3},{3,5},{5,7},{7,1},{8,10},{10,12},{12... | collective-permute-start | bytes 2359304 | tf_op jit(solution)/shard_map/ppermute | solution.py:26
  119.7 26.8 %collective-permute-start.28 = (bf16[128,1536]{1,0:T(8,128)(2,1)S(1)}, bf16[128,1536]{1,0:T(8,128)(2,1)S(1)}, u32[]{:S(2)}, u32[]{:S(2)}) collective-permute-start(bf16[128,1536]{1,0:T(8,128)(2,1)S(1)} %get-tuple-element.128), channel_id=1, source_target_pairs={{0,6},{2,0},{4,2},{6,4},{1,7},{3,1},{5,3},{7,5},{8,14},{10,8},{12,... | collective-permute-start | bytes 1179656 | tf_op jit(solution)/shard_map/ppermute | solution.py:26
  121.2 26.8 %collective-permute-start.29 = (bf16[128,1536]{1,0:T(8,128)(2,1)S(1)}, bf16[128,1536]{1,0:T(8,128)(2,1)S(1)}, u32[]{:S(2)}, u32[]{:S(2)}) collective-permute-start(bf16[128,1536]{1,0:T(8,128)(2,1)S(1)} %get-tuple-element.129), channel_id=1, source_target_pairs={{0,2},{2,4},{4,6},{6,0},{1,3},{3,5},{5,7},{7,1},{8,10},{10,12},{12... | collective-permute-start | bytes 1179656 | tf_op jit(solution)/shard_map/ppermute | solution.py:26
  139.5 16.0 %collective-permute-start.33 = (bf16[128,1536]{1,0:T(8,128)(2,1)S(1)}, bf16[128,1536]{1,0:T(8,128)(2,1)S(1)}, u32[]{:S(2)}, u32[]{:S(2)}) collective-permute-start(bf16[128,1536]{1,0:T(8,128)(2,1)S(1)} %get-tuple-element.132), channel_id=1, source_target_pairs={{0,6},{2,0},{4,2},{6,4},{1,7},{3,1},{5,3},{7,5},{8,14},{10,8},{12,... | collective-permute-start | bytes 1179656 | tf_op jit(solution)/shard_map/ppermute | solution.py:26
  139.6 15.9 %collective-permute-start.34 = (bf16[128,1536]{1,0:T(8,128)(2,1)S(1)}, bf16[128,1536]{1,0:T(8,128)(2,1)S(1)}, u32[]{:S(2)}, u32[]{:S(2)}) collective-permute-start(bf16[128,1536]{1,0:T(8,128)(2,1)S(1)} %get-tuple-element.136), channel_id=1, source_target_pairs={{0,2},{2,4},{4,6},{6,0},{1,3},{3,5},{5,7},{7,1},{8,10},{10,12},{12... | collective-permute-start | bytes 1179656 | tf_op jit(solution)/shard_map/ppermute | solution.py:26
  151.8 3.7 %copy-start.2 = (f32[512,384]{1,0:T(8,128)}, f32[512,384]{1,0:T(8,128)S(1)}, u32[]{:S(2)}) copy-start(f32[512,384]{1,0:T(8,128)S(1)} %get-tuple-element.134) | copy-start | bytes 2359300
  151.8 13.4 %collective-permute-start.32 = (f32[512,384]{1,0:T(8,128)}, f32[512,384]{1,0:T(8,128)}, u32[]{:S(2)}, u32[]{:S(2)}) collective-permute-start(f32[512,384]{1,0:T(8,128)} %get-tuple-element.135), channel_id=1, source_target_pairs={{0,1},{1,0},{2,3},{3,2},{4,5},{5,4},{6,7},{7,6},{8,9},{9,8},{10,11... | collective-permute-start | bytes 2359304 | tf_op jit(solution)/shard_map/ppermute | solution.py:26
  159.5 5.3 %copy-start.4 = (f32[512,384]{1,0:T(8,128)}, f32[512,384]{1,0:T(8,128)S(1)}, u32[]{:S(2)}) copy-start(f32[512,384]{1,0:T(8,128)S(1)} %get-tuple-element.159) | copy-start | bytes 2359300
  159.5 5.8 %collective-permute-start.35 = (f32[512,384]{1,0:T(8,128)}, f32[512,384]{1,0:T(8,128)}, u32[]{:S(2)}, u32[]{:S(2)}) collective-permute-start(f32[512,384]{1,0:T(8,128)} %get-tuple-element.148), channel_id=1, source_target_pairs={{0,1},{1,0},{2,3},{3,2},{4,5},{5,4},{6,7},{7,6},{8,9},{9,8},{10,11... | collective-permute-start | bytes 2359304 | tf_op jit(solution)/shard_map/ppermute | solution.py:26
  164.7 10.6 %collective-permute-start.36 = (bf16[384,1536]{1,0:T(8,128)(2,1)}, bf16[384,1536]{1,0:T(8,128)(2,1)S(1)}, u32[]{:S(2)}, u32[]{:S(2)}) collective-permute-start(bf16[384,1536]{1,0:T(8,128)(2,1)} %get-tuple-element.161), channel_id=1, source_target_pairs={{0,1},{1,0},{2,3},{3,2},{4,5},{5,4},{6,7},{7,6},{8,9},{9,8},{10,11... | collective-permute-start | bytes 3538952 | tf_op jit(solution)/shard_map/ppermute | solution.py:26
  164.7 27.4 %collective-permute-start.37 = (bf16[1536,384]{1,0:T(8,128)(2,1)}, bf16[1536,384]{1,0:T(8,128)(2,1)}, u32[]{:S(2)}, u32[]{:S(2)}) collective-permute-start(bf16[1536,384]{1,0:T(8,128)(2,1)} %get-tuple-element.164), channel_id=1, source_target_pairs={{0,1},{1,0},{2,3},{3,2},{4,5},{5,4},{6,7},{7,6},{8,9},{9,8},{10,11... | collective-permute-start | bytes 3538952 | tf_op jit(solution)/shard_map/ppermute | solution.py:26
  165.2 1.1 copy-start.3
  166.4 1.1 copy-start.5
  171.1 19.1 %all-to-all-start = ((bf16[8,128,384]{2,1,0:T(8,128)(2,1)}), bf16[8,128,384]{2,1,0:T(8,128)(2,1)}, u32[]{:S(2)}, u32[]{:S(2)}) async-start(bf16[8,128,384]{2,1,0:T(8,128)(2,1)} %returns.1), calls=%async_computation | async-start | bytes 1572864 | tf_op jit(solution)/shard_map/all_to_all | solution.py:430

commit v4 on v3

--- a/solution.py
+++ b/solution.py
@@ -34,13 +34,13 @@
     return lax.optimization_barrier((value, after))[0]
 
 
-COST = dict(pack=0.1, weights=0.1, join_a=0.1, join_b=0.1, products=0.1, ring_add=0.1, own_sum=0.1, hidden=0.1, pass_on=0.1, input_a=0.1, input_b=20, grads_a=0.1, grads_b=0.1, returns=0.1, place=5)
+COST = dict(pack=0.1, weights=0.1, join=0.1, products=0.1, ring_add=0.1, own_sum=0.1, hidden=0.1, pass_on=0.1, input_a=0.1, input_b=20, grads_a=0.1, grads_b=0.1, return_a=0.1, return_b=20, place=0.1)
 
 
 def kernel(name, body, grid, ins, outs, scratch=(), scalar=None):
     def spec(block, index):
         def at(i, *refs):
-            return tuple(i if k == "i" else k(i, refs[0][0]) if callable(k) else k for k in index)
+            return tuple(i if k == "i" else k(i, *(r[0] for r in refs)) if callable(k) else k for k in index)
 
         return pl.BlockSpec(block, at)
 
@@ -105,26 +105,6 @@
     )
 
 
-def join(name, pieces, others):
-    zs, piece, width = pieces[0].shape
-    count = len(pieces)
-    per = count * piece
-
-    def body(*refs):
-        for out, side in zip(refs[-2:], (refs[:count], refs[count:])):
-            for k in range(zs):
-                for j in range(count):
-                    out[pl.ds(k * per + j * piece, piece), :] = side[j][k]
-
-    return kernel(
-        name,
-        body,
-        1,
-        [(a, (zs, piece, width), (0, 0, 0)) for a in (*pieces, *others)],
-        [((zs * per, width), BF16, (zs * per, width), (0, 0))] * 2,
-    )
-
-
 def pass_on(above, below):
     _, per, hid = above.shape
 
@@ -141,17 +121,24 @@
     )
 
 
-def products(own, other, wi, wo):
-    rows, width = own.shape
+def products(own, other, wi, wo, row, side):
+    count, per, width = own.shape
     feat, hid = wi.shape
-    half, per, block = width // 2, rows // 4, hid // STEPS
-
-    def body(own, other, wi, wo, pg, up, down, tok, cot):
+    half, block, pieces = width // 2, hid // STEPS, count // 2
+    piece, rows = per // 4, per * pieces
+
+    def body(_, *refs):
+        sides, (wi, wo, pg, up, down, tok, cot) = refs[: 2 * pieces], refs[2 * pieces :]
+
         @pl.when(pl.program_id(0) == 0)
         def _():
-            for side, ref in enumerate((own, other)):
-                tok[:, side * half : (side + 1) * half] = ref[:, :half]
-                cot[:, side * half : (side + 1) * half] = ref[:, half:]
+            for k in range(4):
+                for j, ref in enumerate(sides):
+                    at = pl.ds(k * per + j % pieces * piece, piece)
+                    columns = slice(j // pieces * half, (j // pieces + 1) * half)
+                    part = ref[0, k * piece : (k + 1) * piece, :]
+                    tok[at, columns] = part[:, :half]
+                    cot[at, columns] = part[:, half:]
 
         p = jnp.dot(tok[...], wi[...], preferred_element_type=F32)
         g = dot(cot[...], wo[...], 1, 1)
@@ -160,12 +147,15 @@
         up[...] = p[2 * per : 3 * per].astype(BF16)
         down[...] = g[2 * per : 3 * per].astype(BF16)
 
-    whole = (rows, width)
+    def at(d):
+        return lambda i, r: (r // 2 + d) % 4 * 2 + (r + side) % 2
+
     return kernel(
         "products",
         body,
         STEPS,
-        [(own, whole, (0, 0)), (other, whole, (0, 0)), (wi, (feat, block), (0, "i")), (wo, (block, feat), ("i", 0))],
+        [(a, (1, per, width), (at(d), 0, 0)) for a in (own, other) for d in range(pieces)]
+        + [(wi, (feat, block), (0, "i")), (wo, (block, feat), ("i", 0))],
         [
             ((2, rows, hid), F32, (2, rows, block), (0, 0, "i")),
             ((per, hid), BF16, (per, block), (0, "i")),
@@ -173,6 +163,7 @@
             ((rows, feat), BF16, (rows, feat), (0, 0)),
             ((rows, feat), BF16, (rows, feat), (0, 0)),
         ],
+        scalar=row,
     )
 
 
@@ -234,20 +225,28 @@
     )[0]
 
 
-def input_part(name, mine, above, grad2, below, wi):
+def input_part(name, mine, above, grad2, below, wi, pieces):
     _, per, hid = mine.shape
     half = wi.shape[0] // 2
-
-    def body(mine, above, grad2, below, wi, own, other):
-        for step, out in enumerate((own, other)):
-
-            @pl.when(pl.program_id(0) == step)
-            def _():
-                for k, grad in enumerate((mine.at[0], above.at[0], grad2, below.at[0])):
-                    out[k * per : (k + 1) * per] = dot(grad[...], wi[...], 1, 1)
-
-    second, whole = (1, per, hid), (4 * per, half)
-    return kernel(
+    width = half // pieces
+
+    def body(mine, above, grad2, below, wi, own, *others):
+        grads = (mine.at[0], above.at[0], grad2, below.at[0])
+
+        @pl.when(pl.program_id(0) == 0)
+        def _():
+            for k, grad in enumerate(grads):
+                part = dot(grad[...], wi[...], 1, 1)
+                for j, other in enumerate(others):
+                    other[k * per : (k + 1) * per] = part[:, j * width : (j + 1) * width]
+
+        @pl.when(pl.program_id(0) == 1)
+        def _():
+            for k, grad in enumerate(grads):
+                own[k * per : (k + 1) * per] = dot(grad[...], wi[...], 1, 1)
+
+    second, whole, part = (1, per, hid), (4 * per, half), (4 * per, width)
+    own, *others = kernel(
         name,
         body,
         2,
@@ -256,31 +255,34 @@
             (above, second, (1, 0, 0)),
             (grad2, (per, hid), (0, 0)),
             (below, second, (1, 0, 0)),
-            (wi, (half, hid), ("i", 0)),
+            (wi, (half, hid), (lambda i: 1 - i, 0)),
         ],
-        [(whole, F32, whole, (0, 0))] * 2,
-    )
-
-
-def returns(near, near_got, far, far_got, row):
-    rows, feat = near.shape
-    piece = rows // 16
-
-    def body(row, near, near_got, far, far_got, out):
-        here = row[0] % 2
-        for at, mine, got in ((here, near, near_got), (1 - here, far, far_got)):
-            out[at] = (mine[...] + got[...]).reshape(4 * piece, feat).astype(BF16)
-
-    split = lambda a: a.reshape(4, 4, piece, feat)
-    block = (4, 1, piece, feat)
-    return kernel(
-        "returns",
-        body,
-        4,
-        [(split(a), block, (0, "i", 0, 0)) for a in (near, near_got, far, far_got)],
-        [((8, 4 * piece, feat), BF16, (2, 4 * piece, feat), (lambda i, r: (r // 2 + i) % 4, 0, 0))],
-        scalar=row,
-    )[0]
+        [(whole, F32, whole, (0, 0))] + [(part, F32, part, (0, 0))] * pieces,
+    )
+    return own, others
+
+
+def return_pieces(name, mine, got, kinds):
+    rows, feat = mine.shape
+    width, pieces = got[0].shape[1], len(kinds)
+    piece = rows // 4 // pieces
+
+    def body(mine, *refs):
+        for j, out in enumerate(refs[len(got) :]):
+            for k in range(4):
+                at = pl.ds((k * pieces + j) * piece, piece)
+                for c, ref in enumerate(refs[: len(got)]):
+                    columns = slice(c * width, (c + 1) * width)
+                    out[k, :, columns] = (mine[at, columns] + ref[at, :]).astype(out.dtype)
+
+    part = (4, piece, feat)
+    return kernel(
+        name,
+        body,
+        1,
+        [(mine, (rows, feat), (0, 0))] + [(a, (rows, width), (0, 0)) for a in got],
+        [(part, kind, part, (0, 0, 0)) for kind in kinds],
+    )
 
 
 def weight_grads(name, tok, cot, blocks, sums=None):
@@ -374,23 +376,17 @@
 
     at_core = jnp.reshape(core, (1,)).astype(jnp.int32)
     at_row = jnp.reshape(lax.axis_index(ROWS), (1,)).astype(jnp.int32)
-    own = relative(jnp.concatenate([tokens, cotangent], 1), -1)
-    across = shift(own, "xh", 1)
-    near = [shift(own, "y", -d) for d in (1, 2, 3)]
-    packed = pack(*gate((w_in, w_out), own), at_core)
-    got = shift(packed, "core", 1)
-    across = gate(across, packed)
-    far = [shift(across, "y", -d) for d in (1, 2, 3)]
-    wi, wo = weights(w_in, w_out, gate(got, across), at_core)
-    near = [own, *gate(near, wi)]
-    near = join("join_a", near, to_core(near))
-
-    pg_a, up_a, down_a, tok_a, cot_a = products(*near, wi, wo)
+    own = relative(jnp.concatenate([tokens, cotangent], 1), -1).reshape(1, rows, 2 * feat)
+    every = lax.all_to_all(jnp.broadcast_to(own, (8, rows, 2 * feat)), ROWS, 0, 0, tiled=True)
+    packed = pack(w_in, w_out, at_core)
+    wi, wo = weights(w_in, w_out, shift(packed, "core", 1), at_core)
+    every = gate(every, wi)
+    every_other = shift(every, "core", 1)
+
+    pg_a, up_a, down_a, tok_a, cot_a = products(every, every_other, wi, wo, at_row, 0)
     r_a = up_down(up_a, down_a)
-
-    far = gate([across, *far], up_a)
-    far = join("join_b", far, to_core(far))
-    pg_b, up_b, down_b, tok_b, cot_b = products(*far, wi, wo)
+    every, every_other = gate((every, every_other), up_a)
+    pg_b, up_b, down_b, tok_b, cot_b = products(every, every_other, wi, wo, at_row, 1)
     r_b = up_down(up_b, down_b)
 
     m_a = ring_add(pg_a, *gate(r_a, up_b))
@@ -414,22 +410,28 @@
     f_b = send_on(*s_b)
 
     f_a = gate(f_a, f_b[2])
-    in_a, in_a_other = input_part("input_a", mine_a, s_a[0], f_a[1], s_a[1], wi)
-    in_a_got = shift(in_a_other, "core", 1)
-    sums = weight_grads("grads_a", tok_a, cot_a, gate((mine_a, s_a[0], *f_a, s_a[1]), in_a_other))
-
-    f_b = gate(f_b[:2], sums)
-    in_b, in_b_other = input_part("input_b", mine_b, s_b[0], f_b[1], s_b[1], wi)
-    in_b_got = shift(in_b_other, "core", 1)
-    blocks = gate((mine_b, s_b[0], *f_b, s_b[1]), in_b_other)
+    in_a, others = input_part("input_a", mine_a, s_a[0], f_a[1], s_a[1], wi, 3)
+    kept, *back = return_pieces("return_a", in_a, to_core(others), (F32, BF16, BF16, BF16))
+    sums = weight_grads("grads_a", tok_a, cot_a, gate((mine_a, s_a[0], *f_a, s_a[1]), back), None)
+    back = [shift(a, "y", d) for d, a in zip((1, 2, 3), back)]
+
+    f_b, back = gate((f_b[:2], back), sums)
+    in_b, others = input_part("input_b", mine_b, s_b[0], f_b[1], s_b[1], wi, 1)
+    others_got = to_core(others)
+    blocks = gate((mine_b, s_b[0], *f_b, s_b[1]), others)
     wi_own, wi_other, wo_own, wo_other = weight_grads("grads_b", tok_b, cot_b, blocks, sums)
-    wi_got, wo_got = to_core((wi_other, wo_other))
-
-    in_a_got, in_b_got = gate((in_a_got, in_b_got), wi_own)
-    back = returns(in_a, in_a_got, in_b, in_b_got, at_row)
-    back = lax.all_to_all(back, ROWS, 0, 0, tiled=True)
-    w_in_grad, w_out_grad = place(wi_own, gate(wi_got, back), wo_own, wo_got, at_core)
-    input_grad = relative(jnp.sum(back.astype(F32), 0), 1).reshape(rows, feat).astype(BF16)
+    far = return_pieces("return_b", in_b, gate(others_got, wi_own), (BF16,) * 4)
+    wi_got, wo_got = to_core(gate((wi_other, wo_other), far))
+    far = [
+        lax.ppermute(a, ROWS, [(i, ((i // 2 + d) % 4) * 2 + (i + 1) % 2) for i in range(8)])
+        for d, a in enumerate(far)
+    ]
+    w_in_grad, w_out_grad = place(wi_own, wi_got, wo_own, wo_got, at_core)
+
+    total = kept
+    for part in back + gate(far, w_in_grad):
+        total = total + part.astype(F32)
+    input_grad = relative(total, 1).reshape(rows, feat).astype(BF16)
     return (input_grad, w_in_grad, w_out_grad)
 
 

time: 198 us -> 198 us (level)
  waiting for transfers between devices: 108 us -> 93.8 us
  local copies, waits for them, and re-layouts: 5.6 us -> 14.1 us
  starting transfers between devices: 40.7 us -> 48.6 us
    ppermute x38 -> x29, waiting for transfers between devices: 93.5 us -> 79.3 us  [shift(): return lax.ppermute(x, axis, [(i, (i + by) % n) for i in range(n)])]
    ppermute x0 -> x4, starting transfers between devices: none -> 9.2 us  [local(): lax.ppermute(a, ROWS, [(i, (i // 2 + d) % 4 * 2 + (i + 1) % 2) for i in r...]
    unnamed x12 -> x38, local copies, waits for them, and re-layouts: 5.6 us -> 12.8 us
    ppermute x38 -> x29, starting transfers between devices: 36.5 us -> 32.4 us  [shift(): return lax.ppermute(x, axis, [(i, (i + by) % n) for i in range(n)])]
    all_to_all x1, starting transfers between devices: 4.21 us -> 7.01 us  [local(): lax.all_to_all(jnp.broadcast_to(own, (8, rows, 2 * feat)), ROWS, 0, 0, ti...]
    pallas_call x20 -> x19, Pallas kernels: 39 us -> 37.8 us  [kernel(): pl.pallas_call(body, name=name, grid_spec=pltpu.PrefetchScalarGridSpec(nu...]
  transfers between devices with their start and end apart: 39 -> 34, of which waited for: 19 -> 18; matrix products, arithmetic and copies ran while one was open for 1% -> 1% of each run, Pallas kernels for 17% -> 14%
where the time goes in v4:
time: 198 us; the launch traced here: 197 us
  waiting for transfers between devices  93.8 us (47%)
  starting transfers between devices  48.6 us (25%)
  Pallas kernels  37.8 us (19%)
  local copies, waits for them, and re-layouts  14.1 us (7%)
    ppermute x29, waiting for transfers between devices, shift(): return lax.ppermute(x, axis, [(i, (i + by) % n) for i in range(n)])  79.3 us
    pallas_call x19, Pallas kernels, kernel(): pl.pallas_call(body, name=name, grid_spec=pltpu.PrefetchScalarGridSpec(nu...  37.8 us
    ppermute x29, starting transfers between devices, shift(): return lax.ppermute(x, axis, [(i, (i + by) % n) for i in range(n)])  32.4 us
    all_to_all x1, waiting for transfers between devices, local(): lax.all_to_all(jnp.broadcast_to(own, (8, rows, 2 * feat)), ROWS, 0, 0, ti...  14.5 us
    unnamed x38, local copies, waits for them, and re-layouts  12.8 us
    ppermute x4, starting transfers between devices, local(): lax.ppermute(a, ROWS, [(i, (i // 2 + d) % 4 * 2 + (i + 1) % 2) for i in r...  9.2 us
    all_to_all x1, starting transfers between devices, local(): lax.all_to_all(jnp.broadcast_to(own, (8, rows, 2 * feat)), ROWS, 0, 0, ti...  7.01 us
  transfers between devices with their start and end apart: 34, of which 18 were waited for; matrix products, arithmetic and copies ran while one was open for 1% of the time, Pallas kernels for 14%

profile of v4, /device:TPU:0, one launch (start us, length us, event | category | flops | bytes accessed | tf_op | source)
XLA Modules:
  0.0 197.3 jit_solution(13739820725158066118)
XLA Ops:
  0.6 1.7 copy-done.5
  2.3 1.7 copy-done.7
  4.0 2.0 %pack.1 = bf16[2,4,384,384]{3,2,1,0:T(8,128)(2,1)} custom-call(s32[1]{0:T(128)} %bitcast.3._.core, bf16[384,3072]{1,0:T(8,128)(2,1)S(1)} %copy-done.5, bf16[3072,384]{1,0:T(8,128)(2,1)S(1)} %copy-done.7), custom_call_target="tpu_custom_call" | custom-call | bytes 369000 | tf_op jit(solution)/shard_map/pack/pallas_call | solution.py:47
  6.1 1.3 broadcast_in_dim.8
  7.4 7.0 %all-to-all-start = ((bf16[8,128,768]{2,1,0:T(8,128)(2,1)}), bf16[8,128,768]{2,1,0:T(8,128)(2,1)S(1)}, u32[]{:S(2)}, u32[]{:S(2)}) async-start(bf16[8,128,768]{2,1,0:T(8,128)(2,1)} %broadcast_in_dim.8), calls=%async_computation | async-start | bytes 3145728 | tf_op jit(solution)/shard_map/all_to_all | solution.py:380
  14.4 1.7 copy-done.6
  16.1 1.7 copy-done.8
  17.8 2.8 %weights.1 = (bf16[768,1536]{1,0:T(8,128)(2,1)S(1)}, bf16[1536,768]{1,0:T(8,128)(2,1)S(1)}) custom-call(s32[1]{0:T(128)} %bitcast.3._.core, bf16[384,3072]{1,0:T(8,128)(2,1)S(1)} %copy-done.6, bf16[3072,384]{1,0:T(8,128)(2,1)S(1)} %copy-done.8, bf16[2,4,384,384]{3,2,1,0:T(8,128)(2,1)} %collective-permute-done.got), custom_call_target="tpu_custom_call" | custom-call | bytes 369000 | tf_op jit(solution)/shard_map/weights/pallas_call | solution.py:47
  20.6 1.4 copy-done
  22.0 1.4 copy-done.3
  23.4 14.5 %all-to-all-done.refs_0_.refs_1_.refs_2_.refs_3_ = bf16[8,128,768]{2,1,0:T(8,128)(2,1)S(1)} async-done(((bf16[8,128,768]{2,1,0:T(8,128)(2,1)}), bf16[8,128,768]{2,1,0:T(8,128)(2,1)S(1)}, u32[]{:S(2)}, u32[]{:S(2)}) %all-to-all-start) | async-done | bytes 1572896 | tf_op jit(solution)/shard_map/all_to_all | solution.py:380
  38.0 3.4 %collective-permute-done.1.refs_4_.refs_5_.refs_6_.refs_7_ = bf16[8,128,768]{2,1,0:T(8,128)(2,1)S(1)} collective-permute-done((bf16[8,128,768]{2,1,0:T(8,128)(2,1)S(1)}, bf16[8,128,768]{2,1,0:T(8,128)(2,1)S(1)}, u32[]{:S(2)}, u32[]{:S(2)}) %collective-permute-start.1) | collective-permute-done | bytes 1572896 | tf_op jit(solution)/shard_map/ppermute | solution.py:26
  41.4 1.7 copy-done.1
  43.0 1.7 copy-done.4
  44.7 3.8 %products.2 = (f32[2,512,1536]{2,1,0:T(8,128)S(1)}, bf16[128,1536]{1,0:T(8,128)(2,1)S(1)}, bf16[128,1536]{1,0:T(8,128)(2,1)S(1)}, bf16[512,768]{1,0:T(8,128)(2,1)S(1)}, bf16[512,768]{1,0:T(8,128)(2,1)S(1)}) custom-call(s32[1]{0:T(128)} %bitcast._, bf16[8,128,768]{2,1,0:T(8,128)(2,1)S(1)} %all-to-all-done.refs_0_.refs_1_.refs_2_.refs_3_, ...), custom_call_target="tpu_custom_call" | custom-call | bytes 369000 | tf_op jit(solution)/shard_map/products/pallas_call | solution.py:47
  48.5 4.1 %collective-permute-start.3 = (bf16[128,1536]{1,0:T(8,128)(2,1)S(1)}, bf16[128,1536]{1,0:T(8,128)(2,1)S(1)}, u32[]{:S(2)}, u32[]{:S(2)}) collective-permute-start(bf16[128,1536]{1,0:T(8,128)(2,1)S(1)} %get-tuple-element.95), channel_id=1, source_target_pairs={{0,6},{2,0},{4,2},{6,4},{1,7},{3,1},{5,3},{7,5},{8,14},{10,8},{12,... | collective-permute-start | bytes 1179656 | tf_op jit(solution)/shard_map/ppermute | solution.py:26
  52.7 3.8 %products.3 = (f32[2,512,1536]{2,1,0:T(8,128)S(1)}, bf16[128,1536]{1,0:T(8,128)(2,1)S(1)}, bf16[128,1536]{1,0:T(8,128)(2,1)S(1)}, bf16[512,768]{1,0:T(8,128)(2,1)S(1)}, bf16[512,768]{1,0:T(8,128)(2,1)S(1)}) custom-call(s32[1]{0:T(128)} %bitcast._, bf16[8,128,768]{2,1,0:T(8,128)(2,1)S(1)} %all-to-all-done.refs_0_.refs_1_.refs_2_.refs_3_, ...), custom_call_target="tpu_custom_call" | custom-call | bytes 369000 | tf_op jit(solution)/shard_map/products/pallas_call | solution.py:47
  56.5 3.3 %collective-permute-start.7 = (bf16[128,1536]{1,0:T(8,128)(2,1)S(1)}, bf16[128,1536]{1,0:T(8,128)(2,1)S(1)}, u32[]{:S(2)}, u32[]{:S(2)}) collective-permute-start(bf16[128,1536]{1,0:T(8,128)(2,1)S(1)} %get-tuple-element.104), channel_id=1, source_target_pairs={{0,6},{2,0},{4,2},{6,4},{1,7},{3,1},{5,3},{7,5},{8,14},{10,8},{12,... | collective-permute-start | bytes 1179656 | tf_op jit(solution)/shard_map/ppermute | solution.py:26
  59.8 2.3 %collective-permute-done.3.down = bf16[128,1536]{1,0:T(8,128)(2,1)S(1)} collective-permute-done((bf16[128,1536]{1,0:T(8,128)(2,1)S(1)}, bf16[128,1536]{1,0:T(8,128)(2,1)S(1)}, u32[]{:S(2)}, u32[]{:S(2)}) %collective-permute-start.3) | collective-permute-done | bytes 393248 | tf_op jit(solution)/shard_map/ppermute | solution.py:26
  62.1 3.7 %collective-permute-done.2.up = bf16[128,1536]{1,0:T(8,128)(2,1)S(1)} collective-permute-done((bf16[128,1536]{1,0:T(8,128)(2,1)S(1)}, bf16[128,1536]{1,0:T(8,128)(2,1)S(1)}, u32[]{:S(2)}, u32[]{:S(2)}) %collective-permute-start.2) | collective-permute-done | bytes 393248 | tf_op jit(solution)/shard_map/ppermute | solution.py:26
  65.9 0.6 ring_add.2
  66.6 3.2 %collective-permute-start.5 = (bf16[2,128,1536]{2,1,0:T(8,128)(2,1)S(1)}, bf16[2,128,1536]{2,1,0:T(8,128)(2,1)S(1)}, u32[]{:S(2)}, u32[]{:S(2)}) collective-permute-start(bf16[2,128,1536]{2,1,0:T(8,128)(2,1)S(1)} %get-tuple-element.102), channel_id=1, source_target_pairs={{0,6},{2,0},{4,2},{6,4},{1,7},{3,1},{5,3},{7,5},{8,14},{10,8},{12,... | collective-permute-start | bytes 2359304 | tf_op jit(solution)/shard_map/ppermute | solution.py:26
  69.8 0.7 collective-permute-done.7.down
  70.6 3.7 %collective-permute-done.6.up = bf16[128,1536]{1,0:T(8,128)(2,1)S(1)} collective-permute-done((bf16[128,1536]{1,0:T(8,128)(2,1)S(1)}, bf16[128,1536]{1,0:T(8,128)(2,1)S(1)}, u32[]{:S(2)}, u32[]{:S(2)}) %collective-permute-start.6) | collective-permute-done | bytes 393248 | tf_op jit(solution)/shard_map/ppermute | solution.py:26
  74.3 0.6 ring_add.3
  75.0 3.2 %collective-permute-start.10 = (bf16[2,128,1536]{2,1,0:T(8,128)(2,1)S(1)}, bf16[2,128,1536]{2,1,0:T(8,128)(2,1)S(1)}, u32[]{:S(2)}, u32[]{:S(2)}) collective-permute-start(bf16[2,128,1536]{2,1,0:T(8,128)(2,1)S(1)} %get-tuple-element.108), channel_id=1, source_target_pairs={{0,6},{2,0},{4,2},{6,4},{1,7},{3,1},{5,3},{7,5},{8,14},{10,8},{12,... | collective-permute-start | bytes 2359304 | tf_op jit(solution)/shard_map/ppermute | solution.py:26
  78.2 12.9 %collective-permute-done.4.up = bf16[2,128,1536]{2,1,0:T(8,128)(2,1)S(1)} collective-permute-done((bf16[2,128,1536]{2,1,0:T(8,128)(2,1)S(1)}, bf16[2,128,1536]{2,1,0:T(8,128)(2,1)S(1)}, u32[]{:S(2)}, u32[]{:S(2)}) %collective-permute-start.4) | collective-permute-done | bytes 786464 | tf_op jit(solution)/shard_map/ppermute | solution.py:26
  91.1 0.7 own_sum.2
  91.9 0.7 collective-permute-start.8
  92.5 14.3 %collective-permute-done.9.up = bf16[2,128,1536]{2,1,0:T(8,128)(2,1)S(1)} collective-permute-done((bf16[2,128,1536]{2,1,0:T(8,128)(2,1)S(1)}, bf16[2,128,1536]{2,1,0:T(8,128)(2,1)S(1)}, u32[]{:S(2)}, u32[]{:S(2)}) %collective-permute-start.9) | collective-permute-done | bytes 786464 | tf_op jit(solution)/shard_map/ppermute | solution.py:26
  106.9 0.7 own_sum.3
  107.6 0.7 collective-permute-start.13
  108.3 1.0 collective-permute-done.8.other
  109.3 0.7 hidden.2.mine.refs_0_.refs_1_
  110.1 3.2 %collective-permute-start.11 = (bf16[2,128,1536]{2,1,0:T(8,128)(2,1)S(1)}, bf16[2,128,1536]{2,1,0:T(8,128)(2,1)S(1)}, u32[]{:S(2)}, u32[]{:S(2)}) collective-permute-start(bf16[2,128,1536]{2,1,0:T(8,128)(2,1)S(1)} %hidden.2.mine.refs_0_.refs_1_), channel_id=1, source_target_pairs={{0,6},{2,0},{4,2},{6,4},{1,7},{3,1},{5,3},{7,5},{8,14},{10,8},{12,... | collective-permute-start | bytes 2359304 | tf_op jit(solution)/shard_map/ppermute | solution.py:26
  113.3 12.8 %collective-permute-done.13.other = bf16[2,128,1536]{2,1,0:T(8,128)(2,1)S(1)} collective-permute-done((bf16[2,128,1536]{2,1,0:T(8,128)(2,1)S(1)}, bf16[2,128,1536]{2,1,0:T(8,128)(2,1)S(1)}, u32[]{:S(2)}, u32[]{:S(2)}) %collective-permute-start.13) | collective-permute-done | bytes 786464 | tf_op jit(solution)/shard_map/ppermute | solution.py:26
  126.1 0.7 hidden.3.mine.refs_0_.refs_1_
  127.0 3.2 %collective-permute-start.16 = (bf16[2,128,1536]{2,1,0:T(8,128)(2,1)S(1)}, bf16[2,128,1536]{2,1,0:T(8,128)(2,1)S(1)}, u32[]{:S(2)}, u32[]{:S(2)}) collective-permute-start(bf16[2,128,1536]{2,1,0:T(8,128)(2,1)S(1)} %hidden.3.mine.refs_0_.refs_1_), channel_id=1, source_target_pairs={{0,6},{2,0},{4,2},{6,4},{1,7},{3,1},{5,3},{7,5},{8,14},{10,8},{12,... | collective-permute-start | bytes 2359304 | tf_op jit(solution)/shard_map/ppermute | solution.py:26
  130.2 1.3 collective-permute-start.14
  131.5 0.8 collective-permute-start.15
  132.3 16.3 %collective-permute-done.17.below.refs_6_.refs_7_ = bf16[2,128,1536]{2,1,0:T(8,128)(2,1)S(1)} collective-permute-done((bf16[2,128,1536]{2,1,0:T(8,128)(2,1)S(1)}, bf16[2,128,1536]{2,1,0:T(8,128)(2,1)S(1)}, u32[]{:S(2)}, u32[]{:S(2)}) %collective-permute-start.17) | collective-permute-done | bytes 786464 | tf_op jit(solution)/shard_map/ppermute | solution.py:26
  148.8 3.5 %collective-permute-start.21 = (bf16[128,1536]{1,0:T(8,128)(2,1)S(1)}, bf16[128,1536]{1,0:T(8,128)(2,1)S(1)}, u32[]{:S(2)}, u32[]{:S(2)}) collective-permute-start(bf16[128,1536]{1,0:T(8,128)(2,1)S(1)} %get-tuple-element.125), channel_id=1, source_target_pairs={{0,6},{2,0},{4,2},{6,4},{1,7},{3,1},{5,3},{7,5},{8,14},{10,8},{12,... | collective-permute-start | bytes 1179656 | tf_op jit(solution)/shard_map/ppermute | solution.py:26
  152.3 4.3 %collective-permute-done.14.refs_4_ = bf16[128,1536]{1,0:T(8,128)(2,1)S(1)} collective-permute-done((bf16[128,1536]{1,0:T(8,128)(2,1)S(1)}, bf16[128,1536]{1,0:T(8,128)(2,1)S(1)}, u32[]{:S(2)}, u32[]{:S(2)}) %collective-permute-start.14) | collective-permute-done | bytes 393248 | tf_op jit(solution)/shard_map/ppermute | solution.py:26
  156.6 0.5 collective-permute-done.15.grad2.refs_5_
  157.1 3.0 %input_a.1 = (f32[512,384]{1,0:T(8,128)S(1)}, f32[512,128]{1,0:T(8,128)S(1)}, f32[512,128]{1,0:T(8,128)S(1)}, f32[512,128]{1,0:T(8,128)S(1)}) custom-call(bf16[2,128,1536]{2,1,0:T(8,128)(2,1)S(1)} %hidden.2.mine.refs_0_.refs_1_, bf16[2,128,1536]{2,1,0:T(8,128)(2,1)S(1)} %collective-permute-done.11.above.refs_2_.refs_3_, ...), custom_call_target="tpu_custom_call" | custom-call | bytes 369000 | tf_op jit(solution)/shard_map/input_a/pallas_call | solution.py:47
  160.2 0.5 collective-permute-start.19
  160.8 0.9 collective-permute-done.18.refs_0_
  162.1 0.4 collective-permute-done.20.refs_2_
  162.7 2.8 %collective-permute-start.24 = (bf16[4,32,384]{2,1,0:T(8,128)(2,1)S(1)}, bf16[4,32,384]{2,1,0:T(8,128)(2,1)S(1)}, u32[]{:S(2)}, u32[]{:S(2)}) collective-permute-start(bf16[4,32,384]{2,1,0:T(8,128)(2,1)S(1)} %get-tuple-element.134), channel_id=1, source_target_pairs={{0,64},{32,96},{64,0},{96,32},{1,65},{33,97},{65,1},{97,33},{2,66}... | collective-permute-start | bytes 294920 | tf_op jit(solution)/shard_map/ppermute | solution.py:26
  165.5 0.6 collective-permute-start.25
  166.1 3.7 %grads_a.1 = (f32[768,1536]{1,0:T(8,128)S(1)}, f32[1536,768]{1,0:T(8,128)S(1)}) custom-call(bf16[512,768]{1,0:T(8,128)(2,1)S(1)} %get-tuple-element.136.tok, bf16[512,768]{1,0:T(8,128)(2,1)S(1)} %get-tuple-element.137.cot, bf16[2,128,1536]{2,1,0:T(8,128)(2,1)S(1)} %hidden.2.mine.refs_0_.refs_1_, bf16[2,128,1536]{2,1,0:T(8,128)(2,1)S(1)} %hidden.2.mine.refs_0_.refs_1_, ...), custom_call_target="tpu_custom_call" | custom-call | bytes 369000 | tf_op jit(solution)/shard_map/grads_a/pallas_call | solution.py:47
  169.8 0.9 collective-permute-done.23
  170.8 0.6 collective-permute-done.25
  171.4 3.0 %input_b.1 = (f32[512,384]{1,0:T(8,128)S(1)}, f32[512,384]{1,0:T(8,128)S(1)}) custom-call(bf16[2,128,1536]{2,1,0:T(8,128)(2,1)S(1)} %hidden.3.mine.refs_0_.refs_1_, bf16[2,128,1536]{2,1,0:T(8,128)(2,1)S(1)} %collective-permute-done.16.above.refs_2_.refs_3_, bf16[128,1536]{1,0:T(8,128)(2,1)S(1)} %collective-permute-done.22.grad2.refs_5_, ...), custom_call_target="tpu_custom_call" | custom-call | bytes 73800000 | tf_op jit(solution)/shard_map/input_b/pallas_call | solution.py:47
  174.5 4.7 %grads_b.1 = (bf16[384,1536]{1,0:T(8,128)(2,1)S(1)}, bf16[384,1536]{1,0:T(8,128)(2,1)S(1)}, bf16[1536,384]{1,0:T(8,128)(2,1)S(1)}, bf16[1536,384]{1,0:T(8,128)(2,1)}) custom-call(bf16[512,768]{1,0:T(8,128)(2,1)S(1)} %get-tuple-element.152.tok, bf16[512,768]{1,0:T(8,128)(2,1)S(1)} %get-tuple-element.153.cot, ...), custom_call_target="tpu_custom_call" | custom-call | bytes 369000 | tf_op jit(solution)/shard_map/grads_b/pallas_call | solution.py:47
  179.2 0.8 return_b.1
  180.0 0.5 collective-permute-start.31
  180.5 0.8 collective-permute-start.27
  181.3 2.6 %collective-permute-start.28 = (bf16[4,32,384]{2,1,0:T(8,128)(2,1)}, bf16[4,32,384]{2,1,0:T(8,128)(2,1)}, u32[]{:S(2)}, u32[]{:S(2)}) collective-permute-start(bf16[4,32,384]{2,1,0:T(8,128)(2,1)} %get-tuple-element.163), channel_id=1, source_target_pairs={{0,48},{16,32},{32,80},{48,64},{64,112},{80,96},{96,16},{112,0},{1... | collective-permute-start | bytes 294920 | tf_op jit(solution)/shard_map/ppermute | solution.py:426
  184.0 3.7 %collective-permute-start.29 = (bf16[4,32,384]{2,1,0:T(8,128)(2,1)}, bf16[4,32,384]{2,1,0:T(8,128)(2,1)}, u32[]{:S(2)}, u32[]{:S(2)}) collective-permute-start(bf16[4,32,384]{2,1,0:T(8,128)(2,1)} %get-tuple-element.164), channel_id=1, source_target_pairs={{0,80},{16,64},{32,112},{48,96},{64,16},{80,0},{96,48},{112,32},{1... | collective-permute-start | bytes 294920 | tf_op jit(solution)/shard_map/ppermute | solution.py:426
  187.6 2.1 %collective-permute-start.30 = (bf16[4,32,384]{2,1,0:T(8,128)(2,1)}, bf16[4,32,384]{2,1,0:T(8,128)(2,1)}, u32[]{:S(2)}, u32[]{:S(2)}) collective-permute-start(bf16[4,32,384]{2,1,0:T(8,128)(2,1)} %get-tuple-element.165), channel_id=1, source_target_pairs={{0,112},{16,96},{32,16},{48,0},{64,48},{80,32},{96,80},{112,64},{1... | collective-permute-start | bytes 294920 | tf_op jit(solution)/shard_map/ppermute | solution.py:426
  189.8 5.6 %place.1 = (bf16[384,3072]{1,0:T(8,128)(2,1)}, bf16[3072,384]{1,0:T(8,128)(2,1)}) custom-call(s32[1]{0:T(128)} %bitcast.3._.core, bf16[384,1536]{1,0:T(8,128)(2,1)S(1)} %get-tuple-element.160.wi_own, bf16[384,1536]{1,0:T(8,128)(2,1)S(1)} %collective-permute-done.31.wi_got, bf16[1536,384]{1,0:T(8,128)(2,1)S(1)} %get-tuple-element.169.wo_own, ...), custom_call_target="tpu_custom_call" | custom-call | bytes 369000 | tf_op jit(solution)/shard_map/place/pallas_call | solution.py:47
  195.5 1.1 convert_add_fusion
  196.6 0.7 fusion.1
  (66 shorter events, 1.6 us)
Async XLA Ops:
  0.6 1.7 copy-start.5
  2.3 1.7 copy-start.7
  4.0 2.0 %copy-start.11 = (bf16[128,384]{1,0:T(8,128)(2,1)S(1)}, bf16[128,384]{1,0:T(8,128)(2,1)}, u32[]{:S(2)}) copy-start(bf16[128,384]{1,0:T(8,128)(2,1)} %param.5) | copy-start | bytes 294916
  4.0 2.0 %copy-start.12 = (bf16[128,384]{1,0:T(8,128)(2,1)S(1)}, bf16[128,384]{1,0:T(8,128)(2,1)}, u32[]{:S(2)}) copy-start(bf16[128,384]{1,0:T(8,128)(2,1)} %param.4) | copy-start | bytes 294916
  6.0 8.4 %collective-permute-start = (bf16[2,4,384,384]{3,2,1,0:T(8,128)(2,1)}, bf16[2,4,384,384]{3,2,1,0:T(8,128)(2,1)}, u32[]{:S(2)}, u32[]{:S(2)}) collective-permute-start(bf16[2,4,384,384]{3,2,1,0:T(8,128)(2,1)} %pack.1), channel_id=1, source_target_pairs={{0,1},{1,0},{2,3},{3,2},{4,5},{5,4},{6,7},{7,6},{8,9},{9,8},{10,11... | collective-permute-start | bytes 7077896 | tf_op jit(solution)/shard_map/ppermute | solution.py:26
  7.4 30.5 %all-to-all-start = ((bf16[8,128,768]{2,1,0:T(8,128)(2,1)}), bf16[8,128,768]{2,1,0:T(8,128)(2,1)S(1)}, u32[]{:S(2)}, u32[]{:S(2)}) async-start(bf16[8,128,768]{2,1,0:T(8,128)(2,1)} %broadcast_in_dim.8), calls=%async_computation | async-start | bytes 3145728 | tf_op jit(solution)/shard_map/all_to_all | solution.py:380
  14.4 1.7 copy-start.6
  16.1 1.7 copy-start.8
  20.6 1.4 copy-start
  22.0 1.4 copy-start.3
  38.0 3.4 %collective-permute-start.1 = (bf16[8,128,768]{2,1,0:T(8,128)(2,1)S(1)}, bf16[8,128,768]{2,1,0:T(8,128)(2,1)S(1)}, u32[]{:S(2)}, u32[]{:S(2)}) collective-permute-start(bf16[8,128,768]{2,1,0:T(8,128)(2,1)S(1)} %all-to-all-done.refs_0_.refs_1_.refs_2_.refs_3_), channel_id=1, source_target_pairs={{0,1},{1,0},{2,3},{3,2},{4,5},{5,4},{6,7},{7,6},{8,9},{9,8},{10,11... | collective-permute-start | bytes 4718600 | tf_op jit(solution)/shard_map/ppermute | solution.py:26
  41.4 1.7 copy-start.1
  43.0 1.7 copy-start.4
  48.5 13.6 %collective-permute-start.3 = (bf16[128,1536]{1,0:T(8,128)(2,1)S(1)}, bf16[128,1536]{1,0:T(8,128)(2,1)S(1)}, u32[]{:S(2)}, u32[]{:S(2)}) collective-permute-start(bf16[128,1536]{1,0:T(8,128)(2,1)S(1)} %get-tuple-element.95), channel_id=1, source_target_pairs={{0,6},{2,0},{4,2},{6,4},{1,7},{3,1},{5,3},{7,5},{8,14},{10,8},{12,... | collective-permute-start | bytes 1179656 | tf_op jit(solution)/shard_map/ppermute | solution.py:26
  52.7 13.2 %collective-permute-start.2 = (bf16[128,1536]{1,0:T(8,128)(2,1)S(1)}, bf16[128,1536]{1,0:T(8,128)(2,1)S(1)}, u32[]{:S(2)}, u32[]{:S(2)}) collective-permute-start(bf16[128,1536]{1,0:T(8,128)(2,1)S(1)} %get-tuple-element.94), channel_id=1, source_target_pairs={{0,2},{2,4},{4,6},{6,0},{1,3},{3,5},{5,7},{7,1},{8,10},{10,12},{12... | collective-permute-start | bytes 1179656 | tf_op jit(solution)/shard_map/ppermute | solution.py:26
  56.5 14.0 %collective-permute-start.7 = (bf16[128,1536]{1,0:T(8,128)(2,1)S(1)}, bf16[128,1536]{1,0:T(8,128)(2,1)S(1)}, u32[]{:S(2)}, u32[]{:S(2)}) collective-permute-start(bf16[128,1536]{1,0:T(8,128)(2,1)S(1)} %get-tuple-element.104), channel_id=1, source_target_pairs={{0,6},{2,0},{4,2},{6,4},{1,7},{3,1},{5,3},{7,5},{8,14},{10,8},{12,... | collective-permute-start | bytes 1179656 | tf_op jit(solution)/shard_map/ppermute | solution.py:26
  59.8 14.5 %collective-permute-start.6 = (bf16[128,1536]{1,0:T(8,128)(2,1)S(1)}, bf16[128,1536]{1,0:T(8,128)(2,1)S(1)}, u32[]{:S(2)}, u32[]{:S(2)}) collective-permute-start(bf16[128,1536]{1,0:T(8,128)(2,1)S(1)} %get-tuple-element.98), channel_id=1, source_target_pairs={{0,2},{2,4},{4,6},{6,0},{1,3},{3,5},{5,7},{7,1},{8,10},{10,12},{12... | collective-permute-start | bytes 1179656 | tf_op jit(solution)/shard_map/ppermute | solution.py:26
  66.5 24.6 %collective-permute-start.4 = (bf16[2,128,1536]{2,1,0:T(8,128)(2,1)S(1)}, bf16[2,128,1536]{2,1,0:T(8,128)(2,1)S(1)}, u32[]{:S(2)}, u32[]{:S(2)}) collective-permute-start(bf16[2,128,1536]{2,1,0:T(8,128)(2,1)S(1)} %get-tuple-element.101), channel_id=1, source_target_pairs={{0,2},{2,4},{4,6},{6,0},{1,3},{3,5},{5,7},{7,1},{8,10},{10,12},{12... | collective-permute-start | bytes 2359304 | tf_op jit(solution)/shard_map/ppermute | solution.py:26
  66.6 24.5 %collective-permute-start.5 = (bf16[2,128,1536]{2,1,0:T(8,128)(2,1)S(1)}, bf16[2,128,1536]{2,1,0:T(8,128)(2,1)S(1)}, u32[]{:S(2)}, u32[]{:S(2)}) collective-permute-start(bf16[2,128,1536]{2,1,0:T(8,128)(2,1)S(1)} %get-tuple-element.102), channel_id=1, source_target_pairs={{0,6},{2,0},{4,2},{6,4},{1,7},{3,1},{5,3},{7,5},{8,14},{10,8},{12,... | collective-permute-start | bytes 2359304 | tf_op jit(solution)/shard_map/ppermute | solution.py:26
  74.9 31.9 %collective-permute-start.9 = (bf16[2,128,1536]{2,1,0:T(8,128)(2,1)S(1)}, bf16[2,128,1536]{2,1,0:T(8,128)(2,1)S(1)}, u32[]{:S(2)}, u32[]{:S(2)}) collective-permute-start(bf16[2,128,1536]{2,1,0:T(8,128)(2,1)S(1)} %get-tuple-element.107), channel_id=1, source_target_pairs={{0,2},{2,4},{4,6},{6,0},{1,3},{3,5},{5,7},{7,1},{8,10},{10,12},{12... | collective-permute-start | bytes 2359304 | tf_op jit(solution)/shard_map/ppermute | solution.py:26
  75.0 31.9 %collective-permute-start.10 = (bf16[2,128,1536]{2,1,0:T(8,128)(2,1)S(1)}, bf16[2,128,1536]{2,1,0:T(8,128)(2,1)S(1)}, u32[]{:S(2)}, u32[]{:S(2)}) collective-permute-start(bf16[2,128,1536]{2,1,0:T(8,128)(2,1)S(1)} %get-tuple-element.108), channel_id=1, source_target_pairs={{0,6},{2,0},{4,2},{6,4},{1,7},{3,1},{5,3},{7,5},{8,14},{10,8},{12,... | collective-permute-start | bytes 2359304 | tf_op jit(solution)/shard_map/ppermute | solution.py:26
  91.9 17.4 %collective-permute-start.8 = (bf16[2,128,1536]{2,1,0:T(8,128)(2,1)S(1)}, bf16[2,128,1536]{2,1,0:T(8,128)(2,1)S(1)}, u32[]{:S(2)}, u32[]{:S(2)}) collective-permute-start(bf16[2,128,1536]{2,1,0:T(8,128)(2,1)S(1)} %get-tuple-element.112), channel_id=1, source_target_pairs={{0,8},{8,0},{1,9},{9,1},{2,10},{10,2},{3,11},{11,3},{4,12},{12,4},... | collective-permute-start | bytes 2359304 | tf_op jit(solution)/shard_map/ppermute | solution.py:26
  107.6 18.5 %collective-permute-start.13 = (bf16[2,128,1536]{2,1,0:T(8,128)(2,1)S(1)}, bf16[2,128,1536]{2,1,0:T(8,128)(2,1)S(1)}, u32[]{:S(2)}, u32[]{:S(2)}) collective-permute-start(bf16[2,128,1536]{2,1,0:T(8,128)(2,1)S(1)} %get-tuple-element.115), channel_id=1, source_target_pairs={{0,8},{8,0},{1,9},{9,1},{2,10},{10,2},{3,11},{11,3},{4,12},{12,4},... | collective-permute-start | bytes 2359304 | tf_op jit(solution)/shard_map/ppermute | solution.py:26
  110.0 20.2 %collective-permute-start.12 = (bf16[2,128,1536]{2,1,0:T(8,128)(2,1)S(1)}, bf16[2,128,1536]{2,1,0:T(8,128)(2,1)S(1)}, u32[]{:S(2)}, u32[]{:S(2)}) collective-permute-start(bf16[2,128,1536]{2,1,0:T(8,128)(2,1)S(1)} %hidden.2.mine.refs_0_.refs_1_), channel_id=1, source_target_pairs={{0,2},{2,4},{4,6},{6,0},{1,3},{3,5},{5,7},{7,1},{8,10},{10,12},{12... | collective-permute-start | bytes 2359304 | tf_op jit(solution)/shard_map/ppermute | solution.py:26
  110.1 20.1 %collective-permute-start.11 = (bf16[2,128,1536]{2,1,0:T(8,128)(2,1)S(1)}, bf16[2,128,1536]{2,1,0:T(8,128)(2,1)S(1)}, u32[]{:S(2)}, u32[]{:S(2)}) collective-permute-start(bf16[2,128,1536]{2,1,0:T(8,128)(2,1)S(1)} %hidden.2.mine.refs_0_.refs_1_), channel_id=1, source_target_pairs={{0,6},{2,0},{4,2},{6,4},{1,7},{3,1},{5,3},{7,5},{8,14},{10,8},{12,... | collective-permute-start | bytes 2359304 | tf_op jit(solution)/shard_map/ppermute | solution.py:26
  126.9 30.2 %copy-start.2 = (bf16[768,1536]{1,0:T(8,128)(2,1)S(1)}, bf16[768,1536]{1,0:T(8,128)(2,1)}, u32[]{:S(2)}) copy-start(bf16[768,1536]{1,0:T(8,128)(2,1)} %copy-done) | copy-start | bytes 7077892
  126.9 21.8 %collective-permute-start.17 = (bf16[2,128,1536]{2,1,0:T(8,128)(2,1)S(1)}, bf16[2,128,1536]{2,1,0:T(8,128)(2,1)S(1)}, u32[]{:S(2)}, u32[]{:S(2)}) collective-permute-start(bf16[2,128,1536]{2,1,0:T(8,128)(2,1)S(1)} %hidden.3.mine.refs_0_.refs_1_), channel_id=1, source_target_pairs={{0,2},{2,4},{4,6},{6,0},{1,3},{3,5},{5,7},{7,1},{8,10},{10,12},{12... | collective-permute-start | bytes 2359304 | tf_op jit(solution)/shard_map/ppermute | solution.py:26
  127.0 21.7 %collective-permute-start.16 = (bf16[2,128,1536]{2,1,0:T(8,128)(2,1)S(1)}, bf16[2,128,1536]{2,1,0:T(8,128)(2,1)S(1)}, u32[]{:S(2)}, u32[]{:S(2)}) collective-permute-start(bf16[2,128,1536]{2,1,0:T(8,128)(2,1)S(1)} %hidden.3.mine.refs_0_.refs_1_), channel_id=1, source_target_pairs={{0,6},{2,0},{4,2},{6,4},{1,7},{3,1},{5,3},{7,5},{8,14},{10,8},{12,... | collective-permute-start | bytes 2359304 | tf_op jit(solution)/shard_map/ppermute | solution.py:26
  130.2 26.4 %collective-permute-start.14 = (bf16[128,1536]{1,0:T(8,128)(2,1)S(1)}, bf16[128,1536]{1,0:T(8,128)(2,1)S(1)}, u32[]{:S(2)}, u32[]{:S(2)}) collective-permute-start(bf16[128,1536]{1,0:T(8,128)(2,1)S(1)} %get-tuple-element.121), channel_id=1, source_target_pairs={{0,6},{2,0},{4,2},{6,4},{1,7},{3,1},{5,3},{7,5},{8,14},{10,8},{12,... | collective-permute-start | bytes 1179656 | tf_op jit(solution)/shard_map/ppermute | solution.py:26
  131.5 25.5 %collective-permute-start.15 = (bf16[128,1536]{1,0:T(8,128)(2,1)S(1)}, bf16[128,1536]{1,0:T(8,128)(2,1)S(1)}, u32[]{:S(2)}, u32[]{:S(2)}) collective-permute-start(bf16[128,1536]{1,0:T(8,128)(2,1)S(1)} %get-tuple-element.122), channel_id=1, source_target_pairs={{0,2},{2,4},{4,6},{6,0},{1,3},{3,5},{5,7},{7,1},{8,10},{10,12},{12... | collective-permute-start | bytes 1179656 | tf_op jit(solution)/shard_map/ppermute | solution.py:26
  148.7 21.1 %collective-permute-start.22 = (bf16[128,1536]{1,0:T(8,128)(2,1)S(1)}, bf16[128,1536]{1,0:T(8,128)(2,1)S(1)}, u32[]{:S(2)}, u32[]{:S(2)}) collective-permute-start(bf16[128,1536]{1,0:T(8,128)(2,1)S(1)} %get-tuple-element.132), channel_id=1, source_target_pairs={{0,2},{2,4},{4,6},{6,0},{1,3},{3,5},{5,7},{7,1},{8,10},{10,12},{12... | collective-permute-start | bytes 1179656 | tf_op jit(solution)/shard_map/ppermute | solution.py:26
  148.8 21.1 %collective-permute-start.21 = (bf16[128,1536]{1,0:T(8,128)(2,1)S(1)}, bf16[128,1536]{1,0:T(8,128)(2,1)S(1)}, u32[]{:S(2)}, u32[]{:S(2)}) collective-permute-start(bf16[128,1536]{1,0:T(8,128)(2,1)S(1)} %get-tuple-element.125), channel_id=1, source_target_pairs={{0,6},{2,0},{4,2},{6,4},{1,7},{3,1},{5,3},{7,5},{8,14},{10,8},{12,... | collective-permute-start | bytes 1179656 | tf_op jit(solution)/shard_map/ppermute | solution.py:26
  160.1 1.6 collective-permute-start.18
  160.2 1.9 collective-permute-start.19
  160.7 1.8 collective-permute-start.20
  162.5 7.3 %copy-start.9 = (f32[4,32,384]{2,1,0:T(8,128)}, f32[4,32,384]{2,1,0:T(8,128)S(1)}, u32[]{:S(2)}) copy-start(f32[4,32,384]{2,1,0:T(8,128)S(1)} %get-tuple-element.131) | copy-start | bytes 589828
  162.5 8.2 %collective-permute-start.23 = (bf16[4,32,384]{2,1,0:T(8,128)(2,1)S(1)}, bf16[4,32,384]{2,1,0:T(8,128)(2,1)S(1)}, u32[]{:S(2)}, u32[]{:S(2)}) collective-permute-start(bf16[4,32,384]{2,1,0:T(8,128)(2,1)S(1)} %get-tuple-element.133), channel_id=1, source_target_pairs={{0,32},{32,64},{64,96},{96,0},{1,33},{33,65},{65,97},{97,1},{2,34}... | collective-permute-start | bytes 294920 | tf_op jit(solution)/shard_map/ppermute | solution.py:26
  162.7 8.1 %collective-permute-start.24 = (bf16[4,32,384]{2,1,0:T(8,128)(2,1)S(1)}, bf16[4,32,384]{2,1,0:T(8,128)(2,1)S(1)}, u32[]{:S(2)}, u32[]{:S(2)}) collective-permute-start(bf16[4,32,384]{2,1,0:T(8,128)(2,1)S(1)} %get-tuple-element.134), channel_id=1, source_target_pairs={{0,64},{32,96},{64,0},{96,32},{1,65},{33,97},{65,1},{97,33},{2,66}... | collective-permute-start | bytes 294920 | tf_op jit(solution)/shard_map/ppermute | solution.py:26
  165.5 5.9 %collective-permute-start.25 = (bf16[4,32,384]{2,1,0:T(8,128)(2,1)S(1)}, bf16[4,32,384]{2,1,0:T(8,128)(2,1)S(1)}, u32[]{:S(2)}, u32[]{:S(2)}) collective-permute-start(bf16[4,32,384]{2,1,0:T(8,128)(2,1)S(1)} %get-tuple-element.135), channel_id=1, source_target_pairs={{0,96},{32,0},{64,32},{96,64},{1,97},{33,1},{65,33},{97,65},{2,98}... | collective-permute-start | bytes 294920 | tf_op jit(solution)/shard_map/ppermute | solution.py:26
  170.8 3.7 %copy-start.13 = (bf16[4,32,384]{2,1,0:T(8,128)(2,1)}, bf16[4,32,384]{2,1,0:T(8,128)(2,1)S(1)}, u32[]{:S(2)}) copy-start(bf16[4,32,384]{2,1,0:T(8,128)(2,1)S(1)} %collective-permute-done.23) | copy-start | bytes 294916
  170.8 3.7 %copy-start.15 = (bf16[4,32,384]{2,1,0:T(8,128)(2,1)}, bf16[4,32,384]{2,1,0:T(8,128)(2,1)S(1)}, u32[]{:S(2)}) copy-start(bf16[4,32,384]{2,1,0:T(8,128)(2,1)S(1)} %collective-permute-done.24) | copy-start | bytes 294916
  171.4 3.1 %copy-start.17 = (bf16[4,32,384]{2,1,0:T(8,128)(2,1)}, bf16[4,32,384]{2,1,0:T(8,128)(2,1)S(1)}, u32[]{:S(2)}) copy-start(bf16[4,32,384]{2,1,0:T(8,128)(2,1)S(1)} %collective-permute-done.25) | copy-start | bytes 294916
  174.4 4.8 %collective-permute-start.26 = (f32[512,384]{1,0:T(8,128)S(1)}, f32[512,384]{1,0:T(8,128)S(1)}, u32[]{:S(2)}, u32[]{:S(2)}) collective-permute-start(f32[512,384]{1,0:T(8,128)S(1)} %get-tuple-element.151), channel_id=1, source_target_pairs={{0,1},{1,0},{2,3},{3,2},{4,5},{5,4},{6,7},{7,6},{8,9},{9,8},{10,11... | collective-permute-start | bytes 2359304 | tf_op jit(solution)/shard_map/ppermute | solution.py:26
  180.0 7.6 %collective-permute-start.31 = (bf16[384,1536]{1,0:T(8,128)(2,1)S(1)}, bf16[384,1536]{1,0:T(8,128)(2,1)S(1)}, u32[]{:S(2)}, u32[]{:S(2)}) collective-permute-start(bf16[384,1536]{1,0:T(8,128)(2,1)S(1)} %get-tuple-element.168), channel_id=1, source_target_pairs={{0,1},{1,0},{2,3},{3,2},{4,5},{5,4},{6,7},{7,6},{8,9},{9,8},{10,11... | collective-permute-start | bytes 3538952 | tf_op jit(solution)/shard_map/ppermute | solution.py:26
  180.5 9.2 %collective-permute-start.32 = (bf16[1536,384]{1,0:T(8,128)(2,1)}, bf16[1536,384]{1,0:T(8,128)(2,1)}, u32[]{:S(2)}, u32[]{:S(2)}) collective-permute-start(bf16[1536,384]{1,0:T(8,128)(2,1)} %get-tuple-element.170), channel_id=1, source_target_pairs={{0,1},{1,0},{2,3},{3,2},{4,5},{5,4},{6,7},{7,6},{8,9},{9,8},{10,11... | collective-permute-start | bytes 3538952 | tf_op jit(solution)/shard_map/ppermute | solution.py:26
  180.5 14.9 %collective-permute-start.27 = (bf16[4,32,384]{2,1,0:T(8,128)(2,1)}, bf16[4,32,384]{2,1,0:T(8,128)(2,1)}, u32[]{:S(2)}, u32[]{:S(2)}) collective-permute-start(bf16[4,32,384]{2,1,0:T(8,128)(2,1)} %get-tuple-element.162), channel_id=1, source_target_pairs={{0,16},{16,0},{32,48},{48,32},{64,80},{80,64},{96,112},{112,96},{1... | collective-permute-start | bytes 294920 | tf_op jit(solution)/shard_map/ppermute | solution.py:426
  181.3 14.0 %collective-permute-start.28 = (bf16[4,32,384]{2,1,0:T(8,128)(2,1)}, bf16[4,32,384]{2,1,0:T(8,128)(2,1)}, u32[]{:S(2)}, u32[]{:S(2)}) collective-permute-start(bf16[4,32,384]{2,1,0:T(8,128)(2,1)} %get-tuple-element.163), channel_id=1, source_target_pairs={{0,48},{16,32},{32,80},{48,64},{64,112},{80,96},{96,16},{112,0},{1... | collective-permute-start | bytes 294920 | tf_op jit(solution)/shard_map/ppermute | solution.py:426
  184.0 11.4 %collective-permute-start.29 = (bf16[4,32,384]{2,1,0:T(8,128)(2,1)}, bf16[4,32,384]{2,1,0:T(8,128)(2,1)}, u32[]{:S(2)}, u32[]{:S(2)}) collective-permute-start(bf16[4,32,384]{2,1,0:T(8,128)(2,1)} %get-tuple-element.164), channel_id=1, source_target_pairs={{0,80},{16,64},{32,112},{48,96},{64,16},{80,0},{96,48},{112,32},{1... | collective-permute-start | bytes 294920 | tf_op jit(solution)/shard_map/ppermute | solution.py:426
  187.6 7.8 %collective-permute-start.30 = (bf16[4,32,384]{2,1,0:T(8,128)(2,1)}, bf16[4,32,384]{2,1,0:T(8,128)(2,1)}, u32[]{:S(2)}, u32[]{:S(2)}) collective-permute-start(bf16[4,32,384]{2,1,0:T(8,128)(2,1)} %get-tuple-element.165), channel_id=1, source_target_pairs={{0,112},{16,96},{32,16},{48,0},{64,48},{80,32},{96,80},{112,64},{1... | collective-permute-start | bytes 294920 | tf_op jit(solution)/shard_map/ppermute | solution.py:426
  189.8 5.7 %copy-start.10 = (f32[4,32,384]{2,1,0:T(8,128)S(1)}, f32[4,32,384]{2,1,0:T(8,128)}, u32[]{:S(2)}) copy-start(f32[4,32,384]{2,1,0:T(8,128)} %copy-done.9) | copy-start | bytes 589828
  189.8 5.7 %copy-start.14 = (bf16[4,32,384]{2,1,0:T(8,128)(2,1)S(1)}, bf16[4,32,384]{2,1,0:T(8,128)(2,1)}, u32[]{:S(2)}) copy-start(bf16[4,32,384]{2,1,0:T(8,128)(2,1)} %copy-done.13) | copy-start | bytes 294916
  189.8 5.7 %copy-start.16 = (bf16[4,32,384]{2,1,0:T(8,128)(2,1)S(1)}, bf16[4,32,384]{2,1,0:T(8,128)(2,1)}, u32[]{:S(2)}) copy-start(bf16[4,32,384]{2,1,0:T(8,128)(2,1)} %copy-done.15) | copy-start | bytes 294916
  189.8 5.7 %copy-start.18 = (bf16[4,32,384]{2,1,0:T(8,128)(2,1)S(1)}, bf16[4,32,384]{2,1,0:T(8,128)(2,1)}, u32[]{:S(2)}) copy-start(bf16[4,32,384]{2,1,0:T(8,128)(2,1)} %copy-done.17) | copy-start | bytes 294916

commit v5 on v4

--- a/solution.py
+++ b/solution.py
@@ -34,7 +34,7 @@
     return lax.optimization_barrier((value, after))[0]
 
 
-COST = dict(pack=0.1, weights=0.1, join=0.1, products=0.1, ring_add=0.1, own_sum=0.1, hidden=0.1, pass_on=0.1, input_a=0.1, input_b=20, grads_a=0.1, grads_b=0.1, return_a=0.1, return_b=20, place=0.1)
+COST = dict(pack=0.1, weights=20, join_a=100, join_b=0.1, products=0.1, ring_add=0.1, own_sum=0.1, hidden=0.1, pass_on=0.1, input_a=0.1, input_b=20, grads_a=0.1, grads_b=0.1, return_a=0.1, return_b=20, place=0.1)
 
 
 def kernel(name, body, grid, ins, outs, scratch=(), scalar=None):
@@ -55,7 +55,7 @@
             scratch_shapes=list(scratch),
         ),
         out_shape=[jax.ShapeDtypeStruct(shape, dtype) for shape, dtype, _, _ in outs],
-        cost_estimate=pl.CostEstimate(flops=0, bytes_accessed=int(COST[name] * 3.69e6), transcendentals=0),
+        cost_estimate=pl.CostEstimate(flops=int(COST[name] * 1.15e9), bytes_accessed=int(COST[name] * 3.69e6), transcendentals=0),
         compiler_params=pltpu.CompilerParams(vmem_limit_bytes=24 * 2**20),
     )(*([] if scalar is None else [scalar]), *[a for a, _, _ in ins])
 
@@ -121,24 +121,37 @@
     )
 
 
-def products(own, other, wi, wo, row, side):
-    count, per, width = own.shape
+def join(name, *sides):
+    zs, piece, width = sides[0][0].shape
+    count = len(sides[0])
+    per = count * piece
+
+    def body(*refs):
+        for n, out in enumerate(refs[len(sides) * count :]):
+            for k in range(zs):
+                for j in range(count):
+                    out[pl.ds(k * per + j * piece, piece), :] = refs[n * count + j][k]
+
+    return kernel(
+        name,
+        body,
+        1,
+        [(a, (zs, piece, width), (0, 0, 0)) for side in sides for a in side],
+        [((zs * per, width), BF16, (zs * per, width), (0, 0))] * len(sides),
+    )
+
+
+def products(own, other, wi, wo):
+    rows, width = own.shape
     feat, hid = wi.shape
-    half, block, pieces = width // 2, hid // STEPS, count // 2
-    piece, rows = per // 4, per * pieces
-
-    def body(_, *refs):
-        sides, (wi, wo, pg, up, down, tok, cot) = refs[: 2 * pieces], refs[2 * pieces :]
-
+    half, per, block = width // 2, rows // 4, hid // STEPS
+
+    def body(own, other, wi, wo, pg, up, down, tok, cot):
         @pl.when(pl.program_id(0) == 0)
         def _():
-            for k in range(4):
-                for j, ref in enumerate(sides):
-                    at = pl.ds(k * per + j % pieces * piece, piece)
-                    columns = slice(j // pieces * half, (j // pieces + 1) * half)
-                    part = ref[0, k * piece : (k + 1) * piece, :]
-                    tok[at, columns] = part[:, :half]
-                    cot[at, columns] = part[:, half:]
+            for side, ref in enumerate((own, other)):
+                tok[:, side * half : (side + 1) * half] = ref[:, :half]
+                cot[:, side * half : (side + 1) * half] = ref[:, half:]
 
         p = jnp.dot(tok[...], wi[...], preferred_element_type=F32)
         g = dot(cot[...], wo[...], 1, 1)
@@ -147,15 +160,12 @@
         up[...] = p[2 * per : 3 * per].astype(BF16)
         down[...] = g[2 * per : 3 * per].astype(BF16)
 
-    def at(d):
-        return lambda i, r: (r // 2 + d) % 4 * 2 + (r + side) % 2
-
+    whole = (rows, width)
     return kernel(
         "products",
         body,
         STEPS,
-        [(a, (1, per, width), (at(d), 0, 0)) for a in (own, other) for d in range(pieces)]
-        + [(wi, (feat, block), (0, "i")), (wo, (block, feat), ("i", 0))],
+        [(own, whole, (0, 0)), (other, whole, (0, 0)), (wi, (feat, block), (0, "i")), (wo, (block, feat), ("i", 0))],
         [
             ((2, rows, hid), F32, (2, rows, block), (0, 0, "i")),
             ((per, hid), BF16, (per, block), (0, "i")),
@@ -163,7 +173,6 @@
             ((rows, feat), BF16, (rows, feat), (0, 0)),
             ((rows, feat), BF16, (rows, feat), (0, 0)),
         ],
-        scalar=row,
     )
 
 
@@ -375,18 +384,24 @@
         return shift(act, "z", -1), shift(grad, "z", 1), act
 
     at_core = jnp.reshape(core, (1,)).astype(jnp.int32)
-    at_row = jnp.reshape(lax.axis_index(ROWS), (1,)).astype(jnp.int32)
-    own = relative(jnp.concatenate([tokens, cotangent], 1), -1).reshape(1, rows, 2 * feat)
-    every = lax.all_to_all(jnp.broadcast_to(own, (8, rows, 2 * feat)), ROWS, 0, 0, tiled=True)
-    packed = pack(w_in, w_out, at_core)
-    wi, wo = weights(w_in, w_out, shift(packed, "core", 1), at_core)
-    every = gate(every, wi)
-    every_other = shift(every, "core", 1)
-
-    pg_a, up_a, down_a, tok_a, cot_a = products(every, every_other, wi, wo, at_row, 0)
+    own = relative(jnp.concatenate([tokens, cotangent], 1), -1)
+    near = [own] + [shift(own, "y", -d) for d in (1, 2, 3)]
+    across = shift(own, "xh", 1)
+    packed = pack(*gate((w_in, w_out), own), at_core)
+    got = shift(packed, "core", 1)
+    near = join("join_a", near)[0]
+    near_other = shift(near, "core", 1)
+    across = gate(across, near)
+    far = [shift(across, "y", -d) for d in (1, 2, 3)]
+    across_other = shift(across, "core", 1)
+    wi, wo = weights(w_in, w_out, gate(got, across_other), at_core)
+
+    pg_a, up_a, down_a, tok_a, cot_a = products(near, near_other, wi, wo)
     r_a = up_down(up_a, down_a)
-    every, every_other = gate((every, every_other), up_a)
-    pg_b, up_b, down_b, tok_b, cot_b = products(every, every_other, wi, wo, at_row, 1)
+
+    far = gate(far, up_a)
+    far = join("join_b", [across, *far], [across_other, *to_core(far)])
+    pg_b, up_b, down_b, tok_b, cot_b = products(*far, wi, wo)
     r_b = up_down(up_b, down_b)
 
     m_a = ring_add(pg_a, *gate(r_a, up_b))

time: 198 us -> 179 us (0.904)
  waiting for transfers between devices: 93.8 us -> 82.6 us
  local copies, waits for them, and re-layouts: 14.1 us -> 3.37 us
  starting transfers between devices: 48.6 us -> 54.5 us
  Pallas kernels: 37.8 us -> 34.6 us
    all_to_all x1 -> x0, waiting for transfers between devices: 14.5 us -> none  [local(): lax.all_to_all(jnp.broadcast_to(own, (8, rows, 2 * feat)), ROWS, 0, 0, ti...]
    ppermute x29 -> x40, starting transfers between devices: 32.4 us -> 45.2 us  [shift(): return lax.ppermute(x, axis, [(i, (i + by) % n) for i in range(n)])]
    unnamed x38 -> x22, local copies, waits for them, and re-layouts: 12.8 us -> 3.37 us
    all_to_all x1 -> x0, starting transfers between devices: 7.01 us -> none  [local(): lax.all_to_all(jnp.broadcast_to(own, (8, rows, 2 * feat)), ROWS, 0, 0, ti...]
    pallas_call x19 -> x21, Pallas kernels: 37.8 us -> 34.6 us  [kernel(): pl.pallas_call(body, name=name, grid_spec=pltpu.PrefetchScalarGridSpec(nu...]
    ppermute x29 -> x40, waiting for transfers between devices: 79.3 us -> 80.9 us  [shift(): return lax.ppermute(x, axis, [(i, (i + by) % n) for i in range(n)])]
  transfers between devices with their start and end apart: 34 -> 44, of which waited for: 18 -> 21; matrix products, arithmetic and copies ran while one was open for 1% -> 0% of each run, Pallas kernels for 14% -> 17%
where the time goes in v5:
time: 179 us
  waiting for transfers between devices  82.6 us (46%)
  starting transfers between devices  54.5 us (30%)
  Pallas kernels  34.6 us (19%)
  local copies, waits for them, and re-layouts  3.37 us (2%)
  other arithmetic  2.9 us (2%)
    ppermute x40, waiting for transfers between devices, shift(): return lax.ppermute(x, axis, [(i, (i + by) % n) for i in range(n)])  80.9 us
    ppermute x40, starting transfers between devices, shift(): return lax.ppermute(x, axis, [(i, (i + by) % n) for i in range(n)])  45.2 us
    pallas_call x21, Pallas kernels, kernel(): pl.pallas_call(body, name=name, grid_spec=pltpu.PrefetchScalarGridSpec(nu...  34.6 us
    ppermute x4, starting transfers between devices, local(): lax.ppermute(a, ROWS, [(i, (i // 2 + d) % 4 * 2 + (i + 1) % 2) for i in r...  9.23 us
  transfers between devices with their start and end apart: 44, of which 21 were waited for; matrix products, arithmetic and copies ran while one was open for 0% of the time, Pallas kernels for 17%

profile of v5, /device:TPU:0, one launch (start us, length us, event | category | flops | bytes accessed | tf_op | source)
XLA Modules:
  0.0 179.0 jit_solution(13402960069208388725)
XLA Ops:
  0.7 1.0 pad_maximum_fusion
  1.7 3.2 %collective-permute-start = (bf16[4,32,768]{2,1,0:T(8,128)(2,1)S(1)}, bf16[4,32,768]{2,1,0:T(8,128)(2,1)S(1)}, u32[]{:S(2)}, u32[]{:S(2)}) collective-permute-start(bf16[4,32,768]{2,1,0:T(8,128)(2,1)S(1)} %fusion.2.refs_0_), channel_id=1, source_target_pairs={{0,96},{32,0},{64,32},{96,64},{1,97},{33,1},{65,33},{97,65},{2,98}... | collective-permute-start | bytes 589832 | tf_op jit(solution)/shard_map/ppermute | solution.py:26
  4.9 0.6 collective-permute-start.1
  5.5 1.0 collective-permute-start.2
  6.5 3.0 %collective-permute-start.5 = (bf16[4,32,768]{2,1,0:T(8,128)(2,1)S(1)}, bf16[4,32,768]{2,1,0:T(8,128)(2,1)S(1)}, u32[]{:S(2)}, u32[]{:S(2)}) collective-permute-start(bf16[4,32,768]{2,1,0:T(8,128)(2,1)S(1)} %fusion.2.refs_0_), channel_id=1, source_target_pairs={{0,16},{16,0},{1,17},{17,1},{2,18},{18,2},{3,19},{19,3},{4,20},{20... | collective-permute-start | bytes 589832 | tf_op jit(solution)/shard_map/ppermute | solution.py:26
  9.5 1.7 copy-done
  11.2 1.7 copy-done.2
  12.8 0.7 pack.1
  13.6 0.6 collective-permute-done.1.refs_2_
  14.3 2.7 %collective-permute-done.2.refs_3_ = bf16[4,32,768]{2,1,0:T(8,128)(2,1)S(1)} collective-permute-done((bf16[4,32,768]{2,1,0:T(8,128)(2,1)S(1)}, bf16[4,32,768]{2,1,0:T(8,128)(2,1)S(1)}, u32[]{:S(2)}, u32[]{:S(2)}) %collective-permute-start.2) | collective-permute-done | bytes 196640 | tf_op jit(solution)/shard_map/ppermute | solution.py:26
  17.6 0.6 collective-permute-start.10
  18.3 0.8 collective-permute-start.11
  19.1 2.4 %collective-permute-start.9 = (bf16[4,32,768]{2,1,0:T(8,128)(2,1)S(1)}, bf16[4,32,768]{2,1,0:T(8,128)(2,1)S(1)}, u32[]{:S(2)}, u32[]{:S(2)}) collective-permute-start(bf16[4,32,768]{2,1,0:T(8,128)(2,1)S(1)} %collective-permute-done.5.refs_0_), channel_id=1, source_target_pairs={{0,96},{32,0},{64,32},{96,64},{1,97},{33,1},{65,33},{97,65},{2,98}... | collective-permute-start | bytes 589832 | tf_op jit(solution)/shard_map/ppermute | solution.py:26
  21.5 1.1 weights.1
  22.6 3.7 %products.2 = (f32[2,512,1536]{2,1,0:T(8,128)S(1)}, bf16[128,1536]{1,0:T(8,128)(2,1)S(1)}, bf16[128,1536]{1,0:T(8,128)(2,1)S(1)}, bf16[512,768]{1,0:T(8,128)(2,1)S(1)}, bf16[512,768]{1,0:T(8,128)(2,1)S(1)}) custom-call(bf16[512,768]{1,0:T(8,128)(2,1)S(1)} %join_a.1.own, bf16[512,768]{1,0:T(8,128)(2,1)S(1)} %collective-permute-done.3.other, ...), custom_call_target="tpu_custom_call" | custom-call | flops 115000000 | bytes 369000 | tf_op jit(solution)/shard_map/products/pallas_call | solution.py:47
  26.4 2.0 %collective-permute-start.7 = (bf16[128,1536]{1,0:T(8,128)(2,1)S(1)}, bf16[128,1536]{1,0:T(8,128)(2,1)S(1)}, u32[]{:S(2)}, u32[]{:S(2)}) collective-permute-start(bf16[128,1536]{1,0:T(8,128)(2,1)S(1)} %get-tuple-element.103), channel_id=1, source_target_pairs={{0,2},{2,4},{4,6},{6,0},{1,3},{3,5},{5,7},{7,1},{8,10},{10,12},{12... | collective-permute-start | bytes 1179656 | tf_op jit(solution)/shard_map/ppermute | solution.py:26
  28.4 2.2 %collective-permute-start.8 = (bf16[128,1536]{1,0:T(8,128)(2,1)S(1)}, bf16[128,1536]{1,0:T(8,128)(2,1)S(1)}, u32[]{:S(2)}, u32[]{:S(2)}) collective-permute-start(bf16[128,1536]{1,0:T(8,128)(2,1)S(1)} %get-tuple-element.104), channel_id=1, source_target_pairs={{0,6},{2,0},{4,2},{6,4},{1,7},{3,1},{5,3},{7,5},{8,14},{10,8},{12,... | collective-permute-start | bytes 1179656 | tf_op jit(solution)/shard_map/ppermute | solution.py:26
  30.7 0.5 collective-permute-start.13
  31.3 0.8 collective-permute-done.12.refs_5_
  32.8 3.7 %products.3 = (f32[2,512,1536]{2,1,0:T(8,128)S(1)}, bf16[128,1536]{1,0:T(8,128)(2,1)S(1)}, bf16[128,1536]{1,0:T(8,128)(2,1)S(1)}, bf16[512,768]{1,0:T(8,128)(2,1)S(1)}, bf16[512,768]{1,0:T(8,128)(2,1)S(1)}) custom-call(bf16[512,768]{1,0:T(8,128)(2,1)S(1)} %get-tuple-element.108.own, bf16[512,768]{1,0:T(8,128)(2,1)S(1)} %get-tuple-element.109.other, ...), custom_call_target="tpu_custom_call" | custom-call | flops 115000000 | bytes 369000 | tf_op jit(solution)/shard_map/products/pallas_call | solution.py:47
  36.5 1.6 collective-permute-start.17
  38.1 2.2 %collective-permute-start.18 = (bf16[128,1536]{1,0:T(8,128)(2,1)S(1)}, bf16[128,1536]{1,0:T(8,128)(2,1)S(1)}, u32[]{:S(2)}, u32[]{:S(2)}) collective-permute-start(bf16[128,1536]{1,0:T(8,128)(2,1)S(1)} %get-tuple-element.116), channel_id=1, source_target_pairs={{0,6},{2,0},{4,2},{6,4},{1,7},{3,1},{5,3},{7,5},{8,14},{10,8},{12,... | collective-permute-start | bytes 1179656 | tf_op jit(solution)/shard_map/ppermute | solution.py:26
  40.3 0.6 ring_add.2
  41.0 3.2 %collective-permute-start.16 = (bf16[2,128,1536]{2,1,0:T(8,128)(2,1)S(1)}, bf16[2,128,1536]{2,1,0:T(8,128)(2,1)S(1)}, u32[]{:S(2)}, u32[]{:S(2)}) collective-permute-start(bf16[2,128,1536]{2,1,0:T(8,128)(2,1)S(1)} %get-tuple-element.114), channel_id=1, source_target_pairs={{0,6},{2,0},{4,2},{6,4},{1,7},{3,1},{5,3},{7,5},{8,14},{10,8},{12,... | collective-permute-start | bytes 2359304 | tf_op jit(solution)/shard_map/ppermute | solution.py:26
  44.2 5.8 %collective-permute-done.17.up = bf16[128,1536]{1,0:T(8,128)(2,1)S(1)} collective-permute-done((bf16[128,1536]{1,0:T(8,128)(2,1)S(1)}, bf16[128,1536]{1,0:T(8,128)(2,1)S(1)}, u32[]{:S(2)}, u32[]{:S(2)}) %collective-permute-start.17) | collective-permute-done | bytes 393248 | tf_op jit(solution)/shard_map/ppermute | solution.py:26
  50.1 0.6 ring_add.3
  50.7 2.0 %collective-permute-start.20 = (bf16[2,128,1536]{2,1,0:T(8,128)(2,1)S(1)}, bf16[2,128,1536]{2,1,0:T(8,128)(2,1)S(1)}, u32[]{:S(2)}, u32[]{:S(2)}) collective-permute-start(bf16[2,128,1536]{2,1,0:T(8,128)(2,1)S(1)} %get-tuple-element.119), channel_id=1, source_target_pairs={{0,2},{2,4},{4,6},{6,0},{1,3},{3,5},{5,7},{7,1},{8,10},{10,12},{12... | collective-permute-start | bytes 2359304 | tf_op jit(solution)/shard_map/ppermute | solution.py:26
  52.7 1.5 collective-permute-start.21
  54.2 12.7 %collective-permute-done.15.up = bf16[2,128,1536]{2,1,0:T(8,128)(2,1)S(1)} collective-permute-done((bf16[2,128,1536]{2,1,0:T(8,128)(2,1)S(1)}, bf16[2,128,1536]{2,1,0:T(8,128)(2,1)S(1)}, u32[]{:S(2)}, u32[]{:S(2)}) %collective-permute-start.15) | collective-permute-done | bytes 786464 | tf_op jit(solution)/shard_map/ppermute | solution.py:26
  66.9 0.7 own_sum.2
  67.7 1.6 collective-permute-start.19
  69.2 14.2 %collective-permute-done.20.up = bf16[2,128,1536]{2,1,0:T(8,128)(2,1)S(1)} collective-permute-done((bf16[2,128,1536]{2,1,0:T(8,128)(2,1)S(1)}, bf16[2,128,1536]{2,1,0:T(8,128)(2,1)S(1)}, u32[]{:S(2)}, u32[]{:S(2)}) %collective-permute-start.20) | collective-permute-done | bytes 786464 | tf_op jit(solution)/shard_map/ppermute | solution.py:26
  83.4 0.7 own_sum.3
  84.1 1.6 collective-permute-start.24
  85.7 0.8 collective-permute-done.19.other
  86.5 0.7 hidden.2.mine.refs_0_.refs_1_
  87.3 2.8 %collective-permute-start.22 = (bf16[2,128,1536]{2,1,0:T(8,128)(2,1)S(1)}, bf16[2,128,1536]{2,1,0:T(8,128)(2,1)S(1)}, u32[]{:S(2)}, u32[]{:S(2)}) collective-permute-start(bf16[2,128,1536]{2,1,0:T(8,128)(2,1)S(1)} %hidden.2.mine.refs_0_.refs_1_), channel_id=1, source_target_pairs={{0,6},{2,0},{4,2},{6,4},{1,7},{3,1},{5,3},{7,5},{8,14},{10,8},{12,... | collective-permute-start | bytes 2359304 | tf_op jit(solution)/shard_map/ppermute | solution.py:26
  90.1 13.3 %collective-permute-done.24.other = bf16[2,128,1536]{2,1,0:T(8,128)(2,1)S(1)} collective-permute-done((bf16[2,128,1536]{2,1,0:T(8,128)(2,1)S(1)}, bf16[2,128,1536]{2,1,0:T(8,128)(2,1)S(1)}, u32[]{:S(2)}, u32[]{:S(2)}) %collective-permute-start.24) | collective-permute-done | bytes 786464 | tf_op jit(solution)/shard_map/ppermute | solution.py:26
  103.4 0.7 hidden.3.mine.refs_0_.refs_1_
  104.1 2.8 %collective-permute-start.27 = (bf16[2,128,1536]{2,1,0:T(8,128)(2,1)S(1)}, bf16[2,128,1536]{2,1,0:T(8,128)(2,1)S(1)}, u32[]{:S(2)}, u32[]{:S(2)}) collective-permute-start(bf16[2,128,1536]{2,1,0:T(8,128)(2,1)S(1)} %hidden.3.mine.refs_0_.refs_1_), channel_id=1, source_target_pairs={{0,6},{2,0},{4,2},{6,4},{1,7},{3,1},{5,3},{7,5},{8,14},{10,8},{12,... | collective-permute-start | bytes 2359304 | tf_op jit(solution)/shard_map/ppermute | solution.py:26
  106.9 2.2 %collective-permute-done.23.below.refs_6_.refs_7_ = bf16[2,128,1536]{2,1,0:T(8,128)(2,1)S(1)} collective-permute-done((bf16[2,128,1536]{2,1,0:T(8,128)(2,1)S(1)}, bf16[2,128,1536]{2,1,0:T(8,128)(2,1)S(1)}, u32[]{:S(2)}, u32[]{:S(2)}) %collective-permute-start.23) | collective-permute-done | bytes 786464 | tf_op jit(solution)/shard_map/ppermute | solution.py:26
  109.2 1.1 collective-permute-start.25
  110.3 1.0 collective-permute-start.26
  111.3 13.7 %collective-permute-done.27.above.refs_2_.refs_3_ = bf16[2,128,1536]{2,1,0:T(8,128)(2,1)S(1)} collective-permute-done((bf16[2,128,1536]{2,1,0:T(8,128)(2,1)S(1)}, bf16[2,128,1536]{2,1,0:T(8,128)(2,1)S(1)}, u32[]{:S(2)}, u32[]{:S(2)}) %collective-permute-start.27) | collective-permute-done | bytes 786464 | tf_op jit(solution)/shard_map/ppermute | solution.py:26
  124.9 3.7 %collective-permute-done.28.below.refs_6_.refs_7_ = bf16[2,128,1536]{2,1,0:T(8,128)(2,1)S(1)} collective-permute-done((bf16[2,128,1536]{2,1,0:T(8,128)(2,1)S(1)}, bf16[2,128,1536]{2,1,0:T(8,128)(2,1)S(1)}, u32[]{:S(2)}, u32[]{:S(2)}) %collective-permute-start.28) | collective-permute-done | bytes 786464 | tf_op jit(solution)/shard_map/ppermute | solution.py:26
  128.8 2.0 %collective-permute-start.33 = (bf16[128,1536]{1,0:T(8,128)(2,1)S(1)}, bf16[128,1536]{1,0:T(8,128)(2,1)S(1)}, u32[]{:S(2)}, u32[]{:S(2)}) collective-permute-start(bf16[128,1536]{1,0:T(8,128)(2,1)S(1)} %get-tuple-element.144), channel_id=1, source_target_pairs={{0,2},{2,4},{4,6},{6,0},{1,3},{3,5},{5,7},{7,1},{8,10},{10,12},{12... | collective-permute-start | bytes 1179656 | tf_op jit(solution)/shard_map/ppermute | solution.py:26
  130.8 2.6 %collective-permute-done.25.refs_4_ = bf16[128,1536]{1,0:T(8,128)(2,1)S(1)} collective-permute-done((bf16[128,1536]{1,0:T(8,128)(2,1)S(1)}, bf16[128,1536]{1,0:T(8,128)(2,1)S(1)}, u32[]{:S(2)}, u32[]{:S(2)}) %collective-permute-start.25) | collective-permute-done | bytes 393248 | tf_op jit(solution)/shard_map/ppermute | solution.py:26
  133.3 3.7 %collective-permute-done.26.grad2.refs_5_ = bf16[128,1536]{1,0:T(8,128)(2,1)S(1)} collective-permute-done((bf16[128,1536]{1,0:T(8,128)(2,1)S(1)}, bf16[128,1536]{1,0:T(8,128)(2,1)S(1)}, u32[]{:S(2)}, u32[]{:S(2)}) %collective-permute-start.26) | collective-permute-done | bytes 393248 | tf_op jit(solution)/shard_map/ppermute | solution.py:26
  137.0 3.0 %input_a.1 = (f32[512,384]{1,0:T(8,128)S(1)}, f32[512,128]{1,0:T(8,128)S(1)}, f32[512,128]{1,0:T(8,128)S(1)}, f32[512,128]{1,0:T(8,128)S(1)}) custom-call(bf16[2,128,1536]{2,1,0:T(8,128)(2,1)S(1)} %hidden.2.mine.refs_0_.refs_1_, bf16[2,128,1536]{2,1,0:T(8,128)(2,1)S(1)} %collective-permute-done.22.above.refs_2_.refs_3_, ...), custom_call_target="tpu_custom_call" | custom-call | flops 115000000 | bytes 369000 | tf_op jit(solution)/shard_map/input_a/pallas_call | solution.py:47
  140.7 0.9 collective-permute-done.29.refs_0_
  142.6 2.1 %collective-permute-start.35 = (bf16[4,32,384]{2,1,0:T(8,128)(2,1)S(1)}, bf16[4,32,384]{2,1,0:T(8,128)(2,1)S(1)}, u32[]{:S(2)}, u32[]{:S(2)}) collective-permute-start(bf16[4,32,384]{2,1,0:T(8,128)(2,1)S(1)} %get-tuple-element.146), channel_id=1, source_target_pairs={{0,64},{32,96},{64,0},{96,32},{1,65},{33,97},{65,1},{97,33},{2,66}... | collective-permute-start | bytes 294920 | tf_op jit(solution)/shard_map/ppermute | solution.py:26
  144.7 1.2 collective-permute-start.36
  145.8 3.7 %grads_a.1 = (f32[768,1536]{1,0:T(8,128)S(1)}, f32[1536,768]{1,0:T(8,128)S(1)}) custom-call(bf16[512,768]{1,0:T(8,128)(2,1)S(1)} %get-tuple-element.148.tok, bf16[512,768]{1,0:T(8,128)(2,1)S(1)} %get-tuple-element.149.cot, bf16[2,128,1536]{2,1,0:T(8,128)(2,1)S(1)} %hidden.2.mine.refs_0_.refs_1_, bf16[2,128,1536]{2,1,0:T(8,128)(2,1)S(1)} %hidden.2.mine.refs_0_.refs_1_, ...), custom_call_target="tpu_custom_call" | custom-call | flops 115000000 | bytes 369000 | tf_op jit(solution)/shard_map/grads_a/pallas_call | solution.py:47
  149.6 1.2 collective-permute-done.34
  150.8 0.6 collective-permute-done.36
  151.4 3.0 %input_b.1 = (f32[512,384]{1,0:T(8,128)S(1)}, f32[512,384]{1,0:T(8,128)S(1)}) custom-call(bf16[2,128,1536]{2,1,0:T(8,128)(2,1)S(1)} %hidden.3.mine.refs_0_.refs_1_, bf16[2,128,1536]{2,1,0:T(8,128)(2,1)S(1)} %collective-permute-done.27.above.refs_2_.refs_3_, bf16[128,1536]{1,0:T(8,128)(2,1)S(1)} %collective-permute-done.33.grad2.refs_5_, ...), custom_call_target="tpu_custom_call" | custom-call | flops 23000000512 | bytes 73800000 | tf_op jit(solution)/shard_map/input_b/pallas_call | solution.py:47
  154.5 4.7 %grads_b.1 = (bf16[384,1536]{1,0:T(8,128)(2,1)S(1)}, bf16[384,1536]{1,0:T(8,128)(2,1)S(1)}, bf16[1536,384]{1,0:T(8,128)(2,1)S(1)}, bf16[1536,384]{1,0:T(8,128)(2,1)}) custom-call(bf16[512,768]{1,0:T(8,128)(2,1)S(1)} %get-tuple-element.164.tok, bf16[512,768]{1,0:T(8,128)(2,1)S(1)} %get-tuple-element.165.cot, ...), custom_call_target="tpu_custom_call" | custom-call | flops 115000000 | bytes 369000 | tf_op jit(solution)/shard_map/grads_b/pallas_call | solution.py:47
  159.2 0.8 return_b.1
  160.5 3.0 %collective-permute-start.38 = (bf16[4,32,384]{2,1,0:T(8,128)(2,1)}, bf16[4,32,384]{2,1,0:T(8,128)(2,1)}, u32[]{:S(2)}, u32[]{:S(2)}) collective-permute-start(bf16[4,32,384]{2,1,0:T(8,128)(2,1)} %get-tuple-element.174), channel_id=1, source_target_pairs={{0,16},{16,0},{32,48},{48,32},{64,80},{80,64},{96,112},{112,96},{1... | collective-permute-start | bytes 294920 | tf_op jit(solution)/shard_map/ppermute | solution.py:441
  163.8 5.9 %collective-permute-start.40 = (bf16[4,32,384]{2,1,0:T(8,128)(2,1)}, bf16[4,32,384]{2,1,0:T(8,128)(2,1)}, u32[]{:S(2)}, u32[]{:S(2)}) collective-permute-start(bf16[4,32,384]{2,1,0:T(8,128)(2,1)} %get-tuple-element.176), channel_id=1, source_target_pairs={{0,80},{16,64},{32,112},{48,96},{64,16},{80,0},{96,48},{112,32},{1... | collective-permute-start | bytes 294920 | tf_op jit(solution)/shard_map/ppermute | solution.py:441
  169.8 5.6 %place.1 = (bf16[384,3072]{1,0:T(8,128)(2,1)}, bf16[3072,384]{1,0:T(8,128)(2,1)}) custom-call(s32[1]{0:T(128)} %bitcast.1._.core, bf16[384,1536]{1,0:T(8,128)(2,1)S(1)} %get-tuple-element.172.wi_own, bf16[384,1536]{1,0:T(8,128)(2,1)S(1)} %collective-permute-done.42.wi_got, bf16[1536,384]{1,0:T(8,128)(2,1)S(1)} %get-tuple-element.181.wo_own, ...), custom_call_target="tpu_custom_call" | custom-call | flops 115000000 | bytes 369000 | tf_op jit(solution)/shard_map/place/pallas_call | solution.py:47
  175.4 1.7 collective-permute-done.41
  177.1 1.1 convert_add_fusion
  178.3 0.7 fusion.1
  (71 shorter events, 4.5 us)
Async XLA Ops:
  1.7 11.9 %collective-permute-start = (bf16[4,32,768]{2,1,0:T(8,128)(2,1)S(1)}, bf16[4,32,768]{2,1,0:T(8,128)(2,1)S(1)}, u32[]{:S(2)}, u32[]{:S(2)}) collective-permute-start(bf16[4,32,768]{2,1,0:T(8,128)(2,1)S(1)} %fusion.2.refs_0_), channel_id=1, source_target_pairs={{0,96},{32,0},{64,32},{96,64},{1,97},{33,1},{65,33},{97,65},{2,98}... | collective-permute-start | bytes 589832 | tf_op jit(solution)/shard_map/ppermute | solution.py:26
  4.9 9.4 %collective-permute-start.1 = (bf16[4,32,768]{2,1,0:T(8,128)(2,1)S(1)}, bf16[4,32,768]{2,1,0:T(8,128)(2,1)S(1)}, u32[]{:S(2)}, u32[]{:S(2)}) collective-permute-start(bf16[4,32,768]{2,1,0:T(8,128)(2,1)S(1)} %fusion.2.refs_0_), channel_id=1, source_target_pairs={{0,64},{32,96},{64,0},{96,32},{1,65},{33,97},{65,1},{97,33},{2,66}... | collective-permute-start | bytes 589832 | tf_op jit(solution)/shard_map/ppermute | solution.py:26
  5.5 11.4 %collective-permute-start.2 = (bf16[4,32,768]{2,1,0:T(8,128)(2,1)S(1)}, bf16[4,32,768]{2,1,0:T(8,128)(2,1)S(1)}, u32[]{:S(2)}, u32[]{:S(2)}) collective-permute-start(bf16[4,32,768]{2,1,0:T(8,128)(2,1)S(1)} %fusion.2.refs_0_), channel_id=1, source_target_pairs={{0,32},{32,64},{64,96},{96,0},{1,33},{33,65},{65,97},{97,1},{2,34}... | collective-permute-start | bytes 589832 | tf_op jit(solution)/shard_map/ppermute | solution.py:26
  6.5 10.5 %collective-permute-start.5 = (bf16[4,32,768]{2,1,0:T(8,128)(2,1)S(1)}, bf16[4,32,768]{2,1,0:T(8,128)(2,1)S(1)}, u32[]{:S(2)}, u32[]{:S(2)}) collective-permute-start(bf16[4,32,768]{2,1,0:T(8,128)(2,1)S(1)} %fusion.2.refs_0_), channel_id=1, source_target_pairs={{0,16},{16,0},{1,17},{17,1},{2,18},{18,2},{3,19},{19,3},{4,20},{20... | collective-permute-start | bytes 589832 | tf_op jit(solution)/shard_map/ppermute | solution.py:26
  9.5 1.7 copy-start
  11.2 1.7 copy-start.2
  13.5 8.0 %copy-start.1 = (bf16[384,3072]{1,0:T(8,128)(2,1)S(1)}, bf16[384,3072]{1,0:T(8,128)(2,1)}, u32[]{:S(2)}) copy-start(bf16[384,3072]{1,0:T(8,128)(2,1)} %wi.2) | copy-start | bytes 7077892
  13.5 8.0 %collective-permute-start.4 = (bf16[2,4,384,384]{3,2,1,0:T(8,128)(2,1)S(1)}, bf16[2,4,384,384]{3,2,1,0:T(8,128)(2,1)S(1)}, u32[]{:S(2)}, u32[]{:S(2)}) collective-permute-start(bf16[2,4,384,384]{3,2,1,0:T(8,128)(2,1)S(1)} %pack.1), channel_id=1, source_target_pairs={{0,1},{1,0},{2,3},{3,2},{4,5},{5,4},{6,7},{7,6},{8,9},{9,8},{10,11... | collective-permute-start | bytes 7077896 | tf_op jit(solution)/shard_map/ppermute | solution.py:26
  17.0 2.1 %collective-permute-start.6 = (bf16[4,32,768]{2,1,0:T(8,128)(2,1)S(1)}, bf16[4,32,768]{2,1,0:T(8,128)(2,1)S(1)}, u32[]{:S(2)}, u32[]{:S(2)}) collective-permute-start(bf16[4,32,768]{2,1,0:T(8,128)(2,1)S(1)} %collective-permute-done.5.refs_0_), channel_id=1, source_target_pairs={{0,1},{1,0},{2,3},{3,2},{4,5},{5,4},{6,7},{7,6},{8,9},{9,8},{10,11... | collective-permute-start | bytes 589832 | tf_op jit(solution)/shard_map/ppermute | solution.py:26
  17.1 5.5 %collective-permute-start.3 = (bf16[512,768]{1,0:T(8,128)(2,1)S(1)}, bf16[512,768]{1,0:T(8,128)(2,1)S(1)}, u32[]{:S(2)}, u32[]{:S(2)}) collective-permute-start(bf16[512,768]{1,0:T(8,128)(2,1)S(1)} %join_a.1.own), channel_id=1, source_target_pairs={{0,1},{1,0},{2,3},{3,2},{4,5},{5,4},{6,7},{7,6},{8,9},{9,8},{10,11... | collective-permute-start | bytes 2359304 | tf_op jit(solution)/shard_map/ppermute | solution.py:26
  17.6 12.9 %collective-permute-start.10 = (bf16[4,32,768]{2,1,0:T(8,128)(2,1)S(1)}, bf16[4,32,768]{2,1,0:T(8,128)(2,1)S(1)}, u32[]{:S(2)}, u32[]{:S(2)}) collective-permute-start(bf16[4,32,768]{2,1,0:T(8,128)(2,1)S(1)} %collective-permute-done.5.refs_0_), channel_id=1, source_target_pairs={{0,64},{32,96},{64,0},{96,32},{1,65},{33,97},{65,1},{97,33},{2,66}... | collective-permute-start | bytes 589832 | tf_op jit(solution)/shard_map/ppermute | solution.py:26
  18.3 12.3 %collective-permute-start.11 = (bf16[4,32,768]{2,1,0:T(8,128)(2,1)S(1)}, bf16[4,32,768]{2,1,0:T(8,128)(2,1)S(1)}, u32[]{:S(2)}, u32[]{:S(2)}) collective-permute-start(bf16[4,32,768]{2,1,0:T(8,128)(2,1)S(1)} %collective-permute-done.5.refs_0_), channel_id=1, source_target_pairs={{0,32},{32,64},{64,96},{96,0},{1,33},{33,65},{65,97},{97,1},{2,34}... | collective-permute-start | bytes 589832 | tf_op jit(solution)/shard_map/ppermute | solution.py:26
  19.1 11.5 %collective-permute-start.9 = (bf16[4,32,768]{2,1,0:T(8,128)(2,1)S(1)}, bf16[4,32,768]{2,1,0:T(8,128)(2,1)S(1)}, u32[]{:S(2)}, u32[]{:S(2)}) collective-permute-start(bf16[4,32,768]{2,1,0:T(8,128)(2,1)S(1)} %collective-permute-done.5.refs_0_), channel_id=1, source_target_pairs={{0,96},{32,0},{64,32},{96,64},{1,97},{33,1},{65,33},{97,65},{2,98}... | collective-permute-start | bytes 589832 | tf_op jit(solution)/shard_map/ppermute | solution.py:26
  26.4 13.9 %collective-permute-start.7 = (bf16[128,1536]{1,0:T(8,128)(2,1)S(1)}, bf16[128,1536]{1,0:T(8,128)(2,1)S(1)}, u32[]{:S(2)}, u32[]{:S(2)}) collective-permute-start(bf16[128,1536]{1,0:T(8,128)(2,1)S(1)} %get-tuple-element.103), channel_id=1, source_target_pairs={{0,2},{2,4},{4,6},{6,0},{1,3},{3,5},{5,7},{7,1},{8,10},{10,12},{12... | collective-permute-start | bytes 1179656 | tf_op jit(solution)/shard_map/ppermute | solution.py:26
  28.4 11.9 %collective-permute-start.8 = (bf16[128,1536]{1,0:T(8,128)(2,1)S(1)}, bf16[128,1536]{1,0:T(8,128)(2,1)S(1)}, u32[]{:S(2)}, u32[]{:S(2)}) collective-permute-start(bf16[128,1536]{1,0:T(8,128)(2,1)S(1)} %get-tuple-element.104), channel_id=1, source_target_pairs={{0,6},{2,0},{4,2},{6,4},{1,7},{3,1},{5,3},{7,5},{8,14},{10,8},{12,... | collective-permute-start | bytes 1179656 | tf_op jit(solution)/shard_map/ppermute | solution.py:26
  30.6 1.5 collective-permute-start.12
  30.7 1.7 collective-permute-start.13
  31.2 1.5 collective-permute-start.14
  36.5 13.6 %collective-permute-start.17 = (bf16[128,1536]{1,0:T(8,128)(2,1)S(1)}, bf16[128,1536]{1,0:T(8,128)(2,1)S(1)}, u32[]{:S(2)}, u32[]{:S(2)}) collective-permute-start(bf16[128,1536]{1,0:T(8,128)(2,1)S(1)} %get-tuple-element.110), channel_id=1, source_target_pairs={{0,2},{2,4},{4,6},{6,0},{1,3},{3,5},{5,7},{7,1},{8,10},{10,12},{12... | collective-permute-start | bytes 1179656 | tf_op jit(solution)/shard_map/ppermute | solution.py:26
  38.1 12.0 %collective-permute-start.18 = (bf16[128,1536]{1,0:T(8,128)(2,1)S(1)}, bf16[128,1536]{1,0:T(8,128)(2,1)S(1)}, u32[]{:S(2)}, u32[]{:S(2)}) collective-permute-start(bf16[128,1536]{1,0:T(8,128)(2,1)S(1)} %get-tuple-element.116), channel_id=1, source_target_pairs={{0,6},{2,0},{4,2},{6,4},{1,7},{3,1},{5,3},{7,5},{8,14},{10,8},{12,... | collective-permute-start | bytes 1179656 | tf_op jit(solution)/shard_map/ppermute | solution.py:26
  40.9 26.0 %collective-permute-start.15 = (bf16[2,128,1536]{2,1,0:T(8,128)(2,1)S(1)}, bf16[2,128,1536]{2,1,0:T(8,128)(2,1)S(1)}, u32[]{:S(2)}, u32[]{:S(2)}) collective-permute-start(bf16[2,128,1536]{2,1,0:T(8,128)(2,1)S(1)} %get-tuple-element.113), channel_id=1, source_target_pairs={{0,2},{2,4},{4,6},{6,0},{1,3},{3,5},{5,7},{7,1},{8,10},{10,12},{12... | collective-permute-start | bytes 2359304 | tf_op jit(solution)/shard_map/ppermute | solution.py:26
  41.0 25.9 %collective-permute-start.16 = (bf16[2,128,1536]{2,1,0:T(8,128)(2,1)S(1)}, bf16[2,128,1536]{2,1,0:T(8,128)(2,1)S(1)}, u32[]{:S(2)}, u32[]{:S(2)}) collective-permute-start(bf16[2,128,1536]{2,1,0:T(8,128)(2,1)S(1)} %get-tuple-element.114), channel_id=1, source_target_pairs={{0,6},{2,0},{4,2},{6,4},{1,7},{3,1},{5,3},{7,5},{8,14},{10,8},{12,... | collective-permute-start | bytes 2359304 | tf_op jit(solution)/shard_map/ppermute | solution.py:26
  50.7 32.7 %collective-permute-start.20 = (bf16[2,128,1536]{2,1,0:T(8,128)(2,1)S(1)}, bf16[2,128,1536]{2,1,0:T(8,128)(2,1)S(1)}, u32[]{:S(2)}, u32[]{:S(2)}) collective-permute-start(bf16[2,128,1536]{2,1,0:T(8,128)(2,1)S(1)} %get-tuple-element.119), channel_id=1, source_target_pairs={{0,2},{2,4},{4,6},{6,0},{1,3},{3,5},{5,7},{7,1},{8,10},{10,12},{12... | collective-permute-start | bytes 2359304 | tf_op jit(solution)/shard_map/ppermute | solution.py:26
  52.7 30.7 %collective-permute-start.21 = (bf16[2,128,1536]{2,1,0:T(8,128)(2,1)S(1)}, bf16[2,128,1536]{2,1,0:T(8,128)(2,1)S(1)}, u32[]{:S(2)}, u32[]{:S(2)}) collective-permute-start(bf16[2,128,1536]{2,1,0:T(8,128)(2,1)S(1)} %get-tuple-element.120), channel_id=1, source_target_pairs={{0,6},{2,0},{4,2},{6,4},{1,7},{3,1},{5,3},{7,5},{8,14},{10,8},{12,... | collective-permute-start | bytes 2359304 | tf_op jit(solution)/shard_map/ppermute | solution.py:26
  67.7 18.9 %collective-permute-start.19 = (bf16[2,128,1536]{2,1,0:T(8,128)(2,1)S(1)}, bf16[2,128,1536]{2,1,0:T(8,128)(2,1)S(1)}, u32[]{:S(2)}, u32[]{:S(2)}) collective-permute-start(bf16[2,128,1536]{2,1,0:T(8,128)(2,1)S(1)} %get-tuple-element.124), channel_id=1, source_target_pairs={{0,8},{8,0},{1,9},{9,1},{2,10},{10,2},{3,11},{11,3},{4,12},{12,4},... | collective-permute-start | bytes 2359304 | tf_op jit(solution)/shard_map/ppermute | solution.py:26
  84.1 19.3 %collective-permute-start.24 = (bf16[2,128,1536]{2,1,0:T(8,128)(2,1)S(1)}, bf16[2,128,1536]{2,1,0:T(8,128)(2,1)S(1)}, u32[]{:S(2)}, u32[]{:S(2)}) collective-permute-start(bf16[2,128,1536]{2,1,0:T(8,128)(2,1)S(1)} %get-tuple-element.127), channel_id=1, source_target_pairs={{0,8},{8,0},{1,9},{9,1},{2,10},{10,2},{3,11},{11,3},{4,12},{12,4},... | collective-permute-start | bytes 2359304 | tf_op jit(solution)/shard_map/ppermute | solution.py:26
  87.3 19.6 %collective-permute-start.22 = (bf16[2,128,1536]{2,1,0:T(8,128)(2,1)S(1)}, bf16[2,128,1536]{2,1,0:T(8,128)(2,1)S(1)}, u32[]{:S(2)}, u32[]{:S(2)}) collective-permute-start(bf16[2,128,1536]{2,1,0:T(8,128)(2,1)S(1)} %hidden.2.mine.refs_0_.refs_1_), channel_id=1, source_target_pairs={{0,6},{2,0},{4,2},{6,4},{1,7},{3,1},{5,3},{7,5},{8,14},{10,8},{12,... | collective-permute-start | bytes 2359304 | tf_op jit(solution)/shard_map/ppermute | solution.py:26
  90.1 19.0 %collective-permute-start.23 = (bf16[2,128,1536]{2,1,0:T(8,128)(2,1)S(1)}, bf16[2,128,1536]{2,1,0:T(8,128)(2,1)S(1)}, u32[]{:S(2)}, u32[]{:S(2)}) collective-permute-start(bf16[2,128,1536]{2,1,0:T(8,128)(2,1)S(1)} %hidden.2.mine.refs_0_.refs_1_), channel_id=1, source_target_pairs={{0,2},{2,4},{4,6},{6,0},{1,3},{3,5},{5,7},{7,1},{8,10},{10,12},{12... | collective-permute-start | bytes 2359304 | tf_op jit(solution)/shard_map/ppermute | solution.py:26
  104.1 20.8 %collective-permute-start.27 = (bf16[2,128,1536]{2,1,0:T(8,128)(2,1)S(1)}, bf16[2,128,1536]{2,1,0:T(8,128)(2,1)S(1)}, u32[]{:S(2)}, u32[]{:S(2)}) collective-permute-start(bf16[2,128,1536]{2,1,0:T(8,128)(2,1)S(1)} %hidden.3.mine.refs_0_.refs_1_), channel_id=1, source_target_pairs={{0,6},{2,0},{4,2},{6,4},{1,7},{3,1},{5,3},{7,5},{8,14},{10,8},{12,... | collective-permute-start | bytes 2359304 | tf_op jit(solution)/shard_map/ppermute | solution.py:26
  106.9 21.7 %collective-permute-start.28 = (bf16[2,128,1536]{2,1,0:T(8,128)(2,1)S(1)}, bf16[2,128,1536]{2,1,0:T(8,128)(2,1)S(1)}, u32[]{:S(2)}, u32[]{:S(2)}) collective-permute-start(bf16[2,128,1536]{2,1,0:T(8,128)(2,1)S(1)} %hidden.3.mine.refs_0_.refs_1_), channel_id=1, source_target_pairs={{0,2},{2,4},{4,6},{6,0},{1,3},{3,5},{5,7},{7,1},{8,10},{10,12},{12... | collective-permute-start | bytes 2359304 | tf_op jit(solution)/shard_map/ppermute | solution.py:26
  109.2 24.2 %collective-permute-start.25 = (bf16[128,1536]{1,0:T(8,128)(2,1)S(1)}, bf16[128,1536]{1,0:T(8,128)(2,1)S(1)}, u32[]{:S(2)}, u32[]{:S(2)}) collective-permute-start(bf16[128,1536]{1,0:T(8,128)(2,1)S(1)} %get-tuple-element.133), channel_id=1, source_target_pairs={{0,6},{2,0},{4,2},{6,4},{1,7},{3,1},{5,3},{7,5},{8,14},{10,8},{12,... | collective-permute-start | bytes 1179656 | tf_op jit(solution)/shard_map/ppermute | solution.py:26
  110.3 26.7 %collective-permute-start.26 = (bf16[128,1536]{1,0:T(8,128)(2,1)S(1)}, bf16[128,1536]{1,0:T(8,128)(2,1)S(1)}, u32[]{:S(2)}, u32[]{:S(2)}) collective-permute-start(bf16[128,1536]{1,0:T(8,128)(2,1)S(1)} %get-tuple-element.134), channel_id=1, source_target_pairs={{0,2},{2,4},{4,6},{6,0},{1,3},{3,5},{5,7},{7,1},{8,10},{10,12},{12... | collective-permute-start | bytes 1179656 | tf_op jit(solution)/shard_map/ppermute | solution.py:26
  128.7 20.9 %collective-permute-start.32 = (bf16[128,1536]{1,0:T(8,128)(2,1)S(1)}, bf16[128,1536]{1,0:T(8,128)(2,1)S(1)}, u32[]{:S(2)}, u32[]{:S(2)}) collective-permute-start(bf16[128,1536]{1,0:T(8,128)(2,1)S(1)} %get-tuple-element.137), channel_id=1, source_target_pairs={{0,6},{2,0},{4,2},{6,4},{1,7},{3,1},{5,3},{7,5},{8,14},{10,8},{12,... | collective-permute-start | bytes 1179656 | tf_op jit(solution)/shard_map/ppermute | solution.py:26
  128.8 20.8 %collective-permute-start.33 = (bf16[128,1536]{1,0:T(8,128)(2,1)S(1)}, bf16[128,1536]{1,0:T(8,128)(2,1)S(1)}, u32[]{:S(2)}, u32[]{:S(2)}) collective-permute-start(bf16[128,1536]{1,0:T(8,128)(2,1)S(1)} %get-tuple-element.144), channel_id=1, source_target_pairs={{0,2},{2,4},{4,6},{6,0},{1,3},{3,5},{5,7},{7,1},{8,10},{10,12},{12... | collective-permute-start | bytes 1179656 | tf_op jit(solution)/shard_map/ppermute | solution.py:26
  140.1 1.6 collective-permute-start.29
  140.2 1.9 %collective-permute-start.30 = (f32[512,128]{1,0:T(8,128)S(1)}, f32[512,128]{1,0:T(8,128)S(1)}, u32[]{:S(2)}, u32[]{:S(2)}) collective-permute-start(f32[512,128]{1,0:T(8,128)S(1)} %get-tuple-element.141), channel_id=1, source_target_pairs={{0,1},{1,0},{2,3},{3,2},{4,5},{5,4},{6,7},{7,6},{8,9},{9,8},{10,11... | collective-permute-start | bytes 786440 | tf_op jit(solution)/shard_map/ppermute | solution.py:26
  140.7 1.8 collective-permute-start.31
  142.5 7.0 %copy-start.3 = (f32[4,32,384]{2,1,0:T(8,128)}, f32[4,32,384]{2,1,0:T(8,128)S(1)}, u32[]{:S(2)}) copy-start(f32[4,32,384]{2,1,0:T(8,128)S(1)} %get-tuple-element.143) | copy-start | bytes 589828
  142.5 8.2 %collective-permute-start.34 = (bf16[4,32,384]{2,1,0:T(8,128)(2,1)S(1)}, bf16[4,32,384]{2,1,0:T(8,128)(2,1)S(1)}, u32[]{:S(2)}, u32[]{:S(2)}) collective-permute-start(bf16[4,32,384]{2,1,0:T(8,128)(2,1)S(1)} %get-tuple-element.145), channel_id=1, source_target_pairs={{0,32},{32,64},{64,96},{96,0},{1,33},{33,65},{65,97},{97,1},{2,34}... | collective-permute-start | bytes 294920 | tf_op jit(solution)/shard_map/ppermute | solution.py:26
  142.6 8.1 %collective-permute-start.35 = (bf16[4,32,384]{2,1,0:T(8,128)(2,1)S(1)}, bf16[4,32,384]{2,1,0:T(8,128)(2,1)S(1)}, u32[]{:S(2)}, u32[]{:S(2)}) collective-permute-start(bf16[4,32,384]{2,1,0:T(8,128)(2,1)S(1)} %get-tuple-element.146), channel_id=1, source_target_pairs={{0,64},{32,96},{64,0},{96,32},{1,65},{33,97},{65,1},{97,33},{2,66}... | collective-permute-start | bytes 294920 | tf_op jit(solution)/shard_map/ppermute | solution.py:26
  144.7 6.7 %collective-permute-start.36 = (bf16[4,32,384]{2,1,0:T(8,128)(2,1)S(1)}, bf16[4,32,384]{2,1,0:T(8,128)(2,1)S(1)}, u32[]{:S(2)}, u32[]{:S(2)}) collective-permute-start(bf16[4,32,384]{2,1,0:T(8,128)(2,1)S(1)} %get-tuple-element.147), channel_id=1, source_target_pairs={{0,96},{32,0},{64,32},{96,64},{1,97},{33,1},{65,33},{97,65},{2,98}... | collective-permute-start | bytes 294920 | tf_op jit(solution)/shard_map/ppermute | solution.py:26
  150.7 3.7 %copy-start.5 = (bf16[4,32,384]{2,1,0:T(8,128)(2,1)}, bf16[4,32,384]{2,1,0:T(8,128)(2,1)S(1)}, u32[]{:S(2)}) copy-start(bf16[4,32,384]{2,1,0:T(8,128)(2,1)S(1)} %collective-permute-done.34) | copy-start | bytes 294916
  150.7 3.7 %copy-start.7 = (bf16[4,32,384]{2,1,0:T(8,128)(2,1)}, bf16[4,32,384]{2,1,0:T(8,128)(2,1)S(1)}, u32[]{:S(2)}) copy-start(bf16[4,32,384]{2,1,0:T(8,128)(2,1)S(1)} %collective-permute-done.35) | copy-start | bytes 294916
  151.4 3.1 %copy-start.9 = (bf16[4,32,384]{2,1,0:T(8,128)(2,1)}, bf16[4,32,384]{2,1,0:T(8,128)(2,1)S(1)}, u32[]{:S(2)}) copy-start(bf16[4,32,384]{2,1,0:T(8,128)(2,1)S(1)} %collective-permute-done.36) | copy-start | bytes 294916
  154.4 4.8 %collective-permute-start.37 = (f32[512,384]{1,0:T(8,128)S(1)}, f32[512,384]{1,0:T(8,128)S(1)}, u32[]{:S(2)}, u32[]{:S(2)}) collective-permute-start(f32[512,384]{1,0:T(8,128)S(1)} %get-tuple-element.163), channel_id=1, source_target_pairs={{0,1},{1,0},{2,3},{3,2},{4,5},{5,4},{6,7},{7,6},{8,9},{9,8},{10,11... | collective-permute-start | bytes 2359304 | tf_op jit(solution)/shard_map/ppermute | solution.py:26
  160.0 9.7 %collective-permute-start.42 = (bf16[384,1536]{1,0:T(8,128)(2,1)S(1)}, bf16[384,1536]{1,0:T(8,128)(2,1)S(1)}, u32[]{:S(2)}, u32[]{:S(2)}) collective-permute-start(bf16[384,1536]{1,0:T(8,128)(2,1)S(1)} %get-tuple-element.180), channel_id=1, source_target_pairs={{0,1},{1,0},{2,3},{3,2},{4,5},{5,4},{6,7},{7,6},{8,9},{9,8},{10,11... | collective-permute-start | bytes 3538952 | tf_op jit(solution)/shard_map/ppermute | solution.py:26
  160.5 9.3 %collective-permute-start.43 = (bf16[1536,384]{1,0:T(8,128)(2,1)}, bf16[1536,384]{1,0:T(8,128)(2,1)}, u32[]{:S(2)}, u32[]{:S(2)}) collective-permute-start(bf16[1536,384]{1,0:T(8,128)(2,1)} %get-tuple-element.182), channel_id=1, source_target_pairs={{0,1},{1,0},{2,3},{3,2},{4,5},{5,4},{6,7},{7,6},{8,9},{9,8},{10,11... | collective-permute-start | bytes 3538952 | tf_op jit(solution)/shard_map/ppermute | solution.py:26
  160.5 14.9 %collective-permute-start.38 = (bf16[4,32,384]{2,1,0:T(8,128)(2,1)}, bf16[4,32,384]{2,1,0:T(8,128)(2,1)}, u32[]{:S(2)}, u32[]{:S(2)}) collective-permute-start(bf16[4,32,384]{2,1,0:T(8,128)(2,1)} %get-tuple-element.174), channel_id=1, source_target_pairs={{0,16},{16,0},{32,48},{48,32},{64,80},{80,64},{96,112},{112,96},{1... | collective-permute-start | bytes 294920 | tf_op jit(solution)/shard_map/ppermute | solution.py:441
  163.6 11.9 %collective-permute-start.39 = (bf16[4,32,384]{2,1,0:T(8,128)(2,1)}, bf16[4,32,384]{2,1,0:T(8,128)(2,1)}, u32[]{:S(2)}, u32[]{:S(2)}) collective-permute-start(bf16[4,32,384]{2,1,0:T(8,128)(2,1)} %get-tuple-element.175), channel_id=1, source_target_pairs={{0,48},{16,32},{32,80},{48,64},{64,112},{80,96},{96,16},{112,0},{1... | collective-permute-start | bytes 294920 | tf_op jit(solution)/shard_map/ppermute | solution.py:441
  163.8 11.6 %collective-permute-start.40 = (bf16[4,32,384]{2,1,0:T(8,128)(2,1)}, bf16[4,32,384]{2,1,0:T(8,128)(2,1)}, u32[]{:S(2)}, u32[]{:S(2)}) collective-permute-start(bf16[4,32,384]{2,1,0:T(8,128)(2,1)} %get-tuple-element.176), channel_id=1, source_target_pairs={{0,80},{16,64},{32,112},{48,96},{64,16},{80,0},{96,48},{112,32},{1... | collective-permute-start | bytes 294920 | tf_op jit(solution)/shard_map/ppermute | solution.py:441
  169.8 7.3 %collective-permute-start.41 = (bf16[4,32,384]{2,1,0:T(8,128)(2,1)}, bf16[4,32,384]{2,1,0:T(8,128)(2,1)}, u32[]{:S(2)}, u32[]{:S(2)}) collective-permute-start(bf16[4,32,384]{2,1,0:T(8,128)(2,1)} %get-tuple-element.177), channel_id=1, source_target_pairs={{0,112},{16,96},{32,16},{48,0},{64,48},{80,32},{96,80},{112,64},{1... | collective-permute-start | bytes 294920 | tf_op jit(solution)/shard_map/ppermute | solution.py:441
  169.8 7.3 %copy-start.4 = (f32[4,32,384]{2,1,0:T(8,128)S(1)}, f32[4,32,384]{2,1,0:T(8,128)}, u32[]{:S(2)}) copy-start(f32[4,32,384]{2,1,0:T(8,128)} %copy-done.3) | copy-start | bytes 589828
  169.8 7.3 %copy-start.6 = (bf16[4,32,384]{2,1,0:T(8,128)(2,1)S(1)}, bf16[4,32,384]{2,1,0:T(8,128)(2,1)}, u32[]{:S(2)}) copy-start(bf16[4,32,384]{2,1,0:T(8,128)(2,1)} %copy-done.5) | copy-start | bytes 294916
  169.8 7.3 %copy-start.8 = (bf16[4,32,384]{2,1,0:T(8,128)(2,1)S(1)}, bf16[4,32,384]{2,1,0:T(8,128)(2,1)}, u32[]{:S(2)}) copy-start(bf16[4,32,384]{2,1,0:T(8,128)(2,1)} %copy-done.7) | copy-start | bytes 294916
  169.8 7.3 %copy-start.10 = (bf16[4,32,384]{2,1,0:T(8,128)(2,1)S(1)}, bf16[4,32,384]{2,1,0:T(8,128)(2,1)}, u32[]{:S(2)}) copy-start(bf16[4,32,384]{2,1,0:T(8,128)(2,1)} %copy-done.9) | copy-start | bytes 294916

commit v6 on v5

--- a/solution.py
+++ b/solution.py
@@ -34,15 +34,15 @@
     return lax.optimization_barrier((value, after))[0]
 
 
-COST = dict(pack=0.1, weights=20, join_a=100, join_b=0.1, products=0.1, ring_add=0.1, own_sum=0.1, hidden=0.1, pass_on=0.1, input_a=0.1, input_b=20, grads_a=0.1, grads_b=0.1, return_a=0.1, return_b=20, place=0.1)
-
-
-def kernel(name, body, grid, ins, outs, scratch=(), scalar=None):
+COST = dict(pack=0.1, weights=20, join_a=100, join_b=0.1, products=0.1, ring_add=0.1, own_sum=0.1, hidden=0.1, pass_on=0.1, input_three=0.1, input_last=0.1, grads_a=0.1, grads_b=0.1, grads_last=0.1, return_a=0.1, return_b=20, place=0.1)
+
+
+def kernel(name, body, grid, ins, outs, scratch=(), scalar=None, aliases=None):
     def spec(block, index):
         def at(i, *refs):
             return tuple(i if k == "i" else k(i, *(r[0] for r in refs)) if callable(k) else k for k in index)
 
-        return pl.BlockSpec(block, at)
+        return pl.BlockSpec(memory_space=pl.ANY) if block is None else pl.BlockSpec(block, at)
 
     return pl.pallas_call(
         body,
@@ -55,6 +55,7 @@
             scratch_shapes=list(scratch),
         ),
         out_shape=[jax.ShapeDtypeStruct(shape, dtype) for shape, dtype, _, _ in outs],
+        input_output_aliases=aliases or {},
         cost_estimate=pl.CostEstimate(flops=int(COST[name] * 1.15e9), bytes_accessed=int(COST[name] * 3.69e6), transcendentals=0),
         compiler_params=pltpu.CompilerParams(vmem_limit_bytes=24 * 2**20),
     )(*([] if scalar is None else [scalar]), *[a for a, _, _ in ins])
@@ -234,38 +235,51 @@
     )[0]
 
 
-def input_part(name, mine, above, grad2, below, wi, pieces):
+def input_three(mine, above, below, wi):
     _, per, hid = mine.shape
     half = wi.shape[0] // 2
+
+    def body(mine, above, below, wi, own, other):
+        for step, out in enumerate((own, other)):
+
+            @pl.when(pl.program_id(0) == step)
+            def _():
+                for k, grad in enumerate((mine, above, below)):
+                    out[k] = dot(grad[0], wi[...], 1, 1)
+
+    second, whole = (1, per, hid), (3, per, half)
+    return kernel(
+        "input_three",
+        body,
+        2,
+        [(a, second, (1, 0, 0)) for a in (mine, above, below)] + [(wi, (half, hid), ("i", 0))],
+        [(whole, F32, whole, (0, 0, 0))] * 2,
+    )
+
+
+def input_last(three, grad2, wi, pieces):
+    per, hid = grad2.shape
+    half = wi.shape[0] // 2
     width = half // pieces
 
-    def body(mine, above, grad2, below, wi, own, *others):
-        grads = (mine.at[0], above.at[0], grad2, below.at[0])
-
-        @pl.when(pl.program_id(0) == 0)
-        def _():
-            for k, grad in enumerate(grads):
-                part = dot(grad[...], wi[...], 1, 1)
-                for j, other in enumerate(others):
-                    other[k * per : (k + 1) * per] = part[:, j * width : (j + 1) * width]
-
-        @pl.when(pl.program_id(0) == 1)
-        def _():
-            for k, grad in enumerate(grads):
-                own[k * per : (k + 1) * per] = dot(grad[...], wi[...], 1, 1)
-
-    second, whole, part = (1, per, hid), (4 * per, half), (4 * per, width)
+    def body(own3, other3, grad, wi, own, *others):
+        for k, at in ((0, 0), (1, 1), (2, 3)):
+            rows = pl.ds(at * per, per)
+            own[rows, :] = own3[k]
+            for j, other in enumerate(others):
+                other[rows, :] = other3[k, :, j * width : (j + 1) * width]
+        part = dot(grad[...], wi[...], 1, 1)
+        rows = pl.ds(2 * per, per)
+        own[rows, :] = part[:, :half]
+        for j, other in enumerate(others):
+            other[rows, :] = part[:, half + j * width : half + (j + 1) * width]
+
+    whole, part = (4 * per, half), (4 * per, width)
     own, *others = kernel(
-        name,
-        body,
-        2,
-        [
-            (mine, second, (1, 0, 0)),
-            (above, second, (1, 0, 0)),
-            (grad2, (per, hid), (0, 0)),
-            (below, second, (1, 0, 0)),
-            (wi, (half, hid), (lambda i: 1 - i, 0)),
-        ],
+        "input_last",
+        body,
+        1,
+        [(a, a.shape, (0, 0, 0)) for a in three] + [(a, a.shape, (0, 0)) for a in (grad2, wi)],
         [(whole, F32, whole, (0, 0))] + [(part, F32, part, (0, 0))] * pieces,
     )
     return own, others
@@ -294,70 +308,74 @@
     )
 
 
-def weight_grads(name, tok, cot, blocks, sums=None):
-    rows, feat = tok.shape
-    _, per, hid = blocks[0].shape
-    half, block = feat // 2, hid // STEPS
-    last = sums is not None
-
-    def body(tok, cot, *refs):
-        parts, refs = refs[:8], refs[8:]
-        act, grad = refs[-2:]
-        for k in range(4):
-            for ref, out in zip(parts[2 * k : 2 * k + 2], (act, grad)):
-                out[pl.ds(k * per, per), :] = ref[0] if len(ref.shape) == 3 else ref[...]
+def weight_grads(name, terms, sums=None, core=None):
+    per, hid = terms[0][3].shape[-2:]
+    feat = terms[0][0].shape[1]
+    half, block, count = feat // 2, hid // STEPS, len(terms)
+    rows, last = count * per, core is not None
+
+    def body(*refs):
+        refs = refs[1:] if last else refs
+        given, refs = [refs[k * count : (k + 1) * count] for k in range(4)], refs[4 * count :]
+        both = refs[-4:]
+
+        @pl.when(pl.program_id(0) == 0)
+        def _():
+            for parts, out in zip(given[:2], both[:2]):
+                for k, ref in enumerate(parts):
+                    out[k * per : (k + 1) * per] = ref[...]
+
+        for parts, out in zip(given[2:], both[2:]):
+            for k, ref in enumerate(parts):
+                out[k * per : (k + 1) * per] = ref[0] if len(ref.shape) == 3 else ref[...]
+        tok, cot, act, grad = both
         wi = dot(tok[...], grad[...], 0, 0)
         wo = dot(act[...], cot[...], 0, 0)
-        if not last:
+        if sums is not None:
+            wi, wo, refs = wi + refs[0][...], wo + refs[1][...], refs[2:]
+        if last:
+            refs[0][...] = wi[:half].astype(BF16)
+            refs[1][...] = wo[:, :half].astype(BF16)
+            refs[2][...] = wi[half:].astype(BF16)
+            refs[3][...] = wo[:, half:].astype(BF16)
+        else:
             refs[0][...] = wi
             refs[1][...] = wo
-        else:
-            wi = (wi + refs[0][...]).astype(BF16)
-            wo = (wo + refs[1][...]).astype(BF16)
-            refs[2][...], refs[3][...] = wi[:half], wi[half:]
-            refs[4][...], refs[5][...] = wo[:, :half], wo[:, half:]
-
-    mine, above, act2, grad2, below = blocks
-    ins = [(tok, (rows, feat), (0, 0)), (cot, (rows, feat), (0, 0))]
-    for pair in (mine, above, (act2, grad2), below):
-        if isinstance(pair, tuple):
-            ins += [(a, (per, block), (0, "i")) for a in pair]
-        else:
-            ins += [(pair, (1, per, block), (k, 0, "i")) for k in (0, 1)]
+
+    def hidden_part(a, which):
+        return (a, (1, per, block), (which, 0, "i")) if len(a.shape) == 3 else (a, (per, block), (0, "i"))
+
+    ins = [(term[n], (per, feat), (term[2], 0)) for n in (0, 1) for term in terms]
+    ins += [hidden_part(term[3 + which], which) for which in (0, 1) for term in terms]
+    if sums is not None:
+        ins += [(sums[0], (feat, block), (0, "i")), (sums[1], (block, feat), ("i", 0))]
     if last:
-        ins += [(sums[0], (feat, block), (0, "i")), (sums[1], (block, feat), ("i", 0))]
-        outs = [((half, hid), BF16, (half, block), (0, "i"))] * 2 + [((hid, half), BF16, (block, half), ("i", 0))] * 2
+        at = lambda i, c: c * STEPS + i
+        outs = [((half, 2 * hid), BF16, (half, block), (0, at)), ((2 * hid, half), BF16, (block, half), (at, 0))]
+        outs += [((half, hid), BF16, (half, block), (0, "i")), ((hid, half), BF16, (block, half), ("i", 0))]
     else:
         outs = [((feat, hid), F32, (feat, block), (0, "i")), ((hid, feat), F32, (block, feat), ("i", 0))]
-    return kernel(name, body, STEPS, ins, outs, [pltpu.VMEM((rows, block), BF16)] * 2)
-
-
-def place(wi_own, wi_got, wo_own, wo_got, core):
-    half, hid = wi_own.shape
-
-    def body(core, wi_own, wi_got, wo_own, wo_got, wi, wo):
-        mine = pl.program_id(0) // STEPS == core[0]
-
-        @pl.when(mine)
-        def _():
-            wi[...] = wi_own[...]
-            wo[...] = wo_own[...]
-
-        @pl.when(jnp.logical_not(mine))
-        def _():
-            wi[...] = wi_got[...]
-            wo[...] = wo_got[...]
-
+    scratch = [pltpu.VMEM((rows, feat), BF16)] * 2 + [pltpu.VMEM((rows, block), BF16)] * 2
+    return kernel(name, body, STEPS, ins, outs, scratch, core)
+
+
+def place(wi, wo, wi_got, wo_got, core):
+    half, hid = wi_got.shape
     block = hid // STEPS
-    at = lambda i, c: i % STEPS
-    across, down = ((half, block), (0, at)), ((block, half), (at, 0))
+
+    def body(core, wi, wo, wi_got, wo_got, wi_out, wo_out):
+        wi_out[...] = wi_got[...]
+        wo_out[...] = wo_got[...]
+
+    at = lambda i, c: (1 - c) * STEPS + i
     return kernel(
         "place",
         body,
-        2 * STEPS,
-        [(wi_own, *across), (wi_got, *across), (wo_own, *down), (wo_got, *down)],
-        [((half, 2 * hid), BF16, (half, block), (0, "i")), ((2 * hid, half), BF16, (block, half), ("i", 0))],
+        STEPS,
+        [(wi, None, None), (wo, None, None), (wi_got, (half, block), (0, "i")), (wo_got, (block, half), ("i", 0))],
+        [(wi.shape, BF16, (half, block), (0, at)), (wo.shape, BF16, (block, half), (at, 0))],
         scalar=core,
+        aliases={1: 0, 2: 1},
     )
 
 
@@ -420,28 +438,37 @@
     s_b = send_mine(mine_b)
 
     s_a = gate(s_a, mine_b)
-    f_a = send_on(*s_a)[:2]
-    s_b = gate(s_b, s_a)
-    f_b = send_on(*s_b)
-
-    f_a = gate(f_a, f_b[2])
-    in_a, others = input_part("input_a", mine_a, s_a[0], f_a[1], s_a[1], wi, 3)
+    *f_a, sent_a = send_on(*s_a)
+    three_a = input_three(mine_a, *gate(s_a, sent_a), wi)
+    terms = [(tok_a, cot_a, k, a, a) for k, a in zip((0, 1, 3), gate((mine_a, *s_a), three_a))]
+    sums = weight_grads("grads_a", terms)
+
+    s_b = gate(s_b, sums)
+    *f_b, sent_b = send_on(*s_b)
+    three_b = input_three(mine_b, *gate(s_b, sent_b), wi)
+    terms = [(tok_b, cot_b, k, a, a) for k, a in zip((0, 1, 3), gate((mine_b, *s_b), three_b))]
+    sums = weight_grads("grads_b", terms, sums)
+
+    f_a = gate(f_a, sums)
+    in_a, others = input_last(three_a, f_a[1], wi, 3)
     kept, *back = return_pieces("return_a", in_a, to_core(others), (F32, BF16, BF16, BF16))
-    sums = weight_grads("grads_a", tok_a, cot_a, gate((mine_a, s_a[0], *f_a, s_a[1]), back), None)
     back = [shift(a, "y", d) for d, a in zip((1, 2, 3), back)]
 
-    f_b, back = gate((f_b[:2], back), sums)
-    in_b, others = input_part("input_b", mine_b, s_b[0], f_b[1], s_b[1], wi, 1)
+    f_b = gate(f_b, kept)
+    in_b, others = input_last(three_b, f_b[1], wi, 1)
     others_got = to_core(others)
-    blocks = gate((mine_b, s_b[0], *f_b, s_b[1]), others)
-    wi_own, wi_other, wo_own, wo_other = weight_grads("grads_b", tok_b, cot_b, blocks, sums)
-    far = return_pieces("return_b", in_b, gate(others_got, wi_own), (BF16,) * 4)
-    wi_got, wo_got = to_core(gate((wi_other, wo_other), far))
+    f_a, f_b = gate((f_a, f_b), others)
+    terms = [(tok_a, cot_a, 2, *f_a), (tok_b, cot_b, 2, *f_b)]
+    w_in_grad, w_out_grad, *others = weight_grads("grads_last", terms, sums, at_core)
+
+    others_got, back = gate((others_got, back), others)
+    far = return_pieces("return_b", in_b, others_got, (BF16,) * 4)
+    got = to_core(gate(others, far))
     far = [
         lax.ppermute(a, ROWS, [(i, ((i // 2 + d) % 4) * 2 + (i + 1) % 2) for i in range(8)])
         for d, a in enumerate(far)
     ]
-    w_in_grad, w_out_grad = place(wi_own, wi_got, wo_own, wo_got, at_core)
+    w_in_grad, w_out_grad = place(w_in_grad, w_out_grad, *got, at_core)
 
     total = kept
     for part in back + gate(far, w_in_grad):

time: 179 us -> 171 us (0.955)
  waiting for transfers between devices: 82.6 us -> 68.1 us
  starting transfers between devices: 54.5 us -> 60.1 us
  local copies, waits for them, and re-layouts: 3.37 us -> 5.51 us
    ppermute x40, waiting for transfers between devices: 80.9 us -> 62.9 us  [shift(): return lax.ppermute(x, axis, [(i, (i + by) % n) for i in range(n)])]
    ppermute x40, starting transfers between devices: 45.2 us -> 50.8 us  [shift(): return lax.ppermute(x, axis, [(i, (i + by) % n) for i in range(n)])]
    ppermute x4, waiting for transfers between devices: 1.68 us -> 5.13 us  [local(): lax.ppermute(a, ROWS, [(i, (i // 2 + d) % 4 * 2 + (i + 1) % 2) for i in r...]
    unnamed x22 -> x10, local copies, waits for them, and re-layouts: 3.37 us -> 5.51 us
    pallas_call x21 -> x24, Pallas kernels: 34.6 us -> 33.6 us  [kernel(): pl.pallas_call(body, name=name, grid_spec=pltpu.PrefetchScalarGridSpec(nu...]
  transfers between devices with their start and end apart: 44 -> 44, of which waited for: 21 -> 22; matrix products, arithmetic and copies ran while one was open for 0% -> 0% of each run, Pallas kernels for 17% -> 19%
where the time goes in v6:
time: 171 us
  waiting for transfers between devices  68.1 us (40%)
  starting transfers between devices  60.1 us (35%)
  Pallas kernels  33.6 us (20%)
  local copies, waits for them, and re-layouts  5.51 us (3%)
  other arithmetic  2.75 us (2%)
    ppermute x40, waiting for transfers between devices, shift(): return lax.ppermute(x, axis, [(i, (i + by) % n) for i in range(n)])  62.9 us
    ppermute x40, starting transfers between devices, shift(): return lax.ppermute(x, axis, [(i, (i + by) % n) for i in range(n)])  50.8 us
    pallas_call x24, Pallas kernels, kernel(): pl.pallas_call(body, name=name, grid_spec=pltpu.PrefetchScalarGridSpec(nu...  33.6 us
    ppermute x4, starting transfers between devices, local(): lax.ppermute(a, ROWS, [(i, (i // 2 + d) % 4 * 2 + (i + 1) % 2) for i in r...  9.28 us
    unnamed x10, local copies, waits for them, and re-layouts  5.51 us
    ppermute x4, waiting for transfers between devices, local(): lax.ppermute(a, ROWS, [(i, (i // 2 + d) % 4 * 2 + (i + 1) % 2) for i in r...  5.13 us
  transfers between devices with their start and end apart: 44, of which 22 were waited for; matrix products, arithmetic and copies ran while one was open for 0% of the time, Pallas kernels for 19%

profile of v6, /device:TPU:0, one launch (start us, length us, event | category | flops | bytes accessed | tf_op | source)
XLA Modules:
  0.0 171.1 jit_solution(18041292133725409634)
XLA Ops:
  0.7 1.0 pad_maximum_fusion
  1.7 1.7 %collective-permute-start.2 = (bf16[4,32,768]{2,1,0:T(8,128)(2,1)S(1)}, bf16[4,32,768]{2,1,0:T(8,128)(2,1)S(1)}, u32[]{:S(2)}, u32[]{:S(2)}) collective-permute-start(bf16[4,32,768]{2,1,0:T(8,128)(2,1)S(1)} %fusion.2.refs_0_), channel_id=1, source_target_pairs={{0,32},{32,64},{64,96},{96,0},{1,33},{33,65},{65,97},{97,1},{2,34}... | collective-permute-start | bytes 589832 | tf_op jit(solution)/shard_map/ppermute | solution.py:26
  3.4 2.9 %collective-permute-start.1 = (bf16[4,32,768]{2,1,0:T(8,128)(2,1)S(1)}, bf16[4,32,768]{2,1,0:T(8,128)(2,1)S(1)}, u32[]{:S(2)}, u32[]{:S(2)}) collective-permute-start(bf16[4,32,768]{2,1,0:T(8,128)(2,1)S(1)} %fusion.2.refs_0_), channel_id=1, source_target_pairs={{0,64},{32,96},{64,0},{96,32},{1,65},{33,97},{65,1},{97,33},{2,66}... | collective-permute-start | bytes 589832 | tf_op jit(solution)/shard_map/ppermute | solution.py:26
  6.3 1.3 collective-permute-start
  7.7 3.0 %collective-permute-start.5 = (bf16[4,32,768]{2,1,0:T(8,128)(2,1)S(1)}, bf16[4,32,768]{2,1,0:T(8,128)(2,1)S(1)}, u32[]{:S(2)}, u32[]{:S(2)}) collective-permute-start(bf16[4,32,768]{2,1,0:T(8,128)(2,1)S(1)} %fusion.2.refs_0_), channel_id=1, source_target_pairs={{0,16},{16,0},{1,17},{17,1},{2,18},{18,2},{3,19},{19,3},{4,20},{20... | collective-permute-start | bytes 589832 | tf_op jit(solution)/shard_map/ppermute | solution.py:26
  10.7 1.7 copy-done.2
  12.4 1.7 copy-done.4
  14.1 0.7 pack.1
  15.5 1.1 collective-permute-start.11
  16.6 2.4 %collective-permute-start.10 = (bf16[4,32,768]{2,1,0:T(8,128)(2,1)S(1)}, bf16[4,32,768]{2,1,0:T(8,128)(2,1)S(1)}, u32[]{:S(2)}, u32[]{:S(2)}) collective-permute-start(bf16[4,32,768]{2,1,0:T(8,128)(2,1)S(1)} %collective-permute-done.5.refs_0_), channel_id=1, source_target_pairs={{0,64},{32,96},{64,0},{96,32},{1,65},{33,97},{65,1},{97,33},{2,66}... | collective-permute-start | bytes 589832 | tf_op jit(solution)/shard_map/ppermute | solution.py:26
  19.0 1.6 collective-permute-start.9
  20.6 1.1 weights.1
  21.8 1.1 collective-permute-done.3.other
  22.9 3.7 %products.2 = (f32[2,512,1536]{2,1,0:T(8,128)S(1)}, bf16[128,1536]{1,0:T(8,128)(2,1)S(1)}, bf16[128,1536]{1,0:T(8,128)(2,1)S(1)}, bf16[512,768]{1,0:T(8,128)(2,1)S(1)}, bf16[512,768]{1,0:T(8,128)(2,1)S(1)}) custom-call(bf16[512,768]{1,0:T(8,128)(2,1)S(1)} %join_a.1.own, bf16[512,768]{1,0:T(8,128)(2,1)S(1)} %collective-permute-done.3.other, ...), custom_call_target="tpu_custom_call" | custom-call | flops 115000000 | bytes 369000 | tf_op jit(solution)/shard_map/products/pallas_call | solution.py:47
  26.6 4.1 %collective-permute-start.8 = (bf16[128,1536]{1,0:T(8,128)(2,1)S(1)}, bf16[128,1536]{1,0:T(8,128)(2,1)S(1)}, u32[]{:S(2)}, u32[]{:S(2)}) collective-permute-start(bf16[128,1536]{1,0:T(8,128)(2,1)S(1)} %get-tuple-element.114), channel_id=1, source_target_pairs={{0,6},{2,0},{4,2},{6,4},{1,7},{3,1},{5,3},{7,5},{8,14},{10,8},{12,... | collective-permute-start | bytes 1179656 | tf_op jit(solution)/shard_map/ppermute | solution.py:26
  30.9 0.5 collective-permute-start.13
  31.4 0.8 collective-permute-done.12.refs_5_
  33.0 3.7 %products.3 = (f32[2,512,1536]{2,1,0:T(8,128)S(1)}, bf16[128,1536]{1,0:T(8,128)(2,1)S(1)}, bf16[128,1536]{1,0:T(8,128)(2,1)S(1)}, bf16[512,768]{1,0:T(8,128)(2,1)S(1)}, bf16[512,768]{1,0:T(8,128)(2,1)S(1)}) custom-call(bf16[512,768]{1,0:T(8,128)(2,1)S(1)} %get-tuple-element.118.own, bf16[512,768]{1,0:T(8,128)(2,1)S(1)} %get-tuple-element.119.other, ...), custom_call_target="tpu_custom_call" | custom-call | flops 115000000 | bytes 369000 | tf_op jit(solution)/shard_map/products/pallas_call | solution.py:47
  36.7 3.3 %collective-permute-start.18 = (bf16[128,1536]{1,0:T(8,128)(2,1)S(1)}, bf16[128,1536]{1,0:T(8,128)(2,1)S(1)}, u32[]{:S(2)}, u32[]{:S(2)}) collective-permute-start(bf16[128,1536]{1,0:T(8,128)(2,1)S(1)} %get-tuple-element.126), channel_id=1, source_target_pairs={{0,6},{2,0},{4,2},{6,4},{1,7},{3,1},{5,3},{7,5},{8,14},{10,8},{12,... | collective-permute-start | bytes 1179656 | tf_op jit(solution)/shard_map/ppermute | solution.py:26
  40.0 2.8 %collective-permute-done.7.up = bf16[128,1536]{1,0:T(8,128)(2,1)S(1)} collective-permute-done((bf16[128,1536]{1,0:T(8,128)(2,1)S(1)}, bf16[128,1536]{1,0:T(8,128)(2,1)S(1)}, u32[]{:S(2)}, u32[]{:S(2)}) %collective-permute-start.7) | collective-permute-done | bytes 393248 | tf_op jit(solution)/shard_map/ppermute | solution.py:26
  42.8 0.6 ring_add.2
  43.6 3.2 %collective-permute-start.16 = (bf16[2,128,1536]{2,1,0:T(8,128)(2,1)S(1)}, bf16[2,128,1536]{2,1,0:T(8,128)(2,1)S(1)}, u32[]{:S(2)}, u32[]{:S(2)}) collective-permute-start(bf16[2,128,1536]{2,1,0:T(8,128)(2,1)S(1)} %get-tuple-element.124), channel_id=1, source_target_pairs={{0,6},{2,0},{4,2},{6,4},{1,7},{3,1},{5,3},{7,5},{8,14},{10,8},{12,... | collective-permute-start | bytes 2359304 | tf_op jit(solution)/shard_map/ppermute | solution.py:26
  46.8 2.7 %collective-permute-done.18.down = bf16[128,1536]{1,0:T(8,128)(2,1)S(1)} collective-permute-done((bf16[128,1536]{1,0:T(8,128)(2,1)S(1)}, bf16[128,1536]{1,0:T(8,128)(2,1)S(1)}, u32[]{:S(2)}, u32[]{:S(2)}) %collective-permute-start.18) | collective-permute-done | bytes 393248 | tf_op jit(solution)/shard_map/ppermute | solution.py:26
  49.5 3.7 %collective-permute-done.17.up = bf16[128,1536]{1,0:T(8,128)(2,1)S(1)} collective-permute-done((bf16[128,1536]{1,0:T(8,128)(2,1)S(1)}, bf16[128,1536]{1,0:T(8,128)(2,1)S(1)}, u32[]{:S(2)}, u32[]{:S(2)}) %collective-permute-start.17) | collective-permute-done | bytes 393248 | tf_op jit(solution)/shard_map/ppermute | solution.py:26
  53.2 0.6 ring_add.3
  53.9 3.2 %collective-permute-start.21 = (bf16[2,128,1536]{2,1,0:T(8,128)(2,1)S(1)}, bf16[2,128,1536]{2,1,0:T(8,128)(2,1)S(1)}, u32[]{:S(2)}, u32[]{:S(2)}) collective-permute-start(bf16[2,128,1536]{2,1,0:T(8,128)(2,1)S(1)} %get-tuple-element.130), channel_id=1, source_target_pairs={{0,6},{2,0},{4,2},{6,4},{1,7},{3,1},{5,3},{7,5},{8,14},{10,8},{12,... | collective-permute-start | bytes 2359304 | tf_op jit(solution)/shard_map/ppermute | solution.py:26
  57.1 12.9 %collective-permute-done.15.up = bf16[2,128,1536]{2,1,0:T(8,128)(2,1)S(1)} collective-permute-done((bf16[2,128,1536]{2,1,0:T(8,128)(2,1)S(1)}, bf16[2,128,1536]{2,1,0:T(8,128)(2,1)S(1)}, u32[]{:S(2)}, u32[]{:S(2)}) %collective-permute-start.15) | collective-permute-done | bytes 786464 | tf_op jit(solution)/shard_map/ppermute | solution.py:26
  70.0 0.7 own_sum.2
  70.8 1.6 collective-permute-start.19
  72.3 13.5 %collective-permute-done.20.up = bf16[2,128,1536]{2,1,0:T(8,128)(2,1)S(1)} collective-permute-done((bf16[2,128,1536]{2,1,0:T(8,128)(2,1)S(1)}, bf16[2,128,1536]{2,1,0:T(8,128)(2,1)S(1)}, u32[]{:S(2)}, u32[]{:S(2)}) %collective-permute-start.20) | collective-permute-done | bytes 786464 | tf_op jit(solution)/shard_map/ppermute | solution.py:26
  85.9 0.7 own_sum.3
  86.6 1.6 collective-permute-start.24
  88.4 0.7 hidden.2.mine.refs_6_.refs_9_
  89.2 3.2 %collective-permute-start.22 = (bf16[2,128,1536]{2,1,0:T(8,128)(2,1)S(1)}, bf16[2,128,1536]{2,1,0:T(8,128)(2,1)S(1)}, u32[]{:S(2)}, u32[]{:S(2)}) collective-permute-start(bf16[2,128,1536]{2,1,0:T(8,128)(2,1)S(1)} %hidden.2.mine.refs_6_.refs_9_), channel_id=1, source_target_pairs={{0,6},{2,0},{4,2},{6,4},{1,7},{3,1},{5,3},{7,5},{8,14},{10,8},{12,... | collective-permute-start | bytes 2359304 | tf_op jit(solution)/shard_map/ppermute | solution.py:26
  92.4 12.8 %collective-permute-done.24.other = bf16[2,128,1536]{2,1,0:T(8,128)(2,1)S(1)} collective-permute-done((bf16[2,128,1536]{2,1,0:T(8,128)(2,1)S(1)}, bf16[2,128,1536]{2,1,0:T(8,128)(2,1)S(1)}, u32[]{:S(2)}, u32[]{:S(2)}) %collective-permute-start.24) | collective-permute-done | bytes 786464 | tf_op jit(solution)/shard_map/ppermute | solution.py:26
  105.2 0.7 hidden.3.mine.refs_6_.refs_9_
  106.1 3.2 %collective-permute-start.27 = (bf16[2,128,1536]{2,1,0:T(8,128)(2,1)S(1)}, bf16[2,128,1536]{2,1,0:T(8,128)(2,1)S(1)}, u32[]{:S(2)}, u32[]{:S(2)}) collective-permute-start(bf16[2,128,1536]{2,1,0:T(8,128)(2,1)S(1)} %hidden.3.mine.refs_6_.refs_9_), channel_id=1, source_target_pairs={{0,6},{2,0},{4,2},{6,4},{1,7},{3,1},{5,3},{7,5},{8,14},{10,8},{12,... | collective-permute-start | bytes 2359304 | tf_op jit(solution)/shard_map/ppermute | solution.py:26
  109.4 3.2 %collective-permute-start.25 = (bf16[128,1536]{1,0:T(8,128)(2,1)S(1)}, bf16[128,1536]{1,0:T(8,128)(2,1)S(1)}, u32[]{:S(2)}, u32[]{:S(2)}) collective-permute-start(bf16[128,1536]{1,0:T(8,128)(2,1)S(1)} %get-tuple-element.143), channel_id=1, source_target_pairs={{0,6},{2,0},{4,2},{6,4},{1,7},{3,1},{5,3},{7,5},{8,14},{10,8},{12,... | collective-permute-start | bytes 1179656 | tf_op jit(solution)/shard_map/ppermute | solution.py:26
  112.6 2.2 %input_three.2 = (f32[3,128,384]{2,1,0:T(8,128)S(1)}, f32[3,128,384]{2,1,0:T(8,128)S(1)}) custom-call(bf16[2,128,1536]{2,1,0:T(8,128)(2,1)S(1)} %hidden.2.mine.refs_6_.refs_9_, bf16[2,128,1536]{2,1,0:T(8,128)(2,1)S(1)} %collective-permute-done.22.above.refs_7_.refs_10_, bf16[2,128,1536]{2,1,0:T(8,128)(2,1)S(1)} %collective-permute-done.23.below.refs_8_.refs_11_, ...), custom_call_target="tpu_custom_call" | custom-call | flops 115000000 | bytes 369000 | tf_op jit(solution)/shard_map/input_three/pallas_call | solution.py:47
  114.9 3.8 %grads_a.1 = (f32[768,1536]{1,0:T(8,128)S(1)}, f32[1536,768]{1,0:T(8,128)S(1)}) custom-call(bf16[512,768]{1,0:T(8,128)(2,1)S(1)} %get-tuple-element.151.refs_0_.refs_1_.refs_2_, bf16[512,768]{1,0:T(8,128)(2,1)S(1)} %get-tuple-element.151.refs_0_.refs_1_.refs_2_, bf16[512,768]{1,0:T(8,128)(2,1)S(1)} %get-tuple-element.151.refs_0_.refs_1_.refs_2_, ...), custom_call_target="tpu_custom_call" | custom-call | flops 115000000 | bytes 369000 | tf_op jit(solution)/shard_map/grads_a/pallas_call | solution.py:47
  118.7 2.2 %copy-done = f32[768,1536]{1,0:T(8,128)} copy-done((f32[768,1536]{1,0:T(8,128)}, f32[768,1536]{1,0:T(8,128)S(1)}, u32[]{:S(2)}) %copy-start) | copy-done | bytes 4718616
  120.9 6.8 %collective-permute-done.28.below.refs_8_.refs_11_ = bf16[2,128,1536]{2,1,0:T(8,128)(2,1)S(1)} collective-permute-done((bf16[2,128,1536]{2,1,0:T(8,128)(2,1)S(1)}, bf16[2,128,1536]{2,1,0:T(8,128)(2,1)S(1)}, u32[]{:S(2)}, u32[]{:S(2)}) %collective-permute-start.28) | collective-permute-done | bytes 786464 | tf_op jit(solution)/shard_map/ppermute | solution.py:26
  127.9 3.3 %collective-permute-start.32 = (bf16[128,1536]{1,0:T(8,128)(2,1)S(1)}, bf16[128,1536]{1,0:T(8,128)(2,1)S(1)}, u32[]{:S(2)}, u32[]{:S(2)}) collective-permute-start(bf16[128,1536]{1,0:T(8,128)(2,1)S(1)} %get-tuple-element.160), channel_id=1, source_target_pairs={{0,6},{2,0},{4,2},{6,4},{1,7},{3,1},{5,3},{7,5},{8,14},{10,8},{12,... | collective-permute-start | bytes 1179656 | tf_op jit(solution)/shard_map/ppermute | solution.py:26
  131.2 2.2 %input_three.3 = (f32[3,128,384]{2,1,0:T(8,128)S(1)}, f32[3,128,384]{2,1,0:T(8,128)S(1)}) custom-call(bf16[2,128,1536]{2,1,0:T(8,128)(2,1)S(1)} %hidden.3.mine.refs_6_.refs_9_, bf16[2,128,1536]{2,1,0:T(8,128)(2,1)S(1)} %collective-permute-done.27.above.refs_7_.refs_10_, bf16[2,128,1536]{2,1,0:T(8,128)(2,1)S(1)} %collective-permute-done.28.below.refs_8_.refs_11_, ...), custom_call_target="tpu_custom_call" | custom-call | flops 115000000 | bytes 369000 | tf_op jit(solution)/shard_map/input_three/pallas_call | solution.py:47
  133.4 4.1 %grads_b.1 = (f32[768,1536]{1,0:T(8,128)S(1)}, f32[1536,768]{1,0:T(8,128)S(1)}) custom-call(bf16[512,768]{1,0:T(8,128)(2,1)S(1)} %get-tuple-element.149.refs_0_.refs_1_.refs_2_, bf16[512,768]{1,0:T(8,128)(2,1)S(1)} %get-tuple-element.149.refs_0_.refs_1_.refs_2_, bf16[512,768]{1,0:T(8,128)(2,1)S(1)} %get-tuple-element.149.refs_0_.refs_1_.refs_2_, ...), custom_call_target="tpu_custom_call" | custom-call | flops 115000000 | bytes 369000 | tf_op jit(solution)/shard_map/grads_b/pallas_call | solution.py:47
  137.6 0.9 input_last.2
  139.2 0.9 collective-permute-done.29.refs_0_
  141.0 1.2 collective-permute-done.33.grad.refs_8_
  142.2 0.9 input_last.3
  143.2 0.5 collective-permute-start.35
  143.7 2.3 %collective-permute-start.36 = (bf16[4,32,384]{2,1,0:T(8,128)(2,1)S(1)}, bf16[4,32,384]{2,1,0:T(8,128)(2,1)S(1)}, u32[]{:S(2)}, u32[]{:S(2)}) collective-permute-start(bf16[4,32,384]{2,1,0:T(8,128)(2,1)S(1)} %get-tuple-element.180), channel_id=1, source_target_pairs={{0,64},{32,96},{64,0},{96,32},{1,65},{33,97},{65,1},{97,33},{2,66}... | collective-permute-start | bytes 294920 | tf_op jit(solution)/shard_map/ppermute | solution.py:26
  146.0 1.1 collective-permute-start.37
  147.2 3.5 %grads_last.1 = (bf16[384,3072]{1,0:T(8,128)(2,1)}, bf16[3072,384]{1,0:T(8,128)(2,1)}, bf16[384,1536]{1,0:T(8,128)(2,1)S(1)}, bf16[1536,384]{1,0:T(8,128)(2,1)}) custom-call(s32[1]{0:T(128)} %bitcast.1._.refs_0_.core, bf16[512,768]{1,0:T(8,128)(2,1)S(1)} %get-tuple-element.151.refs_0_.refs_1_.refs_2_, ...), custom_call_target="tpu_custom_call" | custom-call | flops 115000000 | bytes 369000 | tf_op jit(solution)/shard_map/grads_last/pallas_call | solution.py:47
  150.7 1.1 collective-permute-done.35
  151.7 0.6 collective-permute-done.37
  153.0 2.7 %collective-permute-start.38 = (bf16[4,32,384]{2,1,0:T(8,128)(2,1)S(1)}, bf16[4,32,384]{2,1,0:T(8,128)(2,1)S(1)}, u32[]{:S(2)}, u32[]{:S(2)}) collective-permute-start(bf16[4,32,384]{2,1,0:T(8,128)(2,1)S(1)} %get-tuple-element.195), channel_id=1, source_target_pairs={{0,16},{16,0},{32,48},{48,32},{64,80},{80,64},{96,112},{112,96},{1... | collective-permute-start | bytes 294920 | tf_op jit(solution)/shard_map/ppermute | solution.py:468
  155.7 0.9 collective-permute-start.39
  156.6 5.7 %collective-permute-start.40 = (bf16[4,32,384]{2,1,0:T(8,128)(2,1)S(1)}, bf16[4,32,384]{2,1,0:T(8,128)(2,1)S(1)}, u32[]{:S(2)}, u32[]{:S(2)}) collective-permute-start(bf16[4,32,384]{2,1,0:T(8,128)(2,1)S(1)} %get-tuple-element.197), channel_id=1, source_target_pairs={{0,80},{16,64},{32,112},{48,96},{64,16},{80,0},{96,48},{112,32},{1... | collective-permute-start | bytes 294920 | tf_op jit(solution)/shard_map/ppermute | solution.py:468
  162.3 2.0 %place.1 = (bf16[384,3072]{1,0:T(8,128)(2,1)}, bf16[3072,384]{1,0:T(8,128)(2,1)}) custom-call(s32[1]{0:T(128)} %bitcast.1._.refs_0_.core, bf16[384,3072]{1,0:T(8,128)(2,1)} %get-tuple-element.199.wi, bf16[3072,384]{1,0:T(8,128)(2,1)} %get-tuple-element.200.wo, ...), custom_call_target="tpu_custom_call", output_to_operand_aliasing={{0}: (1, {}), {1}: (2, {})} | custom-call | flops 115000000 | bytes 369000 | tf_op jit(solution)/shard_map/place/pallas_call | solution.py:47
  164.3 0.8 collective-permute-done.39
  165.0 2.1 %collective-permute-done.40 = bf16[4,32,384]{2,1,0:T(8,128)(2,1)S(1)} collective-permute-done((bf16[4,32,384]{2,1,0:T(8,128)(2,1)S(1)}, bf16[4,32,384]{2,1,0:T(8,128)(2,1)S(1)}, u32[]{:S(2)}, u32[]{:S(2)}) %collective-permute-start.40) | collective-permute-done | bytes 98336 | tf_op jit(solution)/shard_map/ppermute | solution.py:468
  167.1 2.3 %collective-permute-done.41 = bf16[4,32,384]{2,1,0:T(8,128)(2,1)} collective-permute-done((bf16[4,32,384]{2,1,0:T(8,128)(2,1)S(1)}, bf16[4,32,384]{2,1,0:T(8,128)(2,1)}, u32[]{:S(2)}, u32[]{:S(2)}) %collective-permute-start.41) | collective-permute-done | bytes 98336 | tf_op jit(solution)/shard_map/ppermute | solution.py:468
  169.4 1.0 convert_add_fusion
  170.4 0.7 fusion.1
  (62 shorter events, 4.7 us)
Async XLA Ops:
  1.7 13.1 %collective-permute-start.2 = (bf16[4,32,768]{2,1,0:T(8,128)(2,1)S(1)}, bf16[4,32,768]{2,1,0:T(8,128)(2,1)S(1)}, u32[]{:S(2)}, u32[]{:S(2)}) collective-permute-start(bf16[4,32,768]{2,1,0:T(8,128)(2,1)S(1)} %fusion.2.refs_0_), channel_id=1, source_target_pairs={{0,32},{32,64},{64,96},{96,0},{1,33},{33,65},{65,97},{97,1},{2,34}... | collective-permute-start | bytes 589832 | tf_op jit(solution)/shard_map/ppermute | solution.py:26
  3.4 11.7 %collective-permute-start.1 = (bf16[4,32,768]{2,1,0:T(8,128)(2,1)S(1)}, bf16[4,32,768]{2,1,0:T(8,128)(2,1)S(1)}, u32[]{:S(2)}, u32[]{:S(2)}) collective-permute-start(bf16[4,32,768]{2,1,0:T(8,128)(2,1)S(1)} %fusion.2.refs_0_), channel_id=1, source_target_pairs={{0,64},{32,96},{64,0},{96,32},{1,65},{33,97},{65,1},{97,33},{2,66}... | collective-permute-start | bytes 589832 | tf_op jit(solution)/shard_map/ppermute | solution.py:26
  6.3 8.8 %collective-permute-start = (bf16[4,32,768]{2,1,0:T(8,128)(2,1)S(1)}, bf16[4,32,768]{2,1,0:T(8,128)(2,1)S(1)}, u32[]{:S(2)}, u32[]{:S(2)}) collective-permute-start(bf16[4,32,768]{2,1,0:T(8,128)(2,1)S(1)} %fusion.2.refs_0_), channel_id=1, source_target_pairs={{0,96},{32,0},{64,32},{96,64},{1,97},{33,1},{65,33},{97,65},{2,98}... | collective-permute-start | bytes 589832 | tf_op jit(solution)/shard_map/ppermute | solution.py:26
  7.7 7.5 %collective-permute-start.5 = (bf16[4,32,768]{2,1,0:T(8,128)(2,1)S(1)}, bf16[4,32,768]{2,1,0:T(8,128)(2,1)S(1)}, u32[]{:S(2)}, u32[]{:S(2)}) collective-permute-start(bf16[4,32,768]{2,1,0:T(8,128)(2,1)S(1)} %fusion.2.refs_0_), channel_id=1, source_target_pairs={{0,16},{16,0},{1,17},{17,1},{2,18},{18,2},{3,19},{19,3},{4,20},{20... | collective-permute-start | bytes 589832 | tf_op jit(solution)/shard_map/ppermute | solution.py:26
  10.7 1.7 copy-start.2
  12.4 1.7 copy-start.4
  14.7 5.9 %copy-start.3 = (bf16[384,3072]{1,0:T(8,128)(2,1)S(1)}, bf16[384,3072]{1,0:T(8,128)(2,1)}, u32[]{:S(2)}) copy-start(bf16[384,3072]{1,0:T(8,128)(2,1)} %wi.2) | copy-start | bytes 7077892
  14.7 5.9 %collective-permute-start.4 = (bf16[2,4,384,384]{3,2,1,0:T(8,128)(2,1)S(1)}, bf16[2,4,384,384]{3,2,1,0:T(8,128)(2,1)S(1)}, u32[]{:S(2)}, u32[]{:S(2)}) collective-permute-start(bf16[2,4,384,384]{3,2,1,0:T(8,128)(2,1)S(1)} %pack.1), channel_id=1, source_target_pairs={{0,1},{1,0},{2,3},{3,2},{4,5},{5,4},{6,7},{7,6},{8,9},{9,8},{10,11... | collective-permute-start | bytes 7077896 | tf_op jit(solution)/shard_map/ppermute | solution.py:26
  15.2 5.4 %collective-permute-start.6 = (bf16[4,32,768]{2,1,0:T(8,128)(2,1)S(1)}, bf16[4,32,768]{2,1,0:T(8,128)(2,1)S(1)}, u32[]{:S(2)}, u32[]{:S(2)}) collective-permute-start(bf16[4,32,768]{2,1,0:T(8,128)(2,1)S(1)} %collective-permute-done.5.refs_0_), channel_id=1, source_target_pairs={{0,1},{1,0},{2,3},{3,2},{4,5},{5,4},{6,7},{7,6},{8,9},{9,8},{10,11... | collective-permute-start | bytes 589832 | tf_op jit(solution)/shard_map/ppermute | solution.py:26
  15.5 15.3 %collective-permute-start.11 = (bf16[4,32,768]{2,1,0:T(8,128)(2,1)S(1)}, bf16[4,32,768]{2,1,0:T(8,128)(2,1)S(1)}, u32[]{:S(2)}, u32[]{:S(2)}) collective-permute-start(bf16[4,32,768]{2,1,0:T(8,128)(2,1)S(1)} %collective-permute-done.5.refs_0_), channel_id=1, source_target_pairs={{0,32},{32,64},{64,96},{96,0},{1,33},{33,65},{65,97},{97,1},{2,34}... | collective-permute-start | bytes 589832 | tf_op jit(solution)/shard_map/ppermute | solution.py:26
  16.6 14.1 %collective-permute-start.10 = (bf16[4,32,768]{2,1,0:T(8,128)(2,1)S(1)}, bf16[4,32,768]{2,1,0:T(8,128)(2,1)S(1)}, u32[]{:S(2)}, u32[]{:S(2)}) collective-permute-start(bf16[4,32,768]{2,1,0:T(8,128)(2,1)S(1)} %collective-permute-done.5.refs_0_), channel_id=1, source_target_pairs={{0,64},{32,96},{64,0},{96,32},{1,65},{33,97},{65,1},{97,33},{2,66}... | collective-permute-start | bytes 589832 | tf_op jit(solution)/shard_map/ppermute | solution.py:26
  19.0 11.7 %collective-permute-start.9 = (bf16[4,32,768]{2,1,0:T(8,128)(2,1)S(1)}, bf16[4,32,768]{2,1,0:T(8,128)(2,1)S(1)}, u32[]{:S(2)}, u32[]{:S(2)}) collective-permute-start(bf16[4,32,768]{2,1,0:T(8,128)(2,1)S(1)} %collective-permute-done.5.refs_0_), channel_id=1, source_target_pairs={{0,96},{32,0},{64,32},{96,64},{1,97},{33,1},{65,33},{97,65},{2,98}... | collective-permute-start | bytes 589832 | tf_op jit(solution)/shard_map/ppermute | solution.py:26
  20.6 2.3 %collective-permute-start.3 = (bf16[512,768]{1,0:T(8,128)(2,1)S(1)}, bf16[512,768]{1,0:T(8,128)(2,1)S(1)}, u32[]{:S(2)}, u32[]{:S(2)}) collective-permute-start(bf16[512,768]{1,0:T(8,128)(2,1)S(1)} %join_a.1.own), channel_id=1, source_target_pairs={{0,1},{1,0},{2,3},{3,2},{4,5},{5,4},{6,7},{7,6},{8,9},{9,8},{10,11... | collective-permute-start | bytes 2359304 | tf_op jit(solution)/shard_map/ppermute | solution.py:26
  26.6 13.4 %collective-permute-start.8 = (bf16[128,1536]{1,0:T(8,128)(2,1)S(1)}, bf16[128,1536]{1,0:T(8,128)(2,1)S(1)}, u32[]{:S(2)}, u32[]{:S(2)}) collective-permute-start(bf16[128,1536]{1,0:T(8,128)(2,1)S(1)} %get-tuple-element.114), channel_id=1, source_target_pairs={{0,6},{2,0},{4,2},{6,4},{1,7},{3,1},{5,3},{7,5},{8,14},{10,8},{12,... | collective-permute-start | bytes 1179656 | tf_op jit(solution)/shard_map/ppermute | solution.py:26
  30.7 12.1 %collective-permute-start.7 = (bf16[128,1536]{1,0:T(8,128)(2,1)S(1)}, bf16[128,1536]{1,0:T(8,128)(2,1)S(1)}, u32[]{:S(2)}, u32[]{:S(2)}) collective-permute-start(bf16[128,1536]{1,0:T(8,128)(2,1)S(1)} %get-tuple-element.113), channel_id=1, source_target_pairs={{0,2},{2,4},{4,6},{6,0},{1,3},{3,5},{5,7},{7,1},{8,10},{10,12},{12... | collective-permute-start | bytes 1179656 | tf_op jit(solution)/shard_map/ppermute | solution.py:26
  30.8 1.5 collective-permute-start.12
  30.9 1.7 collective-permute-start.13
  31.4 1.5 collective-permute-start.14
  36.7 12.8 %collective-permute-start.18 = (bf16[128,1536]{1,0:T(8,128)(2,1)S(1)}, bf16[128,1536]{1,0:T(8,128)(2,1)S(1)}, u32[]{:S(2)}, u32[]{:S(2)}) collective-permute-start(bf16[128,1536]{1,0:T(8,128)(2,1)S(1)} %get-tuple-element.126), channel_id=1, source_target_pairs={{0,6},{2,0},{4,2},{6,4},{1,7},{3,1},{5,3},{7,5},{8,14},{10,8},{12,... | collective-permute-start | bytes 1179656 | tf_op jit(solution)/shard_map/ppermute | solution.py:26
  40.0 13.2 %collective-permute-start.17 = (bf16[128,1536]{1,0:T(8,128)(2,1)S(1)}, bf16[128,1536]{1,0:T(8,128)(2,1)S(1)}, u32[]{:S(2)}, u32[]{:S(2)}) collective-permute-start(bf16[128,1536]{1,0:T(8,128)(2,1)S(1)} %get-tuple-element.120), channel_id=1, source_target_pairs={{0,2},{2,4},{4,6},{6,0},{1,3},{3,5},{5,7},{7,1},{8,10},{10,12},{12... | collective-permute-start | bytes 1179656 | tf_op jit(solution)/shard_map/ppermute | solution.py:26
  43.5 26.6 %collective-permute-start.15 = (bf16[2,128,1536]{2,1,0:T(8,128)(2,1)S(1)}, bf16[2,128,1536]{2,1,0:T(8,128)(2,1)S(1)}, u32[]{:S(2)}, u32[]{:S(2)}) collective-permute-start(bf16[2,128,1536]{2,1,0:T(8,128)(2,1)S(1)} %get-tuple-element.123), channel_id=1, source_target_pairs={{0,2},{2,4},{4,6},{6,0},{1,3},{3,5},{5,7},{7,1},{8,10},{10,12},{12... | collective-permute-start | bytes 2359304 | tf_op jit(solution)/shard_map/ppermute | solution.py:26
  43.6 26.5 %collective-permute-start.16 = (bf16[2,128,1536]{2,1,0:T(8,128)(2,1)S(1)}, bf16[2,128,1536]{2,1,0:T(8,128)(2,1)S(1)}, u32[]{:S(2)}, u32[]{:S(2)}) collective-permute-start(bf16[2,128,1536]{2,1,0:T(8,128)(2,1)S(1)} %get-tuple-element.124), channel_id=1, source_target_pairs={{0,6},{2,0},{4,2},{6,4},{1,7},{3,1},{5,3},{7,5},{8,14},{10,8},{12,... | collective-permute-start | bytes 2359304 | tf_op jit(solution)/shard_map/ppermute | solution.py:26
  53.8 32.0 %collective-permute-start.20 = (bf16[2,128,1536]{2,1,0:T(8,128)(2,1)S(1)}, bf16[2,128,1536]{2,1,0:T(8,128)(2,1)S(1)}, u32[]{:S(2)}, u32[]{:S(2)}) collective-permute-start(bf16[2,128,1536]{2,1,0:T(8,128)(2,1)S(1)} %get-tuple-element.129), channel_id=1, source_target_pairs={{0,2},{2,4},{4,6},{6,0},{1,3},{3,5},{5,7},{7,1},{8,10},{10,12},{12... | collective-permute-start | bytes 2359304 | tf_op jit(solution)/shard_map/ppermute | solution.py:26
  53.9 32.0 %collective-permute-start.21 = (bf16[2,128,1536]{2,1,0:T(8,128)(2,1)S(1)}, bf16[2,128,1536]{2,1,0:T(8,128)(2,1)S(1)}, u32[]{:S(2)}, u32[]{:S(2)}) collective-permute-start(bf16[2,128,1536]{2,1,0:T(8,128)(2,1)S(1)} %get-tuple-element.130), channel_id=1, source_target_pairs={{0,6},{2,0},{4,2},{6,4},{1,7},{3,1},{5,3},{7,5},{8,14},{10,8},{12,... | collective-permute-start | bytes 2359304 | tf_op jit(solution)/shard_map/ppermute | solution.py:26
  70.8 17.6 %collective-permute-start.19 = (bf16[2,128,1536]{2,1,0:T(8,128)(2,1)S(1)}, bf16[2,128,1536]{2,1,0:T(8,128)(2,1)S(1)}, u32[]{:S(2)}, u32[]{:S(2)}) collective-permute-start(bf16[2,128,1536]{2,1,0:T(8,128)(2,1)S(1)} %get-tuple-element.134), channel_id=1, source_target_pairs={{0,8},{8,0},{1,9},{9,1},{2,10},{10,2},{3,11},{11,3},{4,12},{12,4},... | collective-permute-start | bytes 2359304 | tf_op jit(solution)/shard_map/ppermute | solution.py:26
  86.6 18.6 %collective-permute-start.24 = (bf16[2,128,1536]{2,1,0:T(8,128)(2,1)S(1)}, bf16[2,128,1536]{2,1,0:T(8,128)(2,1)S(1)}, u32[]{:S(2)}, u32[]{:S(2)}) collective-permute-start(bf16[2,128,1536]{2,1,0:T(8,128)(2,1)S(1)} %get-tuple-element.137), channel_id=1, source_target_pairs={{0,8},{8,0},{1,9},{9,1},{2,10},{10,2},{3,11},{11,3},{4,12},{12,4},... | collective-permute-start | bytes 2359304 | tf_op jit(solution)/shard_map/ppermute | solution.py:26
  89.1 20.2 %collective-permute-start.23 = (bf16[2,128,1536]{2,1,0:T(8,128)(2,1)S(1)}, bf16[2,128,1536]{2,1,0:T(8,128)(2,1)S(1)}, u32[]{:S(2)}, u32[]{:S(2)}) collective-permute-start(bf16[2,128,1536]{2,1,0:T(8,128)(2,1)S(1)} %hidden.2.mine.refs_6_.refs_9_), channel_id=1, source_target_pairs={{0,2},{2,4},{4,6},{6,0},{1,3},{3,5},{5,7},{7,1},{8,10},{10,12},{12... | collective-permute-start | bytes 2359304 | tf_op jit(solution)/shard_map/ppermute | solution.py:26
  89.2 20.1 %collective-permute-start.22 = (bf16[2,128,1536]{2,1,0:T(8,128)(2,1)S(1)}, bf16[2,128,1536]{2,1,0:T(8,128)(2,1)S(1)}, u32[]{:S(2)}, u32[]{:S(2)}) collective-permute-start(bf16[2,128,1536]{2,1,0:T(8,128)(2,1)S(1)} %hidden.2.mine.refs_6_.refs_9_), channel_id=1, source_target_pairs={{0,6},{2,0},{4,2},{6,4},{1,7},{3,1},{5,3},{7,5},{8,14},{10,8},{12,... | collective-permute-start | bytes 2359304 | tf_op jit(solution)/shard_map/ppermute | solution.py:26
  106.0 21.8 %collective-permute-start.28 = (bf16[2,128,1536]{2,1,0:T(8,128)(2,1)S(1)}, bf16[2,128,1536]{2,1,0:T(8,128)(2,1)S(1)}, u32[]{:S(2)}, u32[]{:S(2)}) collective-permute-start(bf16[2,128,1536]{2,1,0:T(8,128)(2,1)S(1)} %hidden.3.mine.refs_6_.refs_9_), channel_id=1, source_target_pairs={{0,2},{2,4},{4,6},{6,0},{1,3},{3,5},{5,7},{7,1},{8,10},{10,12},{12... | collective-permute-start | bytes 2359304 | tf_op jit(solution)/shard_map/ppermute | solution.py:26
  106.1 21.7 %collective-permute-start.27 = (bf16[2,128,1536]{2,1,0:T(8,128)(2,1)S(1)}, bf16[2,128,1536]{2,1,0:T(8,128)(2,1)S(1)}, u32[]{:S(2)}, u32[]{:S(2)}) collective-permute-start(bf16[2,128,1536]{2,1,0:T(8,128)(2,1)S(1)} %hidden.3.mine.refs_6_.refs_9_), channel_id=1, source_target_pairs={{0,6},{2,0},{4,2},{6,4},{1,7},{3,1},{5,3},{7,5},{8,14},{10,8},{12,... | collective-permute-start | bytes 2359304 | tf_op jit(solution)/shard_map/ppermute | solution.py:26
  109.3 28.2 %collective-permute-start.26 = (bf16[128,1536]{1,0:T(8,128)(2,1)S(1)}, bf16[128,1536]{1,0:T(8,128)(2,1)S(1)}, u32[]{:S(2)}, u32[]{:S(2)}) collective-permute-start(bf16[128,1536]{1,0:T(8,128)(2,1)S(1)} %get-tuple-element.148), channel_id=1, source_target_pairs={{0,2},{2,4},{4,6},{6,0},{1,3},{3,5},{5,7},{7,1},{8,10},{10,12},{12... | collective-permute-start | bytes 1179656 | tf_op jit(solution)/shard_map/ppermute | solution.py:26
  109.4 28.1 %collective-permute-start.25 = (bf16[128,1536]{1,0:T(8,128)(2,1)S(1)}, bf16[128,1536]{1,0:T(8,128)(2,1)S(1)}, u32[]{:S(2)}, u32[]{:S(2)}) collective-permute-start(bf16[128,1536]{1,0:T(8,128)(2,1)S(1)} %get-tuple-element.143), channel_id=1, source_target_pairs={{0,6},{2,0},{4,2},{6,4},{1,7},{3,1},{5,3},{7,5},{8,14},{10,8},{12,... | collective-permute-start | bytes 1179656 | tf_op jit(solution)/shard_map/ppermute | solution.py:26
  118.7 2.2 %copy-start = (f32[768,1536]{1,0:T(8,128)}, f32[768,1536]{1,0:T(8,128)S(1)}, u32[]{:S(2)}) copy-start(f32[768,1536]{1,0:T(8,128)S(1)} %get-tuple-element.156.refs_12_) | copy-start | bytes 14155780
  127.8 14.4 %collective-permute-start.33 = (bf16[128,1536]{1,0:T(8,128)(2,1)S(1)}, bf16[128,1536]{1,0:T(8,128)(2,1)S(1)}, u32[]{:S(2)}, u32[]{:S(2)}) collective-permute-start(bf16[128,1536]{1,0:T(8,128)(2,1)S(1)} %get-tuple-element.176), channel_id=1, source_target_pairs={{0,2},{2,4},{4,6},{6,0},{1,3},{3,5},{5,7},{7,1},{8,10},{10,12},{12... | collective-permute-start | bytes 1179656 | tf_op jit(solution)/shard_map/ppermute | solution.py:26
  127.9 5.6 %copy-start.1 = (f32[768,1536]{1,0:T(8,128)S(1)}, f32[768,1536]{1,0:T(8,128)}, u32[]{:S(2)}) copy-start(f32[768,1536]{1,0:T(8,128)} %copy-done) | copy-start | bytes 14155780
  127.9 14.3 %collective-permute-start.32 = (bf16[128,1536]{1,0:T(8,128)(2,1)S(1)}, bf16[128,1536]{1,0:T(8,128)(2,1)S(1)}, u32[]{:S(2)}, u32[]{:S(2)}) collective-permute-start(bf16[128,1536]{1,0:T(8,128)(2,1)S(1)} %get-tuple-element.160), channel_id=1, source_target_pairs={{0,6},{2,0},{4,2},{6,4},{1,7},{3,1},{5,3},{7,5},{8,14},{10,8},{12,... | collective-permute-start | bytes 1179656 | tf_op jit(solution)/shard_map/ppermute | solution.py:26
  138.5 1.6 collective-permute-start.29
  138.6 1.9 %collective-permute-start.30 = (f32[512,128]{1,0:T(8,128)S(1)}, f32[512,128]{1,0:T(8,128)S(1)}, u32[]{:S(2)}, u32[]{:S(2)}) collective-permute-start(f32[512,128]{1,0:T(8,128)S(1)} %get-tuple-element.173), channel_id=1, source_target_pairs={{0,1},{1,0},{2,3},{3,2},{4,5},{5,4},{6,7},{7,6},{8,9},{9,8},{10,11... | collective-permute-start | bytes 786440 | tf_op jit(solution)/shard_map/ppermute | solution.py:26
  139.1 1.8 %collective-permute-start.31 = (f32[512,128]{1,0:T(8,128)S(1)}, f32[512,128]{1,0:T(8,128)S(1)}, u32[]{:S(2)}, u32[]{:S(2)}) collective-permute-start(f32[512,128]{1,0:T(8,128)S(1)} %get-tuple-element.174), channel_id=1, source_target_pairs={{0,1},{1,0},{2,3},{3,2},{4,5},{5,4},{6,7},{7,6},{8,9},{9,8},{10,11... | collective-permute-start | bytes 786440 | tf_op jit(solution)/shard_map/ppermute | solution.py:26
  143.1 9.2 %collective-permute-start.34 = (f32[512,384]{1,0:T(8,128)S(1)}, f32[512,384]{1,0:T(8,128)S(1)}, u32[]{:S(2)}, u32[]{:S(2)}) collective-permute-start(f32[512,384]{1,0:T(8,128)S(1)} %get-tuple-element.178), channel_id=1, source_target_pairs={{0,1},{1,0},{2,3},{3,2},{4,5},{5,4},{6,7},{7,6},{8,9},{9,8},{10,11... | collective-permute-start | bytes 2359304 | tf_op jit(solution)/shard_map/ppermute | solution.py:26
  143.2 8.5 %collective-permute-start.35 = (bf16[4,32,384]{2,1,0:T(8,128)(2,1)S(1)}, bf16[4,32,384]{2,1,0:T(8,128)(2,1)S(1)}, u32[]{:S(2)}, u32[]{:S(2)}) collective-permute-start(bf16[4,32,384]{2,1,0:T(8,128)(2,1)S(1)} %get-tuple-element.179), channel_id=1, source_target_pairs={{0,32},{32,64},{64,96},{96,0},{1,33},{33,65},{65,97},{97,1},{2,34}... | collective-permute-start | bytes 294920 | tf_op jit(solution)/shard_map/ppermute | solution.py:26
  143.7 8.0 %collective-permute-start.36 = (bf16[4,32,384]{2,1,0:T(8,128)(2,1)S(1)}, bf16[4,32,384]{2,1,0:T(8,128)(2,1)S(1)}, u32[]{:S(2)}, u32[]{:S(2)}) collective-permute-start(bf16[4,32,384]{2,1,0:T(8,128)(2,1)S(1)} %get-tuple-element.180), channel_id=1, source_target_pairs={{0,64},{32,96},{64,0},{96,32},{1,65},{33,97},{65,1},{97,33},{2,66}... | collective-permute-start | bytes 294920 | tf_op jit(solution)/shard_map/ppermute | solution.py:26
  146.0 6.3 %collective-permute-start.37 = (bf16[4,32,384]{2,1,0:T(8,128)(2,1)S(1)}, bf16[4,32,384]{2,1,0:T(8,128)(2,1)S(1)}, u32[]{:S(2)}, u32[]{:S(2)}) collective-permute-start(bf16[4,32,384]{2,1,0:T(8,128)(2,1)S(1)} %get-tuple-element.181), channel_id=1, source_target_pairs={{0,96},{32,0},{64,32},{96,64},{1,97},{33,1},{65,33},{97,65},{2,98}... | collective-permute-start | bytes 294920 | tf_op jit(solution)/shard_map/ppermute | solution.py:26
  152.4 9.9 %collective-permute-start.42 = (bf16[384,1536]{1,0:T(8,128)(2,1)S(1)}, bf16[384,1536]{1,0:T(8,128)(2,1)S(1)}, u32[]{:S(2)}, u32[]{:S(2)}) collective-permute-start(bf16[384,1536]{1,0:T(8,128)(2,1)S(1)} %get-tuple-element.201), channel_id=1, source_target_pairs={{0,1},{1,0},{2,3},{3,2},{4,5},{5,4},{6,7},{7,6},{8,9},{9,8},{10,11... | collective-permute-start | bytes 3538952 | tf_op jit(solution)/shard_map/ppermute | solution.py:26
  152.5 9.8 %collective-permute-start.43 = (bf16[1536,384]{1,0:T(8,128)(2,1)}, bf16[1536,384]{1,0:T(8,128)(2,1)S(1)}, u32[]{:S(2)}, u32[]{:S(2)}) collective-permute-start(bf16[1536,384]{1,0:T(8,128)(2,1)} %get-tuple-element.202), channel_id=1, source_target_pairs={{0,1},{1,0},{2,3},{3,2},{4,5},{5,4},{6,7},{7,6},{8,9},{9,8},{10,11... | collective-permute-start | bytes 3538952 | tf_op jit(solution)/shard_map/ppermute | solution.py:26
  153.0 11.3 %collective-permute-start.38 = (bf16[4,32,384]{2,1,0:T(8,128)(2,1)S(1)}, bf16[4,32,384]{2,1,0:T(8,128)(2,1)S(1)}, u32[]{:S(2)}, u32[]{:S(2)}) collective-permute-start(bf16[4,32,384]{2,1,0:T(8,128)(2,1)S(1)} %get-tuple-element.195), channel_id=1, source_target_pairs={{0,16},{16,0},{32,48},{48,32},{64,80},{80,64},{96,112},{112,96},{1... | collective-permute-start | bytes 294920 | tf_op jit(solution)/shard_map/ppermute | solution.py:468
  155.7 9.3 %collective-permute-start.39 = (bf16[4,32,384]{2,1,0:T(8,128)(2,1)S(1)}, bf16[4,32,384]{2,1,0:T(8,128)(2,1)S(1)}, u32[]{:S(2)}, u32[]{:S(2)}) collective-permute-start(bf16[4,32,384]{2,1,0:T(8,128)(2,1)S(1)} %get-tuple-element.196), channel_id=1, source_target_pairs={{0,48},{16,32},{32,80},{48,64},{64,112},{80,96},{96,16},{112,0},{1... | collective-permute-start | bytes 294920 | tf_op jit(solution)/shard_map/ppermute | solution.py:468
  156.6 10.5 %collective-permute-start.40 = (bf16[4,32,384]{2,1,0:T(8,128)(2,1)S(1)}, bf16[4,32,384]{2,1,0:T(8,128)(2,1)S(1)}, u32[]{:S(2)}, u32[]{:S(2)}) collective-permute-start(bf16[4,32,384]{2,1,0:T(8,128)(2,1)S(1)} %get-tuple-element.197), channel_id=1, source_target_pairs={{0,80},{16,64},{32,112},{48,96},{64,16},{80,0},{96,48},{112,32},{1... | collective-permute-start | bytes 294920 | tf_op jit(solution)/shard_map/ppermute | solution.py:468
  162.3 7.1 %collective-permute-start.41 = (bf16[4,32,384]{2,1,0:T(8,128)(2,1)S(1)}, bf16[4,32,384]{2,1,0:T(8,128)(2,1)}, u32[]{:S(2)}, u32[]{:S(2)}) collective-permute-start(bf16[4,32,384]{2,1,0:T(8,128)(2,1)S(1)} %get-tuple-element.198), channel_id=1, source_target_pairs={{0,112},{16,96},{32,16},{48,0},{64,48},{80,32},{96,80},{112,64},{1... | collective-permute-start | bytes 294920 | tf_op jit(solution)/shard_map/ppermute | solution.py:468

commit v7 on v6

--- a/solution.py
+++ b/solution.py
@@ -34,7 +34,7 @@
     return lax.optimization_barrier((value, after))[0]
 
 
-COST = dict(pack=0.1, weights=20, join_a=100, join_b=0.1, products=0.1, ring_add=0.1, own_sum=0.1, hidden=0.1, pass_on=0.1, input_three=0.1, input_last=0.1, grads_a=0.1, grads_b=0.1, grads_last=0.1, return_a=0.1, return_b=20, place=0.1)
+COST = dict(pack=0.1, first_block=0.1, weights=7, join_a=100, join_b=0.1, products=0.1, ring_add=0.1, own_sum=0.1, hidden=0.1, pass_on=0.1, input_three=0.1, input_last=0.1, grads_a=0.1, grads_b=0.1, grads_last=0.1, return_a=0.1, return_b=20, place=0.1)
 
 
 def kernel(name, body, grid, ins, outs, scratch=(), scalar=None, aliases=None):
@@ -42,7 +42,7 @@
         def at(i, *refs):
             return tuple(i if k == "i" else k(i, *(r[0] for r in refs)) if callable(k) else k for k in index)
 
-        return pl.BlockSpec(memory_space=pl.ANY) if block is None else pl.BlockSpec(block, at)
+        return pl.BlockSpec(memory_space=pltpu.HBM) if block is None else pl.BlockSpec(block, at)
 
     return pl.pallas_call(
         body,
@@ -65,18 +65,25 @@
     feat = w_in.shape[0]
     half = w_out.shape[0] // feat // 2
 
-    def body(_, wi, wo, out):
-        out[0, 0] = wi[...]
-        out[1, 0] = wo[...]
-
-    block = (feat, feat)
-    place = lambda i, c: (1 - c) * half + i
+    def body(core, wi, wo, out, sems):
+        copies = []
+        for k in range(half):
+            at = pl.ds(pl.multiple_of(((1 - core[0]) * half + k) * feat, feat), feat)
+            copies.append(pltpu.make_async_copy(wi.at[:, at], out.at[0, k], sems.at[0, k]))
+            copies.append(pltpu.make_async_copy(wo.at[at, :], out.at[1, k], sems.at[1, k]))
+        for copy in copies:
+            copy.start()
+        for copy in copies:
+            copy.wait()
+
+    shape = (2, half, feat, feat)
     return kernel(
         "pack",
         body,
-        half,
-        [(w_in, block, (0, place)), (w_out, block, (place, 0))],
-        [((2, half, feat, feat), BF16, (2, 1, feat, feat), (0, "i", 0, 0))],
+        1,
+        [(w_in, None, None), (w_out, None, None)],
+        [(shape, BF16, shape, (0, 0, 0, 0))],
+        [pltpu.SemaphoreType.DMA((2, half))],
         scalar=core,
     )[0]
 
@@ -139,6 +146,27 @@
         1,
         [(a, (zs, piece, width), (0, 0, 0)) for side in sides for a in side],
         [((zs * per, width), BF16, (zs * per, width), (0, 0))] * len(sides),
+    )
+
+
+def first_block(own, other, wi, wo):
+    rows, width = own.shape
+    feat, hid = wi.shape
+    half, per, block = width // 2, rows // 4, hid // STEPS
+
+    def body(own, other, wi, wo, up, down):
+        tok = jnp.concatenate([own[:, :half], other[:, :half]], 1)
+        cot = jnp.concatenate([own[:, half:], other[:, half:]], 1)
+        up[...] = jnp.dot(tok, wi[...], preferred_element_type=F32).astype(BF16)
+        down[...] = dot(cot, wo[...], 1, 1).astype(BF16)
+
+    part = (per, width)
+    return kernel(
+        "first_block",
+        body,
+        STEPS,
+        [(own, part, (2, 0)), (other, part, (2, 0)), (wi, (feat, block), (0, "i")), (wo, (block, feat), ("i", 0))],
+        [((per, hid), BF16, (per, block), (0, "i"))] * 2,
     )
 
 
@@ -414,10 +442,12 @@
     across_other = shift(across, "core", 1)
     wi, wo = weights(w_in, w_out, gate(got, across_other), at_core)
 
-    pg_a, up_a, down_a, tok_a, cot_a = products(near, near_other, wi, wo)
+    up_a, down_a = first_block(near, near_other, wi, wo)
     r_a = up_down(up_a, down_a)
-
-    far = gate(far, up_a)
+    near, near_other = gate((near, near_other), up_a)
+    pg_a, _, _, tok_a, cot_a = products(near, near_other, wi, wo)
+
+    far = gate(far, pg_a)
     far = join("join_b", [across, *far], [across_other, *to_core(far)])
     pg_b, up_b, down_b, tok_b, cot_b = products(*far, wi, wo)
     r_b = up_down(up_b, down_b)

time: 171 us -> 173 us (1.012)
  Pallas kernels: 33.6 us -> 35.9 us
    pallas_call x24 -> x25, Pallas kernels: 33.6 us -> 35.9 us  [kernel(): pl.pallas_call(body, name=name, grid_spec=pltpu.PrefetchScalarGridSpec(nu...]
  transfers between devices with their start and end apart: 44 -> 44, of which waited for: 22 -> 20; matrix products, arithmetic and copies ran while one was open for 0% -> 0% of each run, Pallas kernels for 19% -> 20%
where the time goes in v7:
time: 173 us
  waiting for transfers between devices  67.4 us (39%)
  starting transfers between devices  60.2 us (35%)
  Pallas kernels  35.9 us (21%)
  local copies, waits for them, and re-layouts  5.5 us (3%)
  other arithmetic  2.75 us (2%)
    ppermute x40, waiting for transfers between devices, shift(): return lax.ppermute(x, axis, [(i, (i + by) % n) for i in range(n)])  62.3 us
    ppermute x40, starting transfers between devices, shift(): return lax.ppermute(x, axis, [(i, (i + by) % n) for i in range(n)])  51.2 us
    pallas_call x25, Pallas kernels, kernel(): pl.pallas_call(body, name=name, grid_spec=pltpu.PrefetchScalarGridSpec(nu...  35.9 us
    ppermute x4, starting transfers between devices, local(): lax.ppermute(a, ROWS, [(i, (i // 2 + d) % 4 * 2 + (i + 1) % 2) for i in r...  9.01 us
    unnamed x10, local copies, waits for them, and re-layouts  5.5 us
    ppermute x4, waiting for transfers between devices, local(): lax.ppermute(a, ROWS, [(i, (i // 2 + d) % 4 * 2 + (i + 1) % 2) for i in r...  5.13 us
  transfers between devices with their start and end apart: 44, of which 20 were waited for; matrix products, arithmetic and copies ran while one was open for 0% of the time, Pallas kernels for 20%

profile of v7, /device:TPU:0, one launch (start us, length us, event | category | flops | bytes accessed | tf_op | source)
XLA Modules:
  0.0 172.8 jit_solution(14557519711793637174)
XLA Ops:
  0.7 1.0 pad_maximum_fusion
  1.7 1.7 %collective-permute-start.2 = (bf16[4,32,768]{2,1,0:T(8,128)(2,1)S(1)}, bf16[4,32,768]{2,1,0:T(8,128)(2,1)S(1)}, u32[]{:S(2)}, u32[]{:S(2)}) collective-permute-start(bf16[4,32,768]{2,1,0:T(8,128)(2,1)S(1)} %fusion.2.refs_0_), channel_id=1, source_target_pairs={{0,32},{32,64},{64,96},{96,0},{1,33},{33,65},{65,97},{97,1},{2,34}... | collective-permute-start | bytes 589832 | tf_op jit(solution)/shard_map/ppermute | solution.py:26
  3.4 2.9 %collective-permute-start.1 = (bf16[4,32,768]{2,1,0:T(8,128)(2,1)S(1)}, bf16[4,32,768]{2,1,0:T(8,128)(2,1)S(1)}, u32[]{:S(2)}, u32[]{:S(2)}) collective-permute-start(bf16[4,32,768]{2,1,0:T(8,128)(2,1)S(1)} %fusion.2.refs_0_), channel_id=1, source_target_pairs={{0,64},{32,96},{64,0},{96,32},{1,65},{33,97},{65,1},{97,33},{2,66}... | collective-permute-start | bytes 589832 | tf_op jit(solution)/shard_map/ppermute | solution.py:26
  6.3 1.3 collective-permute-start
  7.7 3.0 %collective-permute-start.5 = (bf16[4,32,768]{2,1,0:T(8,128)(2,1)S(1)}, bf16[4,32,768]{2,1,0:T(8,128)(2,1)S(1)}, u32[]{:S(2)}, u32[]{:S(2)}) collective-permute-start(bf16[4,32,768]{2,1,0:T(8,128)(2,1)S(1)} %fusion.2.refs_0_), channel_id=1, source_target_pairs={{0,16},{16,0},{1,17},{17,1},{2,18},{18,2},{3,19},{19,3},{4,20},{20... | collective-permute-start | bytes 589832 | tf_op jit(solution)/shard_map/ppermute | solution.py:26
  10.7 1.7 copy-done.2
  12.4 1.7 copy-done.4
  14.7 0.5 collective-permute-done.1.refs_2_
  15.3 0.5 collective-permute-start.3
  15.8 1.2 collective-permute-start.11
  17.1 2.4 %collective-permute-start.10 = (bf16[4,32,768]{2,1,0:T(8,128)(2,1)S(1)}, bf16[4,32,768]{2,1,0:T(8,128)(2,1)S(1)}, u32[]{:S(2)}, u32[]{:S(2)}) collective-permute-start(bf16[4,32,768]{2,1,0:T(8,128)(2,1)S(1)} %collective-permute-done.5.refs_0_), channel_id=1, source_target_pairs={{0,64},{32,96},{64,0},{96,32},{1,65},{33,97},{65,1},{97,33},{2,66}... | collective-permute-start | bytes 589832 | tf_op jit(solution)/shard_map/ppermute | solution.py:26
  19.5 1.6 collective-permute-start.9
  21.1 1.1 weights.1
  22.2 1.8 %first_block.1 = (bf16[128,1536]{1,0:T(8,128)(2,1)S(1)}, bf16[128,1536]{1,0:T(8,128)(2,1)S(1)}) custom-call(bf16[512,768]{1,0:T(8,128)(2,1)S(1)} %join_a.1.own, bf16[512,768]{1,0:T(8,128)(2,1)S(1)} %collective-permute-done.3.other, bf16[768,1536]{1,0:T(8,128)(2,1)S(1)} %get-tuple-element.112.wi, bf16[1536,768]{1,0:T(8,128)(2,1)S(1)} %get-tuple-element.113.wo), custom_call_target="tpu_custom_call" | custom-call | flops 115000000 | bytes 369000 | tf_op jit(solution)/shard_map/first_block/pallas_call | solution.py:47
  24.0 4.1 %collective-permute-start.8 = (bf16[128,1536]{1,0:T(8,128)(2,1)S(1)}, bf16[128,1536]{1,0:T(8,128)(2,1)S(1)}, u32[]{:S(2)}, u32[]{:S(2)}) collective-permute-start(bf16[128,1536]{1,0:T(8,128)(2,1)S(1)} %get-tuple-element.118), channel_id=1, source_target_pairs={{0,6},{2,0},{4,2},{6,4},{1,7},{3,1},{5,3},{7,5},{8,14},{10,8},{12,... | collective-permute-start | bytes 1179656 | tf_op jit(solution)/shard_map/ppermute | solution.py:26
  28.1 4.4 %products.2 = (f32[2,512,1536]{2,1,0:T(8,128)S(1)}, bf16[128,1536]{1,0:T(8,128)(2,1)}, bf16[128,1536]{1,0:T(8,128)(2,1)}, bf16[512,768]{1,0:T(8,128)(2,1)S(1)}, bf16[512,768]{1,0:T(8,128)(2,1)S(1)}) custom-call(bf16[512,768]{1,0:T(8,128)(2,1)S(1)} %join_a.1.own, bf16[512,768]{1,0:T(8,128)(2,1)S(1)} %collective-permute-done.3.other, ...), custom_call_target="tpu_custom_call" | custom-call | flops 115000000 | bytes 369000 | tf_op jit(solution)/shard_map/products/pallas_call | solution.py:47
  32.6 0.5 collective-permute-start.13
  33.2 0.8 collective-permute-done.12.refs_5_
  34.7 3.7 %products.3 = (f32[2,512,1536]{2,1,0:T(8,128)S(1)}, bf16[128,1536]{1,0:T(8,128)(2,1)S(1)}, bf16[128,1536]{1,0:T(8,128)(2,1)S(1)}, bf16[512,768]{1,0:T(8,128)(2,1)S(1)}, bf16[512,768]{1,0:T(8,128)(2,1)S(1)}) custom-call(bf16[512,768]{1,0:T(8,128)(2,1)S(1)} %get-tuple-element.122.own, bf16[512,768]{1,0:T(8,128)(2,1)S(1)} %get-tuple-element.123.other, ...), custom_call_target="tpu_custom_call" | custom-call | flops 115000000 | bytes 369000 | tf_op jit(solution)/shard_map/products/pallas_call | solution.py:47
  38.4 3.3 %collective-permute-start.18 = (bf16[128,1536]{1,0:T(8,128)(2,1)S(1)}, bf16[128,1536]{1,0:T(8,128)(2,1)S(1)}, u32[]{:S(2)}, u32[]{:S(2)}) collective-permute-start(bf16[128,1536]{1,0:T(8,128)(2,1)S(1)} %get-tuple-element.130), channel_id=1, source_target_pairs={{0,6},{2,0},{4,2},{6,4},{1,7},{3,1},{5,3},{7,5},{8,14},{10,8},{12,... | collective-permute-start | bytes 1179656 | tf_op jit(solution)/shard_map/ppermute | solution.py:26
  41.8 0.7 ring_add.2
  42.5 3.3 %collective-permute-start.16 = (bf16[2,128,1536]{2,1,0:T(8,128)(2,1)S(1)}, bf16[2,128,1536]{2,1,0:T(8,128)(2,1)S(1)}, u32[]{:S(2)}, u32[]{:S(2)}) collective-permute-start(bf16[2,128,1536]{2,1,0:T(8,128)(2,1)S(1)} %get-tuple-element.128), channel_id=1, source_target_pairs={{0,6},{2,0},{4,2},{6,4},{1,7},{3,1},{5,3},{7,5},{8,14},{10,8},{12,... | collective-permute-start | bytes 2359304 | tf_op jit(solution)/shard_map/ppermute | solution.py:26
  45.8 5.4 %collective-permute-done.18.down = bf16[128,1536]{1,0:T(8,128)(2,1)S(1)} collective-permute-done((bf16[128,1536]{1,0:T(8,128)(2,1)S(1)}, bf16[128,1536]{1,0:T(8,128)(2,1)S(1)}, u32[]{:S(2)}, u32[]{:S(2)}) %collective-permute-start.18) | collective-permute-done | bytes 393248 | tf_op jit(solution)/shard_map/ppermute | solution.py:26
  51.2 3.7 %collective-permute-done.17.up = bf16[128,1536]{1,0:T(8,128)(2,1)S(1)} collective-permute-done((bf16[128,1536]{1,0:T(8,128)(2,1)S(1)}, bf16[128,1536]{1,0:T(8,128)(2,1)S(1)}, u32[]{:S(2)}, u32[]{:S(2)}) %collective-permute-start.17) | collective-permute-done | bytes 393248 | tf_op jit(solution)/shard_map/ppermute | solution.py:26
  54.9 0.6 ring_add.3
  55.7 3.2 %collective-permute-start.21 = (bf16[2,128,1536]{2,1,0:T(8,128)(2,1)S(1)}, bf16[2,128,1536]{2,1,0:T(8,128)(2,1)S(1)}, u32[]{:S(2)}, u32[]{:S(2)}) collective-permute-start(bf16[2,128,1536]{2,1,0:T(8,128)(2,1)S(1)} %get-tuple-element.134), channel_id=1, source_target_pairs={{0,6},{2,0},{4,2},{6,4},{1,7},{3,1},{5,3},{7,5},{8,14},{10,8},{12,... | collective-permute-start | bytes 2359304 | tf_op jit(solution)/shard_map/ppermute | solution.py:26
  58.9 12.9 %collective-permute-done.15.up = bf16[2,128,1536]{2,1,0:T(8,128)(2,1)S(1)} collective-permute-done((bf16[2,128,1536]{2,1,0:T(8,128)(2,1)S(1)}, bf16[2,128,1536]{2,1,0:T(8,128)(2,1)S(1)}, u32[]{:S(2)}, u32[]{:S(2)}) %collective-permute-start.15) | collective-permute-done | bytes 786464 | tf_op jit(solution)/shard_map/ppermute | solution.py:26
  71.8 0.7 own_sum.2
  72.5 1.6 collective-permute-start.19
  74.1 13.5 %collective-permute-done.20.up = bf16[2,128,1536]{2,1,0:T(8,128)(2,1)S(1)} collective-permute-done((bf16[2,128,1536]{2,1,0:T(8,128)(2,1)S(1)}, bf16[2,128,1536]{2,1,0:T(8,128)(2,1)S(1)}, u32[]{:S(2)}, u32[]{:S(2)}) %collective-permute-start.20) | collective-permute-done | bytes 786464 | tf_op jit(solution)/shard_map/ppermute | solution.py:26
  87.6 0.7 own_sum.3
  88.3 1.6 collective-permute-start.24
  90.1 0.7 hidden.2.mine.refs_6_.refs_9_
  91.1 3.2 %collective-permute-start.22 = (bf16[2,128,1536]{2,1,0:T(8,128)(2,1)S(1)}, bf16[2,128,1536]{2,1,0:T(8,128)(2,1)S(1)}, u32[]{:S(2)}, u32[]{:S(2)}) collective-permute-start(bf16[2,128,1536]{2,1,0:T(8,128)(2,1)S(1)} %hidden.2.mine.refs_6_.refs_9_), channel_id=1, source_target_pairs={{0,6},{2,0},{4,2},{6,4},{1,7},{3,1},{5,3},{7,5},{8,14},{10,8},{12,... | collective-permute-start | bytes 2359304 | tf_op jit(solution)/shard_map/ppermute | solution.py:26
  94.3 12.6 %collective-permute-done.24.other = bf16[2,128,1536]{2,1,0:T(8,128)(2,1)S(1)} collective-permute-done((bf16[2,128,1536]{2,1,0:T(8,128)(2,1)S(1)}, bf16[2,128,1536]{2,1,0:T(8,128)(2,1)S(1)}, u32[]{:S(2)}, u32[]{:S(2)}) %collective-permute-start.24) | collective-permute-done | bytes 786464 | tf_op jit(solution)/shard_map/ppermute | solution.py:26
  107.0 0.7 hidden.3.mine.refs_6_.refs_9_
  107.8 3.2 %collective-permute-start.27 = (bf16[2,128,1536]{2,1,0:T(8,128)(2,1)S(1)}, bf16[2,128,1536]{2,1,0:T(8,128)(2,1)S(1)}, u32[]{:S(2)}, u32[]{:S(2)}) collective-permute-start(bf16[2,128,1536]{2,1,0:T(8,128)(2,1)S(1)} %hidden.3.mine.refs_6_.refs_9_), channel_id=1, source_target_pairs={{0,6},{2,0},{4,2},{6,4},{1,7},{3,1},{5,3},{7,5},{8,14},{10,8},{12,... | collective-permute-start | bytes 2359304 | tf_op jit(solution)/shard_map/ppermute | solution.py:26
  111.2 3.2 %collective-permute-start.25 = (bf16[128,1536]{1,0:T(8,128)(2,1)S(1)}, bf16[128,1536]{1,0:T(8,128)(2,1)S(1)}, u32[]{:S(2)}, u32[]{:S(2)}) collective-permute-start(bf16[128,1536]{1,0:T(8,128)(2,1)S(1)} %get-tuple-element.147), channel_id=1, source_target_pairs={{0,6},{2,0},{4,2},{6,4},{1,7},{3,1},{5,3},{7,5},{8,14},{10,8},{12,... | collective-permute-start | bytes 1179656 | tf_op jit(solution)/shard_map/ppermute | solution.py:26
  114.4 2.2 %input_three.2 = (f32[3,128,384]{2,1,0:T(8,128)S(1)}, f32[3,128,384]{2,1,0:T(8,128)S(1)}) custom-call(bf16[2,128,1536]{2,1,0:T(8,128)(2,1)S(1)} %hidden.2.mine.refs_6_.refs_9_, bf16[2,128,1536]{2,1,0:T(8,128)(2,1)S(1)} %collective-permute-done.22.above.refs_7_.refs_10_, bf16[2,128,1536]{2,1,0:T(8,128)(2,1)S(1)} %collective-permute-done.23.below.refs_8_.refs_11_, ...), custom_call_target="tpu_custom_call" | custom-call | flops 115000000 | bytes 369000 | tf_op jit(solution)/shard_map/input_three/pallas_call | solution.py:47
  116.6 3.8 %grads_a.1 = (f32[768,1536]{1,0:T(8,128)S(1)}, f32[1536,768]{1,0:T(8,128)S(1)}) custom-call(bf16[512,768]{1,0:T(8,128)(2,1)S(1)} %get-tuple-element.155.refs_0_.refs_1_.refs_2_, bf16[512,768]{1,0:T(8,128)(2,1)S(1)} %get-tuple-element.155.refs_0_.refs_1_.refs_2_, bf16[512,768]{1,0:T(8,128)(2,1)S(1)} %get-tuple-element.155.refs_0_.refs_1_.refs_2_, ...), custom_call_target="tpu_custom_call" | custom-call | flops 115000000 | bytes 369000 | tf_op jit(solution)/shard_map/grads_a/pallas_call | solution.py:47
  120.5 2.2 %copy-done = f32[768,1536]{1,0:T(8,128)} copy-done((f32[768,1536]{1,0:T(8,128)}, f32[768,1536]{1,0:T(8,128)S(1)}, u32[]{:S(2)}) %copy-start) | copy-done | bytes 4718616
  122.6 6.9 %collective-permute-done.28.below.refs_8_.refs_11_ = bf16[2,128,1536]{2,1,0:T(8,128)(2,1)S(1)} collective-permute-done((bf16[2,128,1536]{2,1,0:T(8,128)(2,1)S(1)}, bf16[2,128,1536]{2,1,0:T(8,128)(2,1)S(1)}, u32[]{:S(2)}, u32[]{:S(2)}) %collective-permute-start.28) | collective-permute-done | bytes 786464 | tf_op jit(solution)/shard_map/ppermute | solution.py:26
  129.6 3.3 %collective-permute-start.32 = (bf16[128,1536]{1,0:T(8,128)(2,1)S(1)}, bf16[128,1536]{1,0:T(8,128)(2,1)S(1)}, u32[]{:S(2)}, u32[]{:S(2)}) collective-permute-start(bf16[128,1536]{1,0:T(8,128)(2,1)S(1)} %get-tuple-element.164), channel_id=1, source_target_pairs={{0,6},{2,0},{4,2},{6,4},{1,7},{3,1},{5,3},{7,5},{8,14},{10,8},{12,... | collective-permute-start | bytes 1179656 | tf_op jit(solution)/shard_map/ppermute | solution.py:26
  132.9 2.2 %input_three.3 = (f32[3,128,384]{2,1,0:T(8,128)S(1)}, f32[3,128,384]{2,1,0:T(8,128)S(1)}) custom-call(bf16[2,128,1536]{2,1,0:T(8,128)(2,1)S(1)} %hidden.3.mine.refs_6_.refs_9_, bf16[2,128,1536]{2,1,0:T(8,128)(2,1)S(1)} %collective-permute-done.27.above.refs_7_.refs_10_, bf16[2,128,1536]{2,1,0:T(8,128)(2,1)S(1)} %collective-permute-done.28.below.refs_8_.refs_11_, ...), custom_call_target="tpu_custom_call" | custom-call | flops 115000000 | bytes 369000 | tf_op jit(solution)/shard_map/input_three/pallas_call | solution.py:47
  135.2 4.1 %grads_b.1 = (f32[768,1536]{1,0:T(8,128)S(1)}, f32[1536,768]{1,0:T(8,128)S(1)}) custom-call(bf16[512,768]{1,0:T(8,128)(2,1)S(1)} %get-tuple-element.153.refs_0_.refs_1_.refs_2_, bf16[512,768]{1,0:T(8,128)(2,1)S(1)} %get-tuple-element.153.refs_0_.refs_1_.refs_2_, bf16[512,768]{1,0:T(8,128)(2,1)S(1)} %get-tuple-element.153.refs_0_.refs_1_.refs_2_, ...), custom_call_target="tpu_custom_call" | custom-call | flops 115000000 | bytes 369000 | tf_op jit(solution)/shard_map/grads_b/pallas_call | solution.py:47
  139.3 0.9 input_last.2
  140.9 0.9 collective-permute-done.29.refs_0_
  142.7 1.4 collective-permute-done.33.grad.refs_8_
  144.1 0.9 input_last.3
  145.1 0.5 collective-permute-start.35
  145.6 1.2 collective-permute-start.36
  146.8 2.0 %collective-permute-start.37 = (bf16[4,32,384]{2,1,0:T(8,128)(2,1)S(1)}, bf16[4,32,384]{2,1,0:T(8,128)(2,1)S(1)}, u32[]{:S(2)}, u32[]{:S(2)}) collective-permute-start(bf16[4,32,384]{2,1,0:T(8,128)(2,1)S(1)} %get-tuple-element.185), channel_id=1, source_target_pairs={{0,96},{32,0},{64,32},{96,64},{1,97},{33,1},{65,33},{97,65},{2,98}... | collective-permute-start | bytes 294920 | tf_op jit(solution)/shard_map/ppermute | solution.py:26
  148.8 3.5 %grads_last.1 = (bf16[384,3072]{1,0:T(8,128)(2,1)}, bf16[3072,384]{1,0:T(8,128)(2,1)}, bf16[384,1536]{1,0:T(8,128)(2,1)S(1)}, bf16[1536,384]{1,0:T(8,128)(2,1)}) custom-call(s32[1]{0:T(128)} %bitcast.1.core._.refs_0_, bf16[512,768]{1,0:T(8,128)(2,1)S(1)} %get-tuple-element.155.refs_0_.refs_1_.refs_2_, ...), custom_call_target="tpu_custom_call" | custom-call | flops 115000000 | bytes 369000 | tf_op jit(solution)/shard_map/grads_last/pallas_call | solution.py:47
  152.3 1.4 collective-permute-done.35
  153.7 0.6 collective-permute-done.37
  155.0 2.7 %collective-permute-start.38 = (bf16[4,32,384]{2,1,0:T(8,128)(2,1)S(1)}, bf16[4,32,384]{2,1,0:T(8,128)(2,1)S(1)}, u32[]{:S(2)}, u32[]{:S(2)}) collective-permute-start(bf16[4,32,384]{2,1,0:T(8,128)(2,1)S(1)} %get-tuple-element.199), channel_id=1, source_target_pairs={{0,16},{16,0},{32,48},{48,32},{64,80},{80,64},{96,112},{112,96},{1... | collective-permute-start | bytes 294920 | tf_op jit(solution)/shard_map/ppermute | solution.py:498
  157.7 0.6 collective-permute-start.39
  158.3 5.7 %collective-permute-start.40 = (bf16[4,32,384]{2,1,0:T(8,128)(2,1)S(1)}, bf16[4,32,384]{2,1,0:T(8,128)(2,1)S(1)}, u32[]{:S(2)}, u32[]{:S(2)}) collective-permute-start(bf16[4,32,384]{2,1,0:T(8,128)(2,1)S(1)} %get-tuple-element.201), channel_id=1, source_target_pairs={{0,80},{16,64},{32,112},{48,96},{64,16},{80,0},{96,48},{112,32},{1... | collective-permute-start | bytes 294920 | tf_op jit(solution)/shard_map/ppermute | solution.py:498
  164.0 2.0 %place.1 = (bf16[384,3072]{1,0:T(8,128)(2,1)}, bf16[3072,384]{1,0:T(8,128)(2,1)}) custom-call(s32[1]{0:T(128)} %bitcast.1.core._.refs_0_, bf16[384,3072]{1,0:T(8,128)(2,1)} %get-tuple-element.203.wi, bf16[3072,384]{1,0:T(8,128)(2,1)} %get-tuple-element.204.wo, ...), custom_call_target="tpu_custom_call", output_to_operand_aliasing={{0}: (1, {}), {1}: (2, {})} | custom-call | flops 115000000 | bytes 369000 | tf_op jit(solution)/shard_map/place/pallas_call | solution.py:47
  166.0 1.0 collective-permute-done.39
  167.0 1.6 collective-permute-done.40
  168.6 2.5 %collective-permute-done.41 = bf16[4,32,384]{2,1,0:T(8,128)(2,1)} collective-permute-done((bf16[4,32,384]{2,1,0:T(8,128)(2,1)S(1)}, bf16[4,32,384]{2,1,0:T(8,128)(2,1)}, u32[]{:S(2)}, u32[]{:S(2)}) %collective-permute-start.41) | collective-permute-done | bytes 98336 | tf_op jit(solution)/shard_map/ppermute | solution.py:498
  171.1 1.0 convert_add_fusion
  172.1 0.7 fusion.1
  (63 shorter events, 4.9 us)
Async XLA Ops:
  1.7 12.9 %collective-permute-start.2 = (bf16[4,32,768]{2,1,0:T(8,128)(2,1)S(1)}, bf16[4,32,768]{2,1,0:T(8,128)(2,1)S(1)}, u32[]{:S(2)}, u32[]{:S(2)}) collective-permute-start(bf16[4,32,768]{2,1,0:T(8,128)(2,1)S(1)} %fusion.2.refs_0_), channel_id=1, source_target_pairs={{0,32},{32,64},{64,96},{96,0},{1,33},{33,65},{65,97},{97,1},{2,34}... | collective-permute-start | bytes 589832 | tf_op jit(solution)/shard_map/ppermute | solution.py:26
  3.4 11.7 %collective-permute-start.1 = (bf16[4,32,768]{2,1,0:T(8,128)(2,1)S(1)}, bf16[4,32,768]{2,1,0:T(8,128)(2,1)S(1)}, u32[]{:S(2)}, u32[]{:S(2)}) collective-permute-start(bf16[4,32,768]{2,1,0:T(8,128)(2,1)S(1)} %fusion.2.refs_0_), channel_id=1, source_target_pairs={{0,64},{32,96},{64,0},{96,32},{1,65},{33,97},{65,1},{97,33},{2,66}... | collective-permute-start | bytes 589832 | tf_op jit(solution)/shard_map/ppermute | solution.py:26
  6.3 8.8 %collective-permute-start = (bf16[4,32,768]{2,1,0:T(8,128)(2,1)S(1)}, bf16[4,32,768]{2,1,0:T(8,128)(2,1)S(1)}, u32[]{:S(2)}, u32[]{:S(2)}) collective-permute-start(bf16[4,32,768]{2,1,0:T(8,128)(2,1)S(1)} %fusion.2.refs_0_), channel_id=1, source_target_pairs={{0,96},{32,0},{64,32},{96,64},{1,97},{33,1},{65,33},{97,65},{2,98}... | collective-permute-start | bytes 589832 | tf_op jit(solution)/shard_map/ppermute | solution.py:26
  7.7 7.5 %collective-permute-start.5 = (bf16[4,32,768]{2,1,0:T(8,128)(2,1)S(1)}, bf16[4,32,768]{2,1,0:T(8,128)(2,1)S(1)}, u32[]{:S(2)}, u32[]{:S(2)}) collective-permute-start(bf16[4,32,768]{2,1,0:T(8,128)(2,1)S(1)} %fusion.2.refs_0_), channel_id=1, source_target_pairs={{0,16},{16,0},{1,17},{17,1},{2,18},{18,2},{3,19},{19,3},{4,20},{20... | collective-permute-start | bytes 589832 | tf_op jit(solution)/shard_map/ppermute | solution.py:26
  10.7 1.7 copy-start.2
  12.4 1.7 copy-start.4
  14.5 6.5 %copy-start.3 = (bf16[384,3072]{1,0:T(8,128)(2,1)S(1)}, bf16[384,3072]{1,0:T(8,128)(2,1)}, u32[]{:S(2)}) copy-start(bf16[384,3072]{1,0:T(8,128)(2,1)} %wi.2) | copy-start | bytes 7077892
  14.6 6.5 %collective-permute-start.4 = (bf16[2,4,384,384]{3,2,1,0:T(8,128)(2,1)S(1)}, bf16[2,4,384,384]{3,2,1,0:T(8,128)(2,1)S(1)}, u32[]{:S(2)}, u32[]{:S(2)}) collective-permute-start(bf16[2,4,384,384]{3,2,1,0:T(8,128)(2,1)S(1)} %pack.1), channel_id=1, source_target_pairs={{0,1},{1,0},{2,3},{3,2},{4,5},{5,4},{6,7},{7,6},{8,9},{9,8},{10,11... | collective-permute-start | bytes 7077896 | tf_op jit(solution)/shard_map/ppermute | solution.py:26
  15.2 4.2 %collective-permute-start.6 = (bf16[4,32,768]{2,1,0:T(8,128)(2,1)S(1)}, bf16[4,32,768]{2,1,0:T(8,128)(2,1)S(1)}, u32[]{:S(2)}, u32[]{:S(2)}) collective-permute-start(bf16[4,32,768]{2,1,0:T(8,128)(2,1)S(1)} %collective-permute-done.5.refs_0_), channel_id=1, source_target_pairs={{0,1},{1,0},{2,3},{3,2},{4,5},{5,4},{6,7},{7,6},{8,9},{9,8},{10,11... | collective-permute-start | bytes 589832 | tf_op jit(solution)/shard_map/ppermute | solution.py:26
  15.3 6.8 %collective-permute-start.3 = (bf16[512,768]{1,0:T(8,128)(2,1)S(1)}, bf16[512,768]{1,0:T(8,128)(2,1)S(1)}, u32[]{:S(2)}, u32[]{:S(2)}) collective-permute-start(bf16[512,768]{1,0:T(8,128)(2,1)S(1)} %join_a.1.own), channel_id=1, source_target_pairs={{0,1},{1,0},{2,3},{3,2},{4,5},{5,4},{6,7},{7,6},{8,9},{9,8},{10,11... | collective-permute-start | bytes 2359304 | tf_op jit(solution)/shard_map/ppermute | solution.py:26
  15.8 16.7 %collective-permute-start.11 = (bf16[4,32,768]{2,1,0:T(8,128)(2,1)S(1)}, bf16[4,32,768]{2,1,0:T(8,128)(2,1)S(1)}, u32[]{:S(2)}, u32[]{:S(2)}) collective-permute-start(bf16[4,32,768]{2,1,0:T(8,128)(2,1)S(1)} %collective-permute-done.5.refs_0_), channel_id=1, source_target_pairs={{0,32},{32,64},{64,96},{96,0},{1,33},{33,65},{65,97},{97,1},{2,34}... | collective-permute-start | bytes 589832 | tf_op jit(solution)/shard_map/ppermute | solution.py:26
  17.1 15.4 %collective-permute-start.10 = (bf16[4,32,768]{2,1,0:T(8,128)(2,1)S(1)}, bf16[4,32,768]{2,1,0:T(8,128)(2,1)S(1)}, u32[]{:S(2)}, u32[]{:S(2)}) collective-permute-start(bf16[4,32,768]{2,1,0:T(8,128)(2,1)S(1)} %collective-permute-done.5.refs_0_), channel_id=1, source_target_pairs={{0,64},{32,96},{64,0},{96,32},{1,65},{33,97},{65,1},{97,33},{2,66}... | collective-permute-start | bytes 589832 | tf_op jit(solution)/shard_map/ppermute | solution.py:26
  19.5 13.0 %collective-permute-start.9 = (bf16[4,32,768]{2,1,0:T(8,128)(2,1)S(1)}, bf16[4,32,768]{2,1,0:T(8,128)(2,1)S(1)}, u32[]{:S(2)}, u32[]{:S(2)}) collective-permute-start(bf16[4,32,768]{2,1,0:T(8,128)(2,1)S(1)} %collective-permute-done.5.refs_0_), channel_id=1, source_target_pairs={{0,96},{32,0},{64,32},{96,64},{1,97},{33,1},{65,33},{97,65},{2,98}... | collective-permute-start | bytes 589832 | tf_op jit(solution)/shard_map/ppermute | solution.py:26
  24.0 17.7 %collective-permute-start.8 = (bf16[128,1536]{1,0:T(8,128)(2,1)S(1)}, bf16[128,1536]{1,0:T(8,128)(2,1)S(1)}, u32[]{:S(2)}, u32[]{:S(2)}) collective-permute-start(bf16[128,1536]{1,0:T(8,128)(2,1)S(1)} %get-tuple-element.118), channel_id=1, source_target_pairs={{0,6},{2,0},{4,2},{6,4},{1,7},{3,1},{5,3},{7,5},{8,14},{10,8},{12,... | collective-permute-start | bytes 1179656 | tf_op jit(solution)/shard_map/ppermute | solution.py:26
  28.1 13.6 %collective-permute-start.7 = (bf16[128,1536]{1,0:T(8,128)(2,1)S(1)}, bf16[128,1536]{1,0:T(8,128)(2,1)S(1)}, u32[]{:S(2)}, u32[]{:S(2)}) collective-permute-start(bf16[128,1536]{1,0:T(8,128)(2,1)S(1)} %get-tuple-element.114), channel_id=1, source_target_pairs={{0,2},{2,4},{4,6},{6,0},{1,3},{3,5},{5,7},{7,1},{8,10},{10,12},{12... | collective-permute-start | bytes 1179656 | tf_op jit(solution)/shard_map/ppermute | solution.py:26
  32.5 1.5 collective-permute-start.12
  32.6 1.7 collective-permute-start.13
  33.1 1.5 collective-permute-start.14
  38.4 12.8 %collective-permute-start.18 = (bf16[128,1536]{1,0:T(8,128)(2,1)S(1)}, bf16[128,1536]{1,0:T(8,128)(2,1)S(1)}, u32[]{:S(2)}, u32[]{:S(2)}) collective-permute-start(bf16[128,1536]{1,0:T(8,128)(2,1)S(1)} %get-tuple-element.130), channel_id=1, source_target_pairs={{0,6},{2,0},{4,2},{6,4},{1,7},{3,1},{5,3},{7,5},{8,14},{10,8},{12,... | collective-permute-start | bytes 1179656 | tf_op jit(solution)/shard_map/ppermute | solution.py:26
  41.7 13.2 %collective-permute-start.17 = (bf16[128,1536]{1,0:T(8,128)(2,1)S(1)}, bf16[128,1536]{1,0:T(8,128)(2,1)S(1)}, u32[]{:S(2)}, u32[]{:S(2)}) collective-permute-start(bf16[128,1536]{1,0:T(8,128)(2,1)S(1)} %get-tuple-element.124), channel_id=1, source_target_pairs={{0,2},{2,4},{4,6},{6,0},{1,3},{3,5},{5,7},{7,1},{8,10},{10,12},{12... | collective-permute-start | bytes 1179656 | tf_op jit(solution)/shard_map/ppermute | solution.py:26
  42.4 29.4 %collective-permute-start.15 = (bf16[2,128,1536]{2,1,0:T(8,128)(2,1)S(1)}, bf16[2,128,1536]{2,1,0:T(8,128)(2,1)S(1)}, u32[]{:S(2)}, u32[]{:S(2)}) collective-permute-start(bf16[2,128,1536]{2,1,0:T(8,128)(2,1)S(1)} %get-tuple-element.127), channel_id=1, source_target_pairs={{0,2},{2,4},{4,6},{6,0},{1,3},{3,5},{5,7},{7,1},{8,10},{10,12},{12... | collective-permute-start | bytes 2359304 | tf_op jit(solution)/shard_map/ppermute | solution.py:26
  42.5 29.3 %collective-permute-start.16 = (bf16[2,128,1536]{2,1,0:T(8,128)(2,1)S(1)}, bf16[2,128,1536]{2,1,0:T(8,128)(2,1)S(1)}, u32[]{:S(2)}, u32[]{:S(2)}) collective-permute-start(bf16[2,128,1536]{2,1,0:T(8,128)(2,1)S(1)} %get-tuple-element.128), channel_id=1, source_target_pairs={{0,6},{2,0},{4,2},{6,4},{1,7},{3,1},{5,3},{7,5},{8,14},{10,8},{12,... | collective-permute-start | bytes 2359304 | tf_op jit(solution)/shard_map/ppermute | solution.py:26
  55.6 32.0 %collective-permute-start.20 = (bf16[2,128,1536]{2,1,0:T(8,128)(2,1)S(1)}, bf16[2,128,1536]{2,1,0:T(8,128)(2,1)S(1)}, u32[]{:S(2)}, u32[]{:S(2)}) collective-permute-start(bf16[2,128,1536]{2,1,0:T(8,128)(2,1)S(1)} %get-tuple-element.133), channel_id=1, source_target_pairs={{0,2},{2,4},{4,6},{6,0},{1,3},{3,5},{5,7},{7,1},{8,10},{10,12},{12... | collective-permute-start | bytes 2359304 | tf_op jit(solution)/shard_map/ppermute | solution.py:26
  55.7 32.0 %collective-permute-start.21 = (bf16[2,128,1536]{2,1,0:T(8,128)(2,1)S(1)}, bf16[2,128,1536]{2,1,0:T(8,128)(2,1)S(1)}, u32[]{:S(2)}, u32[]{:S(2)}) collective-permute-start(bf16[2,128,1536]{2,1,0:T(8,128)(2,1)S(1)} %get-tuple-element.134), channel_id=1, source_target_pairs={{0,6},{2,0},{4,2},{6,4},{1,7},{3,1},{5,3},{7,5},{8,14},{10,8},{12,... | collective-permute-start | bytes 2359304 | tf_op jit(solution)/shard_map/ppermute | solution.py:26
  72.5 17.6 %collective-permute-start.19 = (bf16[2,128,1536]{2,1,0:T(8,128)(2,1)S(1)}, bf16[2,128,1536]{2,1,0:T(8,128)(2,1)S(1)}, u32[]{:S(2)}, u32[]{:S(2)}) collective-permute-start(bf16[2,128,1536]{2,1,0:T(8,128)(2,1)S(1)} %get-tuple-element.138), channel_id=1, source_target_pairs={{0,8},{8,0},{1,9},{9,1},{2,10},{10,2},{3,11},{11,3},{4,12},{12,4},... | collective-permute-start | bytes 2359304 | tf_op jit(solution)/shard_map/ppermute | solution.py:26
  88.3 18.6 %collective-permute-start.24 = (bf16[2,128,1536]{2,1,0:T(8,128)(2,1)S(1)}, bf16[2,128,1536]{2,1,0:T(8,128)(2,1)S(1)}, u32[]{:S(2)}, u32[]{:S(2)}) collective-permute-start(bf16[2,128,1536]{2,1,0:T(8,128)(2,1)S(1)} %get-tuple-element.141), channel_id=1, source_target_pairs={{0,8},{8,0},{1,9},{9,1},{2,10},{10,2},{3,11},{11,3},{4,12},{12,4},... | collective-permute-start | bytes 2359304 | tf_op jit(solution)/shard_map/ppermute | solution.py:26
  90.9 20.2 %collective-permute-start.23 = (bf16[2,128,1536]{2,1,0:T(8,128)(2,1)S(1)}, bf16[2,128,1536]{2,1,0:T(8,128)(2,1)S(1)}, u32[]{:S(2)}, u32[]{:S(2)}) collective-permute-start(bf16[2,128,1536]{2,1,0:T(8,128)(2,1)S(1)} %hidden.2.mine.refs_6_.refs_9_), channel_id=1, source_target_pairs={{0,2},{2,4},{4,6},{6,0},{1,3},{3,5},{5,7},{7,1},{8,10},{10,12},{12... | collective-permute-start | bytes 2359304 | tf_op jit(solution)/shard_map/ppermute | solution.py:26
  91.1 19.9 %collective-permute-start.22 = (bf16[2,128,1536]{2,1,0:T(8,128)(2,1)S(1)}, bf16[2,128,1536]{2,1,0:T(8,128)(2,1)S(1)}, u32[]{:S(2)}, u32[]{:S(2)}) collective-permute-start(bf16[2,128,1536]{2,1,0:T(8,128)(2,1)S(1)} %hidden.2.mine.refs_6_.refs_9_), channel_id=1, source_target_pairs={{0,6},{2,0},{4,2},{6,4},{1,7},{3,1},{5,3},{7,5},{8,14},{10,8},{12,... | collective-permute-start | bytes 2359304 | tf_op jit(solution)/shard_map/ppermute | solution.py:26
  107.7 21.8 %collective-permute-start.28 = (bf16[2,128,1536]{2,1,0:T(8,128)(2,1)S(1)}, bf16[2,128,1536]{2,1,0:T(8,128)(2,1)S(1)}, u32[]{:S(2)}, u32[]{:S(2)}) collective-permute-start(bf16[2,128,1536]{2,1,0:T(8,128)(2,1)S(1)} %hidden.3.mine.refs_6_.refs_9_), channel_id=1, source_target_pairs={{0,2},{2,4},{4,6},{6,0},{1,3},{3,5},{5,7},{7,1},{8,10},{10,12},{12... | collective-permute-start | bytes 2359304 | tf_op jit(solution)/shard_map/ppermute | solution.py:26
  107.8 21.7 %collective-permute-start.27 = (bf16[2,128,1536]{2,1,0:T(8,128)(2,1)S(1)}, bf16[2,128,1536]{2,1,0:T(8,128)(2,1)S(1)}, u32[]{:S(2)}, u32[]{:S(2)}) collective-permute-start(bf16[2,128,1536]{2,1,0:T(8,128)(2,1)S(1)} %hidden.3.mine.refs_6_.refs_9_), channel_id=1, source_target_pairs={{0,6},{2,0},{4,2},{6,4},{1,7},{3,1},{5,3},{7,5},{8,14},{10,8},{12,... | collective-permute-start | bytes 2359304 | tf_op jit(solution)/shard_map/ppermute | solution.py:26
  111.1 28.2 %collective-permute-start.26 = (bf16[128,1536]{1,0:T(8,128)(2,1)S(1)}, bf16[128,1536]{1,0:T(8,128)(2,1)S(1)}, u32[]{:S(2)}, u32[]{:S(2)}) collective-permute-start(bf16[128,1536]{1,0:T(8,128)(2,1)S(1)} %get-tuple-element.152), channel_id=1, source_target_pairs={{0,2},{2,4},{4,6},{6,0},{1,3},{3,5},{5,7},{7,1},{8,10},{10,12},{12... | collective-permute-start | bytes 1179656 | tf_op jit(solution)/shard_map/ppermute | solution.py:26
  111.2 28.1 %collective-permute-start.25 = (bf16[128,1536]{1,0:T(8,128)(2,1)S(1)}, bf16[128,1536]{1,0:T(8,128)(2,1)S(1)}, u32[]{:S(2)}, u32[]{:S(2)}) collective-permute-start(bf16[128,1536]{1,0:T(8,128)(2,1)S(1)} %get-tuple-element.147), channel_id=1, source_target_pairs={{0,6},{2,0},{4,2},{6,4},{1,7},{3,1},{5,3},{7,5},{8,14},{10,8},{12,... | collective-permute-start | bytes 1179656 | tf_op jit(solution)/shard_map/ppermute | solution.py:26
  120.4 2.2 %copy-start = (f32[768,1536]{1,0:T(8,128)}, f32[768,1536]{1,0:T(8,128)S(1)}, u32[]{:S(2)}) copy-start(f32[768,1536]{1,0:T(8,128)S(1)} %get-tuple-element.160.refs_12_) | copy-start | bytes 14155780
  129.5 14.6 %collective-permute-start.33 = (bf16[128,1536]{1,0:T(8,128)(2,1)S(1)}, bf16[128,1536]{1,0:T(8,128)(2,1)S(1)}, u32[]{:S(2)}, u32[]{:S(2)}) collective-permute-start(bf16[128,1536]{1,0:T(8,128)(2,1)S(1)} %get-tuple-element.180), channel_id=1, source_target_pairs={{0,2},{2,4},{4,6},{6,0},{1,3},{3,5},{5,7},{7,1},{8,10},{10,12},{12... | collective-permute-start | bytes 1179656 | tf_op jit(solution)/shard_map/ppermute | solution.py:26
  129.6 5.5 %copy-start.1 = (f32[768,1536]{1,0:T(8,128)S(1)}, f32[768,1536]{1,0:T(8,128)}, u32[]{:S(2)}) copy-start(f32[768,1536]{1,0:T(8,128)} %copy-done) | copy-start | bytes 14155780
  129.6 14.5 %collective-permute-start.32 = (bf16[128,1536]{1,0:T(8,128)(2,1)S(1)}, bf16[128,1536]{1,0:T(8,128)(2,1)S(1)}, u32[]{:S(2)}, u32[]{:S(2)}) collective-permute-start(bf16[128,1536]{1,0:T(8,128)(2,1)S(1)} %get-tuple-element.164), channel_id=1, source_target_pairs={{0,6},{2,0},{4,2},{6,4},{1,7},{3,1},{5,3},{7,5},{8,14},{10,8},{12,... | collective-permute-start | bytes 1179656 | tf_op jit(solution)/shard_map/ppermute | solution.py:26
  140.2 1.6 collective-permute-start.29
  140.3 1.9 %collective-permute-start.30 = (f32[512,128]{1,0:T(8,128)S(1)}, f32[512,128]{1,0:T(8,128)S(1)}, u32[]{:S(2)}, u32[]{:S(2)}) collective-permute-start(f32[512,128]{1,0:T(8,128)S(1)} %get-tuple-element.177), channel_id=1, source_target_pairs={{0,1},{1,0},{2,3},{3,2},{4,5},{5,4},{6,7},{7,6},{8,9},{9,8},{10,11... | collective-permute-start | bytes 786440 | tf_op jit(solution)/shard_map/ppermute | solution.py:26
  140.8 1.8 %collective-permute-start.31 = (f32[512,128]{1,0:T(8,128)S(1)}, f32[512,128]{1,0:T(8,128)S(1)}, u32[]{:S(2)}, u32[]{:S(2)}) collective-permute-start(f32[512,128]{1,0:T(8,128)S(1)} %get-tuple-element.178), channel_id=1, source_target_pairs={{0,1},{1,0},{2,3},{3,2},{4,5},{5,4},{6,7},{7,6},{8,9},{9,8},{10,11... | collective-permute-start | bytes 786440 | tf_op jit(solution)/shard_map/ppermute | solution.py:26
  145.0 9.3 %collective-permute-start.34 = (f32[512,384]{1,0:T(8,128)S(1)}, f32[512,384]{1,0:T(8,128)S(1)}, u32[]{:S(2)}, u32[]{:S(2)}) collective-permute-start(f32[512,384]{1,0:T(8,128)S(1)} %get-tuple-element.182), channel_id=1, source_target_pairs={{0,1},{1,0},{2,3},{3,2},{4,5},{5,4},{6,7},{7,6},{8,9},{9,8},{10,11... | collective-permute-start | bytes 2359304 | tf_op jit(solution)/shard_map/ppermute | solution.py:26
  145.1 8.5 %collective-permute-start.35 = (bf16[4,32,384]{2,1,0:T(8,128)(2,1)S(1)}, bf16[4,32,384]{2,1,0:T(8,128)(2,1)S(1)}, u32[]{:S(2)}, u32[]{:S(2)}) collective-permute-start(bf16[4,32,384]{2,1,0:T(8,128)(2,1)S(1)} %get-tuple-element.183), channel_id=1, source_target_pairs={{0,32},{32,64},{64,96},{96,0},{1,33},{33,65},{65,97},{97,1},{2,34}... | collective-permute-start | bytes 294920 | tf_op jit(solution)/shard_map/ppermute | solution.py:26
  145.6 8.0 %collective-permute-start.36 = (bf16[4,32,384]{2,1,0:T(8,128)(2,1)S(1)}, bf16[4,32,384]{2,1,0:T(8,128)(2,1)S(1)}, u32[]{:S(2)}, u32[]{:S(2)}) collective-permute-start(bf16[4,32,384]{2,1,0:T(8,128)(2,1)S(1)} %get-tuple-element.184), channel_id=1, source_target_pairs={{0,64},{32,96},{64,0},{96,32},{1,65},{33,97},{65,1},{97,33},{2,66}... | collective-permute-start | bytes 294920 | tf_op jit(solution)/shard_map/ppermute | solution.py:26
  146.8 7.5 %collective-permute-start.37 = (bf16[4,32,384]{2,1,0:T(8,128)(2,1)S(1)}, bf16[4,32,384]{2,1,0:T(8,128)(2,1)S(1)}, u32[]{:S(2)}, u32[]{:S(2)}) collective-permute-start(bf16[4,32,384]{2,1,0:T(8,128)(2,1)S(1)} %get-tuple-element.185), channel_id=1, source_target_pairs={{0,96},{32,0},{64,32},{96,64},{1,97},{33,1},{65,33},{97,65},{2,98}... | collective-permute-start | bytes 294920 | tf_op jit(solution)/shard_map/ppermute | solution.py:26
  154.4 9.6 %collective-permute-start.42 = (bf16[384,1536]{1,0:T(8,128)(2,1)S(1)}, bf16[384,1536]{1,0:T(8,128)(2,1)S(1)}, u32[]{:S(2)}, u32[]{:S(2)}) collective-permute-start(bf16[384,1536]{1,0:T(8,128)(2,1)S(1)} %get-tuple-element.205), channel_id=1, source_target_pairs={{0,1},{1,0},{2,3},{3,2},{4,5},{5,4},{6,7},{7,6},{8,9},{9,8},{10,11... | collective-permute-start | bytes 3538952 | tf_op jit(solution)/shard_map/ppermute | solution.py:26
  154.5 9.5 %collective-permute-start.43 = (bf16[1536,384]{1,0:T(8,128)(2,1)}, bf16[1536,384]{1,0:T(8,128)(2,1)S(1)}, u32[]{:S(2)}, u32[]{:S(2)}) collective-permute-start(bf16[1536,384]{1,0:T(8,128)(2,1)} %get-tuple-element.206), channel_id=1, source_target_pairs={{0,1},{1,0},{2,3},{3,2},{4,5},{5,4},{6,7},{7,6},{8,9},{9,8},{10,11... | collective-permute-start | bytes 3538952 | tf_op jit(solution)/shard_map/ppermute | solution.py:26
  155.0 11.0 %collective-permute-start.38 = (bf16[4,32,384]{2,1,0:T(8,128)(2,1)S(1)}, bf16[4,32,384]{2,1,0:T(8,128)(2,1)S(1)}, u32[]{:S(2)}, u32[]{:S(2)}) collective-permute-start(bf16[4,32,384]{2,1,0:T(8,128)(2,1)S(1)} %get-tuple-element.199), channel_id=1, source_target_pairs={{0,16},{16,0},{32,48},{48,32},{64,80},{80,64},{96,112},{112,96},{1... | collective-permute-start | bytes 294920 | tf_op jit(solution)/shard_map/ppermute | solution.py:498
  157.7 9.3 %collective-permute-start.39 = (bf16[4,32,384]{2,1,0:T(8,128)(2,1)S(1)}, bf16[4,32,384]{2,1,0:T(8,128)(2,1)S(1)}, u32[]{:S(2)}, u32[]{:S(2)}) collective-permute-start(bf16[4,32,384]{2,1,0:T(8,128)(2,1)S(1)} %get-tuple-element.200), channel_id=1, source_target_pairs={{0,48},{16,32},{32,80},{48,64},{64,112},{80,96},{96,16},{112,0},{1... | collective-permute-start | bytes 294920 | tf_op jit(solution)/shard_map/ppermute | solution.py:498
  158.3 10.3 %collective-permute-start.40 = (bf16[4,32,384]{2,1,0:T(8,128)(2,1)S(1)}, bf16[4,32,384]{2,1,0:T(8,128)(2,1)S(1)}, u32[]{:S(2)}, u32[]{:S(2)}) collective-permute-start(bf16[4,32,384]{2,1,0:T(8,128)(2,1)S(1)} %get-tuple-element.201), channel_id=1, source_target_pairs={{0,80},{16,64},{32,112},{48,96},{64,16},{80,0},{96,48},{112,32},{1... | collective-permute-start | bytes 294920 | tf_op jit(solution)/shard_map/ppermute | solution.py:498
  164.0 7.1 %collective-permute-start.41 = (bf16[4,32,384]{2,1,0:T(8,128)(2,1)S(1)}, bf16[4,32,384]{2,1,0:T(8,128)(2,1)}, u32[]{:S(2)}, u32[]{:S(2)}) collective-permute-start(bf16[4,32,384]{2,1,0:T(8,128)(2,1)S(1)} %get-tuple-element.202), channel_id=1, source_target_pairs={{0,112},{16,96},{32,16},{48,0},{64,48},{80,32},{96,80},{112,64},{1... | collective-permute-start | bytes 294920 | tf_op jit(solution)/shard_map/ppermute | solution.py:498

commit v8 on v7

--- a/solution.py
+++ b/solution.py
@@ -37,12 +37,15 @@
 COST = dict(pack=0.1, first_block=0.1, weights=7, join_a=100, join_b=0.1, products=0.1, ring_add=0.1, own_sum=0.1, hidden=0.1, pass_on=0.1, input_three=0.1, input_last=0.1, grads_a=0.1, grads_b=0.1, grads_last=0.1, return_a=0.1, return_b=20, place=0.1)
 
 
-def kernel(name, body, grid, ins, outs, scratch=(), scalar=None, aliases=None):
+def kernel(name, body, grid, ins, outs, scratch=(), scalar=None, aliases=None, vmem=24):
     def spec(block, index):
+        if block is None:
+            return pl.BlockSpec(memory_space=pltpu.HBM if index == "hbm" else pl.ANY)
+
         def at(i, *refs):
             return tuple(i if k == "i" else k(i, *(r[0] for r in refs)) if callable(k) else k for k in index)
 
-        return pl.BlockSpec(memory_space=pltpu.HBM) if block is None else pl.BlockSpec(block, at)
+        return pl.BlockSpec(block, at)
 
     return pl.pallas_call(
         body,
@@ -57,7 +60,7 @@
         out_shape=[jax.ShapeDtypeStruct(shape, dtype) for shape, dtype, _, _ in outs],
         input_output_aliases=aliases or {},
         cost_estimate=pl.CostEstimate(flops=int(COST[name] * 1.15e9), bytes_accessed=int(COST[name] * 3.69e6), transcendentals=0),
-        compiler_params=pltpu.CompilerParams(vmem_limit_bytes=24 * 2**20),
+        compiler_params=pltpu.CompilerParams(vmem_limit_bytes=vmem * 2**20),
     )(*([] if scalar is None else [scalar]), *[a for a, _, _ in ins])
 
 
@@ -81,34 +84,41 @@
         "pack",
         body,
         1,
-        [(w_in, None, None), (w_out, None, None)],
-        [(shape, BF16, shape, (0, 0, 0, 0))],
+        [(w_in, None, "hbm"), (w_out, None, "hbm")],
+        [(shape, BF16, None, None)],
         [pltpu.SemaphoreType.DMA((2, half))],
         scalar=core,
+        vmem=60,
     )[0]
 
 
 def weights(w_in, w_out, got, core):
     feat = w_in.shape[0]
     half = w_out.shape[0] // feat // 2
-
-    def body(_, wi, wo, got, wi_out, wo_out):
-        wi_out[:feat] = wi[...]
-        wi_out[feat:] = got[0, 0]
-        wo_out[:, :feat] = wo[...]
-        wo_out[:, feat:] = got[1, 0]
-
-    block = (feat, feat)
-    place = lambda i, c: c * half + i
+    hid = half * feat
+
+    def body(core, wi, wo, got, wi_out, wo_out, sems):
+        mine = pl.ds(pl.multiple_of(core[0] * hid, hid), hid)
+        copies = [
+            pltpu.make_async_copy(wi.at[:, mine], wi_out.at[pl.ds(0, feat), :], sems.at[0, half]),
+            pltpu.make_async_copy(wo.at[mine, :], wo_out.at[:, pl.ds(0, feat)], sems.at[1, half]),
+        ]
+        for k in range(half):
+            at, other = pl.ds(k * feat, feat), pl.ds(feat, feat)
+            copies.append(pltpu.make_async_copy(got.at[0, k], wi_out.at[other, at], sems.at[0, k]))
+            copies.append(pltpu.make_async_copy(got.at[1, k], wo_out.at[at, other], sems.at[1, k]))
+        for copy in copies:
+            copy.start()
+        for copy in copies:
+            copy.wait()
+
     return kernel(
         "weights",
         body,
-        half,
-        [(w_in, block, (0, place)), (w_out, block, (place, 0)), (got, (2, 1, feat, feat), (0, "i", 0, 0))],
-        [
-            ((2 * feat, half * feat), BF16, (2 * feat, feat), (0, "i")),
-            ((half * feat, 2 * feat), BF16, (feat, 2 * feat), ("i", 0)),
-        ],
+        1,
+        [(w_in, None, "hbm"), (w_out, None, "hbm"), (got, None, None)],
+        [((2 * feat, hid), BF16, None, None), ((hid, 2 * feat), BF16, None, None)],
+        [pltpu.SemaphoreType.DMA((2, half + 1))],
         scalar=core,
     )
 
@@ -173,9 +183,9 @@
 def products(own, other, wi, wo):
     rows, width = own.shape
     feat, hid = wi.shape
-    half, per, block = width // 2, rows // 4, hid // STEPS
-
-    def body(own, other, wi, wo, pg, up, down, tok, cot):
+    half, block = width // 2, hid // STEPS
+
+    def body(own, other, wi, wo, pg, tok, cot):
         @pl.when(pl.program_id(0) == 0)
         def _():
             for side, ref in enumerate((own, other)):
@@ -186,8 +196,6 @@
         g = dot(cot[...], wo[...], 1, 1)
         pg[0] = p
         pg[1] = g
-        up[...] = p[2 * per : 3 * per].astype(BF16)
-        down[...] = g[2 * per : 3 * per].astype(BF16)
 
     whole = (rows, width)
     return kernel(
@@ -197,8 +205,6 @@
         [(own, whole, (0, 0)), (other, whole, (0, 0)), (wi, (feat, block), (0, "i")), (wo, (block, feat), ("i", 0))],
         [
             ((2, rows, hid), F32, (2, rows, block), (0, 0, "i")),
-            ((per, hid), BF16, (per, block), (0, "i")),
-            ((per, hid), BF16, (per, block), (0, "i")),
             ((rows, feat), BF16, (rows, feat), (0, 0)),
             ((rows, feat), BF16, (rows, feat), (0, 0)),
         ],
@@ -444,17 +450,17 @@
 
     up_a, down_a = first_block(near, near_other, wi, wo)
     r_a = up_down(up_a, down_a)
-    near, near_other = gate((near, near_other), up_a)
-    pg_a, _, _, tok_a, cot_a = products(near, near_other, wi, wo)
-
-    far = gate(far, pg_a)
+    far = gate(far, up_a)
     far = join("join_b", [across, *far], [across_other, *to_core(far)])
-    pg_b, up_b, down_b, tok_b, cot_b = products(*far, wi, wo)
+    up_b, down_b = first_block(*far, wi, wo)
     r_b = up_down(up_b, down_b)
 
-    m_a = ring_add(pg_a, *gate(r_a, up_b))
+    near, near_other = gate((near, near_other), up_b)
+    pg_a, tok_a, cot_a = products(near, near_other, wi, wo)
+    m_a = ring_add(pg_a, *gate(r_a, pg_a))
     r_a = up_down(*m_a)
-    m_b = ring_add(pg_b, *gate(r_b, m_a))
+    pg_b, tok_b, cot_b = products(*gate(far, m_a), wi, wo)
+    m_b = ring_add(pg_b, *gate(r_b, pg_b))
     r_b = up_down(*m_b)
 
     t_a, m_a = own_sum(pg_a, *gate(r_a, m_b))

time: 173 us -> 235 us (1.36)
  Pallas kernels: 35.9 us -> 108 us
  starting transfers between devices: 60.2 us -> 56.1 us
  local copies, waits for them, and re-layouts: 5.5 us -> 2.18 us
  waiting for transfers between devices: 67.4 us -> 64.7 us
    pallas_call x25 -> x26, Pallas kernels: 35.9 us -> 108 us  [kernel(): pl.pallas_call(body, name=name, grid_spec=pltpu.PrefetchScalarGridSpec(nu...]
    ppermute x40, starting transfers between devices: 51.2 us -> 46.9 us  [shift(): return lax.ppermute(x, axis, [(i, (i + by) % n) for i in range(n)])]
    unnamed x10 -> x8, local copies, waits for them, and re-layouts: 5.5 us -> 2.18 us
  transfers between devices with their start and end apart: 44 -> 44, of which waited for: 20 -> 20; matrix products, arithmetic and copies ran while one was open for 0% -> 0% of each run, Pallas kernels for 20% -> 46%
where the time goes in v8:
time: 235 us
  Pallas kernels  108 us (46%)
  waiting for transfers between devices  64.7 us (28%)
  starting transfers between devices  56.1 us (24%)
  other arithmetic  2.75 us (1%)
    pallas_call x26, Pallas kernels, kernel(): pl.pallas_call(body, name=name, grid_spec=pltpu.PrefetchScalarGridSpec(nu...  108 us
    ppermute x40, waiting for transfers between devices, shift(): return lax.ppermute(x, axis, [(i, (i + by) % n) for i in range(n)])  60.8 us
    ppermute x40, starting transfers between devices, shift(): return lax.ppermute(x, axis, [(i, (i + by) % n) for i in range(n)])  46.9 us
    ppermute x4, starting transfers between devices, local(): lax.ppermute(a, ROWS, [(i, (i // 2 + d) % 4 * 2 + (i + 1) % 2) for i in r...  9.14 us
  transfers between devices with their start and end apart: 44, of which 20 were waited for; matrix products, arithmetic and copies ran while one was open for 0% of the time, Pallas kernels for 46%

profile of v8, /device:TPU:0, one launch (start us, length us, event | category | flops | bytes accessed | tf_op | source)
XLA Modules:
  0.0 235.2 jit_solution(12954355830682947041)
XLA Ops:
  0.7 1.0 pad_maximum_fusion
  1.7 1.7 collective-permute-start.2
  3.4 2.9 %collective-permute-start.1 = (bf16[4,32,768]{2,1,0:T(8,128)(2,1)S(1)}, bf16[4,32,768]{2,1,0:T(8,128)(2,1)S(1)}, u32[]{:S(2)}, u32[]{:S(2)}) collective-permute-start(bf16[4,32,768]{2,1,0:T(8,128)(2,1)S(1)} %fusion.2.refs_0_), channel_id=1, source_target_pairs={{0,64},{32,96},{64,0},{96,32},{1,65},{33,97},{65,1},{97,33},{2,66}... | collective-permute-start | bytes 589832 | tf_op jit(solution)/shard_map/ppermute | solution.py:26
  6.3 1.3 collective-permute-start
  7.7 3.0 %collective-permute-start.4 = (bf16[4,32,768]{2,1,0:T(8,128)(2,1)S(1)}, bf16[4,32,768]{2,1,0:T(8,128)(2,1)S(1)}, u32[]{:S(2)}, u32[]{:S(2)}) collective-permute-start(bf16[4,32,768]{2,1,0:T(8,128)(2,1)S(1)} %fusion.2.refs_0_), channel_id=1, source_target_pairs={{0,16},{16,0},{1,17},{17,1},{2,18},{18,2},{3,19},{19,3},{4,20},{20... | collective-permute-start | bytes 589832 | tf_op jit(solution)/shard_map/ppermute | solution.py:26
  10.7 72.6 %pack.1 = bf16[2,4,384,384]{3,2,1,0:T(8,128)(2,1)} custom-call(s32[1]{0:T(128)} %bitcast.1.core.refs_0_, bf16[384,3072]{1,0:T(8,128)(2,1)} %wi.2, bf16[3072,384]{1,0:T(8,128)(2,1)} %wo.2), custom_call_target="tpu_custom_call" | custom-call | flops 115000000 | bytes 369000 | tf_op jit(solution)/shard_map/pack/pallas_call | solution.py:50
  83.6 0.6 collective-permute-start.9
  84.2 0.7 collective-permute-start.7
  84.9 0.8 collective-permute-start.6
  85.7 2.2 collective-permute-done.9.refs_4_
  87.9 1.7 collective-permute-done.8.got
  89.6 0.6 weights.1
  90.2 1.8 first_block.2
  92.0 4.1 %collective-permute-start.14 = (bf16[128,1536]{1,0:T(8,128)(2,1)S(1)}, bf16[128,1536]{1,0:T(8,128)(2,1)S(1)}, u32[]{:S(2)}, u32[]{:S(2)}) collective-permute-start(bf16[128,1536]{1,0:T(8,128)(2,1)S(1)} %get-tuple-element.126), channel_id=1, source_target_pairs={{0,6},{2,0},{4,2},{6,4},{1,7},{3,1},{5,3},{7,5},{8,14},{10,8},{12,... | collective-permute-start | bytes 1179656 | tf_op jit(solution)/shard_map/ppermute | solution.py:26
  96.1 0.8 collective-permute-done.7.refs_3_
  96.9 0.6 collective-permute-done.5.refs_1_
  97.5 0.5 collective-permute-start.11
  98.0 0.9 collective-permute-done.10.refs_5_
  99.6 1.8 first_block.3
  101.5 4.1 %collective-permute-start.18 = (bf16[128,1536]{1,0:T(8,128)(2,1)S(1)}, bf16[128,1536]{1,0:T(8,128)(2,1)S(1)}, u32[]{:S(2)}, u32[]{:S(2)}) collective-permute-start(bf16[128,1536]{1,0:T(8,128)(2,1)S(1)} %get-tuple-element.134), channel_id=1, source_target_pairs={{0,6},{2,0},{4,2},{6,4},{1,7},{3,1},{5,3},{7,5},{8,14},{10,8},{12,... | collective-permute-start | bytes 1179656 | tf_op jit(solution)/shard_map/ppermute | solution.py:26
  105.6 3.7 %products.2 = (f32[2,512,1536]{2,1,0:T(8,128)S(1)}, bf16[512,768]{1,0:T(8,128)(2,1)S(1)}, bf16[512,768]{1,0:T(8,128)(2,1)S(1)}) custom-call(bf16[512,768]{1,0:T(8,128)(2,1)S(1)} %join_a.1.own, bf16[512,768]{1,0:T(8,128)(2,1)S(1)} %collective-permute-done.3.other, bf16[768,1536]{1,0:T(8,128)(2,1)S(1)} %get-tuple-element.114.wi, ...), custom_call_target="tpu_custom_call" | custom-call | flops 115000000 | bytes 369000 | tf_op jit(solution)/shard_map/products/pallas_call | solution.py:50
  109.3 0.7 ring_add.2
  110.0 3.3 %collective-permute-start.16 = (bf16[2,128,1536]{2,1,0:T(8,128)(2,1)S(1)}, bf16[2,128,1536]{2,1,0:T(8,128)(2,1)S(1)}, u32[]{:S(2)}, u32[]{:S(2)}) collective-permute-start(bf16[2,128,1536]{2,1,0:T(8,128)(2,1)S(1)} %get-tuple-element.130), channel_id=1, source_target_pairs={{0,6},{2,0},{4,2},{6,4},{1,7},{3,1},{5,3},{7,5},{8,14},{10,8},{12,... | collective-permute-start | bytes 2359304 | tf_op jit(solution)/shard_map/ppermute | solution.py:26
  113.3 3.7 %products.3 = (f32[2,512,1536]{2,1,0:T(8,128)S(1)}, bf16[512,768]{1,0:T(8,128)(2,1)S(1)}, bf16[512,768]{1,0:T(8,128)(2,1)S(1)}) custom-call(bf16[512,768]{1,0:T(8,128)(2,1)S(1)} %get-tuple-element.131.own, bf16[512,768]{1,0:T(8,128)(2,1)S(1)} %get-tuple-element.132.other, bf16[768,1536]{1,0:T(8,128)(2,1)S(1)} %get-tuple-element.114.wi, ...), custom_call_target="tpu_custom_call" | custom-call | flops 115000000 | bytes 369000 | tf_op jit(solution)/shard_map/products/pallas_call | solution.py:50
  117.0 1.8 collective-permute-done.17.up
  118.8 0.6 ring_add.3
  119.5 3.2 %collective-permute-start.21 = (bf16[2,128,1536]{2,1,0:T(8,128)(2,1)S(1)}, bf16[2,128,1536]{2,1,0:T(8,128)(2,1)S(1)}, u32[]{:S(2)}, u32[]{:S(2)}) collective-permute-start(bf16[2,128,1536]{2,1,0:T(8,128)(2,1)S(1)} %get-tuple-element.138), channel_id=1, source_target_pairs={{0,6},{2,0},{4,2},{6,4},{1,7},{3,1},{5,3},{7,5},{8,14},{10,8},{12,... | collective-permute-start | bytes 2359304 | tf_op jit(solution)/shard_map/ppermute | solution.py:26
  122.7 12.9 %collective-permute-done.15.up = bf16[2,128,1536]{2,1,0:T(8,128)(2,1)S(1)} collective-permute-done((bf16[2,128,1536]{2,1,0:T(8,128)(2,1)S(1)}, bf16[2,128,1536]{2,1,0:T(8,128)(2,1)S(1)}, u32[]{:S(2)}, u32[]{:S(2)}) %collective-permute-start.15) | collective-permute-done | bytes 786464 | tf_op jit(solution)/shard_map/ppermute | solution.py:26
  135.6 0.7 own_sum.2
  136.3 0.7 collective-permute-start.19
  137.0 14.4 %collective-permute-done.20.up = bf16[2,128,1536]{2,1,0:T(8,128)(2,1)S(1)} collective-permute-done((bf16[2,128,1536]{2,1,0:T(8,128)(2,1)S(1)}, bf16[2,128,1536]{2,1,0:T(8,128)(2,1)S(1)}, u32[]{:S(2)}, u32[]{:S(2)}) %collective-permute-start.20) | collective-permute-done | bytes 786464 | tf_op jit(solution)/shard_map/ppermute | solution.py:26
  151.5 0.7 own_sum.3
  152.2 0.8 collective-permute-start.24
  153.0 0.9 collective-permute-done.19.other
  153.9 0.7 hidden.2.mine.refs_6_.refs_9_
  154.8 3.2 %collective-permute-start.22 = (bf16[2,128,1536]{2,1,0:T(8,128)(2,1)S(1)}, bf16[2,128,1536]{2,1,0:T(8,128)(2,1)S(1)}, u32[]{:S(2)}, u32[]{:S(2)}) collective-permute-start(bf16[2,128,1536]{2,1,0:T(8,128)(2,1)S(1)} %hidden.2.mine.refs_6_.refs_9_), channel_id=1, source_target_pairs={{0,6},{2,0},{4,2},{6,4},{1,7},{3,1},{5,3},{7,5},{8,14},{10,8},{12,... | collective-permute-start | bytes 2359304 | tf_op jit(solution)/shard_map/ppermute | solution.py:26
  158.0 13.0 %collective-permute-done.24.other = bf16[2,128,1536]{2,1,0:T(8,128)(2,1)S(1)} collective-permute-done((bf16[2,128,1536]{2,1,0:T(8,128)(2,1)S(1)}, bf16[2,128,1536]{2,1,0:T(8,128)(2,1)S(1)}, u32[]{:S(2)}, u32[]{:S(2)}) %collective-permute-start.24) | collective-permute-done | bytes 786464 | tf_op jit(solution)/shard_map/ppermute | solution.py:26
  171.0 0.7 hidden.3.mine.refs_6_.refs_9_
  171.8 3.2 %collective-permute-start.27 = (bf16[2,128,1536]{2,1,0:T(8,128)(2,1)S(1)}, bf16[2,128,1536]{2,1,0:T(8,128)(2,1)S(1)}, u32[]{:S(2)}, u32[]{:S(2)}) collective-permute-start(bf16[2,128,1536]{2,1,0:T(8,128)(2,1)S(1)} %hidden.3.mine.refs_6_.refs_9_), channel_id=1, source_target_pairs={{0,6},{2,0},{4,2},{6,4},{1,7},{3,1},{5,3},{7,5},{8,14},{10,8},{12,... | collective-permute-start | bytes 2359304 | tf_op jit(solution)/shard_map/ppermute | solution.py:26
  175.2 3.2 %collective-permute-start.25 = (bf16[128,1536]{1,0:T(8,128)(2,1)S(1)}, bf16[128,1536]{1,0:T(8,128)(2,1)S(1)}, u32[]{:S(2)}, u32[]{:S(2)}) collective-permute-start(bf16[128,1536]{1,0:T(8,128)(2,1)S(1)} %get-tuple-element.151), channel_id=1, source_target_pairs={{0,6},{2,0},{4,2},{6,4},{1,7},{3,1},{5,3},{7,5},{8,14},{10,8},{12,... | collective-permute-start | bytes 1179656 | tf_op jit(solution)/shard_map/ppermute | solution.py:26
  178.4 2.2 input_three.2
  180.6 3.8 %grads_a.1 = (f32[768,1536]{1,0:T(8,128)S(1)}, f32[1536,768]{1,0:T(8,128)S(1)}) custom-call(bf16[512,768]{1,0:T(8,128)(2,1)S(1)} %get-tuple-element.159.refs_0_.refs_1_.refs_2_, bf16[512,768]{1,0:T(8,128)(2,1)S(1)} %get-tuple-element.159.refs_0_.refs_1_.refs_2_, bf16[512,768]{1,0:T(8,128)(2,1)S(1)} %get-tuple-element.159.refs_0_.refs_1_.refs_2_, ...), custom_call_target="tpu_custom_call" | custom-call | flops 115000000 | bytes 369000 | tf_op jit(solution)/shard_map/grads_a/pallas_call | solution.py:50
  184.5 2.2 copy-done
  186.6 6.8 %collective-permute-done.28.below.refs_8_.refs_11_ = bf16[2,128,1536]{2,1,0:T(8,128)(2,1)S(1)} collective-permute-done((bf16[2,128,1536]{2,1,0:T(8,128)(2,1)S(1)}, bf16[2,128,1536]{2,1,0:T(8,128)(2,1)S(1)}, u32[]{:S(2)}, u32[]{:S(2)}) %collective-permute-start.28) | collective-permute-done | bytes 786464 | tf_op jit(solution)/shard_map/ppermute | solution.py:26
  193.6 3.3 %collective-permute-start.32 = (bf16[128,1536]{1,0:T(8,128)(2,1)S(1)}, bf16[128,1536]{1,0:T(8,128)(2,1)S(1)}, u32[]{:S(2)}, u32[]{:S(2)}) collective-permute-start(bf16[128,1536]{1,0:T(8,128)(2,1)S(1)} %get-tuple-element.168), channel_id=1, source_target_pairs={{0,6},{2,0},{4,2},{6,4},{1,7},{3,1},{5,3},{7,5},{8,14},{10,8},{12,... | collective-permute-start | bytes 1179656 | tf_op jit(solution)/shard_map/ppermute | solution.py:26
  196.9 2.2 input_three.3
  199.2 4.1 %grads_b.1 = (f32[768,1536]{1,0:T(8,128)S(1)}, f32[1536,768]{1,0:T(8,128)S(1)}) custom-call(bf16[512,768]{1,0:T(8,128)(2,1)S(1)} %get-tuple-element.157.refs_0_.refs_1_.refs_2_, bf16[512,768]{1,0:T(8,128)(2,1)S(1)} %get-tuple-element.157.refs_0_.refs_1_.refs_2_, bf16[512,768]{1,0:T(8,128)(2,1)S(1)} %get-tuple-element.157.refs_0_.refs_1_.refs_2_, ...), custom_call_target="tpu_custom_call" | custom-call | flops 115000000 | bytes 369000 | tf_op jit(solution)/shard_map/grads_b/pallas_call | solution.py:50
  203.3 0.9 input_last.2
  204.4 0.5 collective-permute-start.30
  204.9 0.9 collective-permute-done.29.refs_0_
  206.7 0.8 collective-permute-done.33.grad.refs_8_
  207.5 0.9 input_last.3
  208.9 3.7 %collective-permute-start.36 = (bf16[4,32,384]{2,1,0:T(8,128)(2,1)S(1)}, bf16[4,32,384]{2,1,0:T(8,128)(2,1)S(1)}, u32[]{:S(2)}, u32[]{:S(2)}) collective-permute-start(bf16[4,32,384]{2,1,0:T(8,128)(2,1)S(1)} %get-tuple-element.188), channel_id=1, source_target_pairs={{0,64},{32,96},{64,0},{96,32},{1,65},{33,97},{65,1},{97,33},{2,66}... | collective-permute-start | bytes 294920 | tf_op jit(solution)/shard_map/ppermute | solution.py:26
  212.7 3.5 %grads_last.1 = (bf16[384,3072]{1,0:T(8,128)(2,1)}, bf16[3072,384]{1,0:T(8,128)(2,1)}, bf16[384,1536]{1,0:T(8,128)(2,1)S(1)}, bf16[1536,384]{1,0:T(8,128)(2,1)}) custom-call(s32[1]{0:T(128)} %bitcast.1.core.refs_0_, bf16[512,768]{1,0:T(8,128)(2,1)S(1)} %get-tuple-element.159.refs_0_.refs_1_.refs_2_, ...), custom_call_target="tpu_custom_call" | custom-call | flops 115000000 | bytes 369000 | tf_op jit(solution)/shard_map/grads_last/pallas_call | solution.py:50
  216.2 1.7 collective-permute-done.36
  218.6 1.6 collective-permute-start.38
  220.1 1.7 collective-permute-start.39
  221.9 4.5 %collective-permute-start.40 = (bf16[4,32,384]{2,1,0:T(8,128)(2,1)S(1)}, bf16[4,32,384]{2,1,0:T(8,128)(2,1)S(1)}, u32[]{:S(2)}, u32[]{:S(2)}) collective-permute-start(bf16[4,32,384]{2,1,0:T(8,128)(2,1)S(1)} %get-tuple-element.205), channel_id=1, source_target_pairs={{0,80},{16,64},{32,112},{48,96},{64,16},{80,0},{96,48},{112,32},{1... | collective-permute-start | bytes 294920 | tf_op jit(solution)/shard_map/ppermute | solution.py:504
  226.4 1.3 collective-permute-start.41
  227.7 2.0 place.1
  229.7 1.4 collective-permute-done.40
  231.1 2.4 %collective-permute-done.41 = bf16[4,32,384]{2,1,0:T(8,128)(2,1)} collective-permute-done((bf16[4,32,384]{2,1,0:T(8,128)(2,1)S(1)}, bf16[4,32,384]{2,1,0:T(8,128)(2,1)}, u32[]{:S(2)}, u32[]{:S(2)}) %collective-permute-start.41) | collective-permute-done | bytes 98336 | tf_op jit(solution)/shard_map/ppermute | solution.py:504
  233.5 1.0 convert_add_fusion
  234.5 0.7 fusion.1
  (62 shorter events, 3.8 us)
Async XLA Ops:
  1.7 81.8 %collective-permute-start.2 = (bf16[4,32,768]{2,1,0:T(8,128)(2,1)S(1)}, bf16[4,32,768]{2,1,0:T(8,128)(2,1)S(1)}, u32[]{:S(2)}, u32[]{:S(2)}) collective-permute-start(bf16[4,32,768]{2,1,0:T(8,128)(2,1)S(1)} %fusion.2.refs_0_), channel_id=1, source_target_pairs={{0,32},{32,64},{64,96},{96,0},{1,33},{33,65},{65,97},{97,1},{2,34}... | collective-permute-start | bytes 589832 | tf_op jit(solution)/shard_map/ppermute | solution.py:26
  3.4 80.1 %collective-permute-start.1 = (bf16[4,32,768]{2,1,0:T(8,128)(2,1)S(1)}, bf16[4,32,768]{2,1,0:T(8,128)(2,1)S(1)}, u32[]{:S(2)}, u32[]{:S(2)}) collective-permute-start(bf16[4,32,768]{2,1,0:T(8,128)(2,1)S(1)} %fusion.2.refs_0_), channel_id=1, source_target_pairs={{0,64},{32,96},{64,0},{96,32},{1,65},{33,97},{65,1},{97,33},{2,66}... | collective-permute-start | bytes 589832 | tf_op jit(solution)/shard_map/ppermute | solution.py:26
  6.3 77.2 %collective-permute-start = (bf16[4,32,768]{2,1,0:T(8,128)(2,1)S(1)}, bf16[4,32,768]{2,1,0:T(8,128)(2,1)S(1)}, u32[]{:S(2)}, u32[]{:S(2)}) collective-permute-start(bf16[4,32,768]{2,1,0:T(8,128)(2,1)S(1)} %fusion.2.refs_0_), channel_id=1, source_target_pairs={{0,96},{32,0},{64,32},{96,64},{1,97},{33,1},{65,33},{97,65},{2,98}... | collective-permute-start | bytes 589832 | tf_op jit(solution)/shard_map/ppermute | solution.py:26
  7.7 75.9 %collective-permute-start.4 = (bf16[4,32,768]{2,1,0:T(8,128)(2,1)S(1)}, bf16[4,32,768]{2,1,0:T(8,128)(2,1)S(1)}, u32[]{:S(2)}, u32[]{:S(2)}) collective-permute-start(bf16[4,32,768]{2,1,0:T(8,128)(2,1)S(1)} %fusion.2.refs_0_), channel_id=1, source_target_pairs={{0,16},{16,0},{1,17},{17,1},{2,18},{18,2},{3,19},{19,3},{4,20},{20... | collective-permute-start | bytes 589832 | tf_op jit(solution)/shard_map/ppermute | solution.py:26
  83.4 6.3 %copy-start.2 = (bf16[384,3072]{1,0:T(8,128)(2,1)S(1)}, bf16[384,3072]{1,0:T(8,128)(2,1)}, u32[]{:S(2)}) copy-start(bf16[384,3072]{1,0:T(8,128)(2,1)} %wi.2) | copy-start | bytes 7077892
  83.4 6.2 %copy-start.3 = (bf16[3072,384]{1,0:T(8,128)(2,1)S(1)}, bf16[3072,384]{1,0:T(8,128)(2,1)}, u32[]{:S(2)}) copy-start(bf16[3072,384]{1,0:T(8,128)(2,1)} %wo.2) | copy-start | bytes 7077892
  83.4 6.2 %collective-permute-start.8 = (bf16[2,4,384,384]{3,2,1,0:T(8,128)(2,1)}, bf16[2,4,384,384]{3,2,1,0:T(8,128)(2,1)S(1)}, u32[]{:S(2)}, u32[]{:S(2)}) collective-permute-start(bf16[2,4,384,384]{3,2,1,0:T(8,128)(2,1)} %pack.1), channel_id=1, source_target_pairs={{0,1},{1,0},{2,3},{3,2},{4,5},{5,4},{6,7},{7,6},{8,9},{9,8},{10,11... | collective-permute-start | bytes 7077896 | tf_op jit(solution)/shard_map/ppermute | solution.py:26
  83.6 4.3 %collective-permute-start.9 = (bf16[4,32,768]{2,1,0:T(8,128)(2,1)S(1)}, bf16[4,32,768]{2,1,0:T(8,128)(2,1)S(1)}, u32[]{:S(2)}, u32[]{:S(2)}) collective-permute-start(bf16[4,32,768]{2,1,0:T(8,128)(2,1)S(1)} %collective-permute-done.4.refs_0_), channel_id=1, source_target_pairs={{0,1},{1,0},{2,3},{3,2},{4,5},{5,4},{6,7},{7,6},{8,9},{9,8},{10,11... | collective-permute-start | bytes 589832 | tf_op jit(solution)/shard_map/ppermute | solution.py:26
  84.1 6.0 %collective-permute-start.3 = (bf16[512,768]{1,0:T(8,128)(2,1)S(1)}, bf16[512,768]{1,0:T(8,128)(2,1)S(1)}, u32[]{:S(2)}, u32[]{:S(2)}) collective-permute-start(bf16[512,768]{1,0:T(8,128)(2,1)S(1)} %join_a.1.own), channel_id=1, source_target_pairs={{0,1},{1,0},{2,3},{3,2},{4,5},{5,4},{6,7},{7,6},{8,9},{9,8},{10,11... | collective-permute-start | bytes 2359304 | tf_op jit(solution)/shard_map/ppermute | solution.py:26
  84.2 12.7 %collective-permute-start.7 = (bf16[4,32,768]{2,1,0:T(8,128)(2,1)S(1)}, bf16[4,32,768]{2,1,0:T(8,128)(2,1)S(1)}, u32[]{:S(2)}, u32[]{:S(2)}) collective-permute-start(bf16[4,32,768]{2,1,0:T(8,128)(2,1)S(1)} %collective-permute-done.4.refs_0_), channel_id=1, source_target_pairs={{0,32},{32,64},{64,96},{96,0},{1,33},{33,65},{65,97},{97,1},{2,34}... | collective-permute-start | bytes 589832 | tf_op jit(solution)/shard_map/ppermute | solution.py:26
  84.9 12.0 %collective-permute-start.6 = (bf16[4,32,768]{2,1,0:T(8,128)(2,1)S(1)}, bf16[4,32,768]{2,1,0:T(8,128)(2,1)S(1)}, u32[]{:S(2)}, u32[]{:S(2)}) collective-permute-start(bf16[4,32,768]{2,1,0:T(8,128)(2,1)S(1)} %collective-permute-done.4.refs_0_), channel_id=1, source_target_pairs={{0,64},{32,96},{64,0},{96,32},{1,65},{33,97},{65,1},{97,33},{2,66}... | collective-permute-start | bytes 589832 | tf_op jit(solution)/shard_map/ppermute | solution.py:26
  87.9 9.6 %collective-permute-start.5 = (bf16[4,32,768]{2,1,0:T(8,128)(2,1)S(1)}, bf16[4,32,768]{2,1,0:T(8,128)(2,1)S(1)}, u32[]{:S(2)}, u32[]{:S(2)}) collective-permute-start(bf16[4,32,768]{2,1,0:T(8,128)(2,1)S(1)} %collective-permute-done.4.refs_0_), channel_id=1, source_target_pairs={{0,96},{32,0},{64,32},{96,64},{1,97},{33,1},{65,33},{97,65},{2,98}... | collective-permute-start | bytes 589832 | tf_op jit(solution)/shard_map/ppermute | solution.py:26
  92.0 17.2 %collective-permute-start.14 = (bf16[128,1536]{1,0:T(8,128)(2,1)S(1)}, bf16[128,1536]{1,0:T(8,128)(2,1)S(1)}, u32[]{:S(2)}, u32[]{:S(2)}) collective-permute-start(bf16[128,1536]{1,0:T(8,128)(2,1)S(1)} %get-tuple-element.126), channel_id=1, source_target_pairs={{0,6},{2,0},{4,2},{6,4},{1,7},{3,1},{5,3},{7,5},{8,14},{10,8},{12,... | collective-permute-start | bytes 1179656 | tf_op jit(solution)/shard_map/ppermute | solution.py:26
  96.1 13.1 %collective-permute-start.13 = (bf16[128,1536]{1,0:T(8,128)(2,1)S(1)}, bf16[128,1536]{1,0:T(8,128)(2,1)S(1)}, u32[]{:S(2)}, u32[]{:S(2)}) collective-permute-start(bf16[128,1536]{1,0:T(8,128)(2,1)S(1)} %get-tuple-element.116), channel_id=1, source_target_pairs={{0,2},{2,4},{4,6},{6,0},{1,3},{3,5},{5,7},{7,1},{8,10},{10,12},{12... | collective-permute-start | bytes 1179656 | tf_op jit(solution)/shard_map/ppermute | solution.py:26
  97.5 1.4 collective-permute-start.10
  97.5 1.7 collective-permute-start.11
  98.0 1.5 collective-permute-start.12
  101.5 15.5 %collective-permute-start.18 = (bf16[128,1536]{1,0:T(8,128)(2,1)S(1)}, bf16[128,1536]{1,0:T(8,128)(2,1)S(1)}, u32[]{:S(2)}, u32[]{:S(2)}) collective-permute-start(bf16[128,1536]{1,0:T(8,128)(2,1)S(1)} %get-tuple-element.134), channel_id=1, source_target_pairs={{0,6},{2,0},{4,2},{6,4},{1,7},{3,1},{5,3},{7,5},{8,14},{10,8},{12,... | collective-permute-start | bytes 1179656 | tf_op jit(solution)/shard_map/ppermute | solution.py:26
  105.6 13.2 %collective-permute-start.17 = (bf16[128,1536]{1,0:T(8,128)(2,1)S(1)}, bf16[128,1536]{1,0:T(8,128)(2,1)S(1)}, u32[]{:S(2)}, u32[]{:S(2)}) collective-permute-start(bf16[128,1536]{1,0:T(8,128)(2,1)S(1)} %get-tuple-element.122), channel_id=1, source_target_pairs={{0,2},{2,4},{4,6},{6,0},{1,3},{3,5},{5,7},{7,1},{8,10},{10,12},{12... | collective-permute-start | bytes 1179656 | tf_op jit(solution)/shard_map/ppermute | solution.py:26
  109.9 25.7 %collective-permute-start.15 = (bf16[2,128,1536]{2,1,0:T(8,128)(2,1)S(1)}, bf16[2,128,1536]{2,1,0:T(8,128)(2,1)S(1)}, u32[]{:S(2)}, u32[]{:S(2)}) collective-permute-start(bf16[2,128,1536]{2,1,0:T(8,128)(2,1)S(1)} %get-tuple-element.129), channel_id=1, source_target_pairs={{0,2},{2,4},{4,6},{6,0},{1,3},{3,5},{5,7},{7,1},{8,10},{10,12},{12... | collective-permute-start | bytes 2359304 | tf_op jit(solution)/shard_map/ppermute | solution.py:26
  110.0 25.6 %collective-permute-start.16 = (bf16[2,128,1536]{2,1,0:T(8,128)(2,1)S(1)}, bf16[2,128,1536]{2,1,0:T(8,128)(2,1)S(1)}, u32[]{:S(2)}, u32[]{:S(2)}) collective-permute-start(bf16[2,128,1536]{2,1,0:T(8,128)(2,1)S(1)} %get-tuple-element.130), channel_id=1, source_target_pairs={{0,6},{2,0},{4,2},{6,4},{1,7},{3,1},{5,3},{7,5},{8,14},{10,8},{12,... | collective-permute-start | bytes 2359304 | tf_op jit(solution)/shard_map/ppermute | solution.py:26
  119.4 32.0 %collective-permute-start.20 = (bf16[2,128,1536]{2,1,0:T(8,128)(2,1)S(1)}, bf16[2,128,1536]{2,1,0:T(8,128)(2,1)S(1)}, u32[]{:S(2)}, u32[]{:S(2)}) collective-permute-start(bf16[2,128,1536]{2,1,0:T(8,128)(2,1)S(1)} %get-tuple-element.137), channel_id=1, source_target_pairs={{0,2},{2,4},{4,6},{6,0},{1,3},{3,5},{5,7},{7,1},{8,10},{10,12},{12... | collective-permute-start | bytes 2359304 | tf_op jit(solution)/shard_map/ppermute | solution.py:26
  119.5 32.0 %collective-permute-start.21 = (bf16[2,128,1536]{2,1,0:T(8,128)(2,1)S(1)}, bf16[2,128,1536]{2,1,0:T(8,128)(2,1)S(1)}, u32[]{:S(2)}, u32[]{:S(2)}) collective-permute-start(bf16[2,128,1536]{2,1,0:T(8,128)(2,1)S(1)} %get-tuple-element.138), channel_id=1, source_target_pairs={{0,6},{2,0},{4,2},{6,4},{1,7},{3,1},{5,3},{7,5},{8,14},{10,8},{12,... | collective-permute-start | bytes 2359304 | tf_op jit(solution)/shard_map/ppermute | solution.py:26
  136.3 17.6 %collective-permute-start.19 = (bf16[2,128,1536]{2,1,0:T(8,128)(2,1)S(1)}, bf16[2,128,1536]{2,1,0:T(8,128)(2,1)S(1)}, u32[]{:S(2)}, u32[]{:S(2)}) collective-permute-start(bf16[2,128,1536]{2,1,0:T(8,128)(2,1)S(1)} %get-tuple-element.142), channel_id=1, source_target_pairs={{0,8},{8,0},{1,9},{9,1},{2,10},{10,2},{3,11},{11,3},{4,12},{12,4},... | collective-permute-start | bytes 2359304 | tf_op jit(solution)/shard_map/ppermute | solution.py:26
  152.2 18.8 %collective-permute-start.24 = (bf16[2,128,1536]{2,1,0:T(8,128)(2,1)S(1)}, bf16[2,128,1536]{2,1,0:T(8,128)(2,1)S(1)}, u32[]{:S(2)}, u32[]{:S(2)}) collective-permute-start(bf16[2,128,1536]{2,1,0:T(8,128)(2,1)S(1)} %get-tuple-element.145), channel_id=1, source_target_pairs={{0,8},{8,0},{1,9},{9,1},{2,10},{10,2},{3,11},{11,3},{4,12},{12,4},... | collective-permute-start | bytes 2359304 | tf_op jit(solution)/shard_map/ppermute | solution.py:26
  154.7 20.3 %collective-permute-start.23 = (bf16[2,128,1536]{2,1,0:T(8,128)(2,1)S(1)}, bf16[2,128,1536]{2,1,0:T(8,128)(2,1)S(1)}, u32[]{:S(2)}, u32[]{:S(2)}) collective-permute-start(bf16[2,128,1536]{2,1,0:T(8,128)(2,1)S(1)} %hidden.2.mine.refs_6_.refs_9_), channel_id=1, source_target_pairs={{0,2},{2,4},{4,6},{6,0},{1,3},{3,5},{5,7},{7,1},{8,10},{10,12},{12... | collective-permute-start | bytes 2359304 | tf_op jit(solution)/shard_map/ppermute | solution.py:26
  154.8 20.3 %collective-permute-start.22 = (bf16[2,128,1536]{2,1,0:T(8,128)(2,1)S(1)}, bf16[2,128,1536]{2,1,0:T(8,128)(2,1)S(1)}, u32[]{:S(2)}, u32[]{:S(2)}) collective-permute-start(bf16[2,128,1536]{2,1,0:T(8,128)(2,1)S(1)} %hidden.2.mine.refs_6_.refs_9_), channel_id=1, source_target_pairs={{0,6},{2,0},{4,2},{6,4},{1,7},{3,1},{5,3},{7,5},{8,14},{10,8},{12,... | collective-permute-start | bytes 2359304 | tf_op jit(solution)/shard_map/ppermute | solution.py:26
  171.7 21.8 %collective-permute-start.28 = (bf16[2,128,1536]{2,1,0:T(8,128)(2,1)S(1)}, bf16[2,128,1536]{2,1,0:T(8,128)(2,1)S(1)}, u32[]{:S(2)}, u32[]{:S(2)}) collective-permute-start(bf16[2,128,1536]{2,1,0:T(8,128)(2,1)S(1)} %hidden.3.mine.refs_6_.refs_9_), channel_id=1, source_target_pairs={{0,2},{2,4},{4,6},{6,0},{1,3},{3,5},{5,7},{7,1},{8,10},{10,12},{12... | collective-permute-start | bytes 2359304 | tf_op jit(solution)/shard_map/ppermute | solution.py:26
  171.8 21.7 %collective-permute-start.27 = (bf16[2,128,1536]{2,1,0:T(8,128)(2,1)S(1)}, bf16[2,128,1536]{2,1,0:T(8,128)(2,1)S(1)}, u32[]{:S(2)}, u32[]{:S(2)}) collective-permute-start(bf16[2,128,1536]{2,1,0:T(8,128)(2,1)S(1)} %hidden.3.mine.refs_6_.refs_9_), channel_id=1, source_target_pairs={{0,6},{2,0},{4,2},{6,4},{1,7},{3,1},{5,3},{7,5},{8,14},{10,8},{12,... | collective-permute-start | bytes 2359304 | tf_op jit(solution)/shard_map/ppermute | solution.py:26
  175.1 28.2 %collective-permute-start.26 = (bf16[128,1536]{1,0:T(8,128)(2,1)S(1)}, bf16[128,1536]{1,0:T(8,128)(2,1)S(1)}, u32[]{:S(2)}, u32[]{:S(2)}) collective-permute-start(bf16[128,1536]{1,0:T(8,128)(2,1)S(1)} %get-tuple-element.156), channel_id=1, source_target_pairs={{0,2},{2,4},{4,6},{6,0},{1,3},{3,5},{5,7},{7,1},{8,10},{10,12},{12... | collective-permute-start | bytes 1179656 | tf_op jit(solution)/shard_map/ppermute | solution.py:26
  175.2 28.1 %collective-permute-start.25 = (bf16[128,1536]{1,0:T(8,128)(2,1)S(1)}, bf16[128,1536]{1,0:T(8,128)(2,1)S(1)}, u32[]{:S(2)}, u32[]{:S(2)}) collective-permute-start(bf16[128,1536]{1,0:T(8,128)(2,1)S(1)} %get-tuple-element.151), channel_id=1, source_target_pairs={{0,6},{2,0},{4,2},{6,4},{1,7},{3,1},{5,3},{7,5},{8,14},{10,8},{12,... | collective-permute-start | bytes 1179656 | tf_op jit(solution)/shard_map/ppermute | solution.py:26
  184.5 2.2 copy-start
  193.5 13.9 %collective-permute-start.33 = (bf16[128,1536]{1,0:T(8,128)(2,1)S(1)}, bf16[128,1536]{1,0:T(8,128)(2,1)S(1)}, u32[]{:S(2)}, u32[]{:S(2)}) collective-permute-start(bf16[128,1536]{1,0:T(8,128)(2,1)S(1)} %get-tuple-element.184), channel_id=1, source_target_pairs={{0,2},{2,4},{4,6},{6,0},{1,3},{3,5},{5,7},{7,1},{8,10},{10,12},{12... | collective-permute-start | bytes 1179656 | tf_op jit(solution)/shard_map/ppermute | solution.py:26
  193.6 5.6 %copy-start.1 = (f32[768,1536]{1,0:T(8,128)S(1)}, f32[768,1536]{1,0:T(8,128)}, u32[]{:S(2)}) copy-start(f32[768,1536]{1,0:T(8,128)} %copy-done) | copy-start | bytes 14155780
  193.6 13.8 %collective-permute-start.32 = (bf16[128,1536]{1,0:T(8,128)(2,1)S(1)}, bf16[128,1536]{1,0:T(8,128)(2,1)S(1)}, u32[]{:S(2)}, u32[]{:S(2)}) collective-permute-start(bf16[128,1536]{1,0:T(8,128)(2,1)S(1)} %get-tuple-element.168), channel_id=1, source_target_pairs={{0,6},{2,0},{4,2},{6,4},{1,7},{3,1},{5,3},{7,5},{8,14},{10,8},{12,... | collective-permute-start | bytes 1179656 | tf_op jit(solution)/shard_map/ppermute | solution.py:26
  204.3 1.6 collective-permute-start.29
  204.4 1.9 collective-permute-start.30
  204.8 1.8 collective-permute-start.31
  208.4 9.5 %collective-permute-start.34 = (f32[512,384]{1,0:T(8,128)S(1)}, f32[512,384]{1,0:T(8,128)S(1)}, u32[]{:S(2)}, u32[]{:S(2)}) collective-permute-start(f32[512,384]{1,0:T(8,128)S(1)} %get-tuple-element.186), channel_id=1, source_target_pairs={{0,1},{1,0},{2,3},{3,2},{4,5},{5,4},{6,7},{7,6},{8,9},{9,8},{10,11... | collective-permute-start | bytes 2359304 | tf_op jit(solution)/shard_map/ppermute | solution.py:26
  208.5 7.7 %collective-permute-start.35 = (bf16[4,32,384]{2,1,0:T(8,128)(2,1)S(1)}, bf16[4,32,384]{2,1,0:T(8,128)(2,1)S(1)}, u32[]{:S(2)}, u32[]{:S(2)}) collective-permute-start(bf16[4,32,384]{2,1,0:T(8,128)(2,1)S(1)} %get-tuple-element.187), channel_id=1, source_target_pairs={{0,32},{32,64},{64,96},{96,0},{1,33},{33,65},{65,97},{97,1},{2,34}... | collective-permute-start | bytes 294920 | tf_op jit(solution)/shard_map/ppermute | solution.py:26
  208.9 8.9 %collective-permute-start.36 = (bf16[4,32,384]{2,1,0:T(8,128)(2,1)S(1)}, bf16[4,32,384]{2,1,0:T(8,128)(2,1)S(1)}, u32[]{:S(2)}, u32[]{:S(2)}) collective-permute-start(bf16[4,32,384]{2,1,0:T(8,128)(2,1)S(1)} %get-tuple-element.188), channel_id=1, source_target_pairs={{0,64},{32,96},{64,0},{96,32},{1,65},{33,97},{65,1},{97,33},{2,66}... | collective-permute-start | bytes 294920 | tf_op jit(solution)/shard_map/ppermute | solution.py:26
  212.7 5.2 %collective-permute-start.37 = (bf16[4,32,384]{2,1,0:T(8,128)(2,1)S(1)}, bf16[4,32,384]{2,1,0:T(8,128)(2,1)S(1)}, u32[]{:S(2)}, u32[]{:S(2)}) collective-permute-start(bf16[4,32,384]{2,1,0:T(8,128)(2,1)S(1)} %get-tuple-element.189), channel_id=1, source_target_pairs={{0,96},{32,0},{64,32},{96,64},{1,97},{33,1},{65,33},{97,65},{2,98}... | collective-permute-start | bytes 294920 | tf_op jit(solution)/shard_map/ppermute | solution.py:26
  218.0 8.4 %collective-permute-start.42 = (bf16[384,1536]{1,0:T(8,128)(2,1)S(1)}, bf16[384,1536]{1,0:T(8,128)(2,1)S(1)}, u32[]{:S(2)}, u32[]{:S(2)}) collective-permute-start(bf16[384,1536]{1,0:T(8,128)(2,1)S(1)} %get-tuple-element.209), channel_id=1, source_target_pairs={{0,1},{1,0},{2,3},{3,2},{4,5},{5,4},{6,7},{7,6},{8,9},{9,8},{10,11... | collective-permute-start | bytes 3538952 | tf_op jit(solution)/shard_map/ppermute | solution.py:26
  218.1 9.7 %collective-permute-start.43 = (bf16[1536,384]{1,0:T(8,128)(2,1)}, bf16[1536,384]{1,0:T(8,128)(2,1)S(1)}, u32[]{:S(2)}, u32[]{:S(2)}) collective-permute-start(bf16[1536,384]{1,0:T(8,128)(2,1)} %get-tuple-element.210), channel_id=1, source_target_pairs={{0,1},{1,0},{2,3},{3,2},{4,5},{5,4},{6,7},{7,6},{8,9},{9,8},{10,11... | collective-permute-start | bytes 3538952 | tf_op jit(solution)/shard_map/ppermute | solution.py:26
  218.6 11.1 %collective-permute-start.38 = (bf16[4,32,384]{2,1,0:T(8,128)(2,1)S(1)}, bf16[4,32,384]{2,1,0:T(8,128)(2,1)S(1)}, u32[]{:S(2)}, u32[]{:S(2)}) collective-permute-start(bf16[4,32,384]{2,1,0:T(8,128)(2,1)S(1)} %get-tuple-element.203), channel_id=1, source_target_pairs={{0,16},{16,0},{32,48},{48,32},{64,80},{80,64},{96,112},{112,96},{1... | collective-permute-start | bytes 294920 | tf_op jit(solution)/shard_map/ppermute | solution.py:504
  220.1 9.6 %collective-permute-start.39 = (bf16[4,32,384]{2,1,0:T(8,128)(2,1)S(1)}, bf16[4,32,384]{2,1,0:T(8,128)(2,1)S(1)}, u32[]{:S(2)}, u32[]{:S(2)}) collective-permute-start(bf16[4,32,384]{2,1,0:T(8,128)(2,1)S(1)} %get-tuple-element.204), channel_id=1, source_target_pairs={{0,48},{16,32},{32,80},{48,64},{64,112},{80,96},{96,16},{112,0},{1... | collective-permute-start | bytes 294920 | tf_op jit(solution)/shard_map/ppermute | solution.py:504
  221.9 9.3 %collective-permute-start.40 = (bf16[4,32,384]{2,1,0:T(8,128)(2,1)S(1)}, bf16[4,32,384]{2,1,0:T(8,128)(2,1)S(1)}, u32[]{:S(2)}, u32[]{:S(2)}) collective-permute-start(bf16[4,32,384]{2,1,0:T(8,128)(2,1)S(1)} %get-tuple-element.205), channel_id=1, source_target_pairs={{0,80},{16,64},{32,112},{48,96},{64,16},{80,0},{96,48},{112,32},{1... | collective-permute-start | bytes 294920 | tf_op jit(solution)/shard_map/ppermute | solution.py:504
  226.4 7.1 %collective-permute-start.41 = (bf16[4,32,384]{2,1,0:T(8,128)(2,1)S(1)}, bf16[4,32,384]{2,1,0:T(8,128)(2,1)}, u32[]{:S(2)}, u32[]{:S(2)}) collective-permute-start(bf16[4,32,384]{2,1,0:T(8,128)(2,1)S(1)} %get-tuple-element.206), channel_id=1, source_target_pairs={{0,112},{16,96},{32,16},{48,0},{64,48},{80,32},{96,80},{112,64},{1... | collective-permute-start | bytes 294920 | tf_op jit(solution)/shard_map/ppermute | solution.py:504

commit v9 on v8

--- a/solution.py
+++ b/solution.py
@@ -68,25 +68,18 @@
     feat = w_in.shape[0]
     half = w_out.shape[0] // feat // 2
 
-    def body(core, wi, wo, out, sems):
-        copies = []
-        for k in range(half):
-            at = pl.ds(pl.multiple_of(((1 - core[0]) * half + k) * feat, feat), feat)
-            copies.append(pltpu.make_async_copy(wi.at[:, at], out.at[0, k], sems.at[0, k]))
-            copies.append(pltpu.make_async_copy(wo.at[at, :], out.at[1, k], sems.at[1, k]))
-        for copy in copies:
-            copy.start()
-        for copy in copies:
-            copy.wait()
-
-    shape = (2, half, feat, feat)
+    def body(_, wi, wo, out):
+        out[0, 0] = wi[...]
+        out[1, 0] = wo[...]
+
+    block = (feat, feat)
+    place = lambda i, c: (1 - c) * half + i
     return kernel(
         "pack",
         body,
-        1,
-        [(w_in, None, "hbm"), (w_out, None, "hbm")],
-        [(shape, BF16, None, None)],
-        [pltpu.SemaphoreType.DMA((2, half))],
+        half,
+        [(w_in, block, (0, place)), (w_out, block, (place, 0))],
+        [((2, half, feat, feat), BF16, (2, 1, feat, feat), (0, "i", 0, 0))],
         scalar=core,
         vmem=60,
     )[0]

time: 235 us -> 168 us (0.71)
  Pallas kernels: 108 us -> 39.7 us
  starting transfers between devices: 56.1 us -> 63.8 us
  waiting for transfers between devices: 64.7 us -> 58.6 us
    pallas_call x26, Pallas kernels: 108 us -> 39.7 us  [kernel(): pl.pallas_call(body, name=name, grid_spec=pltpu.PrefetchScalarGridSpec(nu...]
    ppermute x40, starting transfers between devices: 46.9 us -> 53.4 us  [shift(): return lax.ppermute(x, axis, [(i, (i + by) % n) for i in range(n)])]
    ppermute x40, waiting for transfers between devices: 60.8 us -> 54.8 us  [shift(): return lax.ppermute(x, axis, [(i, (i + by) % n) for i in range(n)])]
  transfers between devices with their start and end apart: 44 -> 44, of which waited for: 20 -> 18; matrix products, arithmetic and copies ran while one was open for 0% -> 0% of each run, Pallas kernels for 46% -> 23%
where the time goes in v9:
time: 168 us
  starting transfers between devices  63.8 us (38%)
  waiting for transfers between devices  58.6 us (35%)
  Pallas kernels  39.7 us (24%)
  other arithmetic  2.75 us (2%)
  local copies, waits for them, and re-layouts  2.18 us (1%)
    ppermute x40, waiting for transfers between devices, shift(): return lax.ppermute(x, axis, [(i, (i + by) % n) for i in range(n)])  54.8 us
    ppermute x40, starting transfers between devices, shift(): return lax.ppermute(x, axis, [(i, (i + by) % n) for i in range(n)])  53.4 us
    pallas_call x26, Pallas kernels, kernel(): pl.pallas_call(body, name=name, grid_spec=pltpu.PrefetchScalarGridSpec(nu...  39.7 us
    ppermute x4, starting transfers between devices, local(): lax.ppermute(a, ROWS, [(i, (i // 2 + d) % 4 * 2 + (i + 1) % 2) for i in r...  10.3 us
    ppermute x4, waiting for transfers between devices, local(): lax.ppermute(a, ROWS, [(i, (i // 2 + d) % 4 * 2 + (i + 1) % 2) for i in r...  3.78 us
  transfers between devices with their start and end apart: 44, of which 18 were waited for; matrix products, arithmetic and copies ran while one was open for 0% of the time, Pallas kernels for 23%

profile of v9, /device:TPU:0, one launch (start us, length us, event | category | flops | bytes accessed | tf_op | source)
XLA Modules:
  0.0 168.1 jit_solution(15153392466089425634)
XLA Ops:
  0.7 1.0 pad_maximum_fusion
  1.7 1.7 %collective-permute-start.2 = (bf16[4,32,768]{2,1,0:T(8,128)(2,1)S(1)}, bf16[4,32,768]{2,1,0:T(8,128)(2,1)S(1)}, u32[]{:S(2)}, u32[]{:S(2)}) collective-permute-start(bf16[4,32,768]{2,1,0:T(8,128)(2,1)S(1)} %fusion.2.refs_0_), channel_id=1, source_target_pairs={{0,32},{32,64},{64,96},{96,0},{1,33},{33,65},{65,97},{97,1},{2,34}... | collective-permute-start | bytes 589832 | tf_op jit(solution)/shard_map/ppermute | solution.py:26
  3.4 2.9 %collective-permute-start.1 = (bf16[4,32,768]{2,1,0:T(8,128)(2,1)S(1)}, bf16[4,32,768]{2,1,0:T(8,128)(2,1)S(1)}, u32[]{:S(2)}, u32[]{:S(2)}) collective-permute-start(bf16[4,32,768]{2,1,0:T(8,128)(2,1)S(1)} %fusion.2.refs_0_), channel_id=1, source_target_pairs={{0,64},{32,96},{64,0},{96,32},{1,65},{33,97},{65,1},{97,33},{2,66}... | collective-permute-start | bytes 589832 | tf_op jit(solution)/shard_map/ppermute | solution.py:26
  6.3 1.3 collective-permute-start
  7.7 3.0 %collective-permute-start.4 = (bf16[4,32,768]{2,1,0:T(8,128)(2,1)S(1)}, bf16[4,32,768]{2,1,0:T(8,128)(2,1)S(1)}, u32[]{:S(2)}, u32[]{:S(2)}) collective-permute-start(bf16[4,32,768]{2,1,0:T(8,128)(2,1)S(1)} %fusion.2.refs_0_), channel_id=1, source_target_pairs={{0,16},{16,0},{1,17},{17,1},{2,18},{18,2},{3,19},{19,3},{4,20},{20... | collective-permute-start | bytes 589832 | tf_op jit(solution)/shard_map/ppermute | solution.py:26
  10.7 3.9 %pack.1 = bf16[2,4,384,384]{3,2,1,0:T(8,128)(2,1)} custom-call(s32[1]{0:T(128)} %bitcast.1._.core.refs_0_, bf16[384,3072]{1,0:T(8,128)(2,1)} %wi.2, bf16[3072,384]{1,0:T(8,128)(2,1)} %wo.2), custom_call_target="tpu_custom_call" | custom-call | flops 115000000 | bytes 369000 | tf_op jit(solution)/shard_map/pack/pallas_call | solution.py:50
  14.6 0.5 collective-permute-done.1.refs_2_
  15.3 0.5 collective-permute-start.3
  15.8 1.2 collective-permute-start.7
  17.1 2.4 %collective-permute-start.6 = (bf16[4,32,768]{2,1,0:T(8,128)(2,1)S(1)}, bf16[4,32,768]{2,1,0:T(8,128)(2,1)S(1)}, u32[]{:S(2)}, u32[]{:S(2)}) collective-permute-start(bf16[4,32,768]{2,1,0:T(8,128)(2,1)S(1)} %collective-permute-done.4.refs_0_), channel_id=1, source_target_pairs={{0,64},{32,96},{64,0},{96,32},{1,65},{33,97},{65,1},{97,33},{2,66}... | collective-permute-start | bytes 589832 | tf_op jit(solution)/shard_map/ppermute | solution.py:26
  19.5 1.6 collective-permute-start.5
  21.1 0.6 weights.1
  21.6 1.8 %first_block.2 = (bf16[128,1536]{1,0:T(8,128)(2,1)S(1)}, bf16[128,1536]{1,0:T(8,128)(2,1)S(1)}) custom-call(bf16[512,768]{1,0:T(8,128)(2,1)S(1)} %join_a.1.own, bf16[512,768]{1,0:T(8,128)(2,1)S(1)} %collective-permute-done.3.other, bf16[768,1536]{1,0:T(8,128)(2,1)S(1)} %get-tuple-element.114.wi, bf16[1536,768]{1,0:T(8,128)(2,1)S(1)} %get-tuple-element.115.wo), custom_call_target="tpu_custom_call" | custom-call | flops 115000000 | bytes 369000 | tf_op jit(solution)/shard_map/first_block/pallas_call | solution.py:50
  23.5 4.1 %collective-permute-start.14 = (bf16[128,1536]{1,0:T(8,128)(2,1)S(1)}, bf16[128,1536]{1,0:T(8,128)(2,1)S(1)}, u32[]{:S(2)}, u32[]{:S(2)}) collective-permute-start(bf16[128,1536]{1,0:T(8,128)(2,1)S(1)} %get-tuple-element.126), channel_id=1, source_target_pairs={{0,6},{2,0},{4,2},{6,4},{1,7},{3,1},{5,3},{7,5},{8,14},{10,8},{12,... | collective-permute-start | bytes 1179656 | tf_op jit(solution)/shard_map/ppermute | solution.py:26
  27.6 1.0 collective-permute-done.6.refs_2_
  28.8 0.5 collective-permute-start.11
  29.3 0.9 collective-permute-done.10.refs_5_
  30.9 1.8 %first_block.3 = (bf16[128,1536]{1,0:T(8,128)(2,1)S(1)}, bf16[128,1536]{1,0:T(8,128)(2,1)S(1)}) custom-call(bf16[512,768]{1,0:T(8,128)(2,1)S(1)} %get-tuple-element.131.own, bf16[512,768]{1,0:T(8,128)(2,1)S(1)} %get-tuple-element.132.other, bf16[768,1536]{1,0:T(8,128)(2,1)S(1)} %get-tuple-element.114.wi, bf16[1536,768]{1,0:T(8,128)(2,1)S(1)} %get-tuple-element.115.wo), custom_call_target="tpu_custom_call" | custom-call | flops 115000000 | bytes 369000 | tf_op jit(solution)/shard_map/first_block/pallas_call | solution.py:50
  32.7 4.1 %collective-permute-start.18 = (bf16[128,1536]{1,0:T(8,128)(2,1)S(1)}, bf16[128,1536]{1,0:T(8,128)(2,1)S(1)}, u32[]{:S(2)}, u32[]{:S(2)}) collective-permute-start(bf16[128,1536]{1,0:T(8,128)(2,1)S(1)} %get-tuple-element.134), channel_id=1, source_target_pairs={{0,6},{2,0},{4,2},{6,4},{1,7},{3,1},{5,3},{7,5},{8,14},{10,8},{12,... | collective-permute-start | bytes 1179656 | tf_op jit(solution)/shard_map/ppermute | solution.py:26
  36.8 3.7 %products.2 = (f32[2,512,1536]{2,1,0:T(8,128)S(1)}, bf16[512,768]{1,0:T(8,128)(2,1)S(1)}, bf16[512,768]{1,0:T(8,128)(2,1)S(1)}) custom-call(bf16[512,768]{1,0:T(8,128)(2,1)S(1)} %join_a.1.own, bf16[512,768]{1,0:T(8,128)(2,1)S(1)} %collective-permute-done.3.other, bf16[768,1536]{1,0:T(8,128)(2,1)S(1)} %get-tuple-element.114.wi, ...), custom_call_target="tpu_custom_call" | custom-call | flops 115000000 | bytes 369000 | tf_op jit(solution)/shard_map/products/pallas_call | solution.py:50
  40.5 0.7 ring_add.2
  41.2 3.3 %collective-permute-start.16 = (bf16[2,128,1536]{2,1,0:T(8,128)(2,1)S(1)}, bf16[2,128,1536]{2,1,0:T(8,128)(2,1)S(1)}, u32[]{:S(2)}, u32[]{:S(2)}) collective-permute-start(bf16[2,128,1536]{2,1,0:T(8,128)(2,1)S(1)} %get-tuple-element.130), channel_id=1, source_target_pairs={{0,6},{2,0},{4,2},{6,4},{1,7},{3,1},{5,3},{7,5},{8,14},{10,8},{12,... | collective-permute-start | bytes 2359304 | tf_op jit(solution)/shard_map/ppermute | solution.py:26
  44.5 3.7 %products.3 = (f32[2,512,1536]{2,1,0:T(8,128)S(1)}, bf16[512,768]{1,0:T(8,128)(2,1)S(1)}, bf16[512,768]{1,0:T(8,128)(2,1)S(1)}) custom-call(bf16[512,768]{1,0:T(8,128)(2,1)S(1)} %get-tuple-element.131.own, bf16[512,768]{1,0:T(8,128)(2,1)S(1)} %get-tuple-element.132.other, bf16[768,1536]{1,0:T(8,128)(2,1)S(1)} %get-tuple-element.114.wi, ...), custom_call_target="tpu_custom_call" | custom-call | flops 115000000 | bytes 369000 | tf_op jit(solution)/shard_map/products/pallas_call | solution.py:50
  48.2 1.8 %collective-permute-done.17.up = bf16[128,1536]{1,0:T(8,128)(2,1)S(1)} collective-permute-done((bf16[128,1536]{1,0:T(8,128)(2,1)S(1)}, bf16[128,1536]{1,0:T(8,128)(2,1)S(1)}, u32[]{:S(2)}, u32[]{:S(2)}) %collective-permute-start.17) | collective-permute-done | bytes 393248 | tf_op jit(solution)/shard_map/ppermute | solution.py:26
  50.0 0.6 ring_add.3
  50.7 3.2 %collective-permute-start.21 = (bf16[2,128,1536]{2,1,0:T(8,128)(2,1)S(1)}, bf16[2,128,1536]{2,1,0:T(8,128)(2,1)S(1)}, u32[]{:S(2)}, u32[]{:S(2)}) collective-permute-start(bf16[2,128,1536]{2,1,0:T(8,128)(2,1)S(1)} %get-tuple-element.138), channel_id=1, source_target_pairs={{0,6},{2,0},{4,2},{6,4},{1,7},{3,1},{5,3},{7,5},{8,14},{10,8},{12,... | collective-permute-start | bytes 2359304 | tf_op jit(solution)/shard_map/ppermute | solution.py:26
  53.9 12.9 %collective-permute-done.15.up = bf16[2,128,1536]{2,1,0:T(8,128)(2,1)S(1)} collective-permute-done((bf16[2,128,1536]{2,1,0:T(8,128)(2,1)S(1)}, bf16[2,128,1536]{2,1,0:T(8,128)(2,1)S(1)}, u32[]{:S(2)}, u32[]{:S(2)}) %collective-permute-start.15) | collective-permute-done | bytes 786464 | tf_op jit(solution)/shard_map/ppermute | solution.py:26
  66.8 0.7 own_sum.2
  67.6 1.6 collective-permute-start.19
  69.1 13.5 %collective-permute-done.20.up = bf16[2,128,1536]{2,1,0:T(8,128)(2,1)S(1)} collective-permute-done((bf16[2,128,1536]{2,1,0:T(8,128)(2,1)S(1)}, bf16[2,128,1536]{2,1,0:T(8,128)(2,1)S(1)}, u32[]{:S(2)}, u32[]{:S(2)}) %collective-permute-start.20) | collective-permute-done | bytes 786464 | tf_op jit(solution)/shard_map/ppermute | solution.py:26
  82.7 0.7 own_sum.3
  83.4 1.7 %collective-permute-start.24 = (bf16[2,128,1536]{2,1,0:T(8,128)(2,1)S(1)}, bf16[2,128,1536]{2,1,0:T(8,128)(2,1)S(1)}, u32[]{:S(2)}, u32[]{:S(2)}) collective-permute-start(bf16[2,128,1536]{2,1,0:T(8,128)(2,1)S(1)} %get-tuple-element.145), channel_id=1, source_target_pairs={{0,8},{8,0},{1,9},{9,1},{2,10},{10,2},{3,11},{11,3},{4,12},{12,4},... | collective-permute-start | bytes 2359304 | tf_op jit(solution)/shard_map/ppermute | solution.py:26
  85.2 0.7 hidden.2.mine.refs_6_.refs_9_
  86.0 3.2 %collective-permute-start.22 = (bf16[2,128,1536]{2,1,0:T(8,128)(2,1)S(1)}, bf16[2,128,1536]{2,1,0:T(8,128)(2,1)S(1)}, u32[]{:S(2)}, u32[]{:S(2)}) collective-permute-start(bf16[2,128,1536]{2,1,0:T(8,128)(2,1)S(1)} %hidden.2.mine.refs_6_.refs_9_), channel_id=1, source_target_pairs={{0,6},{2,0},{4,2},{6,4},{1,7},{3,1},{5,3},{7,5},{8,14},{10,8},{12,... | collective-permute-start | bytes 2359304 | tf_op jit(solution)/shard_map/ppermute | solution.py:26
  89.2 13.0 %collective-permute-done.24.other = bf16[2,128,1536]{2,1,0:T(8,128)(2,1)S(1)} collective-permute-done((bf16[2,128,1536]{2,1,0:T(8,128)(2,1)S(1)}, bf16[2,128,1536]{2,1,0:T(8,128)(2,1)S(1)}, u32[]{:S(2)}, u32[]{:S(2)}) %collective-permute-start.24) | collective-permute-done | bytes 786464 | tf_op jit(solution)/shard_map/ppermute | solution.py:26
  102.2 0.7 hidden.3.mine.refs_6_.refs_9_
  103.0 3.2 %collective-permute-start.27 = (bf16[2,128,1536]{2,1,0:T(8,128)(2,1)S(1)}, bf16[2,128,1536]{2,1,0:T(8,128)(2,1)S(1)}, u32[]{:S(2)}, u32[]{:S(2)}) collective-permute-start(bf16[2,128,1536]{2,1,0:T(8,128)(2,1)S(1)} %hidden.3.mine.refs_6_.refs_9_), channel_id=1, source_target_pairs={{0,6},{2,0},{4,2},{6,4},{1,7},{3,1},{5,3},{7,5},{8,14},{10,8},{12,... | collective-permute-start | bytes 2359304 | tf_op jit(solution)/shard_map/ppermute | solution.py:26
  106.4 3.2 %collective-permute-start.25 = (bf16[128,1536]{1,0:T(8,128)(2,1)S(1)}, bf16[128,1536]{1,0:T(8,128)(2,1)S(1)}, u32[]{:S(2)}, u32[]{:S(2)}) collective-permute-start(bf16[128,1536]{1,0:T(8,128)(2,1)S(1)} %get-tuple-element.151), channel_id=1, source_target_pairs={{0,6},{2,0},{4,2},{6,4},{1,7},{3,1},{5,3},{7,5},{8,14},{10,8},{12,... | collective-permute-start | bytes 1179656 | tf_op jit(solution)/shard_map/ppermute | solution.py:26
  109.6 2.2 %input_three.2 = (f32[3,128,384]{2,1,0:T(8,128)S(1)}, f32[3,128,384]{2,1,0:T(8,128)S(1)}) custom-call(bf16[2,128,1536]{2,1,0:T(8,128)(2,1)S(1)} %hidden.2.mine.refs_6_.refs_9_, bf16[2,128,1536]{2,1,0:T(8,128)(2,1)S(1)} %collective-permute-done.22.above.refs_7_.refs_10_, bf16[2,128,1536]{2,1,0:T(8,128)(2,1)S(1)} %collective-permute-done.23.below.refs_8_.refs_11_, ...), custom_call_target="tpu_custom_call" | custom-call | flops 115000000 | bytes 369000 | tf_op jit(solution)/shard_map/input_three/pallas_call | solution.py:50
  111.9 3.8 %grads_a.1 = (f32[768,1536]{1,0:T(8,128)S(1)}, f32[1536,768]{1,0:T(8,128)S(1)}) custom-call(bf16[512,768]{1,0:T(8,128)(2,1)S(1)} %get-tuple-element.159.refs_0_.refs_1_.refs_2_, bf16[512,768]{1,0:T(8,128)(2,1)S(1)} %get-tuple-element.159.refs_0_.refs_1_.refs_2_, bf16[512,768]{1,0:T(8,128)(2,1)S(1)} %get-tuple-element.159.refs_0_.refs_1_.refs_2_, ...), custom_call_target="tpu_custom_call" | custom-call | flops 115000000 | bytes 369000 | tf_op jit(solution)/shard_map/grads_a/pallas_call | solution.py:50
  115.7 2.2 %copy-done = f32[768,1536]{1,0:T(8,128)} copy-done((f32[768,1536]{1,0:T(8,128)}, f32[768,1536]{1,0:T(8,128)S(1)}, u32[]{:S(2)}) %copy-start) | copy-done | bytes 4718616
  117.9 6.9 %collective-permute-done.28.below.refs_8_.refs_11_ = bf16[2,128,1536]{2,1,0:T(8,128)(2,1)S(1)} collective-permute-done((bf16[2,128,1536]{2,1,0:T(8,128)(2,1)S(1)}, bf16[2,128,1536]{2,1,0:T(8,128)(2,1)S(1)}, u32[]{:S(2)}, u32[]{:S(2)}) %collective-permute-start.28) | collective-permute-done | bytes 786464 | tf_op jit(solution)/shard_map/ppermute | solution.py:26
  124.9 3.3 %collective-permute-start.32 = (bf16[128,1536]{1,0:T(8,128)(2,1)S(1)}, bf16[128,1536]{1,0:T(8,128)(2,1)S(1)}, u32[]{:S(2)}, u32[]{:S(2)}) collective-permute-start(bf16[128,1536]{1,0:T(8,128)(2,1)S(1)} %get-tuple-element.168), channel_id=1, source_target_pairs={{0,6},{2,0},{4,2},{6,4},{1,7},{3,1},{5,3},{7,5},{8,14},{10,8},{12,... | collective-permute-start | bytes 1179656 | tf_op jit(solution)/shard_map/ppermute | solution.py:26
  128.2 2.2 %input_three.3 = (f32[3,128,384]{2,1,0:T(8,128)S(1)}, f32[3,128,384]{2,1,0:T(8,128)S(1)}) custom-call(bf16[2,128,1536]{2,1,0:T(8,128)(2,1)S(1)} %hidden.3.mine.refs_6_.refs_9_, bf16[2,128,1536]{2,1,0:T(8,128)(2,1)S(1)} %collective-permute-done.27.above.refs_7_.refs_10_, bf16[2,128,1536]{2,1,0:T(8,128)(2,1)S(1)} %collective-permute-done.28.below.refs_8_.refs_11_, ...), custom_call_target="tpu_custom_call" | custom-call | flops 115000000 | bytes 369000 | tf_op jit(solution)/shard_map/input_three/pallas_call | solution.py:50
  130.4 4.1 %grads_b.1 = (f32[768,1536]{1,0:T(8,128)S(1)}, f32[1536,768]{1,0:T(8,128)S(1)}) custom-call(bf16[512,768]{1,0:T(8,128)(2,1)S(1)} %get-tuple-element.157.refs_0_.refs_1_.refs_2_, bf16[512,768]{1,0:T(8,128)(2,1)S(1)} %get-tuple-element.157.refs_0_.refs_1_.refs_2_, bf16[512,768]{1,0:T(8,128)(2,1)S(1)} %get-tuple-element.157.refs_0_.refs_1_.refs_2_, ...), custom_call_target="tpu_custom_call" | custom-call | flops 115000000 | bytes 369000 | tf_op jit(solution)/shard_map/grads_b/pallas_call | solution.py:50
  134.6 0.9 input_last.2
  135.6 0.5 collective-permute-start.30
  136.2 0.9 collective-permute-done.29.refs_0_
  137.9 1.2 collective-permute-done.33.grad.refs_8_
  139.2 0.9 input_last.3
  140.2 1.8 %collective-permute-start.35 = (bf16[4,32,384]{2,1,0:T(8,128)(2,1)S(1)}, bf16[4,32,384]{2,1,0:T(8,128)(2,1)S(1)}, u32[]{:S(2)}, u32[]{:S(2)}) collective-permute-start(bf16[4,32,384]{2,1,0:T(8,128)(2,1)S(1)} %get-tuple-element.187), channel_id=1, source_target_pairs={{0,32},{32,64},{64,96},{96,0},{1,33},{33,65},{65,97},{97,1},{2,34}... | collective-permute-start | bytes 294920 | tf_op jit(solution)/shard_map/ppermute | solution.py:26
  142.0 2.4 %collective-permute-start.36 = (bf16[4,32,384]{2,1,0:T(8,128)(2,1)S(1)}, bf16[4,32,384]{2,1,0:T(8,128)(2,1)S(1)}, u32[]{:S(2)}, u32[]{:S(2)}) collective-permute-start(bf16[4,32,384]{2,1,0:T(8,128)(2,1)S(1)} %get-tuple-element.188), channel_id=1, source_target_pairs={{0,64},{32,96},{64,0},{96,32},{1,65},{33,97},{65,1},{97,33},{2,66}... | collective-permute-start | bytes 294920 | tf_op jit(solution)/shard_map/ppermute | solution.py:26
  144.4 1.1 collective-permute-start.37
  145.5 3.5 %grads_last.1 = (bf16[384,3072]{1,0:T(8,128)(2,1)}, bf16[3072,384]{1,0:T(8,128)(2,1)}, bf16[384,1536]{1,0:T(8,128)(2,1)S(1)}, bf16[1536,384]{1,0:T(8,128)(2,1)}) custom-call(s32[1]{0:T(128)} %bitcast.1._.core.refs_0_, bf16[512,768]{1,0:T(8,128)(2,1)S(1)} %get-tuple-element.159.refs_0_.refs_1_.refs_2_, ...), custom_call_target="tpu_custom_call" | custom-call | flops 115000000 | bytes 369000 | tf_op jit(solution)/shard_map/grads_last/pallas_call | solution.py:50
  149.0 0.6 collective-permute-done.36
  150.3 2.7 %collective-permute-start.38 = (bf16[4,32,384]{2,1,0:T(8,128)(2,1)S(1)}, bf16[4,32,384]{2,1,0:T(8,128)(2,1)S(1)}, u32[]{:S(2)}, u32[]{:S(2)}) collective-permute-start(bf16[4,32,384]{2,1,0:T(8,128)(2,1)S(1)} %get-tuple-element.203), channel_id=1, source_target_pairs={{0,16},{16,0},{32,48},{48,32},{64,80},{80,64},{96,112},{112,96},{1... | collective-permute-start | bytes 294920 | tf_op jit(solution)/shard_map/ppermute | solution.py:497
  153.0 1.7 %collective-permute-start.39 = (bf16[4,32,384]{2,1,0:T(8,128)(2,1)S(1)}, bf16[4,32,384]{2,1,0:T(8,128)(2,1)S(1)}, u32[]{:S(2)}, u32[]{:S(2)}) collective-permute-start(bf16[4,32,384]{2,1,0:T(8,128)(2,1)S(1)} %get-tuple-element.204), channel_id=1, source_target_pairs={{0,48},{16,32},{32,80},{48,64},{64,112},{80,96},{96,16},{112,0},{1... | collective-permute-start | bytes 294920 | tf_op jit(solution)/shard_map/ppermute | solution.py:497
  154.7 4.5 %collective-permute-start.40 = (bf16[4,32,384]{2,1,0:T(8,128)(2,1)S(1)}, bf16[4,32,384]{2,1,0:T(8,128)(2,1)S(1)}, u32[]{:S(2)}, u32[]{:S(2)}) collective-permute-start(bf16[4,32,384]{2,1,0:T(8,128)(2,1)S(1)} %get-tuple-element.205), channel_id=1, source_target_pairs={{0,80},{16,64},{32,112},{48,96},{64,16},{80,0},{96,48},{112,32},{1... | collective-permute-start | bytes 294920 | tf_op jit(solution)/shard_map/ppermute | solution.py:497
  159.2 1.4 collective-permute-start.41
  160.6 2.0 %place.1 = (bf16[384,3072]{1,0:T(8,128)(2,1)}, bf16[3072,384]{1,0:T(8,128)(2,1)}) custom-call(s32[1]{0:T(128)} %bitcast.1._.core.refs_0_, bf16[384,3072]{1,0:T(8,128)(2,1)} %get-tuple-element.207.wi, bf16[3072,384]{1,0:T(8,128)(2,1)} %get-tuple-element.208.wo, ...), custom_call_target="tpu_custom_call", output_to_operand_aliasing={{0}: (1, {}), {1}: (2, {})} | custom-call | flops 115000000 | bytes 369000 | tf_op jit(solution)/shard_map/place/pallas_call | solution.py:50
  162.6 1.3 collective-permute-done.40
  163.9 2.5 %collective-permute-done.41 = bf16[4,32,384]{2,1,0:T(8,128)(2,1)} collective-permute-done((bf16[4,32,384]{2,1,0:T(8,128)(2,1)S(1)}, bf16[4,32,384]{2,1,0:T(8,128)(2,1)}, u32[]{:S(2)}, u32[]{:S(2)}) %collective-permute-start.41) | collective-permute-done | bytes 98336 | tf_op jit(solution)/shard_map/ppermute | solution.py:497
  166.4 1.0 convert_add_fusion
  167.4 0.7 fusion.1
  (62 shorter events, 3.5 us)
Async XLA Ops:
  1.7 12.9 %collective-permute-start.2 = (bf16[4,32,768]{2,1,0:T(8,128)(2,1)S(1)}, bf16[4,32,768]{2,1,0:T(8,128)(2,1)S(1)}, u32[]{:S(2)}, u32[]{:S(2)}) collective-permute-start(bf16[4,32,768]{2,1,0:T(8,128)(2,1)S(1)} %fusion.2.refs_0_), channel_id=1, source_target_pairs={{0,32},{32,64},{64,96},{96,0},{1,33},{33,65},{65,97},{97,1},{2,34}... | collective-permute-start | bytes 589832 | tf_op jit(solution)/shard_map/ppermute | solution.py:26
  3.4 11.7 %collective-permute-start.1 = (bf16[4,32,768]{2,1,0:T(8,128)(2,1)S(1)}, bf16[4,32,768]{2,1,0:T(8,128)(2,1)S(1)}, u32[]{:S(2)}, u32[]{:S(2)}) collective-permute-start(bf16[4,32,768]{2,1,0:T(8,128)(2,1)S(1)} %fusion.2.refs_0_), channel_id=1, source_target_pairs={{0,64},{32,96},{64,0},{96,32},{1,65},{33,97},{65,1},{97,33},{2,66}... | collective-permute-start | bytes 589832 | tf_op jit(solution)/shard_map/ppermute | solution.py:26
  6.3 8.8 %collective-permute-start = (bf16[4,32,768]{2,1,0:T(8,128)(2,1)S(1)}, bf16[4,32,768]{2,1,0:T(8,128)(2,1)S(1)}, u32[]{:S(2)}, u32[]{:S(2)}) collective-permute-start(bf16[4,32,768]{2,1,0:T(8,128)(2,1)S(1)} %fusion.2.refs_0_), channel_id=1, source_target_pairs={{0,96},{32,0},{64,32},{96,64},{1,97},{33,1},{65,33},{97,65},{2,98}... | collective-permute-start | bytes 589832 | tf_op jit(solution)/shard_map/ppermute | solution.py:26
  7.7 7.5 %collective-permute-start.4 = (bf16[4,32,768]{2,1,0:T(8,128)(2,1)S(1)}, bf16[4,32,768]{2,1,0:T(8,128)(2,1)S(1)}, u32[]{:S(2)}, u32[]{:S(2)}) collective-permute-start(bf16[4,32,768]{2,1,0:T(8,128)(2,1)S(1)} %fusion.2.refs_0_), channel_id=1, source_target_pairs={{0,16},{16,0},{1,17},{17,1},{2,18},{18,2},{3,19},{19,3},{4,20},{20... | collective-permute-start | bytes 589832 | tf_op jit(solution)/shard_map/ppermute | solution.py:26
  14.6 6.4 %copy-start.2 = (bf16[384,3072]{1,0:T(8,128)(2,1)S(1)}, bf16[384,3072]{1,0:T(8,128)(2,1)}, u32[]{:S(2)}) copy-start(bf16[384,3072]{1,0:T(8,128)(2,1)} %wi.2) | copy-start | bytes 7077892
  14.6 6.4 %copy-start.3 = (bf16[3072,384]{1,0:T(8,128)(2,1)S(1)}, bf16[3072,384]{1,0:T(8,128)(2,1)}, u32[]{:S(2)}) copy-start(bf16[3072,384]{1,0:T(8,128)(2,1)} %wo.2) | copy-start | bytes 7077892
  14.6 6.4 %collective-permute-start.8 = (bf16[2,4,384,384]{3,2,1,0:T(8,128)(2,1)}, bf16[2,4,384,384]{3,2,1,0:T(8,128)(2,1)S(1)}, u32[]{:S(2)}, u32[]{:S(2)}) collective-permute-start(bf16[2,4,384,384]{3,2,1,0:T(8,128)(2,1)} %pack.1), channel_id=1, source_target_pairs={{0,1},{1,0},{2,3},{3,2},{4,5},{5,4},{6,7},{7,6},{8,9},{9,8},{10,11... | collective-permute-start | bytes 7077896 | tf_op jit(solution)/shard_map/ppermute | solution.py:26
  15.2 4.2 %collective-permute-start.9 = (bf16[4,32,768]{2,1,0:T(8,128)(2,1)S(1)}, bf16[4,32,768]{2,1,0:T(8,128)(2,1)S(1)}, u32[]{:S(2)}, u32[]{:S(2)}) collective-permute-start(bf16[4,32,768]{2,1,0:T(8,128)(2,1)S(1)} %collective-permute-done.4.refs_0_), channel_id=1, source_target_pairs={{0,1},{1,0},{2,3},{3,2},{4,5},{5,4},{6,7},{7,6},{8,9},{9,8},{10,11... | collective-permute-start | bytes 589832 | tf_op jit(solution)/shard_map/ppermute | solution.py:26
  15.3 6.3 %collective-permute-start.3 = (bf16[512,768]{1,0:T(8,128)(2,1)S(1)}, bf16[512,768]{1,0:T(8,128)(2,1)S(1)}, u32[]{:S(2)}, u32[]{:S(2)}) collective-permute-start(bf16[512,768]{1,0:T(8,128)(2,1)S(1)} %join_a.1.own), channel_id=1, source_target_pairs={{0,1},{1,0},{2,3},{3,2},{4,5},{5,4},{6,7},{7,6},{8,9},{9,8},{10,11... | collective-permute-start | bytes 2359304 | tf_op jit(solution)/shard_map/ppermute | solution.py:26
  15.8 11.7 %collective-permute-start.7 = (bf16[4,32,768]{2,1,0:T(8,128)(2,1)S(1)}, bf16[4,32,768]{2,1,0:T(8,128)(2,1)S(1)}, u32[]{:S(2)}, u32[]{:S(2)}) collective-permute-start(bf16[4,32,768]{2,1,0:T(8,128)(2,1)S(1)} %collective-permute-done.4.refs_0_), channel_id=1, source_target_pairs={{0,32},{32,64},{64,96},{96,0},{1,33},{33,65},{65,97},{97,1},{2,34}... | collective-permute-start | bytes 589832 | tf_op jit(solution)/shard_map/ppermute | solution.py:26
  17.1 11.5 %collective-permute-start.6 = (bf16[4,32,768]{2,1,0:T(8,128)(2,1)S(1)}, bf16[4,32,768]{2,1,0:T(8,128)(2,1)S(1)}, u32[]{:S(2)}, u32[]{:S(2)}) collective-permute-start(bf16[4,32,768]{2,1,0:T(8,128)(2,1)S(1)} %collective-permute-done.4.refs_0_), channel_id=1, source_target_pairs={{0,64},{32,96},{64,0},{96,32},{1,65},{33,97},{65,1},{97,33},{2,66}... | collective-permute-start | bytes 589832 | tf_op jit(solution)/shard_map/ppermute | solution.py:26
  19.5 9.3 %collective-permute-start.5 = (bf16[4,32,768]{2,1,0:T(8,128)(2,1)S(1)}, bf16[4,32,768]{2,1,0:T(8,128)(2,1)S(1)}, u32[]{:S(2)}, u32[]{:S(2)}) collective-permute-start(bf16[4,32,768]{2,1,0:T(8,128)(2,1)S(1)} %collective-permute-done.4.refs_0_), channel_id=1, source_target_pairs={{0,96},{32,0},{64,32},{96,64},{1,97},{33,1},{65,33},{97,65},{2,98}... | collective-permute-start | bytes 589832 | tf_op jit(solution)/shard_map/ppermute | solution.py:26
  23.5 17.0 %collective-permute-start.14 = (bf16[128,1536]{1,0:T(8,128)(2,1)S(1)}, bf16[128,1536]{1,0:T(8,128)(2,1)S(1)}, u32[]{:S(2)}, u32[]{:S(2)}) collective-permute-start(bf16[128,1536]{1,0:T(8,128)(2,1)S(1)} %get-tuple-element.126), channel_id=1, source_target_pairs={{0,6},{2,0},{4,2},{6,4},{1,7},{3,1},{5,3},{7,5},{8,14},{10,8},{12,... | collective-permute-start | bytes 1179656 | tf_op jit(solution)/shard_map/ppermute | solution.py:26
  27.6 12.9 %collective-permute-start.13 = (bf16[128,1536]{1,0:T(8,128)(2,1)S(1)}, bf16[128,1536]{1,0:T(8,128)(2,1)S(1)}, u32[]{:S(2)}, u32[]{:S(2)}) collective-permute-start(bf16[128,1536]{1,0:T(8,128)(2,1)S(1)} %get-tuple-element.116), channel_id=1, source_target_pairs={{0,2},{2,4},{4,6},{6,0},{1,3},{3,5},{5,7},{7,1},{8,10},{10,12},{12... | collective-permute-start | bytes 1179656 | tf_op jit(solution)/shard_map/ppermute | solution.py:26
  28.8 1.4 collective-permute-start.10
  28.8 1.7 %collective-permute-start.11 = (bf16[4,32,768]{2,1,0:T(8,128)(2,1)S(1)}, bf16[4,32,768]{2,1,0:T(8,128)(2,1)S(1)}, u32[]{:S(2)}, u32[]{:S(2)}) collective-permute-start(bf16[4,32,768]{2,1,0:T(8,128)(2,1)S(1)} %collective-permute-done.6.refs_2_), channel_id=1, source_target_pairs={{0,1},{1,0},{2,3},{3,2},{4,5},{5,4},{6,7},{7,6},{8,9},{9,8},{10,11... | collective-permute-start | bytes 589832 | tf_op jit(solution)/shard_map/ppermute | solution.py:26
  29.3 1.5 collective-permute-start.12
  32.7 15.5 %collective-permute-start.18 = (bf16[128,1536]{1,0:T(8,128)(2,1)S(1)}, bf16[128,1536]{1,0:T(8,128)(2,1)S(1)}, u32[]{:S(2)}, u32[]{:S(2)}) collective-permute-start(bf16[128,1536]{1,0:T(8,128)(2,1)S(1)} %get-tuple-element.134), channel_id=1, source_target_pairs={{0,6},{2,0},{4,2},{6,4},{1,7},{3,1},{5,3},{7,5},{8,14},{10,8},{12,... | collective-permute-start | bytes 1179656 | tf_op jit(solution)/shard_map/ppermute | solution.py:26
  36.8 13.2 %collective-permute-start.17 = (bf16[128,1536]{1,0:T(8,128)(2,1)S(1)}, bf16[128,1536]{1,0:T(8,128)(2,1)S(1)}, u32[]{:S(2)}, u32[]{:S(2)}) collective-permute-start(bf16[128,1536]{1,0:T(8,128)(2,1)S(1)} %get-tuple-element.122), channel_id=1, source_target_pairs={{0,2},{2,4},{4,6},{6,0},{1,3},{3,5},{5,7},{7,1},{8,10},{10,12},{12... | collective-permute-start | bytes 1179656 | tf_op jit(solution)/shard_map/ppermute | solution.py:26
  41.1 25.7 %collective-permute-start.15 = (bf16[2,128,1536]{2,1,0:T(8,128)(2,1)S(1)}, bf16[2,128,1536]{2,1,0:T(8,128)(2,1)S(1)}, u32[]{:S(2)}, u32[]{:S(2)}) collective-permute-start(bf16[2,128,1536]{2,1,0:T(8,128)(2,1)S(1)} %get-tuple-element.129), channel_id=1, source_target_pairs={{0,2},{2,4},{4,6},{6,0},{1,3},{3,5},{5,7},{7,1},{8,10},{10,12},{12... | collective-permute-start | bytes 2359304 | tf_op jit(solution)/shard_map/ppermute | solution.py:26
  41.2 25.6 %collective-permute-start.16 = (bf16[2,128,1536]{2,1,0:T(8,128)(2,1)S(1)}, bf16[2,128,1536]{2,1,0:T(8,128)(2,1)S(1)}, u32[]{:S(2)}, u32[]{:S(2)}) collective-permute-start(bf16[2,128,1536]{2,1,0:T(8,128)(2,1)S(1)} %get-tuple-element.130), channel_id=1, source_target_pairs={{0,6},{2,0},{4,2},{6,4},{1,7},{3,1},{5,3},{7,5},{8,14},{10,8},{12,... | collective-permute-start | bytes 2359304 | tf_op jit(solution)/shard_map/ppermute | solution.py:26
  50.6 32.0 %collective-permute-start.20 = (bf16[2,128,1536]{2,1,0:T(8,128)(2,1)S(1)}, bf16[2,128,1536]{2,1,0:T(8,128)(2,1)S(1)}, u32[]{:S(2)}, u32[]{:S(2)}) collective-permute-start(bf16[2,128,1536]{2,1,0:T(8,128)(2,1)S(1)} %get-tuple-element.137), channel_id=1, source_target_pairs={{0,2},{2,4},{4,6},{6,0},{1,3},{3,5},{5,7},{7,1},{8,10},{10,12},{12... | collective-permute-start | bytes 2359304 | tf_op jit(solution)/shard_map/ppermute | solution.py:26
  50.7 32.0 %collective-permute-start.21 = (bf16[2,128,1536]{2,1,0:T(8,128)(2,1)S(1)}, bf16[2,128,1536]{2,1,0:T(8,128)(2,1)S(1)}, u32[]{:S(2)}, u32[]{:S(2)}) collective-permute-start(bf16[2,128,1536]{2,1,0:T(8,128)(2,1)S(1)} %get-tuple-element.138), channel_id=1, source_target_pairs={{0,6},{2,0},{4,2},{6,4},{1,7},{3,1},{5,3},{7,5},{8,14},{10,8},{12,... | collective-permute-start | bytes 2359304 | tf_op jit(solution)/shard_map/ppermute | solution.py:26
  67.6 17.6 %collective-permute-start.19 = (bf16[2,128,1536]{2,1,0:T(8,128)(2,1)S(1)}, bf16[2,128,1536]{2,1,0:T(8,128)(2,1)S(1)}, u32[]{:S(2)}, u32[]{:S(2)}) collective-permute-start(bf16[2,128,1536]{2,1,0:T(8,128)(2,1)S(1)} %get-tuple-element.142), channel_id=1, source_target_pairs={{0,8},{8,0},{1,9},{9,1},{2,10},{10,2},{3,11},{11,3},{4,12},{12,4},... | collective-permute-start | bytes 2359304 | tf_op jit(solution)/shard_map/ppermute | solution.py:26
  83.4 18.8 %collective-permute-start.24 = (bf16[2,128,1536]{2,1,0:T(8,128)(2,1)S(1)}, bf16[2,128,1536]{2,1,0:T(8,128)(2,1)S(1)}, u32[]{:S(2)}, u32[]{:S(2)}) collective-permute-start(bf16[2,128,1536]{2,1,0:T(8,128)(2,1)S(1)} %get-tuple-element.145), channel_id=1, source_target_pairs={{0,8},{8,0},{1,9},{9,1},{2,10},{10,2},{3,11},{11,3},{4,12},{12,4},... | collective-permute-start | bytes 2359304 | tf_op jit(solution)/shard_map/ppermute | solution.py:26
  85.9 20.3 %collective-permute-start.23 = (bf16[2,128,1536]{2,1,0:T(8,128)(2,1)S(1)}, bf16[2,128,1536]{2,1,0:T(8,128)(2,1)S(1)}, u32[]{:S(2)}, u32[]{:S(2)}) collective-permute-start(bf16[2,128,1536]{2,1,0:T(8,128)(2,1)S(1)} %hidden.2.mine.refs_6_.refs_9_), channel_id=1, source_target_pairs={{0,2},{2,4},{4,6},{6,0},{1,3},{3,5},{5,7},{7,1},{8,10},{10,12},{12... | collective-permute-start | bytes 2359304 | tf_op jit(solution)/shard_map/ppermute | solution.py:26
  86.0 20.3 %collective-permute-start.22 = (bf16[2,128,1536]{2,1,0:T(8,128)(2,1)S(1)}, bf16[2,128,1536]{2,1,0:T(8,128)(2,1)S(1)}, u32[]{:S(2)}, u32[]{:S(2)}) collective-permute-start(bf16[2,128,1536]{2,1,0:T(8,128)(2,1)S(1)} %hidden.2.mine.refs_6_.refs_9_), channel_id=1, source_target_pairs={{0,6},{2,0},{4,2},{6,4},{1,7},{3,1},{5,3},{7,5},{8,14},{10,8},{12,... | collective-permute-start | bytes 2359304 | tf_op jit(solution)/shard_map/ppermute | solution.py:26
  103.0 21.8 %collective-permute-start.28 = (bf16[2,128,1536]{2,1,0:T(8,128)(2,1)S(1)}, bf16[2,128,1536]{2,1,0:T(8,128)(2,1)S(1)}, u32[]{:S(2)}, u32[]{:S(2)}) collective-permute-start(bf16[2,128,1536]{2,1,0:T(8,128)(2,1)S(1)} %hidden.3.mine.refs_6_.refs_9_), channel_id=1, source_target_pairs={{0,2},{2,4},{4,6},{6,0},{1,3},{3,5},{5,7},{7,1},{8,10},{10,12},{12... | collective-permute-start | bytes 2359304 | tf_op jit(solution)/shard_map/ppermute | solution.py:26
  103.0 21.7 %collective-permute-start.27 = (bf16[2,128,1536]{2,1,0:T(8,128)(2,1)S(1)}, bf16[2,128,1536]{2,1,0:T(8,128)(2,1)S(1)}, u32[]{:S(2)}, u32[]{:S(2)}) collective-permute-start(bf16[2,128,1536]{2,1,0:T(8,128)(2,1)S(1)} %hidden.3.mine.refs_6_.refs_9_), channel_id=1, source_target_pairs={{0,6},{2,0},{4,2},{6,4},{1,7},{3,1},{5,3},{7,5},{8,14},{10,8},{12,... | collective-permute-start | bytes 2359304 | tf_op jit(solution)/shard_map/ppermute | solution.py:26
  106.3 28.2 %collective-permute-start.26 = (bf16[128,1536]{1,0:T(8,128)(2,1)S(1)}, bf16[128,1536]{1,0:T(8,128)(2,1)S(1)}, u32[]{:S(2)}, u32[]{:S(2)}) collective-permute-start(bf16[128,1536]{1,0:T(8,128)(2,1)S(1)} %get-tuple-element.156), channel_id=1, source_target_pairs={{0,2},{2,4},{4,6},{6,0},{1,3},{3,5},{5,7},{7,1},{8,10},{10,12},{12... | collective-permute-start | bytes 1179656 | tf_op jit(solution)/shard_map/ppermute | solution.py:26
  106.4 28.1 %collective-permute-start.25 = (bf16[128,1536]{1,0:T(8,128)(2,1)S(1)}, bf16[128,1536]{1,0:T(8,128)(2,1)S(1)}, u32[]{:S(2)}, u32[]{:S(2)}) collective-permute-start(bf16[128,1536]{1,0:T(8,128)(2,1)S(1)} %get-tuple-element.151), channel_id=1, source_target_pairs={{0,6},{2,0},{4,2},{6,4},{1,7},{3,1},{5,3},{7,5},{8,14},{10,8},{12,... | collective-permute-start | bytes 1179656 | tf_op jit(solution)/shard_map/ppermute | solution.py:26
  115.7 2.2 %copy-start = (f32[768,1536]{1,0:T(8,128)}, f32[768,1536]{1,0:T(8,128)S(1)}, u32[]{:S(2)}) copy-start(f32[768,1536]{1,0:T(8,128)S(1)} %get-tuple-element.164.refs_12_) | copy-start | bytes 14155780
  124.8 14.4 %collective-permute-start.33 = (bf16[128,1536]{1,0:T(8,128)(2,1)S(1)}, bf16[128,1536]{1,0:T(8,128)(2,1)S(1)}, u32[]{:S(2)}, u32[]{:S(2)}) collective-permute-start(bf16[128,1536]{1,0:T(8,128)(2,1)S(1)} %get-tuple-element.184), channel_id=1, source_target_pairs={{0,2},{2,4},{4,6},{6,0},{1,3},{3,5},{5,7},{7,1},{8,10},{10,12},{12... | collective-permute-start | bytes 1179656 | tf_op jit(solution)/shard_map/ppermute | solution.py:26
  124.9 5.6 %copy-start.1 = (f32[768,1536]{1,0:T(8,128)S(1)}, f32[768,1536]{1,0:T(8,128)}, u32[]{:S(2)}) copy-start(f32[768,1536]{1,0:T(8,128)} %copy-done) | copy-start | bytes 14155780
  124.9 14.3 %collective-permute-start.32 = (bf16[128,1536]{1,0:T(8,128)(2,1)S(1)}, bf16[128,1536]{1,0:T(8,128)(2,1)S(1)}, u32[]{:S(2)}, u32[]{:S(2)}) collective-permute-start(bf16[128,1536]{1,0:T(8,128)(2,1)S(1)} %get-tuple-element.168), channel_id=1, source_target_pairs={{0,6},{2,0},{4,2},{6,4},{1,7},{3,1},{5,3},{7,5},{8,14},{10,8},{12,... | collective-permute-start | bytes 1179656 | tf_op jit(solution)/shard_map/ppermute | solution.py:26
  135.5 1.6 collective-permute-start.29
  135.6 1.9 %collective-permute-start.30 = (f32[512,128]{1,0:T(8,128)S(1)}, f32[512,128]{1,0:T(8,128)S(1)}, u32[]{:S(2)}, u32[]{:S(2)}) collective-permute-start(f32[512,128]{1,0:T(8,128)S(1)} %get-tuple-element.181), channel_id=1, source_target_pairs={{0,1},{1,0},{2,3},{3,2},{4,5},{5,4},{6,7},{7,6},{8,9},{9,8},{10,11... | collective-permute-start | bytes 786440 | tf_op jit(solution)/shard_map/ppermute | solution.py:26
  136.1 1.8 %collective-permute-start.31 = (f32[512,128]{1,0:T(8,128)S(1)}, f32[512,128]{1,0:T(8,128)S(1)}, u32[]{:S(2)}, u32[]{:S(2)}) collective-permute-start(f32[512,128]{1,0:T(8,128)S(1)} %get-tuple-element.182), channel_id=1, source_target_pairs={{0,1},{1,0},{2,3},{3,2},{4,5},{5,4},{6,7},{7,6},{8,9},{9,8},{10,11... | collective-permute-start | bytes 786440 | tf_op jit(solution)/shard_map/ppermute | solution.py:26
  140.1 9.5 %collective-permute-start.34 = (f32[512,384]{1,0:T(8,128)S(1)}, f32[512,384]{1,0:T(8,128)S(1)}, u32[]{:S(2)}, u32[]{:S(2)}) collective-permute-start(f32[512,384]{1,0:T(8,128)S(1)} %get-tuple-element.186), channel_id=1, source_target_pairs={{0,1},{1,0},{2,3},{3,2},{4,5},{5,4},{6,7},{7,6},{8,9},{9,8},{10,11... | collective-permute-start | bytes 2359304 | tf_op jit(solution)/shard_map/ppermute | solution.py:26
  140.2 8.8 %collective-permute-start.35 = (bf16[4,32,384]{2,1,0:T(8,128)(2,1)S(1)}, bf16[4,32,384]{2,1,0:T(8,128)(2,1)S(1)}, u32[]{:S(2)}, u32[]{:S(2)}) collective-permute-start(bf16[4,32,384]{2,1,0:T(8,128)(2,1)S(1)} %get-tuple-element.187), channel_id=1, source_target_pairs={{0,32},{32,64},{64,96},{96,0},{1,33},{33,65},{65,97},{97,1},{2,34}... | collective-permute-start | bytes 294920 | tf_op jit(solution)/shard_map/ppermute | solution.py:26
  142.0 7.6 %collective-permute-start.36 = (bf16[4,32,384]{2,1,0:T(8,128)(2,1)S(1)}, bf16[4,32,384]{2,1,0:T(8,128)(2,1)S(1)}, u32[]{:S(2)}, u32[]{:S(2)}) collective-permute-start(bf16[4,32,384]{2,1,0:T(8,128)(2,1)S(1)} %get-tuple-element.188), channel_id=1, source_target_pairs={{0,64},{32,96},{64,0},{96,32},{1,65},{33,97},{65,1},{97,33},{2,66}... | collective-permute-start | bytes 294920 | tf_op jit(solution)/shard_map/ppermute | solution.py:26
  144.4 5.2 %collective-permute-start.37 = (bf16[4,32,384]{2,1,0:T(8,128)(2,1)S(1)}, bf16[4,32,384]{2,1,0:T(8,128)(2,1)S(1)}, u32[]{:S(2)}, u32[]{:S(2)}) collective-permute-start(bf16[4,32,384]{2,1,0:T(8,128)(2,1)S(1)} %get-tuple-element.189), channel_id=1, source_target_pairs={{0,96},{32,0},{64,32},{96,64},{1,97},{33,1},{65,33},{97,65},{2,98}... | collective-permute-start | bytes 294920 | tf_op jit(solution)/shard_map/ppermute | solution.py:26
  149.7 9.6 %collective-permute-start.42 = (bf16[384,1536]{1,0:T(8,128)(2,1)S(1)}, bf16[384,1536]{1,0:T(8,128)(2,1)S(1)}, u32[]{:S(2)}, u32[]{:S(2)}) collective-permute-start(bf16[384,1536]{1,0:T(8,128)(2,1)S(1)} %get-tuple-element.209), channel_id=1, source_target_pairs={{0,1},{1,0},{2,3},{3,2},{4,5},{5,4},{6,7},{7,6},{8,9},{9,8},{10,11... | collective-permute-start | bytes 3538952 | tf_op jit(solution)/shard_map/ppermute | solution.py:26
  149.8 10.8 %collective-permute-start.43 = (bf16[1536,384]{1,0:T(8,128)(2,1)}, bf16[1536,384]{1,0:T(8,128)(2,1)S(1)}, u32[]{:S(2)}, u32[]{:S(2)}) collective-permute-start(bf16[1536,384]{1,0:T(8,128)(2,1)} %get-tuple-element.210), channel_id=1, source_target_pairs={{0,1},{1,0},{2,3},{3,2},{4,5},{5,4},{6,7},{7,6},{8,9},{9,8},{10,11... | collective-permute-start | bytes 3538952 | tf_op jit(solution)/shard_map/ppermute | solution.py:26
  150.3 12.3 %collective-permute-start.38 = (bf16[4,32,384]{2,1,0:T(8,128)(2,1)S(1)}, bf16[4,32,384]{2,1,0:T(8,128)(2,1)S(1)}, u32[]{:S(2)}, u32[]{:S(2)}) collective-permute-start(bf16[4,32,384]{2,1,0:T(8,128)(2,1)S(1)} %get-tuple-element.203), channel_id=1, source_target_pairs={{0,16},{16,0},{32,48},{48,32},{64,80},{80,64},{96,112},{112,96},{1... | collective-permute-start | bytes 294920 | tf_op jit(solution)/shard_map/ppermute | solution.py:497
  153.0 9.6 %collective-permute-start.39 = (bf16[4,32,384]{2,1,0:T(8,128)(2,1)S(1)}, bf16[4,32,384]{2,1,0:T(8,128)(2,1)S(1)}, u32[]{:S(2)}, u32[]{:S(2)}) collective-permute-start(bf16[4,32,384]{2,1,0:T(8,128)(2,1)S(1)} %get-tuple-element.204), channel_id=1, source_target_pairs={{0,48},{16,32},{32,80},{48,64},{64,112},{80,96},{96,16},{112,0},{1... | collective-permute-start | bytes 294920 | tf_op jit(solution)/shard_map/ppermute | solution.py:497
  154.7 9.2 %collective-permute-start.40 = (bf16[4,32,384]{2,1,0:T(8,128)(2,1)S(1)}, bf16[4,32,384]{2,1,0:T(8,128)(2,1)S(1)}, u32[]{:S(2)}, u32[]{:S(2)}) collective-permute-start(bf16[4,32,384]{2,1,0:T(8,128)(2,1)S(1)} %get-tuple-element.205), channel_id=1, source_target_pairs={{0,80},{16,64},{32,112},{48,96},{64,16},{80,0},{96,48},{112,32},{1... | collective-permute-start | bytes 294920 | tf_op jit(solution)/shard_map/ppermute | solution.py:497
  159.2 7.1 %collective-permute-start.41 = (bf16[4,32,384]{2,1,0:T(8,128)(2,1)S(1)}, bf16[4,32,384]{2,1,0:T(8,128)(2,1)}, u32[]{:S(2)}, u32[]{:S(2)}) collective-permute-start(bf16[4,32,384]{2,1,0:T(8,128)(2,1)S(1)} %get-tuple-element.206), channel_id=1, source_target_pairs={{0,112},{16,96},{32,16},{48,0},{64,48},{80,32},{96,80},{112,64},{1... | collective-permute-start | bytes 294920 | tf_op jit(solution)/shard_map/ppermute | solution.py:497

commit v10 on v9

--- a/solution.py
+++ b/solution.py
@@ -12,7 +12,7 @@
 COLS = ("xl", "z", "core")
 F32 = jnp.float32
 BF16 = jnp.bfloat16
-STEPS = 3
+STEPS = 2
 
 
 def gelu_parts(pre):

time: 168 us -> 168 us (level)
  Pallas kernels: 39.7 us -> 37.7 us
    pallas_call x26, Pallas kernels: 39.7 us -> 37.7 us  [kernel(): pl.pallas_call(body, name=name, grid_spec=pltpu.PrefetchScalarGridSpec(nu...]
  transfers between devices with their start and end apart: 44 -> 44, of which waited for: 18 -> 19; matrix products, arithmetic and copies ran while one was open for 0% -> 0% of each run, Pallas kernels for 23% -> 22%
where the time goes in v10:
time: 168 us
  starting transfers between devices  64 us (38%)
  waiting for transfers between devices  59.9 us (36%)
  Pallas kernels  37.7 us (22%)
  other arithmetic  2.75 us (2%)
  local copies, waits for them, and re-layouts  2.18 us (1%)
    ppermute x40, waiting for transfers between devices, shift(): return lax.ppermute(x, axis, [(i, (i + by) % n) for i in range(n)])  55.8 us
    ppermute x40, starting transfers between devices, shift(): return lax.ppermute(x, axis, [(i, (i + by) % n) for i in range(n)])  53.7 us
    pallas_call x26, Pallas kernels, kernel(): pl.pallas_call(body, name=name, grid_spec=pltpu.PrefetchScalarGridSpec(nu...  37.7 us
    ppermute x4, starting transfers between devices, local(): lax.ppermute(a, ROWS, [(i, (i // 2 + d) % 4 * 2 + (i + 1) % 2) for i in r...  10.4 us
    ppermute x4, waiting for transfers between devices, local(): lax.ppermute(a, ROWS, [(i, (i // 2 + d) % 4 * 2 + (i + 1) % 2) for i in r...  4.13 us
  transfers between devices with their start and end apart: 44, of which 19 were waited for; matrix products, arithmetic and copies ran while one was open for 0% of the time, Pallas kernels for 22%

profile of v10, /device:TPU:0, one launch (start us, length us, event | category | flops | bytes accessed | tf_op | source)
XLA Modules:
  0.0 167.6 jit_solution(4643416515695445455)
XLA Ops:
  0.7 1.0 pad_maximum_fusion
  1.7 1.7 %collective-permute-start.2 = (bf16[4,32,768]{2,1,0:T(8,128)(2,1)S(1)}, bf16[4,32,768]{2,1,0:T(8,128)(2,1)S(1)}, u32[]{:S(2)}, u32[]{:S(2)}) collective-permute-start(bf16[4,32,768]{2,1,0:T(8,128)(2,1)S(1)} %fusion.2.refs_0_), channel_id=1, source_target_pairs={{0,32},{32,64},{64,96},{96,0},{1,33},{33,65},{65,97},{97,1},{2,34}... | collective-permute-start | bytes 589832 | tf_op jit(solution)/shard_map/ppermute | solution.py:26
  3.4 2.9 %collective-permute-start.1 = (bf16[4,32,768]{2,1,0:T(8,128)(2,1)S(1)}, bf16[4,32,768]{2,1,0:T(8,128)(2,1)S(1)}, u32[]{:S(2)}, u32[]{:S(2)}) collective-permute-start(bf16[4,32,768]{2,1,0:T(8,128)(2,1)S(1)} %fusion.2.refs_0_), channel_id=1, source_target_pairs={{0,64},{32,96},{64,0},{96,32},{1,65},{33,97},{65,1},{97,33},{2,66}... | collective-permute-start | bytes 589832 | tf_op jit(solution)/shard_map/ppermute | solution.py:26
  6.3 1.3 collective-permute-start
  7.7 3.0 %collective-permute-start.4 = (bf16[4,32,768]{2,1,0:T(8,128)(2,1)S(1)}, bf16[4,32,768]{2,1,0:T(8,128)(2,1)S(1)}, u32[]{:S(2)}, u32[]{:S(2)}) collective-permute-start(bf16[4,32,768]{2,1,0:T(8,128)(2,1)S(1)} %fusion.2.refs_0_), channel_id=1, source_target_pairs={{0,16},{16,0},{1,17},{17,1},{2,18},{18,2},{3,19},{19,3},{4,20},{20... | collective-permute-start | bytes 589832 | tf_op jit(solution)/shard_map/ppermute | solution.py:26
  10.7 3.9 %pack.1 = bf16[2,4,384,384]{3,2,1,0:T(8,128)(2,1)} custom-call(s32[1]{0:T(128)} %bitcast.1._.core.refs_0_, bf16[384,3072]{1,0:T(8,128)(2,1)} %wi.2, bf16[3072,384]{1,0:T(8,128)(2,1)} %wo.2), custom_call_target="tpu_custom_call" | custom-call | flops 115000000 | bytes 369000 | tf_op jit(solution)/shard_map/pack/pallas_call | solution.py:50
  14.6 0.5 collective-permute-done.1.refs_2_
  15.3 0.5 collective-permute-start.3
  15.8 1.2 collective-permute-start.7
  17.1 2.4 %collective-permute-start.6 = (bf16[4,32,768]{2,1,0:T(8,128)(2,1)S(1)}, bf16[4,32,768]{2,1,0:T(8,128)(2,1)S(1)}, u32[]{:S(2)}, u32[]{:S(2)}) collective-permute-start(bf16[4,32,768]{2,1,0:T(8,128)(2,1)S(1)} %collective-permute-done.4.refs_0_), channel_id=1, source_target_pairs={{0,64},{32,96},{64,0},{96,32},{1,65},{33,97},{65,1},{97,33},{2,66}... | collective-permute-start | bytes 589832 | tf_op jit(solution)/shard_map/ppermute | solution.py:26
  19.5 1.6 collective-permute-start.5
  21.1 0.6 weights.1
  21.6 1.6 first_block.2
  23.2 4.1 %collective-permute-start.14 = (bf16[128,1536]{1,0:T(8,128)(2,1)S(1)}, bf16[128,1536]{1,0:T(8,128)(2,1)S(1)}, u32[]{:S(2)}, u32[]{:S(2)}) collective-permute-start(bf16[128,1536]{1,0:T(8,128)(2,1)S(1)} %get-tuple-element.126), channel_id=1, source_target_pairs={{0,6},{2,0},{4,2},{6,4},{1,7},{3,1},{5,3},{7,5},{8,14},{10,8},{12,... | collective-permute-start | bytes 1179656 | tf_op jit(solution)/shard_map/ppermute | solution.py:26
  27.3 1.2 collective-permute-done.6.refs_2_
  28.8 0.5 collective-permute-start.11
  29.3 0.9 collective-permute-done.10.refs_5_
  30.9 1.6 first_block.3
  32.4 4.1 %collective-permute-start.18 = (bf16[128,1536]{1,0:T(8,128)(2,1)S(1)}, bf16[128,1536]{1,0:T(8,128)(2,1)S(1)}, u32[]{:S(2)}, u32[]{:S(2)}) collective-permute-start(bf16[128,1536]{1,0:T(8,128)(2,1)S(1)} %get-tuple-element.134), channel_id=1, source_target_pairs={{0,6},{2,0},{4,2},{6,4},{1,7},{3,1},{5,3},{7,5},{8,14},{10,8},{12,... | collective-permute-start | bytes 1179656 | tf_op jit(solution)/shard_map/ppermute | solution.py:26
  36.5 3.5 %products.2 = (f32[2,512,1536]{2,1,0:T(8,128)S(1)}, bf16[512,768]{1,0:T(8,128)(2,1)S(1)}, bf16[512,768]{1,0:T(8,128)(2,1)S(1)}) custom-call(bf16[512,768]{1,0:T(8,128)(2,1)S(1)} %join_a.1.own, bf16[512,768]{1,0:T(8,128)(2,1)S(1)} %collective-permute-done.3.other, bf16[768,1536]{1,0:T(8,128)(2,1)S(1)} %get-tuple-element.114.wi, ...), custom_call_target="tpu_custom_call" | custom-call | flops 115000000 | bytes 369000 | tf_op jit(solution)/shard_map/products/pallas_call | solution.py:50
  40.1 0.6 ring_add.2
  40.8 3.3 %collective-permute-start.16 = (bf16[2,128,1536]{2,1,0:T(8,128)(2,1)S(1)}, bf16[2,128,1536]{2,1,0:T(8,128)(2,1)S(1)}, u32[]{:S(2)}, u32[]{:S(2)}) collective-permute-start(bf16[2,128,1536]{2,1,0:T(8,128)(2,1)S(1)} %get-tuple-element.130), channel_id=1, source_target_pairs={{0,6},{2,0},{4,2},{6,4},{1,7},{3,1},{5,3},{7,5},{8,14},{10,8},{12,... | collective-permute-start | bytes 2359304 | tf_op jit(solution)/shard_map/ppermute | solution.py:26
  44.1 3.5 %products.3 = (f32[2,512,1536]{2,1,0:T(8,128)S(1)}, bf16[512,768]{1,0:T(8,128)(2,1)S(1)}, bf16[512,768]{1,0:T(8,128)(2,1)S(1)}) custom-call(bf16[512,768]{1,0:T(8,128)(2,1)S(1)} %get-tuple-element.131.own, bf16[512,768]{1,0:T(8,128)(2,1)S(1)} %get-tuple-element.132.other, bf16[768,1536]{1,0:T(8,128)(2,1)S(1)} %get-tuple-element.114.wi, ...), custom_call_target="tpu_custom_call" | custom-call | flops 115000000 | bytes 369000 | tf_op jit(solution)/shard_map/products/pallas_call | solution.py:50
  47.6 2.1 %collective-permute-done.17.up = bf16[128,1536]{1,0:T(8,128)(2,1)S(1)} collective-permute-done((bf16[128,1536]{1,0:T(8,128)(2,1)S(1)}, bf16[128,1536]{1,0:T(8,128)(2,1)S(1)}, u32[]{:S(2)}, u32[]{:S(2)}) %collective-permute-start.17) | collective-permute-done | bytes 393248 | tf_op jit(solution)/shard_map/ppermute | solution.py:26
  49.7 0.6 ring_add.3
  50.6 3.2 %collective-permute-start.21 = (bf16[2,128,1536]{2,1,0:T(8,128)(2,1)S(1)}, bf16[2,128,1536]{2,1,0:T(8,128)(2,1)S(1)}, u32[]{:S(2)}, u32[]{:S(2)}) collective-permute-start(bf16[2,128,1536]{2,1,0:T(8,128)(2,1)S(1)} %get-tuple-element.138), channel_id=1, source_target_pairs={{0,6},{2,0},{4,2},{6,4},{1,7},{3,1},{5,3},{7,5},{8,14},{10,8},{12,... | collective-permute-start | bytes 2359304 | tf_op jit(solution)/shard_map/ppermute | solution.py:26
  53.9 12.7 %collective-permute-done.15.up = bf16[2,128,1536]{2,1,0:T(8,128)(2,1)S(1)} collective-permute-done((bf16[2,128,1536]{2,1,0:T(8,128)(2,1)S(1)}, bf16[2,128,1536]{2,1,0:T(8,128)(2,1)S(1)}, u32[]{:S(2)}, u32[]{:S(2)}) %collective-permute-start.15) | collective-permute-done | bytes 786464 | tf_op jit(solution)/shard_map/ppermute | solution.py:26
  66.6 0.7 own_sum.2
  67.3 1.6 collective-permute-start.19
  68.9 13.5 %collective-permute-done.20.up = bf16[2,128,1536]{2,1,0:T(8,128)(2,1)S(1)} collective-permute-done((bf16[2,128,1536]{2,1,0:T(8,128)(2,1)S(1)}, bf16[2,128,1536]{2,1,0:T(8,128)(2,1)S(1)}, u32[]{:S(2)}, u32[]{:S(2)}) %collective-permute-start.20) | collective-permute-done | bytes 786464 | tf_op jit(solution)/shard_map/ppermute | solution.py:26
  82.4 0.7 own_sum.3
  83.1 1.6 collective-permute-start.24
  84.9 0.7 hidden.2.mine.refs_6_.refs_9_
  85.7 3.2 %collective-permute-start.22 = (bf16[2,128,1536]{2,1,0:T(8,128)(2,1)S(1)}, bf16[2,128,1536]{2,1,0:T(8,128)(2,1)S(1)}, u32[]{:S(2)}, u32[]{:S(2)}) collective-permute-start(bf16[2,128,1536]{2,1,0:T(8,128)(2,1)S(1)} %hidden.2.mine.refs_6_.refs_9_), channel_id=1, source_target_pairs={{0,6},{2,0},{4,2},{6,4},{1,7},{3,1},{5,3},{7,5},{8,14},{10,8},{12,... | collective-permute-start | bytes 2359304 | tf_op jit(solution)/shard_map/ppermute | solution.py:26
  88.9 12.8 %collective-permute-done.24.other = bf16[2,128,1536]{2,1,0:T(8,128)(2,1)S(1)} collective-permute-done((bf16[2,128,1536]{2,1,0:T(8,128)(2,1)S(1)}, bf16[2,128,1536]{2,1,0:T(8,128)(2,1)S(1)}, u32[]{:S(2)}, u32[]{:S(2)}) %collective-permute-start.24) | collective-permute-done | bytes 786464 | tf_op jit(solution)/shard_map/ppermute | solution.py:26
  101.8 0.7 hidden.3.mine.refs_6_.refs_9_
  102.6 3.2 %collective-permute-start.27 = (bf16[2,128,1536]{2,1,0:T(8,128)(2,1)S(1)}, bf16[2,128,1536]{2,1,0:T(8,128)(2,1)S(1)}, u32[]{:S(2)}, u32[]{:S(2)}) collective-permute-start(bf16[2,128,1536]{2,1,0:T(8,128)(2,1)S(1)} %hidden.3.mine.refs_6_.refs_9_), channel_id=1, source_target_pairs={{0,6},{2,0},{4,2},{6,4},{1,7},{3,1},{5,3},{7,5},{8,14},{10,8},{12,... | collective-permute-start | bytes 2359304 | tf_op jit(solution)/shard_map/ppermute | solution.py:26
  105.9 3.2 %collective-permute-start.25 = (bf16[128,1536]{1,0:T(8,128)(2,1)S(1)}, bf16[128,1536]{1,0:T(8,128)(2,1)S(1)}, u32[]{:S(2)}, u32[]{:S(2)}) collective-permute-start(bf16[128,1536]{1,0:T(8,128)(2,1)S(1)} %get-tuple-element.151), channel_id=1, source_target_pairs={{0,6},{2,0},{4,2},{6,4},{1,7},{3,1},{5,3},{7,5},{8,14},{10,8},{12,... | collective-permute-start | bytes 1179656 | tf_op jit(solution)/shard_map/ppermute | solution.py:26
  109.2 2.2 %input_three.2 = (f32[3,128,384]{2,1,0:T(8,128)S(1)}, f32[3,128,384]{2,1,0:T(8,128)S(1)}) custom-call(bf16[2,128,1536]{2,1,0:T(8,128)(2,1)S(1)} %hidden.2.mine.refs_6_.refs_9_, bf16[2,128,1536]{2,1,0:T(8,128)(2,1)S(1)} %collective-permute-done.22.above.refs_7_.refs_10_, bf16[2,128,1536]{2,1,0:T(8,128)(2,1)S(1)} %collective-permute-done.23.below.refs_8_.refs_11_, ...), custom_call_target="tpu_custom_call" | custom-call | flops 115000000 | bytes 369000 | tf_op jit(solution)/shard_map/input_three/pallas_call | solution.py:50
  111.4 3.5 %grads_a.1 = (f32[768,1536]{1,0:T(8,128)S(1)}, f32[1536,768]{1,0:T(8,128)S(1)}) custom-call(bf16[512,768]{1,0:T(8,128)(2,1)S(1)} %get-tuple-element.159.refs_0_.refs_1_.refs_2_, bf16[512,768]{1,0:T(8,128)(2,1)S(1)} %get-tuple-element.159.refs_0_.refs_1_.refs_2_, bf16[512,768]{1,0:T(8,128)(2,1)S(1)} %get-tuple-element.159.refs_0_.refs_1_.refs_2_, ...), custom_call_target="tpu_custom_call" | custom-call | flops 115000000 | bytes 369000 | tf_op jit(solution)/shard_map/grads_a/pallas_call | solution.py:50
  114.9 2.2 %copy-done = f32[768,1536]{1,0:T(8,128)} copy-done((f32[768,1536]{1,0:T(8,128)}, f32[768,1536]{1,0:T(8,128)S(1)}, u32[]{:S(2)}) %copy-start) | copy-done | bytes 4718616
  117.1 7.2 %collective-permute-done.28.below.refs_8_.refs_11_ = bf16[2,128,1536]{2,1,0:T(8,128)(2,1)S(1)} collective-permute-done((bf16[2,128,1536]{2,1,0:T(8,128)(2,1)S(1)}, bf16[2,128,1536]{2,1,0:T(8,128)(2,1)S(1)}, u32[]{:S(2)}, u32[]{:S(2)}) %collective-permute-start.28) | collective-permute-done | bytes 786464 | tf_op jit(solution)/shard_map/ppermute | solution.py:26
  124.4 3.3 %collective-permute-start.32 = (bf16[128,1536]{1,0:T(8,128)(2,1)S(1)}, bf16[128,1536]{1,0:T(8,128)(2,1)S(1)}, u32[]{:S(2)}, u32[]{:S(2)}) collective-permute-start(bf16[128,1536]{1,0:T(8,128)(2,1)S(1)} %get-tuple-element.168), channel_id=1, source_target_pairs={{0,6},{2,0},{4,2},{6,4},{1,7},{3,1},{5,3},{7,5},{8,14},{10,8},{12,... | collective-permute-start | bytes 1179656 | tf_op jit(solution)/shard_map/ppermute | solution.py:26
  127.7 2.2 %input_three.3 = (f32[3,128,384]{2,1,0:T(8,128)S(1)}, f32[3,128,384]{2,1,0:T(8,128)S(1)}) custom-call(bf16[2,128,1536]{2,1,0:T(8,128)(2,1)S(1)} %hidden.3.mine.refs_6_.refs_9_, bf16[2,128,1536]{2,1,0:T(8,128)(2,1)S(1)} %collective-permute-done.27.above.refs_7_.refs_10_, bf16[2,128,1536]{2,1,0:T(8,128)(2,1)S(1)} %collective-permute-done.28.below.refs_8_.refs_11_, ...), custom_call_target="tpu_custom_call" | custom-call | flops 115000000 | bytes 369000 | tf_op jit(solution)/shard_map/input_three/pallas_call | solution.py:50
  129.9 3.8 %grads_b.1 = (f32[768,1536]{1,0:T(8,128)S(1)}, f32[1536,768]{1,0:T(8,128)S(1)}) custom-call(bf16[512,768]{1,0:T(8,128)(2,1)S(1)} %get-tuple-element.157.refs_0_.refs_1_.refs_2_, bf16[512,768]{1,0:T(8,128)(2,1)S(1)} %get-tuple-element.157.refs_0_.refs_1_.refs_2_, bf16[512,768]{1,0:T(8,128)(2,1)S(1)} %get-tuple-element.157.refs_0_.refs_1_.refs_2_, ...), custom_call_target="tpu_custom_call" | custom-call | flops 115000000 | bytes 369000 | tf_op jit(solution)/shard_map/grads_b/pallas_call | solution.py:50
  133.8 0.9 input_last.2
  134.8 0.5 collective-permute-start.30
  135.6 0.7 collective-permute-done.29.refs_0_
  137.2 1.5 collective-permute-done.33.grad.refs_8_
  138.7 0.9 input_last.3
  139.7 1.8 %collective-permute-start.35 = (bf16[4,32,384]{2,1,0:T(8,128)(2,1)S(1)}, bf16[4,32,384]{2,1,0:T(8,128)(2,1)S(1)}, u32[]{:S(2)}, u32[]{:S(2)}) collective-permute-start(bf16[4,32,384]{2,1,0:T(8,128)(2,1)S(1)} %get-tuple-element.187), channel_id=1, source_target_pairs={{0,32},{32,64},{64,96},{96,0},{1,33},{33,65},{65,97},{97,1},{2,34}... | collective-permute-start | bytes 294920 | tf_op jit(solution)/shard_map/ppermute | solution.py:26
  141.5 2.4 %collective-permute-start.36 = (bf16[4,32,384]{2,1,0:T(8,128)(2,1)S(1)}, bf16[4,32,384]{2,1,0:T(8,128)(2,1)S(1)}, u32[]{:S(2)}, u32[]{:S(2)}) collective-permute-start(bf16[4,32,384]{2,1,0:T(8,128)(2,1)S(1)} %get-tuple-element.188), channel_id=1, source_target_pairs={{0,64},{32,96},{64,0},{96,32},{1,65},{33,97},{65,1},{97,33},{2,66}... | collective-permute-start | bytes 294920 | tf_op jit(solution)/shard_map/ppermute | solution.py:26
  143.9 1.1 collective-permute-start.37
  145.0 3.3 %grads_last.1 = (bf16[384,3072]{1,0:T(8,128)(2,1)}, bf16[3072,384]{1,0:T(8,128)(2,1)}, bf16[384,1536]{1,0:T(8,128)(2,1)S(1)}, bf16[1536,384]{1,0:T(8,128)(2,1)}) custom-call(s32[1]{0:T(128)} %bitcast.1._.core.refs_0_, bf16[512,768]{1,0:T(8,128)(2,1)S(1)} %get-tuple-element.159.refs_0_.refs_1_.refs_2_, ...), custom_call_target="tpu_custom_call" | custom-call | flops 115000000 | bytes 369000 | tf_op jit(solution)/shard_map/grads_last/pallas_call | solution.py:50
  148.4 0.8 collective-permute-done.36
  149.8 2.7 %collective-permute-start.38 = (bf16[4,32,384]{2,1,0:T(8,128)(2,1)S(1)}, bf16[4,32,384]{2,1,0:T(8,128)(2,1)S(1)}, u32[]{:S(2)}, u32[]{:S(2)}) collective-permute-start(bf16[4,32,384]{2,1,0:T(8,128)(2,1)S(1)} %get-tuple-element.203), channel_id=1, source_target_pairs={{0,16},{16,0},{32,48},{48,32},{64,80},{80,64},{96,112},{112,96},{1... | collective-permute-start | bytes 294920 | tf_op jit(solution)/shard_map/ppermute | solution.py:497
  152.5 1.7 collective-permute-start.39
  154.2 4.5 %collective-permute-start.40 = (bf16[4,32,384]{2,1,0:T(8,128)(2,1)S(1)}, bf16[4,32,384]{2,1,0:T(8,128)(2,1)S(1)}, u32[]{:S(2)}, u32[]{:S(2)}) collective-permute-start(bf16[4,32,384]{2,1,0:T(8,128)(2,1)S(1)} %get-tuple-element.205), channel_id=1, source_target_pairs={{0,80},{16,64},{32,112},{48,96},{64,16},{80,0},{96,48},{112,32},{1... | collective-permute-start | bytes 294920 | tf_op jit(solution)/shard_map/ppermute | solution.py:497
  158.8 1.4 collective-permute-start.41
  160.2 1.6 place.1
  161.8 1.6 collective-permute-done.40
  163.4 2.5 %collective-permute-done.41 = bf16[4,32,384]{2,1,0:T(8,128)(2,1)} collective-permute-done((bf16[4,32,384]{2,1,0:T(8,128)(2,1)S(1)}, bf16[4,32,384]{2,1,0:T(8,128)(2,1)}, u32[]{:S(2)}, u32[]{:S(2)}) %collective-permute-start.41) | collective-permute-done | bytes 98336 | tf_op jit(solution)/shard_map/ppermute | solution.py:497
  165.9 1.0 convert_add_fusion
  166.9 0.7 fusion.1
  (62 shorter events, 4.1 us)
Async XLA Ops:
  1.7 12.9 %collective-permute-start.2 = (bf16[4,32,768]{2,1,0:T(8,128)(2,1)S(1)}, bf16[4,32,768]{2,1,0:T(8,128)(2,1)S(1)}, u32[]{:S(2)}, u32[]{:S(2)}) collective-permute-start(bf16[4,32,768]{2,1,0:T(8,128)(2,1)S(1)} %fusion.2.refs_0_), channel_id=1, source_target_pairs={{0,32},{32,64},{64,96},{96,0},{1,33},{33,65},{65,97},{97,1},{2,34}... | collective-permute-start | bytes 589832 | tf_op jit(solution)/shard_map/ppermute | solution.py:26
  3.4 11.7 %collective-permute-start.1 = (bf16[4,32,768]{2,1,0:T(8,128)(2,1)S(1)}, bf16[4,32,768]{2,1,0:T(8,128)(2,1)S(1)}, u32[]{:S(2)}, u32[]{:S(2)}) collective-permute-start(bf16[4,32,768]{2,1,0:T(8,128)(2,1)S(1)} %fusion.2.refs_0_), channel_id=1, source_target_pairs={{0,64},{32,96},{64,0},{96,32},{1,65},{33,97},{65,1},{97,33},{2,66}... | collective-permute-start | bytes 589832 | tf_op jit(solution)/shard_map/ppermute | solution.py:26
  6.3 8.8 %collective-permute-start = (bf16[4,32,768]{2,1,0:T(8,128)(2,1)S(1)}, bf16[4,32,768]{2,1,0:T(8,128)(2,1)S(1)}, u32[]{:S(2)}, u32[]{:S(2)}) collective-permute-start(bf16[4,32,768]{2,1,0:T(8,128)(2,1)S(1)} %fusion.2.refs_0_), channel_id=1, source_target_pairs={{0,96},{32,0},{64,32},{96,64},{1,97},{33,1},{65,33},{97,65},{2,98}... | collective-permute-start | bytes 589832 | tf_op jit(solution)/shard_map/ppermute | solution.py:26
  7.7 7.5 %collective-permute-start.4 = (bf16[4,32,768]{2,1,0:T(8,128)(2,1)S(1)}, bf16[4,32,768]{2,1,0:T(8,128)(2,1)S(1)}, u32[]{:S(2)}, u32[]{:S(2)}) collective-permute-start(bf16[4,32,768]{2,1,0:T(8,128)(2,1)S(1)} %fusion.2.refs_0_), channel_id=1, source_target_pairs={{0,16},{16,0},{1,17},{17,1},{2,18},{18,2},{3,19},{19,3},{4,20},{20... | collective-permute-start | bytes 589832 | tf_op jit(solution)/shard_map/ppermute | solution.py:26
  14.6 6.4 %copy-start.2 = (bf16[384,3072]{1,0:T(8,128)(2,1)S(1)}, bf16[384,3072]{1,0:T(8,128)(2,1)}, u32[]{:S(2)}) copy-start(bf16[384,3072]{1,0:T(8,128)(2,1)} %wi.2) | copy-start | bytes 7077892
  14.6 6.4 %copy-start.3 = (bf16[3072,384]{1,0:T(8,128)(2,1)S(1)}, bf16[3072,384]{1,0:T(8,128)(2,1)}, u32[]{:S(2)}) copy-start(bf16[3072,384]{1,0:T(8,128)(2,1)} %wo.2) | copy-start | bytes 7077892
  14.6 6.4 %collective-permute-start.8 = (bf16[2,4,384,384]{3,2,1,0:T(8,128)(2,1)}, bf16[2,4,384,384]{3,2,1,0:T(8,128)(2,1)S(1)}, u32[]{:S(2)}, u32[]{:S(2)}) collective-permute-start(bf16[2,4,384,384]{3,2,1,0:T(8,128)(2,1)} %pack.1), channel_id=1, source_target_pairs={{0,1},{1,0},{2,3},{3,2},{4,5},{5,4},{6,7},{7,6},{8,9},{9,8},{10,11... | collective-permute-start | bytes 7077896 | tf_op jit(solution)/shard_map/ppermute | solution.py:26
  15.2 4.2 %collective-permute-start.9 = (bf16[4,32,768]{2,1,0:T(8,128)(2,1)S(1)}, bf16[4,32,768]{2,1,0:T(8,128)(2,1)S(1)}, u32[]{:S(2)}, u32[]{:S(2)}) collective-permute-start(bf16[4,32,768]{2,1,0:T(8,128)(2,1)S(1)} %collective-permute-done.4.refs_0_), channel_id=1, source_target_pairs={{0,1},{1,0},{2,3},{3,2},{4,5},{5,4},{6,7},{7,6},{8,9},{9,8},{10,11... | collective-permute-start | bytes 589832 | tf_op jit(solution)/shard_map/ppermute | solution.py:26
  15.3 6.3 %collective-permute-start.3 = (bf16[512,768]{1,0:T(8,128)(2,1)S(1)}, bf16[512,768]{1,0:T(8,128)(2,1)S(1)}, u32[]{:S(2)}, u32[]{:S(2)}) collective-permute-start(bf16[512,768]{1,0:T(8,128)(2,1)S(1)} %join_a.1.own), channel_id=1, source_target_pairs={{0,1},{1,0},{2,3},{3,2},{4,5},{5,4},{6,7},{7,6},{8,9},{9,8},{10,11... | collective-permute-start | bytes 2359304 | tf_op jit(solution)/shard_map/ppermute | solution.py:26
  15.8 11.5 %collective-permute-start.7 = (bf16[4,32,768]{2,1,0:T(8,128)(2,1)S(1)}, bf16[4,32,768]{2,1,0:T(8,128)(2,1)S(1)}, u32[]{:S(2)}, u32[]{:S(2)}) collective-permute-start(bf16[4,32,768]{2,1,0:T(8,128)(2,1)S(1)} %collective-permute-done.4.refs_0_), channel_id=1, source_target_pairs={{0,32},{32,64},{64,96},{96,0},{1,33},{33,65},{65,97},{97,1},{2,34}... | collective-permute-start | bytes 589832 | tf_op jit(solution)/shard_map/ppermute | solution.py:26
  17.1 11.5 %collective-permute-start.6 = (bf16[4,32,768]{2,1,0:T(8,128)(2,1)S(1)}, bf16[4,32,768]{2,1,0:T(8,128)(2,1)S(1)}, u32[]{:S(2)}, u32[]{:S(2)}) collective-permute-start(bf16[4,32,768]{2,1,0:T(8,128)(2,1)S(1)} %collective-permute-done.4.refs_0_), channel_id=1, source_target_pairs={{0,64},{32,96},{64,0},{96,32},{1,65},{33,97},{65,1},{97,33},{2,66}... | collective-permute-start | bytes 589832 | tf_op jit(solution)/shard_map/ppermute | solution.py:26
  19.5 9.3 %collective-permute-start.5 = (bf16[4,32,768]{2,1,0:T(8,128)(2,1)S(1)}, bf16[4,32,768]{2,1,0:T(8,128)(2,1)S(1)}, u32[]{:S(2)}, u32[]{:S(2)}) collective-permute-start(bf16[4,32,768]{2,1,0:T(8,128)(2,1)S(1)} %collective-permute-done.4.refs_0_), channel_id=1, source_target_pairs={{0,96},{32,0},{64,32},{96,64},{1,97},{33,1},{65,33},{97,65},{2,98}... | collective-permute-start | bytes 589832 | tf_op jit(solution)/shard_map/ppermute | solution.py:26
  23.2 16.8 %collective-permute-start.14 = (bf16[128,1536]{1,0:T(8,128)(2,1)S(1)}, bf16[128,1536]{1,0:T(8,128)(2,1)S(1)}, u32[]{:S(2)}, u32[]{:S(2)}) collective-permute-start(bf16[128,1536]{1,0:T(8,128)(2,1)S(1)} %get-tuple-element.126), channel_id=1, source_target_pairs={{0,6},{2,0},{4,2},{6,4},{1,7},{3,1},{5,3},{7,5},{8,14},{10,8},{12,... | collective-permute-start | bytes 1179656 | tf_op jit(solution)/shard_map/ppermute | solution.py:26
  27.3 12.7 %collective-permute-start.13 = (bf16[128,1536]{1,0:T(8,128)(2,1)S(1)}, bf16[128,1536]{1,0:T(8,128)(2,1)S(1)}, u32[]{:S(2)}, u32[]{:S(2)}) collective-permute-start(bf16[128,1536]{1,0:T(8,128)(2,1)S(1)} %get-tuple-element.116), channel_id=1, source_target_pairs={{0,2},{2,4},{4,6},{6,0},{1,3},{3,5},{5,7},{7,1},{8,10},{10,12},{12... | collective-permute-start | bytes 1179656 | tf_op jit(solution)/shard_map/ppermute | solution.py:26
  28.8 1.4 collective-permute-start.10
  28.8 1.7 %collective-permute-start.11 = (bf16[4,32,768]{2,1,0:T(8,128)(2,1)S(1)}, bf16[4,32,768]{2,1,0:T(8,128)(2,1)S(1)}, u32[]{:S(2)}, u32[]{:S(2)}) collective-permute-start(bf16[4,32,768]{2,1,0:T(8,128)(2,1)S(1)} %collective-permute-done.6.refs_2_), channel_id=1, source_target_pairs={{0,1},{1,0},{2,3},{3,2},{4,5},{5,4},{6,7},{7,6},{8,9},{9,8},{10,11... | collective-permute-start | bytes 589832 | tf_op jit(solution)/shard_map/ppermute | solution.py:26
  29.3 1.5 collective-permute-start.12
  32.4 15.2 %collective-permute-start.18 = (bf16[128,1536]{1,0:T(8,128)(2,1)S(1)}, bf16[128,1536]{1,0:T(8,128)(2,1)S(1)}, u32[]{:S(2)}, u32[]{:S(2)}) collective-permute-start(bf16[128,1536]{1,0:T(8,128)(2,1)S(1)} %get-tuple-element.134), channel_id=1, source_target_pairs={{0,6},{2,0},{4,2},{6,4},{1,7},{3,1},{5,3},{7,5},{8,14},{10,8},{12,... | collective-permute-start | bytes 1179656 | tf_op jit(solution)/shard_map/ppermute | solution.py:26
  36.5 13.2 %collective-permute-start.17 = (bf16[128,1536]{1,0:T(8,128)(2,1)S(1)}, bf16[128,1536]{1,0:T(8,128)(2,1)S(1)}, u32[]{:S(2)}, u32[]{:S(2)}) collective-permute-start(bf16[128,1536]{1,0:T(8,128)(2,1)S(1)} %get-tuple-element.122), channel_id=1, source_target_pairs={{0,2},{2,4},{4,6},{6,0},{1,3},{3,5},{5,7},{7,1},{8,10},{10,12},{12... | collective-permute-start | bytes 1179656 | tf_op jit(solution)/shard_map/ppermute | solution.py:26
  40.7 25.9 %collective-permute-start.15 = (bf16[2,128,1536]{2,1,0:T(8,128)(2,1)S(1)}, bf16[2,128,1536]{2,1,0:T(8,128)(2,1)S(1)}, u32[]{:S(2)}, u32[]{:S(2)}) collective-permute-start(bf16[2,128,1536]{2,1,0:T(8,128)(2,1)S(1)} %get-tuple-element.129), channel_id=1, source_target_pairs={{0,2},{2,4},{4,6},{6,0},{1,3},{3,5},{5,7},{7,1},{8,10},{10,12},{12... | collective-permute-start | bytes 2359304 | tf_op jit(solution)/shard_map/ppermute | solution.py:26
  40.8 25.8 %collective-permute-start.16 = (bf16[2,128,1536]{2,1,0:T(8,128)(2,1)S(1)}, bf16[2,128,1536]{2,1,0:T(8,128)(2,1)S(1)}, u32[]{:S(2)}, u32[]{:S(2)}) collective-permute-start(bf16[2,128,1536]{2,1,0:T(8,128)(2,1)S(1)} %get-tuple-element.130), channel_id=1, source_target_pairs={{0,6},{2,0},{4,2},{6,4},{1,7},{3,1},{5,3},{7,5},{8,14},{10,8},{12,... | collective-permute-start | bytes 2359304 | tf_op jit(solution)/shard_map/ppermute | solution.py:26
  50.4 32.0 %collective-permute-start.20 = (bf16[2,128,1536]{2,1,0:T(8,128)(2,1)S(1)}, bf16[2,128,1536]{2,1,0:T(8,128)(2,1)S(1)}, u32[]{:S(2)}, u32[]{:S(2)}) collective-permute-start(bf16[2,128,1536]{2,1,0:T(8,128)(2,1)S(1)} %get-tuple-element.137), channel_id=1, source_target_pairs={{0,2},{2,4},{4,6},{6,0},{1,3},{3,5},{5,7},{7,1},{8,10},{10,12},{12... | collective-permute-start | bytes 2359304 | tf_op jit(solution)/shard_map/ppermute | solution.py:26
  50.6 31.8 %collective-permute-start.21 = (bf16[2,128,1536]{2,1,0:T(8,128)(2,1)S(1)}, bf16[2,128,1536]{2,1,0:T(8,128)(2,1)S(1)}, u32[]{:S(2)}, u32[]{:S(2)}) collective-permute-start(bf16[2,128,1536]{2,1,0:T(8,128)(2,1)S(1)} %get-tuple-element.138), channel_id=1, source_target_pairs={{0,6},{2,0},{4,2},{6,4},{1,7},{3,1},{5,3},{7,5},{8,14},{10,8},{12,... | collective-permute-start | bytes 2359304 | tf_op jit(solution)/shard_map/ppermute | solution.py:26
  67.3 17.6 %collective-permute-start.19 = (bf16[2,128,1536]{2,1,0:T(8,128)(2,1)S(1)}, bf16[2,128,1536]{2,1,0:T(8,128)(2,1)S(1)}, u32[]{:S(2)}, u32[]{:S(2)}) collective-permute-start(bf16[2,128,1536]{2,1,0:T(8,128)(2,1)S(1)} %get-tuple-element.142), channel_id=1, source_target_pairs={{0,8},{8,0},{1,9},{9,1},{2,10},{10,2},{3,11},{11,3},{4,12},{12,4},... | collective-permute-start | bytes 2359304 | tf_op jit(solution)/shard_map/ppermute | solution.py:26
  83.1 18.6 %collective-permute-start.24 = (bf16[2,128,1536]{2,1,0:T(8,128)(2,1)S(1)}, bf16[2,128,1536]{2,1,0:T(8,128)(2,1)S(1)}, u32[]{:S(2)}, u32[]{:S(2)}) collective-permute-start(bf16[2,128,1536]{2,1,0:T(8,128)(2,1)S(1)} %get-tuple-element.145), channel_id=1, source_target_pairs={{0,8},{8,0},{1,9},{9,1},{2,10},{10,2},{3,11},{11,3},{4,12},{12,4},... | collective-permute-start | bytes 2359304 | tf_op jit(solution)/shard_map/ppermute | solution.py:26
  85.6 20.2 %collective-permute-start.23 = (bf16[2,128,1536]{2,1,0:T(8,128)(2,1)S(1)}, bf16[2,128,1536]{2,1,0:T(8,128)(2,1)S(1)}, u32[]{:S(2)}, u32[]{:S(2)}) collective-permute-start(bf16[2,128,1536]{2,1,0:T(8,128)(2,1)S(1)} %hidden.2.mine.refs_6_.refs_9_), channel_id=1, source_target_pairs={{0,2},{2,4},{4,6},{6,0},{1,3},{3,5},{5,7},{7,1},{8,10},{10,12},{12... | collective-permute-start | bytes 2359304 | tf_op jit(solution)/shard_map/ppermute | solution.py:26
  85.7 20.1 %collective-permute-start.22 = (bf16[2,128,1536]{2,1,0:T(8,128)(2,1)S(1)}, bf16[2,128,1536]{2,1,0:T(8,128)(2,1)S(1)}, u32[]{:S(2)}, u32[]{:S(2)}) collective-permute-start(bf16[2,128,1536]{2,1,0:T(8,128)(2,1)S(1)} %hidden.2.mine.refs_6_.refs_9_), channel_id=1, source_target_pairs={{0,6},{2,0},{4,2},{6,4},{1,7},{3,1},{5,3},{7,5},{8,14},{10,8},{12,... | collective-permute-start | bytes 2359304 | tf_op jit(solution)/shard_map/ppermute | solution.py:26
  102.5 21.8 %collective-permute-start.28 = (bf16[2,128,1536]{2,1,0:T(8,128)(2,1)S(1)}, bf16[2,128,1536]{2,1,0:T(8,128)(2,1)S(1)}, u32[]{:S(2)}, u32[]{:S(2)}) collective-permute-start(bf16[2,128,1536]{2,1,0:T(8,128)(2,1)S(1)} %hidden.3.mine.refs_6_.refs_9_), channel_id=1, source_target_pairs={{0,2},{2,4},{4,6},{6,0},{1,3},{3,5},{5,7},{7,1},{8,10},{10,12},{12... | collective-permute-start | bytes 2359304 | tf_op jit(solution)/shard_map/ppermute | solution.py:26
  102.6 21.7 %collective-permute-start.27 = (bf16[2,128,1536]{2,1,0:T(8,128)(2,1)S(1)}, bf16[2,128,1536]{2,1,0:T(8,128)(2,1)S(1)}, u32[]{:S(2)}, u32[]{:S(2)}) collective-permute-start(bf16[2,128,1536]{2,1,0:T(8,128)(2,1)S(1)} %hidden.3.mine.refs_6_.refs_9_), channel_id=1, source_target_pairs={{0,6},{2,0},{4,2},{6,4},{1,7},{3,1},{5,3},{7,5},{8,14},{10,8},{12,... | collective-permute-start | bytes 2359304 | tf_op jit(solution)/shard_map/ppermute | solution.py:26
  105.9 27.9 %collective-permute-start.26 = (bf16[128,1536]{1,0:T(8,128)(2,1)S(1)}, bf16[128,1536]{1,0:T(8,128)(2,1)S(1)}, u32[]{:S(2)}, u32[]{:S(2)}) collective-permute-start(bf16[128,1536]{1,0:T(8,128)(2,1)S(1)} %get-tuple-element.156), channel_id=1, source_target_pairs={{0,2},{2,4},{4,6},{6,0},{1,3},{3,5},{5,7},{7,1},{8,10},{10,12},{12... | collective-permute-start | bytes 1179656 | tf_op jit(solution)/shard_map/ppermute | solution.py:26
  105.9 27.8 %collective-permute-start.25 = (bf16[128,1536]{1,0:T(8,128)(2,1)S(1)}, bf16[128,1536]{1,0:T(8,128)(2,1)S(1)}, u32[]{:S(2)}, u32[]{:S(2)}) collective-permute-start(bf16[128,1536]{1,0:T(8,128)(2,1)S(1)} %get-tuple-element.151), channel_id=1, source_target_pairs={{0,6},{2,0},{4,2},{6,4},{1,7},{3,1},{5,3},{7,5},{8,14},{10,8},{12,... | collective-permute-start | bytes 1179656 | tf_op jit(solution)/shard_map/ppermute | solution.py:26
  114.9 2.2 %copy-start = (f32[768,1536]{1,0:T(8,128)}, f32[768,1536]{1,0:T(8,128)S(1)}, u32[]{:S(2)}) copy-start(f32[768,1536]{1,0:T(8,128)S(1)} %get-tuple-element.164.refs_12_) | copy-start | bytes 14155780
  124.3 14.4 %collective-permute-start.33 = (bf16[128,1536]{1,0:T(8,128)(2,1)S(1)}, bf16[128,1536]{1,0:T(8,128)(2,1)S(1)}, u32[]{:S(2)}, u32[]{:S(2)}) collective-permute-start(bf16[128,1536]{1,0:T(8,128)(2,1)S(1)} %get-tuple-element.184), channel_id=1, source_target_pairs={{0,2},{2,4},{4,6},{6,0},{1,3},{3,5},{5,7},{7,1},{8,10},{10,12},{12... | collective-permute-start | bytes 1179656 | tf_op jit(solution)/shard_map/ppermute | solution.py:26
  124.4 5.5 %copy-start.1 = (f32[768,1536]{1,0:T(8,128)S(1)}, f32[768,1536]{1,0:T(8,128)}, u32[]{:S(2)}) copy-start(f32[768,1536]{1,0:T(8,128)} %copy-done) | copy-start | bytes 14155780
  124.4 14.3 %collective-permute-start.32 = (bf16[128,1536]{1,0:T(8,128)(2,1)S(1)}, bf16[128,1536]{1,0:T(8,128)(2,1)S(1)}, u32[]{:S(2)}, u32[]{:S(2)}) collective-permute-start(bf16[128,1536]{1,0:T(8,128)(2,1)S(1)} %get-tuple-element.168), channel_id=1, source_target_pairs={{0,6},{2,0},{4,2},{6,4},{1,7},{3,1},{5,3},{7,5},{8,14},{10,8},{12,... | collective-permute-start | bytes 1179656 | tf_op jit(solution)/shard_map/ppermute | solution.py:26
  134.7 1.6 collective-permute-start.29
  134.8 1.9 %collective-permute-start.30 = (f32[512,128]{1,0:T(8,128)S(1)}, f32[512,128]{1,0:T(8,128)S(1)}, u32[]{:S(2)}, u32[]{:S(2)}) collective-permute-start(f32[512,128]{1,0:T(8,128)S(1)} %get-tuple-element.181), channel_id=1, source_target_pairs={{0,1},{1,0},{2,3},{3,2},{4,5},{5,4},{6,7},{7,6},{8,9},{9,8},{10,11... | collective-permute-start | bytes 786440 | tf_op jit(solution)/shard_map/ppermute | solution.py:26
  135.3 1.8 %collective-permute-start.31 = (f32[512,128]{1,0:T(8,128)S(1)}, f32[512,128]{1,0:T(8,128)S(1)}, u32[]{:S(2)}, u32[]{:S(2)}) collective-permute-start(f32[512,128]{1,0:T(8,128)S(1)} %get-tuple-element.182), channel_id=1, source_target_pairs={{0,1},{1,0},{2,3},{3,2},{4,5},{5,4},{6,7},{7,6},{8,9},{9,8},{10,11... | collective-permute-start | bytes 786440 | tf_op jit(solution)/shard_map/ppermute | solution.py:26
  139.6 9.5 %collective-permute-start.34 = (f32[512,384]{1,0:T(8,128)S(1)}, f32[512,384]{1,0:T(8,128)S(1)}, u32[]{:S(2)}, u32[]{:S(2)}) collective-permute-start(f32[512,384]{1,0:T(8,128)S(1)} %get-tuple-element.186), channel_id=1, source_target_pairs={{0,1},{1,0},{2,3},{3,2},{4,5},{5,4},{6,7},{7,6},{8,9},{9,8},{10,11... | collective-permute-start | bytes 2359304 | tf_op jit(solution)/shard_map/ppermute | solution.py:26
  139.7 8.7 %collective-permute-start.35 = (bf16[4,32,384]{2,1,0:T(8,128)(2,1)S(1)}, bf16[4,32,384]{2,1,0:T(8,128)(2,1)S(1)}, u32[]{:S(2)}, u32[]{:S(2)}) collective-permute-start(bf16[4,32,384]{2,1,0:T(8,128)(2,1)S(1)} %get-tuple-element.187), channel_id=1, source_target_pairs={{0,32},{32,64},{64,96},{96,0},{1,33},{33,65},{65,97},{97,1},{2,34}... | collective-permute-start | bytes 294920 | tf_op jit(solution)/shard_map/ppermute | solution.py:26
  141.5 7.6 %collective-permute-start.36 = (bf16[4,32,384]{2,1,0:T(8,128)(2,1)S(1)}, bf16[4,32,384]{2,1,0:T(8,128)(2,1)S(1)}, u32[]{:S(2)}, u32[]{:S(2)}) collective-permute-start(bf16[4,32,384]{2,1,0:T(8,128)(2,1)S(1)} %get-tuple-element.188), channel_id=1, source_target_pairs={{0,64},{32,96},{64,0},{96,32},{1,65},{33,97},{65,1},{97,33},{2,66}... | collective-permute-start | bytes 294920 | tf_op jit(solution)/shard_map/ppermute | solution.py:26
  143.9 5.2 %collective-permute-start.37 = (bf16[4,32,384]{2,1,0:T(8,128)(2,1)S(1)}, bf16[4,32,384]{2,1,0:T(8,128)(2,1)S(1)}, u32[]{:S(2)}, u32[]{:S(2)}) collective-permute-start(bf16[4,32,384]{2,1,0:T(8,128)(2,1)S(1)} %get-tuple-element.189), channel_id=1, source_target_pairs={{0,96},{32,0},{64,32},{96,64},{1,97},{33,1},{65,33},{97,65},{2,98}... | collective-permute-start | bytes 294920 | tf_op jit(solution)/shard_map/ppermute | solution.py:26
  149.2 9.6 %collective-permute-start.42 = (bf16[384,1536]{1,0:T(8,128)(2,1)S(1)}, bf16[384,1536]{1,0:T(8,128)(2,1)S(1)}, u32[]{:S(2)}, u32[]{:S(2)}) collective-permute-start(bf16[384,1536]{1,0:T(8,128)(2,1)S(1)} %get-tuple-element.209), channel_id=1, source_target_pairs={{0,1},{1,0},{2,3},{3,2},{4,5},{5,4},{6,7},{7,6},{8,9},{9,8},{10,11... | collective-permute-start | bytes 3538952 | tf_op jit(solution)/shard_map/ppermute | solution.py:26
  149.3 10.9 %collective-permute-start.43 = (bf16[1536,384]{1,0:T(8,128)(2,1)}, bf16[1536,384]{1,0:T(8,128)(2,1)S(1)}, u32[]{:S(2)}, u32[]{:S(2)}) collective-permute-start(bf16[1536,384]{1,0:T(8,128)(2,1)} %get-tuple-element.210), channel_id=1, source_target_pairs={{0,1},{1,0},{2,3},{3,2},{4,5},{5,4},{6,7},{7,6},{8,9},{9,8},{10,11... | collective-permute-start | bytes 3538952 | tf_op jit(solution)/shard_map/ppermute | solution.py:26
  149.8 12.0 %collective-permute-start.38 = (bf16[4,32,384]{2,1,0:T(8,128)(2,1)S(1)}, bf16[4,32,384]{2,1,0:T(8,128)(2,1)S(1)}, u32[]{:S(2)}, u32[]{:S(2)}) collective-permute-start(bf16[4,32,384]{2,1,0:T(8,128)(2,1)S(1)} %get-tuple-element.203), channel_id=1, source_target_pairs={{0,16},{16,0},{32,48},{48,32},{64,80},{80,64},{96,112},{112,96},{1... | collective-permute-start | bytes 294920 | tf_op jit(solution)/shard_map/ppermute | solution.py:497
  152.5 9.2 %collective-permute-start.39 = (bf16[4,32,384]{2,1,0:T(8,128)(2,1)S(1)}, bf16[4,32,384]{2,1,0:T(8,128)(2,1)S(1)}, u32[]{:S(2)}, u32[]{:S(2)}) collective-permute-start(bf16[4,32,384]{2,1,0:T(8,128)(2,1)S(1)} %get-tuple-element.204), channel_id=1, source_target_pairs={{0,48},{16,32},{32,80},{48,64},{64,112},{80,96},{96,16},{112,0},{1... | collective-permute-start | bytes 294920 | tf_op jit(solution)/shard_map/ppermute | solution.py:497
  154.2 9.2 %collective-permute-start.40 = (bf16[4,32,384]{2,1,0:T(8,128)(2,1)S(1)}, bf16[4,32,384]{2,1,0:T(8,128)(2,1)S(1)}, u32[]{:S(2)}, u32[]{:S(2)}) collective-permute-start(bf16[4,32,384]{2,1,0:T(8,128)(2,1)S(1)} %get-tuple-element.205), channel_id=1, source_target_pairs={{0,80},{16,64},{32,112},{48,96},{64,16},{80,0},{96,48},{112,32},{1... | collective-permute-start | bytes 294920 | tf_op jit(solution)/shard_map/ppermute | solution.py:497
  158.8 7.1 %collective-permute-start.41 = (bf16[4,32,384]{2,1,0:T(8,128)(2,1)S(1)}, bf16[4,32,384]{2,1,0:T(8,128)(2,1)}, u32[]{:S(2)}, u32[]{:S(2)}) collective-permute-start(bf16[4,32,384]{2,1,0:T(8,128)(2,1)S(1)} %get-tuple-element.206), channel_id=1, source_target_pairs={{0,112},{16,96},{32,16},{48,0},{64,48},{80,32},{96,80},{112,64},{1... | collective-permute-start | bytes 294920 | tf_op jit(solution)/shard_map/ppermute | solution.py:497

commit v11 on v10

--- a/solution.py
+++ b/solution.py
@@ -34,7 +34,7 @@
     return lax.optimization_barrier((value, after))[0]
 
 
-COST = dict(pack=0.1, first_block=0.1, weights=7, join_a=100, join_b=0.1, products=0.1, ring_add=0.1, own_sum=0.1, hidden=0.1, pass_on=0.1, input_three=0.1, input_last=0.1, grads_a=0.1, grads_b=0.1, grads_last=0.1, return_a=0.1, return_b=20, place=0.1)
+COST = dict(pack=0.1, first_block=0.1, weights=7, join_a=100, join_b=0.1, products=0.1, ring_add=0.1, own_sum=0.1, hidden=0.1, pass_on=0.1, input_three=0.1, input_last=0.1, grads_a=0.1, grads_b=0.1, grads_last=0.1, return_a=0.1, return_b=20, place=0.1, finish=0.1)
 
 
 def kernel(name, body, grid, ins, outs, scratch=(), scalar=None, aliases=None, vmem=24):
@@ -67,19 +67,22 @@
 def pack(w_in, w_out, core):
     feat = w_in.shape[0]
     half = w_out.shape[0] // feat // 2
+    steps = 2
+    width = half // steps
 
     def body(_, wi, wo, out):
-        out[0, 0] = wi[...]
-        out[1, 0] = wo[...]
-
-    block = (feat, feat)
-    place = lambda i, c: (1 - c) * half + i
+        for k in range(width):
+            at = slice(k * feat, (k + 1) * feat)
+            out[0, k] = wi[:, at]
+            out[1, k] = wo[at, :]
+
+    place = lambda i, c: (1 - c) * steps + i
     return kernel(
         "pack",
         body,
-        half,
-        [(w_in, block, (0, place)), (w_out, block, (place, 0))],
-        [((2, half, feat, feat), BF16, (2, 1, feat, feat), (0, "i", 0, 0))],
+        steps,
+        [(w_in, (feat, width * feat), (0, place)), (w_out, (width * feat, feat), (place, 0))],
+        [((2, half, feat, feat), BF16, (2, width, feat, feat), (0, "i", 0, 0))],
         scalar=core,
         vmem=60,
     )[0]
@@ -406,6 +409,21 @@
     )
 
 
+def finish(parts, z):
+    shape = parts[0].shape
+
+    def body(z, *refs):
+        for k in range(shape[0]):
+            at = (k + shape[0] - z[0]) % shape[0]
+            total = refs[0][at]
+            for ref in refs[1:-1]:
+                total = total + ref[at].astype(F32)
+            refs[-1][k] = total.astype(BF16)
+
+    ins = [(a, shape, (0, 0, 0)) for a in parts]
+    return kernel("finish", body, 1, ins, [(shape, BF16, shape, (0, 0, 0))], scalar=z)[0]
+
+
 def local(tokens, cotangent, w_in, w_out):
     z, core = lax.axis_index("z"), lax.axis_index("core")
     rows, feat = tokens.shape
@@ -499,10 +517,8 @@
     ]
     w_in_grad, w_out_grad = place(w_in_grad, w_out_grad, *got, at_core)
 
-    total = kept
-    for part in back + gate(far, w_in_grad):
-        total = total + part.astype(F32)
-    input_grad = relative(total, 1).reshape(rows, feat).astype(BF16)
+    parts = [kept, *back, *gate(far, w_in_grad)]
+    input_grad = finish(parts, jnp.reshape(z, (1,)).astype(jnp.int32)).reshape(rows, feat)
     return (input_grad, w_in_grad, w_out_grad)
 
 

time: 168 us -> 167 us (level)
  other arithmetic: 2.75 us -> 1.05 us
    pallas_call x26 -> x27, Pallas kernels: 37.7 us -> 37 us  [kernel(): pl.pallas_call(body, name=name, grid_spec=pltpu.PrefetchScalarGridSpec(nu...]
  transfers between devices with their start and end apart: 44 -> 44, of which waited for: 19 -> 19; matrix products, arithmetic and copies ran while one was open for 0% -> 0% of each run, Pallas kernels for 22% -> 21%
where the time goes in v11:
time: 167 us
  starting transfers between devices  64 us (38%)
  waiting for transfers between devices  61.3 us (37%)
  Pallas kernels  37 us (22%)
  local copies, waits for them, and re-layouts  2.18 us (1%)
    ppermute x40, waiting for transfers between devices, shift(): return lax.ppermute(x, axis, [(i, (i + by) % n) for i in range(n)])  57.2 us
    ppermute x40, starting transfers between devices, shift(): return lax.ppermute(x, axis, [(i, (i + by) % n) for i in range(n)])  53.7 us
    pallas_call x27, Pallas kernels, kernel(): pl.pallas_call(body, name=name, grid_spec=pltpu.PrefetchScalarGridSpec(nu...  37 us
    ppermute x4, starting transfers between devices, local(): lax.ppermute(a, ROWS, [(i, (i // 2 + d) % 4 * 2 + (i + 1) % 2) for i in r...  10.4 us
    ppermute x4, waiting for transfers between devices, local(): lax.ppermute(a, ROWS, [(i, (i // 2 + d) % 4 * 2 + (i + 1) % 2) for i in r...  4.03 us
  transfers between devices with their start and end apart: 44, of which 19 were waited for; matrix products, arithmetic and copies ran while one was open for 0% of the time, Pallas kernels for 21%

profile of v11, /device:TPU:0, one launch (start us, length us, event | category | flops | bytes accessed | tf_op | source)
XLA Modules:
  0.0 166.5 jit_solution(8919258820668776884)
XLA Ops:
  0.7 1.0 pad_maximum_fusion
  1.7 1.7 %collective-permute-start.2 = (bf16[4,32,768]{2,1,0:T(8,128)(2,1)S(1)}, bf16[4,32,768]{2,1,0:T(8,128)(2,1)S(1)}, u32[]{:S(2)}, u32[]{:S(2)}) collective-permute-start(bf16[4,32,768]{2,1,0:T(8,128)(2,1)S(1)} %fusion.refs_0_), channel_id=1, source_target_pairs={{0,32},{32,64},{64,96},{96,0},{1,33},{33,65},{65,97},{97,1},{2,34}... | collective-permute-start | bytes 589832 | tf_op jit(solution)/shard_map/ppermute | solution.py:26
  3.4 2.9 %collective-permute-start.1 = (bf16[4,32,768]{2,1,0:T(8,128)(2,1)S(1)}, bf16[4,32,768]{2,1,0:T(8,128)(2,1)S(1)}, u32[]{:S(2)}, u32[]{:S(2)}) collective-permute-start(bf16[4,32,768]{2,1,0:T(8,128)(2,1)S(1)} %fusion.refs_0_), channel_id=1, source_target_pairs={{0,64},{32,96},{64,0},{96,32},{1,65},{33,97},{65,1},{97,33},{2,66}... | collective-permute-start | bytes 589832 | tf_op jit(solution)/shard_map/ppermute | solution.py:26
  6.3 1.3 collective-permute-start
  7.7 3.0 %collective-permute-start.4 = (bf16[4,32,768]{2,1,0:T(8,128)(2,1)S(1)}, bf16[4,32,768]{2,1,0:T(8,128)(2,1)S(1)}, u32[]{:S(2)}, u32[]{:S(2)}) collective-permute-start(bf16[4,32,768]{2,1,0:T(8,128)(2,1)S(1)} %fusion.refs_0_), channel_id=1, source_target_pairs={{0,16},{16,0},{1,17},{17,1},{2,18},{18,2},{3,19},{19,3},{4,20},{20... | collective-permute-start | bytes 589832 | tf_op jit(solution)/shard_map/ppermute | solution.py:26
  10.7 2.8 %pack.1 = bf16[2,4,384,384]{3,2,1,0:T(8,128)(2,1)} custom-call(s32[1]{0:T(128)} %bitcast.2._.core.refs_0_, bf16[384,3072]{1,0:T(8,128)(2,1)} %wi.2, bf16[3072,384]{1,0:T(8,128)(2,1)} %wo.2), custom_call_target="tpu_custom_call" | custom-call | flops 115000000 | bytes 369000 | tf_op jit(solution)/shard_map/pack/pallas_call | solution.py:50
  13.5 1.7 %collective-permute-done.1.refs_2_ = bf16[4,32,768]{2,1,0:T(8,128)(2,1)S(1)} collective-permute-done((bf16[4,32,768]{2,1,0:T(8,128)(2,1)S(1)}, bf16[4,32,768]{2,1,0:T(8,128)(2,1)S(1)}, u32[]{:S(2)}, u32[]{:S(2)}) %collective-permute-start.1) | collective-permute-done | bytes 196640 | tf_op jit(solution)/shard_map/ppermute | solution.py:26
  15.3 0.5 collective-permute-start.3
  15.8 1.2 collective-permute-start.7
  17.1 2.4 %collective-permute-start.6 = (bf16[4,32,768]{2,1,0:T(8,128)(2,1)S(1)}, bf16[4,32,768]{2,1,0:T(8,128)(2,1)S(1)}, u32[]{:S(2)}, u32[]{:S(2)}) collective-permute-start(bf16[4,32,768]{2,1,0:T(8,128)(2,1)S(1)} %collective-permute-done.4.refs_0_), channel_id=1, source_target_pairs={{0,64},{32,96},{64,0},{96,32},{1,65},{33,97},{65,1},{97,33},{2,66}... | collective-permute-start | bytes 589832 | tf_op jit(solution)/shard_map/ppermute | solution.py:26
  19.5 1.6 collective-permute-start.5
  21.1 0.6 weights.1
  21.6 1.6 first_block.2
  23.2 4.1 %collective-permute-start.14 = (bf16[128,1536]{1,0:T(8,128)(2,1)S(1)}, bf16[128,1536]{1,0:T(8,128)(2,1)S(1)}, u32[]{:S(2)}, u32[]{:S(2)}) collective-permute-start(bf16[128,1536]{1,0:T(8,128)(2,1)S(1)} %get-tuple-element.126), channel_id=1, source_target_pairs={{0,6},{2,0},{4,2},{6,4},{1,7},{3,1},{5,3},{7,5},{8,14},{10,8},{12,... | collective-permute-start | bytes 1179656 | tf_op jit(solution)/shard_map/ppermute | solution.py:26
  27.3 1.2 collective-permute-done.6.refs_2_
  28.8 0.5 collective-permute-start.11
  29.3 0.9 collective-permute-done.10.refs_5_
  30.9 1.6 first_block.3
  32.4 4.1 %collective-permute-start.18 = (bf16[128,1536]{1,0:T(8,128)(2,1)S(1)}, bf16[128,1536]{1,0:T(8,128)(2,1)S(1)}, u32[]{:S(2)}, u32[]{:S(2)}) collective-permute-start(bf16[128,1536]{1,0:T(8,128)(2,1)S(1)} %get-tuple-element.134), channel_id=1, source_target_pairs={{0,6},{2,0},{4,2},{6,4},{1,7},{3,1},{5,3},{7,5},{8,14},{10,8},{12,... | collective-permute-start | bytes 1179656 | tf_op jit(solution)/shard_map/ppermute | solution.py:26
  36.5 3.5 %products.2 = (f32[2,512,1536]{2,1,0:T(8,128)S(1)}, bf16[512,768]{1,0:T(8,128)(2,1)S(1)}, bf16[512,768]{1,0:T(8,128)(2,1)S(1)}) custom-call(bf16[512,768]{1,0:T(8,128)(2,1)S(1)} %join_a.1.own, bf16[512,768]{1,0:T(8,128)(2,1)S(1)} %collective-permute-done.3.other, bf16[768,1536]{1,0:T(8,128)(2,1)S(1)} %get-tuple-element.114.wi, ...), custom_call_target="tpu_custom_call" | custom-call | flops 115000000 | bytes 369000 | tf_op jit(solution)/shard_map/products/pallas_call | solution.py:50
  40.1 0.6 ring_add.2
  40.8 3.3 %collective-permute-start.16 = (bf16[2,128,1536]{2,1,0:T(8,128)(2,1)S(1)}, bf16[2,128,1536]{2,1,0:T(8,128)(2,1)S(1)}, u32[]{:S(2)}, u32[]{:S(2)}) collective-permute-start(bf16[2,128,1536]{2,1,0:T(8,128)(2,1)S(1)} %get-tuple-element.130), channel_id=1, source_target_pairs={{0,6},{2,0},{4,2},{6,4},{1,7},{3,1},{5,3},{7,5},{8,14},{10,8},{12,... | collective-permute-start | bytes 2359304 | tf_op jit(solution)/shard_map/ppermute | solution.py:26
  44.1 3.5 %products.3 = (f32[2,512,1536]{2,1,0:T(8,128)S(1)}, bf16[512,768]{1,0:T(8,128)(2,1)S(1)}, bf16[512,768]{1,0:T(8,128)(2,1)S(1)}) custom-call(bf16[512,768]{1,0:T(8,128)(2,1)S(1)} %get-tuple-element.131.own, bf16[512,768]{1,0:T(8,128)(2,1)S(1)} %get-tuple-element.132.other, bf16[768,1536]{1,0:T(8,128)(2,1)S(1)} %get-tuple-element.114.wi, ...), custom_call_target="tpu_custom_call" | custom-call | flops 115000000 | bytes 369000 | tf_op jit(solution)/shard_map/products/pallas_call | solution.py:50
  47.6 2.1 %collective-permute-done.17.up = bf16[128,1536]{1,0:T(8,128)(2,1)S(1)} collective-permute-done((bf16[128,1536]{1,0:T(8,128)(2,1)S(1)}, bf16[128,1536]{1,0:T(8,128)(2,1)S(1)}, u32[]{:S(2)}, u32[]{:S(2)}) %collective-permute-start.17) | collective-permute-done | bytes 393248 | tf_op jit(solution)/shard_map/ppermute | solution.py:26
  49.7 0.6 ring_add.3
  50.6 3.2 %collective-permute-start.21 = (bf16[2,128,1536]{2,1,0:T(8,128)(2,1)S(1)}, bf16[2,128,1536]{2,1,0:T(8,128)(2,1)S(1)}, u32[]{:S(2)}, u32[]{:S(2)}) collective-permute-start(bf16[2,128,1536]{2,1,0:T(8,128)(2,1)S(1)} %get-tuple-element.138), channel_id=1, source_target_pairs={{0,6},{2,0},{4,2},{6,4},{1,7},{3,1},{5,3},{7,5},{8,14},{10,8},{12,... | collective-permute-start | bytes 2359304 | tf_op jit(solution)/shard_map/ppermute | solution.py:26
  53.9 12.7 %collective-permute-done.15.up = bf16[2,128,1536]{2,1,0:T(8,128)(2,1)S(1)} collective-permute-done((bf16[2,128,1536]{2,1,0:T(8,128)(2,1)S(1)}, bf16[2,128,1536]{2,1,0:T(8,128)(2,1)S(1)}, u32[]{:S(2)}, u32[]{:S(2)}) %collective-permute-start.15) | collective-permute-done | bytes 786464 | tf_op jit(solution)/shard_map/ppermute | solution.py:26
  66.6 0.7 own_sum.2
  67.3 1.6 collective-permute-start.19
  68.9 13.5 %collective-permute-done.20.up = bf16[2,128,1536]{2,1,0:T(8,128)(2,1)S(1)} collective-permute-done((bf16[2,128,1536]{2,1,0:T(8,128)(2,1)S(1)}, bf16[2,128,1536]{2,1,0:T(8,128)(2,1)S(1)}, u32[]{:S(2)}, u32[]{:S(2)}) %collective-permute-start.20) | collective-permute-done | bytes 786464 | tf_op jit(solution)/shard_map/ppermute | solution.py:26
  82.4 0.7 own_sum.3
  83.1 1.6 collective-permute-start.24
  84.9 0.7 hidden.2.mine.refs_6_.refs_9_
  85.7 3.2 %collective-permute-start.22 = (bf16[2,128,1536]{2,1,0:T(8,128)(2,1)S(1)}, bf16[2,128,1536]{2,1,0:T(8,128)(2,1)S(1)}, u32[]{:S(2)}, u32[]{:S(2)}) collective-permute-start(bf16[2,128,1536]{2,1,0:T(8,128)(2,1)S(1)} %hidden.2.mine.refs_6_.refs_9_), channel_id=1, source_target_pairs={{0,6},{2,0},{4,2},{6,4},{1,7},{3,1},{5,3},{7,5},{8,14},{10,8},{12,... | collective-permute-start | bytes 2359304 | tf_op jit(solution)/shard_map/ppermute | solution.py:26
  88.9 12.8 %collective-permute-done.24.other = bf16[2,128,1536]{2,1,0:T(8,128)(2,1)S(1)} collective-permute-done((bf16[2,128,1536]{2,1,0:T(8,128)(2,1)S(1)}, bf16[2,128,1536]{2,1,0:T(8,128)(2,1)S(1)}, u32[]{:S(2)}, u32[]{:S(2)}) %collective-permute-start.24) | collective-permute-done | bytes 786464 | tf_op jit(solution)/shard_map/ppermute | solution.py:26
  101.8 0.7 hidden.3.mine.refs_6_.refs_9_
  102.6 3.2 %collective-permute-start.27 = (bf16[2,128,1536]{2,1,0:T(8,128)(2,1)S(1)}, bf16[2,128,1536]{2,1,0:T(8,128)(2,1)S(1)}, u32[]{:S(2)}, u32[]{:S(2)}) collective-permute-start(bf16[2,128,1536]{2,1,0:T(8,128)(2,1)S(1)} %hidden.3.mine.refs_6_.refs_9_), channel_id=1, source_target_pairs={{0,6},{2,0},{4,2},{6,4},{1,7},{3,1},{5,3},{7,5},{8,14},{10,8},{12,... | collective-permute-start | bytes 2359304 | tf_op jit(solution)/shard_map/ppermute | solution.py:26
  105.9 3.2 %collective-permute-start.25 = (bf16[128,1536]{1,0:T(8,128)(2,1)S(1)}, bf16[128,1536]{1,0:T(8,128)(2,1)S(1)}, u32[]{:S(2)}, u32[]{:S(2)}) collective-permute-start(bf16[128,1536]{1,0:T(8,128)(2,1)S(1)} %get-tuple-element.151), channel_id=1, source_target_pairs={{0,6},{2,0},{4,2},{6,4},{1,7},{3,1},{5,3},{7,5},{8,14},{10,8},{12,... | collective-permute-start | bytes 1179656 | tf_op jit(solution)/shard_map/ppermute | solution.py:26
  109.2 2.2 %input_three.2 = (f32[3,128,384]{2,1,0:T(8,128)S(1)}, f32[3,128,384]{2,1,0:T(8,128)S(1)}) custom-call(bf16[2,128,1536]{2,1,0:T(8,128)(2,1)S(1)} %hidden.2.mine.refs_6_.refs_9_, bf16[2,128,1536]{2,1,0:T(8,128)(2,1)S(1)} %collective-permute-done.22.above.refs_7_.refs_10_, bf16[2,128,1536]{2,1,0:T(8,128)(2,1)S(1)} %collective-permute-done.23.below.refs_8_.refs_11_, ...), custom_call_target="tpu_custom_call" | custom-call | flops 115000000 | bytes 369000 | tf_op jit(solution)/shard_map/input_three/pallas_call | solution.py:50
  111.4 3.5 %grads_a.1 = (f32[768,1536]{1,0:T(8,128)S(1)}, f32[1536,768]{1,0:T(8,128)S(1)}) custom-call(bf16[512,768]{1,0:T(8,128)(2,1)S(1)} %get-tuple-element.159.refs_0_.refs_1_.refs_2_, bf16[512,768]{1,0:T(8,128)(2,1)S(1)} %get-tuple-element.159.refs_0_.refs_1_.refs_2_, bf16[512,768]{1,0:T(8,128)(2,1)S(1)} %get-tuple-element.159.refs_0_.refs_1_.refs_2_, ...), custom_call_target="tpu_custom_call" | custom-call | flops 115000000 | bytes 369000 | tf_op jit(solution)/shard_map/grads_a/pallas_call | solution.py:50
  114.9 2.2 %copy-done = f32[768,1536]{1,0:T(8,128)} copy-done((f32[768,1536]{1,0:T(8,128)}, f32[768,1536]{1,0:T(8,128)S(1)}, u32[]{:S(2)}) %copy-start) | copy-done | bytes 4718616
  117.1 7.2 %collective-permute-done.28.below.refs_8_.refs_11_ = bf16[2,128,1536]{2,1,0:T(8,128)(2,1)S(1)} collective-permute-done((bf16[2,128,1536]{2,1,0:T(8,128)(2,1)S(1)}, bf16[2,128,1536]{2,1,0:T(8,128)(2,1)S(1)}, u32[]{:S(2)}, u32[]{:S(2)}) %collective-permute-start.28) | collective-permute-done | bytes 786464 | tf_op jit(solution)/shard_map/ppermute | solution.py:26
  124.4 3.3 %collective-permute-start.32 = (bf16[128,1536]{1,0:T(8,128)(2,1)S(1)}, bf16[128,1536]{1,0:T(8,128)(2,1)S(1)}, u32[]{:S(2)}, u32[]{:S(2)}) collective-permute-start(bf16[128,1536]{1,0:T(8,128)(2,1)S(1)} %get-tuple-element.168), channel_id=1, source_target_pairs={{0,6},{2,0},{4,2},{6,4},{1,7},{3,1},{5,3},{7,5},{8,14},{10,8},{12,... | collective-permute-start | bytes 1179656 | tf_op jit(solution)/shard_map/ppermute | solution.py:26
  127.7 2.2 %input_three.3 = (f32[3,128,384]{2,1,0:T(8,128)S(1)}, f32[3,128,384]{2,1,0:T(8,128)S(1)}) custom-call(bf16[2,128,1536]{2,1,0:T(8,128)(2,1)S(1)} %hidden.3.mine.refs_6_.refs_9_, bf16[2,128,1536]{2,1,0:T(8,128)(2,1)S(1)} %collective-permute-done.27.above.refs_7_.refs_10_, bf16[2,128,1536]{2,1,0:T(8,128)(2,1)S(1)} %collective-permute-done.28.below.refs_8_.refs_11_, ...), custom_call_target="tpu_custom_call" | custom-call | flops 115000000 | bytes 369000 | tf_op jit(solution)/shard_map/input_three/pallas_call | solution.py:50
  129.9 3.8 %grads_b.1 = (f32[768,1536]{1,0:T(8,128)S(1)}, f32[1536,768]{1,0:T(8,128)S(1)}) custom-call(bf16[512,768]{1,0:T(8,128)(2,1)S(1)} %get-tuple-element.157.refs_0_.refs_1_.refs_2_, bf16[512,768]{1,0:T(8,128)(2,1)S(1)} %get-tuple-element.157.refs_0_.refs_1_.refs_2_, bf16[512,768]{1,0:T(8,128)(2,1)S(1)} %get-tuple-element.157.refs_0_.refs_1_.refs_2_, ...), custom_call_target="tpu_custom_call" | custom-call | flops 115000000 | bytes 369000 | tf_op jit(solution)/shard_map/grads_b/pallas_call | solution.py:50
  133.8 0.9 input_last.2
  134.8 0.5 collective-permute-start.30
  135.6 0.7 collective-permute-done.29.refs_0_
  137.2 1.5 collective-permute-done.33.grad.refs_8_
  138.7 0.9 input_last.3
  139.7 1.8 %collective-permute-start.35 = (bf16[4,32,384]{2,1,0:T(8,128)(2,1)S(1)}, bf16[4,32,384]{2,1,0:T(8,128)(2,1)S(1)}, u32[]{:S(2)}, u32[]{:S(2)}) collective-permute-start(bf16[4,32,384]{2,1,0:T(8,128)(2,1)S(1)} %get-tuple-element.187), channel_id=1, source_target_pairs={{0,32},{32,64},{64,96},{96,0},{1,33},{33,65},{65,97},{97,1},{2,34}... | collective-permute-start | bytes 294920 | tf_op jit(solution)/shard_map/ppermute | solution.py:26
  141.5 2.4 %collective-permute-start.36 = (bf16[4,32,384]{2,1,0:T(8,128)(2,1)S(1)}, bf16[4,32,384]{2,1,0:T(8,128)(2,1)S(1)}, u32[]{:S(2)}, u32[]{:S(2)}) collective-permute-start(bf16[4,32,384]{2,1,0:T(8,128)(2,1)S(1)} %get-tuple-element.188), channel_id=1, source_target_pairs={{0,64},{32,96},{64,0},{96,32},{1,65},{33,97},{65,1},{97,33},{2,66}... | collective-permute-start | bytes 294920 | tf_op jit(solution)/shard_map/ppermute | solution.py:26
  143.9 1.1 collective-permute-start.37
  145.0 3.1 %grads_last.1 = (bf16[384,3072]{1,0:T(8,128)(2,1)}, bf16[3072,384]{1,0:T(8,128)(2,1)}, bf16[384,1536]{1,0:T(8,128)(2,1)S(1)}, bf16[1536,384]{1,0:T(8,128)(2,1)S(1)}) custom-call(s32[1]{0:T(128)} %bitcast.2._.core.refs_0_, bf16[512,768]{1,0:T(8,128)(2,1)S(1)} %get-tuple-element.159.refs_0_.refs_1_.refs_2_, ...), custom_call_target="tpu_custom_call" | custom-call | flops 115000000 | bytes 369000 | tf_op jit(solution)/shard_map/grads_last/pallas_call | solution.py:50
  148.1 1.0 collective-permute-done.36.refs_2_
  149.3 0.5 collective-permute-start.43
  149.8 2.7 %collective-permute-start.38 = (bf16[4,32,384]{2,1,0:T(8,128)(2,1)S(1)}, bf16[4,32,384]{2,1,0:T(8,128)(2,1)S(1)}, u32[]{:S(2)}, u32[]{:S(2)}) collective-permute-start(bf16[4,32,384]{2,1,0:T(8,128)(2,1)S(1)} %get-tuple-element.203), channel_id=1, source_target_pairs={{0,16},{16,0},{32,48},{48,32},{64,80},{80,64},{96,112},{112,96},{1... | collective-permute-start | bytes 294920 | tf_op jit(solution)/shard_map/ppermute | solution.py:515
  152.5 1.7 %collective-permute-start.39 = (bf16[4,32,384]{2,1,0:T(8,128)(2,1)S(1)}, bf16[4,32,384]{2,1,0:T(8,128)(2,1)S(1)}, u32[]{:S(2)}, u32[]{:S(2)}) collective-permute-start(bf16[4,32,384]{2,1,0:T(8,128)(2,1)S(1)} %get-tuple-element.204), channel_id=1, source_target_pairs={{0,48},{16,32},{32,80},{48,64},{64,112},{80,96},{96,16},{112,0},{1... | collective-permute-start | bytes 294920 | tf_op jit(solution)/shard_map/ppermute | solution.py:515
  154.2 4.6 %collective-permute-start.40 = (bf16[4,32,384]{2,1,0:T(8,128)(2,1)S(1)}, bf16[4,32,384]{2,1,0:T(8,128)(2,1)S(1)}, u32[]{:S(2)}, u32[]{:S(2)}) collective-permute-start(bf16[4,32,384]{2,1,0:T(8,128)(2,1)S(1)} %get-tuple-element.205), channel_id=1, source_target_pairs={{0,80},{16,64},{32,112},{48,96},{64,16},{80,0},{96,48},{112,32},{1... | collective-permute-start | bytes 294920 | tf_op jit(solution)/shard_map/ppermute | solution.py:515
  158.8 1.4 collective-permute-start.41
  160.2 1.6 place.1
  161.8 1.6 collective-permute-done.40.refs_6_
  163.4 2.4 %collective-permute-done.41.refs_7_ = bf16[4,32,384]{2,1,0:T(8,128)(2,1)S(1)} collective-permute-done((bf16[4,32,384]{2,1,0:T(8,128)(2,1)S(1)}, bf16[4,32,384]{2,1,0:T(8,128)(2,1)S(1)}, u32[]{:S(2)}, u32[]{:S(2)}) %collective-permute-start.41) | collective-permute-done | bytes 98336 | tf_op jit(solution)/shard_map/ppermute | solution.py:515
  165.8 0.7 finish.1
  (61 shorter events, 3.6 us)
Async XLA Ops:
  1.7 11.8 %collective-permute-start.2 = (bf16[4,32,768]{2,1,0:T(8,128)(2,1)S(1)}, bf16[4,32,768]{2,1,0:T(8,128)(2,1)S(1)}, u32[]{:S(2)}, u32[]{:S(2)}) collective-permute-start(bf16[4,32,768]{2,1,0:T(8,128)(2,1)S(1)} %fusion.refs_0_), channel_id=1, source_target_pairs={{0,32},{32,64},{64,96},{96,0},{1,33},{33,65},{65,97},{97,1},{2,34}... | collective-permute-start | bytes 589832 | tf_op jit(solution)/shard_map/ppermute | solution.py:26
  3.4 11.7 %collective-permute-start.1 = (bf16[4,32,768]{2,1,0:T(8,128)(2,1)S(1)}, bf16[4,32,768]{2,1,0:T(8,128)(2,1)S(1)}, u32[]{:S(2)}, u32[]{:S(2)}) collective-permute-start(bf16[4,32,768]{2,1,0:T(8,128)(2,1)S(1)} %fusion.refs_0_), channel_id=1, source_target_pairs={{0,64},{32,96},{64,0},{96,32},{1,65},{33,97},{65,1},{97,33},{2,66}... | collective-permute-start | bytes 589832 | tf_op jit(solution)/shard_map/ppermute | solution.py:26
  6.3 8.8 %collective-permute-start = (bf16[4,32,768]{2,1,0:T(8,128)(2,1)S(1)}, bf16[4,32,768]{2,1,0:T(8,128)(2,1)S(1)}, u32[]{:S(2)}, u32[]{:S(2)}) collective-permute-start(bf16[4,32,768]{2,1,0:T(8,128)(2,1)S(1)} %fusion.refs_0_), channel_id=1, source_target_pairs={{0,96},{32,0},{64,32},{96,64},{1,97},{33,1},{65,33},{97,65},{2,98}... | collective-permute-start | bytes 589832 | tf_op jit(solution)/shard_map/ppermute | solution.py:26
  7.7 7.5 %collective-permute-start.4 = (bf16[4,32,768]{2,1,0:T(8,128)(2,1)S(1)}, bf16[4,32,768]{2,1,0:T(8,128)(2,1)S(1)}, u32[]{:S(2)}, u32[]{:S(2)}) collective-permute-start(bf16[4,32,768]{2,1,0:T(8,128)(2,1)S(1)} %fusion.refs_0_), channel_id=1, source_target_pairs={{0,16},{16,0},{1,17},{17,1},{2,18},{18,2},{3,19},{19,3},{4,20},{20... | collective-permute-start | bytes 589832 | tf_op jit(solution)/shard_map/ppermute | solution.py:26
  13.5 7.6 %copy-start.2 = (bf16[384,3072]{1,0:T(8,128)(2,1)S(1)}, bf16[384,3072]{1,0:T(8,128)(2,1)}, u32[]{:S(2)}) copy-start(bf16[384,3072]{1,0:T(8,128)(2,1)} %wi.2) | copy-start | bytes 7077892
  13.5 7.6 %copy-start.3 = (bf16[3072,384]{1,0:T(8,128)(2,1)S(1)}, bf16[3072,384]{1,0:T(8,128)(2,1)}, u32[]{:S(2)}) copy-start(bf16[3072,384]{1,0:T(8,128)(2,1)} %wo.2) | copy-start | bytes 7077892
  13.5 7.6 %collective-permute-start.8 = (bf16[2,4,384,384]{3,2,1,0:T(8,128)(2,1)}, bf16[2,4,384,384]{3,2,1,0:T(8,128)(2,1)S(1)}, u32[]{:S(2)}, u32[]{:S(2)}) collective-permute-start(bf16[2,4,384,384]{3,2,1,0:T(8,128)(2,1)} %pack.1), channel_id=1, source_target_pairs={{0,1},{1,0},{2,3},{3,2},{4,5},{5,4},{6,7},{7,6},{8,9},{9,8},{10,11... | collective-permute-start | bytes 7077896 | tf_op jit(solution)/shard_map/ppermute | solution.py:26
  15.2 4.2 %collective-permute-start.9 = (bf16[4,32,768]{2,1,0:T(8,128)(2,1)S(1)}, bf16[4,32,768]{2,1,0:T(8,128)(2,1)S(1)}, u32[]{:S(2)}, u32[]{:S(2)}) collective-permute-start(bf16[4,32,768]{2,1,0:T(8,128)(2,1)S(1)} %collective-permute-done.4.refs_0_), channel_id=1, source_target_pairs={{0,1},{1,0},{2,3},{3,2},{4,5},{5,4},{6,7},{7,6},{8,9},{9,8},{10,11... | collective-permute-start | bytes 589832 | tf_op jit(solution)/shard_map/ppermute | solution.py:26
  15.3 6.3 %collective-permute-start.3 = (bf16[512,768]{1,0:T(8,128)(2,1)S(1)}, bf16[512,768]{1,0:T(8,128)(2,1)S(1)}, u32[]{:S(2)}, u32[]{:S(2)}) collective-permute-start(bf16[512,768]{1,0:T(8,128)(2,1)S(1)} %join_a.1.own), channel_id=1, source_target_pairs={{0,1},{1,0},{2,3},{3,2},{4,5},{5,4},{6,7},{7,6},{8,9},{9,8},{10,11... | collective-permute-start | bytes 2359304 | tf_op jit(solution)/shard_map/ppermute | solution.py:26
  15.8 11.5 %collective-permute-start.7 = (bf16[4,32,768]{2,1,0:T(8,128)(2,1)S(1)}, bf16[4,32,768]{2,1,0:T(8,128)(2,1)S(1)}, u32[]{:S(2)}, u32[]{:S(2)}) collective-permute-start(bf16[4,32,768]{2,1,0:T(8,128)(2,1)S(1)} %collective-permute-done.4.refs_0_), channel_id=1, source_target_pairs={{0,32},{32,64},{64,96},{96,0},{1,33},{33,65},{65,97},{97,1},{2,34}... | collective-permute-start | bytes 589832 | tf_op jit(solution)/shard_map/ppermute | solution.py:26
  17.1 11.5 %collective-permute-start.6 = (bf16[4,32,768]{2,1,0:T(8,128)(2,1)S(1)}, bf16[4,32,768]{2,1,0:T(8,128)(2,1)S(1)}, u32[]{:S(2)}, u32[]{:S(2)}) collective-permute-start(bf16[4,32,768]{2,1,0:T(8,128)(2,1)S(1)} %collective-permute-done.4.refs_0_), channel_id=1, source_target_pairs={{0,64},{32,96},{64,0},{96,32},{1,65},{33,97},{65,1},{97,33},{2,66}... | collective-permute-start | bytes 589832 | tf_op jit(solution)/shard_map/ppermute | solution.py:26
  19.5 9.3 %collective-permute-start.5 = (bf16[4,32,768]{2,1,0:T(8,128)(2,1)S(1)}, bf16[4,32,768]{2,1,0:T(8,128)(2,1)S(1)}, u32[]{:S(2)}, u32[]{:S(2)}) collective-permute-start(bf16[4,32,768]{2,1,0:T(8,128)(2,1)S(1)} %collective-permute-done.4.refs_0_), channel_id=1, source_target_pairs={{0,96},{32,0},{64,32},{96,64},{1,97},{33,1},{65,33},{97,65},{2,98}... | collective-permute-start | bytes 589832 | tf_op jit(solution)/shard_map/ppermute | solution.py:26
  23.2 16.8 %collective-permute-start.14 = (bf16[128,1536]{1,0:T(8,128)(2,1)S(1)}, bf16[128,1536]{1,0:T(8,128)(2,1)S(1)}, u32[]{:S(2)}, u32[]{:S(2)}) collective-permute-start(bf16[128,1536]{1,0:T(8,128)(2,1)S(1)} %get-tuple-element.126), channel_id=1, source_target_pairs={{0,6},{2,0},{4,2},{6,4},{1,7},{3,1},{5,3},{7,5},{8,14},{10,8},{12,... | collective-permute-start | bytes 1179656 | tf_op jit(solution)/shard_map/ppermute | solution.py:26
  27.3 12.8 %collective-permute-start.13 = (bf16[128,1536]{1,0:T(8,128)(2,1)S(1)}, bf16[128,1536]{1,0:T(8,128)(2,1)S(1)}, u32[]{:S(2)}, u32[]{:S(2)}) collective-permute-start(bf16[128,1536]{1,0:T(8,128)(2,1)S(1)} %get-tuple-element.116), channel_id=1, source_target_pairs={{0,2},{2,4},{4,6},{6,0},{1,3},{3,5},{5,7},{7,1},{8,10},{10,12},{12... | collective-permute-start | bytes 1179656 | tf_op jit(solution)/shard_map/ppermute | solution.py:26
  28.8 1.4 collective-permute-start.10
  28.8 1.7 %collective-permute-start.11 = (bf16[4,32,768]{2,1,0:T(8,128)(2,1)S(1)}, bf16[4,32,768]{2,1,0:T(8,128)(2,1)S(1)}, u32[]{:S(2)}, u32[]{:S(2)}) collective-permute-start(bf16[4,32,768]{2,1,0:T(8,128)(2,1)S(1)} %collective-permute-done.6.refs_2_), channel_id=1, source_target_pairs={{0,1},{1,0},{2,3},{3,2},{4,5},{5,4},{6,7},{7,6},{8,9},{9,8},{10,11... | collective-permute-start | bytes 589832 | tf_op jit(solution)/shard_map/ppermute | solution.py:26
  29.3 1.5 collective-permute-start.12
  32.4 15.2 %collective-permute-start.18 = (bf16[128,1536]{1,0:T(8,128)(2,1)S(1)}, bf16[128,1536]{1,0:T(8,128)(2,1)S(1)}, u32[]{:S(2)}, u32[]{:S(2)}) collective-permute-start(bf16[128,1536]{1,0:T(8,128)(2,1)S(1)} %get-tuple-element.134), channel_id=1, source_target_pairs={{0,6},{2,0},{4,2},{6,4},{1,7},{3,1},{5,3},{7,5},{8,14},{10,8},{12,... | collective-permute-start | bytes 1179656 | tf_op jit(solution)/shard_map/ppermute | solution.py:26
  36.5 13.2 %collective-permute-start.17 = (bf16[128,1536]{1,0:T(8,128)(2,1)S(1)}, bf16[128,1536]{1,0:T(8,128)(2,1)S(1)}, u32[]{:S(2)}, u32[]{:S(2)}) collective-permute-start(bf16[128,1536]{1,0:T(8,128)(2,1)S(1)} %get-tuple-element.122), channel_id=1, source_target_pairs={{0,2},{2,4},{4,6},{6,0},{1,3},{3,5},{5,7},{7,1},{8,10},{10,12},{12... | collective-permute-start | bytes 1179656 | tf_op jit(solution)/shard_map/ppermute | solution.py:26
  40.7 25.9 %collective-permute-start.15 = (bf16[2,128,1536]{2,1,0:T(8,128)(2,1)S(1)}, bf16[2,128,1536]{2,1,0:T(8,128)(2,1)S(1)}, u32[]{:S(2)}, u32[]{:S(2)}) collective-permute-start(bf16[2,128,1536]{2,1,0:T(8,128)(2,1)S(1)} %get-tuple-element.129), channel_id=1, source_target_pairs={{0,2},{2,4},{4,6},{6,0},{1,3},{3,5},{5,7},{7,1},{8,10},{10,12},{12... | collective-permute-start | bytes 2359304 | tf_op jit(solution)/shard_map/ppermute | solution.py:26
  40.8 25.8 %collective-permute-start.16 = (bf16[2,128,1536]{2,1,0:T(8,128)(2,1)S(1)}, bf16[2,128,1536]{2,1,0:T(8,128)(2,1)S(1)}, u32[]{:S(2)}, u32[]{:S(2)}) collective-permute-start(bf16[2,128,1536]{2,1,0:T(8,128)(2,1)S(1)} %get-tuple-element.130), channel_id=1, source_target_pairs={{0,6},{2,0},{4,2},{6,4},{1,7},{3,1},{5,3},{7,5},{8,14},{10,8},{12,... | collective-permute-start | bytes 2359304 | tf_op jit(solution)/shard_map/ppermute | solution.py:26
  50.4 32.0 %collective-permute-start.20 = (bf16[2,128,1536]{2,1,0:T(8,128)(2,1)S(1)}, bf16[2,128,1536]{2,1,0:T(8,128)(2,1)S(1)}, u32[]{:S(2)}, u32[]{:S(2)}) collective-permute-start(bf16[2,128,1536]{2,1,0:T(8,128)(2,1)S(1)} %get-tuple-element.137), channel_id=1, source_target_pairs={{0,2},{2,4},{4,6},{6,0},{1,3},{3,5},{5,7},{7,1},{8,10},{10,12},{12... | collective-permute-start | bytes 2359304 | tf_op jit(solution)/shard_map/ppermute | solution.py:26
  50.6 31.8 %collective-permute-start.21 = (bf16[2,128,1536]{2,1,0:T(8,128)(2,1)S(1)}, bf16[2,128,1536]{2,1,0:T(8,128)(2,1)S(1)}, u32[]{:S(2)}, u32[]{:S(2)}) collective-permute-start(bf16[2,128,1536]{2,1,0:T(8,128)(2,1)S(1)} %get-tuple-element.138), channel_id=1, source_target_pairs={{0,6},{2,0},{4,2},{6,4},{1,7},{3,1},{5,3},{7,5},{8,14},{10,8},{12,... | collective-permute-start | bytes 2359304 | tf_op jit(solution)/shard_map/ppermute | solution.py:26
  67.3 17.6 %collective-permute-start.19 = (bf16[2,128,1536]{2,1,0:T(8,128)(2,1)S(1)}, bf16[2,128,1536]{2,1,0:T(8,128)(2,1)S(1)}, u32[]{:S(2)}, u32[]{:S(2)}) collective-permute-start(bf16[2,128,1536]{2,1,0:T(8,128)(2,1)S(1)} %get-tuple-element.142), channel_id=1, source_target_pairs={{0,8},{8,0},{1,9},{9,1},{2,10},{10,2},{3,11},{11,3},{4,12},{12,4},... | collective-permute-start | bytes 2359304 | tf_op jit(solution)/shard_map/ppermute | solution.py:26
  83.1 18.6 %collective-permute-start.24 = (bf16[2,128,1536]{2,1,0:T(8,128)(2,1)S(1)}, bf16[2,128,1536]{2,1,0:T(8,128)(2,1)S(1)}, u32[]{:S(2)}, u32[]{:S(2)}) collective-permute-start(bf16[2,128,1536]{2,1,0:T(8,128)(2,1)S(1)} %get-tuple-element.145), channel_id=1, source_target_pairs={{0,8},{8,0},{1,9},{9,1},{2,10},{10,2},{3,11},{11,3},{4,12},{12,4},... | collective-permute-start | bytes 2359304 | tf_op jit(solution)/shard_map/ppermute | solution.py:26
  85.6 20.2 %collective-permute-start.23 = (bf16[2,128,1536]{2,1,0:T(8,128)(2,1)S(1)}, bf16[2,128,1536]{2,1,0:T(8,128)(2,1)S(1)}, u32[]{:S(2)}, u32[]{:S(2)}) collective-permute-start(bf16[2,128,1536]{2,1,0:T(8,128)(2,1)S(1)} %hidden.2.mine.refs_6_.refs_9_), channel_id=1, source_target_pairs={{0,2},{2,4},{4,6},{6,0},{1,3},{3,5},{5,7},{7,1},{8,10},{10,12},{12... | collective-permute-start | bytes 2359304 | tf_op jit(solution)/shard_map/ppermute | solution.py:26
  85.7 20.1 %collective-permute-start.22 = (bf16[2,128,1536]{2,1,0:T(8,128)(2,1)S(1)}, bf16[2,128,1536]{2,1,0:T(8,128)(2,1)S(1)}, u32[]{:S(2)}, u32[]{:S(2)}) collective-permute-start(bf16[2,128,1536]{2,1,0:T(8,128)(2,1)S(1)} %hidden.2.mine.refs_6_.refs_9_), channel_id=1, source_target_pairs={{0,6},{2,0},{4,2},{6,4},{1,7},{3,1},{5,3},{7,5},{8,14},{10,8},{12,... | collective-permute-start | bytes 2359304 | tf_op jit(solution)/shard_map/ppermute | solution.py:26
  102.5 21.8 %collective-permute-start.28 = (bf16[2,128,1536]{2,1,0:T(8,128)(2,1)S(1)}, bf16[2,128,1536]{2,1,0:T(8,128)(2,1)S(1)}, u32[]{:S(2)}, u32[]{:S(2)}) collective-permute-start(bf16[2,128,1536]{2,1,0:T(8,128)(2,1)S(1)} %hidden.3.mine.refs_6_.refs_9_), channel_id=1, source_target_pairs={{0,2},{2,4},{4,6},{6,0},{1,3},{3,5},{5,7},{7,1},{8,10},{10,12},{12... | collective-permute-start | bytes 2359304 | tf_op jit(solution)/shard_map/ppermute | solution.py:26
  102.6 21.7 %collective-permute-start.27 = (bf16[2,128,1536]{2,1,0:T(8,128)(2,1)S(1)}, bf16[2,128,1536]{2,1,0:T(8,128)(2,1)S(1)}, u32[]{:S(2)}, u32[]{:S(2)}) collective-permute-start(bf16[2,128,1536]{2,1,0:T(8,128)(2,1)S(1)} %hidden.3.mine.refs_6_.refs_9_), channel_id=1, source_target_pairs={{0,6},{2,0},{4,2},{6,4},{1,7},{3,1},{5,3},{7,5},{8,14},{10,8},{12,... | collective-permute-start | bytes 2359304 | tf_op jit(solution)/shard_map/ppermute | solution.py:26
  105.9 27.9 %collective-permute-start.26 = (bf16[128,1536]{1,0:T(8,128)(2,1)S(1)}, bf16[128,1536]{1,0:T(8,128)(2,1)S(1)}, u32[]{:S(2)}, u32[]{:S(2)}) collective-permute-start(bf16[128,1536]{1,0:T(8,128)(2,1)S(1)} %get-tuple-element.156), channel_id=1, source_target_pairs={{0,2},{2,4},{4,6},{6,0},{1,3},{3,5},{5,7},{7,1},{8,10},{10,12},{12... | collective-permute-start | bytes 1179656 | tf_op jit(solution)/shard_map/ppermute | solution.py:26
  105.9 27.8 %collective-permute-start.25 = (bf16[128,1536]{1,0:T(8,128)(2,1)S(1)}, bf16[128,1536]{1,0:T(8,128)(2,1)S(1)}, u32[]{:S(2)}, u32[]{:S(2)}) collective-permute-start(bf16[128,1536]{1,0:T(8,128)(2,1)S(1)} %get-tuple-element.151), channel_id=1, source_target_pairs={{0,6},{2,0},{4,2},{6,4},{1,7},{3,1},{5,3},{7,5},{8,14},{10,8},{12,... | collective-permute-start | bytes 1179656 | tf_op jit(solution)/shard_map/ppermute | solution.py:26
  114.9 2.2 %copy-start = (f32[768,1536]{1,0:T(8,128)}, f32[768,1536]{1,0:T(8,128)S(1)}, u32[]{:S(2)}) copy-start(f32[768,1536]{1,0:T(8,128)S(1)} %get-tuple-element.164.refs_12_) | copy-start | bytes 14155780
  124.3 14.4 %collective-permute-start.33 = (bf16[128,1536]{1,0:T(8,128)(2,1)S(1)}, bf16[128,1536]{1,0:T(8,128)(2,1)S(1)}, u32[]{:S(2)}, u32[]{:S(2)}) collective-permute-start(bf16[128,1536]{1,0:T(8,128)(2,1)S(1)} %get-tuple-element.184), channel_id=1, source_target_pairs={{0,2},{2,4},{4,6},{6,0},{1,3},{3,5},{5,7},{7,1},{8,10},{10,12},{12... | collective-permute-start | bytes 1179656 | tf_op jit(solution)/shard_map/ppermute | solution.py:26
  124.4 5.5 %copy-start.1 = (f32[768,1536]{1,0:T(8,128)S(1)}, f32[768,1536]{1,0:T(8,128)}, u32[]{:S(2)}) copy-start(f32[768,1536]{1,0:T(8,128)} %copy-done) | copy-start | bytes 14155780
  124.4 14.3 %collective-permute-start.32 = (bf16[128,1536]{1,0:T(8,128)(2,1)S(1)}, bf16[128,1536]{1,0:T(8,128)(2,1)S(1)}, u32[]{:S(2)}, u32[]{:S(2)}) collective-permute-start(bf16[128,1536]{1,0:T(8,128)(2,1)S(1)} %get-tuple-element.168), channel_id=1, source_target_pairs={{0,6},{2,0},{4,2},{6,4},{1,7},{3,1},{5,3},{7,5},{8,14},{10,8},{12,... | collective-permute-start | bytes 1179656 | tf_op jit(solution)/shard_map/ppermute | solution.py:26
  134.7 1.6 collective-permute-start.29
  134.8 1.9 %collective-permute-start.30 = (f32[512,128]{1,0:T(8,128)S(1)}, f32[512,128]{1,0:T(8,128)S(1)}, u32[]{:S(2)}, u32[]{:S(2)}) collective-permute-start(f32[512,128]{1,0:T(8,128)S(1)} %get-tuple-element.181), channel_id=1, source_target_pairs={{0,1},{1,0},{2,3},{3,2},{4,5},{5,4},{6,7},{7,6},{8,9},{9,8},{10,11... | collective-permute-start | bytes 786440 | tf_op jit(solution)/shard_map/ppermute | solution.py:26
  135.3 1.8 %collective-permute-start.31 = (f32[512,128]{1,0:T(8,128)S(1)}, f32[512,128]{1,0:T(8,128)S(1)}, u32[]{:S(2)}, u32[]{:S(2)}) collective-permute-start(f32[512,128]{1,0:T(8,128)S(1)} %get-tuple-element.182), channel_id=1, source_target_pairs={{0,1},{1,0},{2,3},{3,2},{4,5},{5,4},{6,7},{7,6},{8,9},{9,8},{10,11... | collective-permute-start | bytes 786440 | tf_op jit(solution)/shard_map/ppermute | solution.py:26
  139.6 9.5 %collective-permute-start.34 = (f32[512,384]{1,0:T(8,128)S(1)}, f32[512,384]{1,0:T(8,128)S(1)}, u32[]{:S(2)}, u32[]{:S(2)}) collective-permute-start(f32[512,384]{1,0:T(8,128)S(1)} %get-tuple-element.186), channel_id=1, source_target_pairs={{0,1},{1,0},{2,3},{3,2},{4,5},{5,4},{6,7},{7,6},{8,9},{9,8},{10,11... | collective-permute-start | bytes 2359304 | tf_op jit(solution)/shard_map/ppermute | solution.py:26
  139.7 8.4 %collective-permute-start.35 = (bf16[4,32,384]{2,1,0:T(8,128)(2,1)S(1)}, bf16[4,32,384]{2,1,0:T(8,128)(2,1)S(1)}, u32[]{:S(2)}, u32[]{:S(2)}) collective-permute-start(bf16[4,32,384]{2,1,0:T(8,128)(2,1)S(1)} %get-tuple-element.187), channel_id=1, source_target_pairs={{0,32},{32,64},{64,96},{96,0},{1,33},{33,65},{65,97},{97,1},{2,34}... | collective-permute-start | bytes 294920 | tf_op jit(solution)/shard_map/ppermute | solution.py:26
  141.5 7.6 %collective-permute-start.36 = (bf16[4,32,384]{2,1,0:T(8,128)(2,1)S(1)}, bf16[4,32,384]{2,1,0:T(8,128)(2,1)S(1)}, u32[]{:S(2)}, u32[]{:S(2)}) collective-permute-start(bf16[4,32,384]{2,1,0:T(8,128)(2,1)S(1)} %get-tuple-element.188), channel_id=1, source_target_pairs={{0,64},{32,96},{64,0},{96,32},{1,65},{33,97},{65,1},{97,33},{2,66}... | collective-permute-start | bytes 294920 | tf_op jit(solution)/shard_map/ppermute | solution.py:26
  143.9 5.2 %collective-permute-start.37 = (bf16[4,32,384]{2,1,0:T(8,128)(2,1)S(1)}, bf16[4,32,384]{2,1,0:T(8,128)(2,1)S(1)}, u32[]{:S(2)}, u32[]{:S(2)}) collective-permute-start(bf16[4,32,384]{2,1,0:T(8,128)(2,1)S(1)} %get-tuple-element.189), channel_id=1, source_target_pairs={{0,96},{32,0},{64,32},{96,64},{1,97},{33,1},{65,33},{97,65},{2,98}... | collective-permute-start | bytes 294920 | tf_op jit(solution)/shard_map/ppermute | solution.py:26
  149.2 9.6 %collective-permute-start.42 = (bf16[384,1536]{1,0:T(8,128)(2,1)S(1)}, bf16[384,1536]{1,0:T(8,128)(2,1)S(1)}, u32[]{:S(2)}, u32[]{:S(2)}) collective-permute-start(bf16[384,1536]{1,0:T(8,128)(2,1)S(1)} %get-tuple-element.209), channel_id=1, source_target_pairs={{0,1},{1,0},{2,3},{3,2},{4,5},{5,4},{6,7},{7,6},{8,9},{9,8},{10,11... | collective-permute-start | bytes 3538952 | tf_op jit(solution)/shard_map/ppermute | solution.py:26
  149.3 10.9 %collective-permute-start.43 = (bf16[1536,384]{1,0:T(8,128)(2,1)S(1)}, bf16[1536,384]{1,0:T(8,128)(2,1)S(1)}, u32[]{:S(2)}, u32[]{:S(2)}) collective-permute-start(bf16[1536,384]{1,0:T(8,128)(2,1)S(1)} %get-tuple-element.210), channel_id=1, source_target_pairs={{0,1},{1,0},{2,3},{3,2},{4,5},{5,4},{6,7},{7,6},{8,9},{9,8},{10,11... | collective-permute-start | bytes 3538952 | tf_op jit(solution)/shard_map/ppermute | solution.py:26
  149.8 12.0 %collective-permute-start.38 = (bf16[4,32,384]{2,1,0:T(8,128)(2,1)S(1)}, bf16[4,32,384]{2,1,0:T(8,128)(2,1)S(1)}, u32[]{:S(2)}, u32[]{:S(2)}) collective-permute-start(bf16[4,32,384]{2,1,0:T(8,128)(2,1)S(1)} %get-tuple-element.203), channel_id=1, source_target_pairs={{0,16},{16,0},{32,48},{48,32},{64,80},{80,64},{96,112},{112,96},{1... | collective-permute-start | bytes 294920 | tf_op jit(solution)/shard_map/ppermute | solution.py:515
  152.5 9.2 %collective-permute-start.39 = (bf16[4,32,384]{2,1,0:T(8,128)(2,1)S(1)}, bf16[4,32,384]{2,1,0:T(8,128)(2,1)S(1)}, u32[]{:S(2)}, u32[]{:S(2)}) collective-permute-start(bf16[4,32,384]{2,1,0:T(8,128)(2,1)S(1)} %get-tuple-element.204), channel_id=1, source_target_pairs={{0,48},{16,32},{32,80},{48,64},{64,112},{80,96},{96,16},{112,0},{1... | collective-permute-start | bytes 294920 | tf_op jit(solution)/shard_map/ppermute | solution.py:515
  154.2 9.2 %collective-permute-start.40 = (bf16[4,32,384]{2,1,0:T(8,128)(2,1)S(1)}, bf16[4,32,384]{2,1,0:T(8,128)(2,1)S(1)}, u32[]{:S(2)}, u32[]{:S(2)}) collective-permute-start(bf16[4,32,384]{2,1,0:T(8,128)(2,1)S(1)} %get-tuple-element.205), channel_id=1, source_target_pairs={{0,80},{16,64},{32,112},{48,96},{64,16},{80,0},{96,48},{112,32},{1... | collective-permute-start | bytes 294920 | tf_op jit(solution)/shard_map/ppermute | solution.py:515
  158.8 7.0 %collective-permute-start.41 = (bf16[4,32,384]{2,1,0:T(8,128)(2,1)S(1)}, bf16[4,32,384]{2,1,0:T(8,128)(2,1)S(1)}, u32[]{:S(2)}, u32[]{:S(2)}) collective-permute-start(bf16[4,32,384]{2,1,0:T(8,128)(2,1)S(1)} %get-tuple-element.206), channel_id=1, source_target_pairs={{0,112},{16,96},{32,16},{48,0},{64,48},{80,32},{96,80},{112,64},{1... | collective-permute-start | bytes 294920 | tf_op jit(solution)/shard_map/ppermute | solution.py:515

commit v12 on v11

--- a/solution.py
+++ b/solution.py
@@ -513,7 +513,7 @@
     got = to_core(gate(others, far))
     far = [
         lax.ppermute(a, ROWS, [(i, ((i // 2 + d) % 4) * 2 + (i + 1) % 2) for i in range(8)])
-        for d, a in enumerate(far)
+        for d, a in sorted(enumerate(far), key=lambda pair: (2, 1, 3, 0).index(pair[0]))
     ]
     w_in_grad, w_out_grad = place(w_in_grad, w_out_grad, *got, at_core)
 

time: 167 us -> 167 us (level)
  no operation moved by 1% of the time
where the time goes in v12:
time: 167 us
  starting transfers between devices  64.6 us (39%)
  waiting for transfers between devices  61 us (37%)
  Pallas kernels  37 us (22%)
  local copies, waits for them, and re-layouts  2.18 us (1%)
    ppermute x40, waiting for transfers between devices, shift(): return lax.ppermute(x, axis, [(i, (i + by) % n) for i in range(n)])  57.2 us
    ppermute x40, starting transfers between devices, shift(): return lax.ppermute(x, axis, [(i, (i + by) % n) for i in range(n)])  53.7 us
    pallas_call x27, Pallas kernels, kernel(): pl.pallas_call(body, name=name, grid_spec=pltpu.PrefetchScalarGridSpec(nu...  37 us
    ppermute x4, starting transfers between devices, local(): lax.ppermute(a, ROWS, [(i, (i // 2 + d) % 4 * 2 + (i + 1) % 2) for i in r...  11 us
    ppermute x4, waiting for transfers between devices, local(): lax.ppermute(a, ROWS, [(i, (i // 2 + d) % 4 * 2 + (i + 1) % 2) for i in r...  3.71 us
  transfers between devices with their start and end apart: 44, of which 19 were waited for; matrix products, arithmetic and copies ran while one was open for 0% of the time, Pallas kernels for 21%

profile of v12, /device:TPU:0, one launch (start us, length us, event | category | flops | bytes accessed | tf_op | source)
XLA Modules:
  0.0 166.8 jit_solution(16354116712511815854)
XLA Ops:
  0.7 1.0 pad_maximum_fusion
  1.7 1.7 %collective-permute-start.2 = (bf16[4,32,768]{2,1,0:T(8,128)(2,1)S(1)}, bf16[4,32,768]{2,1,0:T(8,128)(2,1)S(1)}, u32[]{:S(2)}, u32[]{:S(2)}) collective-permute-start(bf16[4,32,768]{2,1,0:T(8,128)(2,1)S(1)} %fusion.refs_0_), channel_id=1, source_target_pairs={{0,32},{32,64},{64,96},{96,0},{1,33},{33,65},{65,97},{97,1},{2,34}... | collective-permute-start | bytes 589832 | tf_op jit(solution)/shard_map/ppermute | solution.py:26
  3.4 2.9 %collective-permute-start.1 = (bf16[4,32,768]{2,1,0:T(8,128)(2,1)S(1)}, bf16[4,32,768]{2,1,0:T(8,128)(2,1)S(1)}, u32[]{:S(2)}, u32[]{:S(2)}) collective-permute-start(bf16[4,32,768]{2,1,0:T(8,128)(2,1)S(1)} %fusion.refs_0_), channel_id=1, source_target_pairs={{0,64},{32,96},{64,0},{96,32},{1,65},{33,97},{65,1},{97,33},{2,66}... | collective-permute-start | bytes 589832 | tf_op jit(solution)/shard_map/ppermute | solution.py:26
  6.3 1.3 collective-permute-start
  7.7 3.0 %collective-permute-start.4 = (bf16[4,32,768]{2,1,0:T(8,128)(2,1)S(1)}, bf16[4,32,768]{2,1,0:T(8,128)(2,1)S(1)}, u32[]{:S(2)}, u32[]{:S(2)}) collective-permute-start(bf16[4,32,768]{2,1,0:T(8,128)(2,1)S(1)} %fusion.refs_0_), channel_id=1, source_target_pairs={{0,16},{16,0},{1,17},{17,1},{2,18},{18,2},{3,19},{19,3},{4,20},{20... | collective-permute-start | bytes 589832 | tf_op jit(solution)/shard_map/ppermute | solution.py:26
  10.7 2.8 %pack.1 = bf16[2,4,384,384]{3,2,1,0:T(8,128)(2,1)} custom-call(s32[1]{0:T(128)} %bitcast.2._.core.refs_0_, bf16[384,3072]{1,0:T(8,128)(2,1)} %wi.2, bf16[3072,384]{1,0:T(8,128)(2,1)} %wo.2), custom_call_target="tpu_custom_call" | custom-call | flops 115000000 | bytes 369000 | tf_op jit(solution)/shard_map/pack/pallas_call | solution.py:50
  13.5 1.7 %collective-permute-done.1.refs_2_ = bf16[4,32,768]{2,1,0:T(8,128)(2,1)S(1)} collective-permute-done((bf16[4,32,768]{2,1,0:T(8,128)(2,1)S(1)}, bf16[4,32,768]{2,1,0:T(8,128)(2,1)S(1)}, u32[]{:S(2)}, u32[]{:S(2)}) %collective-permute-start.1) | collective-permute-done | bytes 196640 | tf_op jit(solution)/shard_map/ppermute | solution.py:26
  15.3 0.5 collective-permute-start.3
  15.8 1.2 collective-permute-start.7
  17.1 2.4 %collective-permute-start.6 = (bf16[4,32,768]{2,1,0:T(8,128)(2,1)S(1)}, bf16[4,32,768]{2,1,0:T(8,128)(2,1)S(1)}, u32[]{:S(2)}, u32[]{:S(2)}) collective-permute-start(bf16[4,32,768]{2,1,0:T(8,128)(2,1)S(1)} %collective-permute-done.4.refs_0_), channel_id=1, source_target_pairs={{0,64},{32,96},{64,0},{96,32},{1,65},{33,97},{65,1},{97,33},{2,66}... | collective-permute-start | bytes 589832 | tf_op jit(solution)/shard_map/ppermute | solution.py:26
  19.5 1.6 collective-permute-start.5
  21.1 0.6 weights.1
  21.6 1.6 first_block.2
  23.2 4.1 %collective-permute-start.14 = (bf16[128,1536]{1,0:T(8,128)(2,1)S(1)}, bf16[128,1536]{1,0:T(8,128)(2,1)S(1)}, u32[]{:S(2)}, u32[]{:S(2)}) collective-permute-start(bf16[128,1536]{1,0:T(8,128)(2,1)S(1)} %get-tuple-element.126), channel_id=1, source_target_pairs={{0,6},{2,0},{4,2},{6,4},{1,7},{3,1},{5,3},{7,5},{8,14},{10,8},{12,... | collective-permute-start | bytes 1179656 | tf_op jit(solution)/shard_map/ppermute | solution.py:26
  27.3 1.2 collective-permute-done.6.refs_2_
  28.8 0.5 collective-permute-start.11
  29.3 0.9 collective-permute-done.10.refs_5_
  30.9 1.6 first_block.3
  32.4 4.1 %collective-permute-start.18 = (bf16[128,1536]{1,0:T(8,128)(2,1)S(1)}, bf16[128,1536]{1,0:T(8,128)(2,1)S(1)}, u32[]{:S(2)}, u32[]{:S(2)}) collective-permute-start(bf16[128,1536]{1,0:T(8,128)(2,1)S(1)} %get-tuple-element.134), channel_id=1, source_target_pairs={{0,6},{2,0},{4,2},{6,4},{1,7},{3,1},{5,3},{7,5},{8,14},{10,8},{12,... | collective-permute-start | bytes 1179656 | tf_op jit(solution)/shard_map/ppermute | solution.py:26
  36.5 3.5 %products.2 = (f32[2,512,1536]{2,1,0:T(8,128)S(1)}, bf16[512,768]{1,0:T(8,128)(2,1)S(1)}, bf16[512,768]{1,0:T(8,128)(2,1)S(1)}) custom-call(bf16[512,768]{1,0:T(8,128)(2,1)S(1)} %join_a.1.own, bf16[512,768]{1,0:T(8,128)(2,1)S(1)} %collective-permute-done.3.other, bf16[768,1536]{1,0:T(8,128)(2,1)S(1)} %get-tuple-element.114.wi, ...), custom_call_target="tpu_custom_call" | custom-call | flops 115000000 | bytes 369000 | tf_op jit(solution)/shard_map/products/pallas_call | solution.py:50
  40.1 0.6 ring_add.2
  40.8 3.3 %collective-permute-start.16 = (bf16[2,128,1536]{2,1,0:T(8,128)(2,1)S(1)}, bf16[2,128,1536]{2,1,0:T(8,128)(2,1)S(1)}, u32[]{:S(2)}, u32[]{:S(2)}) collective-permute-start(bf16[2,128,1536]{2,1,0:T(8,128)(2,1)S(1)} %get-tuple-element.130), channel_id=1, source_target_pairs={{0,6},{2,0},{4,2},{6,4},{1,7},{3,1},{5,3},{7,5},{8,14},{10,8},{12,... | collective-permute-start | bytes 2359304 | tf_op jit(solution)/shard_map/ppermute | solution.py:26
  44.1 3.5 %products.3 = (f32[2,512,1536]{2,1,0:T(8,128)S(1)}, bf16[512,768]{1,0:T(8,128)(2,1)S(1)}, bf16[512,768]{1,0:T(8,128)(2,1)S(1)}) custom-call(bf16[512,768]{1,0:T(8,128)(2,1)S(1)} %get-tuple-element.131.own, bf16[512,768]{1,0:T(8,128)(2,1)S(1)} %get-tuple-element.132.other, bf16[768,1536]{1,0:T(8,128)(2,1)S(1)} %get-tuple-element.114.wi, ...), custom_call_target="tpu_custom_call" | custom-call | flops 115000000 | bytes 369000 | tf_op jit(solution)/shard_map/products/pallas_call | solution.py:50
  47.6 2.1 %collective-permute-done.17.up = bf16[128,1536]{1,0:T(8,128)(2,1)S(1)} collective-permute-done((bf16[128,1536]{1,0:T(8,128)(2,1)S(1)}, bf16[128,1536]{1,0:T(8,128)(2,1)S(1)}, u32[]{:S(2)}, u32[]{:S(2)}) %collective-permute-start.17) | collective-permute-done | bytes 393248 | tf_op jit(solution)/shard_map/ppermute | solution.py:26
  49.7 0.6 ring_add.3
  50.6 3.2 %collective-permute-start.21 = (bf16[2,128,1536]{2,1,0:T(8,128)(2,1)S(1)}, bf16[2,128,1536]{2,1,0:T(8,128)(2,1)S(1)}, u32[]{:S(2)}, u32[]{:S(2)}) collective-permute-start(bf16[2,128,1536]{2,1,0:T(8,128)(2,1)S(1)} %get-tuple-element.138), channel_id=1, source_target_pairs={{0,6},{2,0},{4,2},{6,4},{1,7},{3,1},{5,3},{7,5},{8,14},{10,8},{12,... | collective-permute-start | bytes 2359304 | tf_op jit(solution)/shard_map/ppermute | solution.py:26
  53.9 12.7 %collective-permute-done.15.up = bf16[2,128,1536]{2,1,0:T(8,128)(2,1)S(1)} collective-permute-done((bf16[2,128,1536]{2,1,0:T(8,128)(2,1)S(1)}, bf16[2,128,1536]{2,1,0:T(8,128)(2,1)S(1)}, u32[]{:S(2)}, u32[]{:S(2)}) %collective-permute-start.15) | collective-permute-done | bytes 786464 | tf_op jit(solution)/shard_map/ppermute | solution.py:26
  66.6 0.7 own_sum.2
  67.3 1.6 collective-permute-start.19
  68.9 13.5 %collective-permute-done.20.up = bf16[2,128,1536]{2,1,0:T(8,128)(2,1)S(1)} collective-permute-done((bf16[2,128,1536]{2,1,0:T(8,128)(2,1)S(1)}, bf16[2,128,1536]{2,1,0:T(8,128)(2,1)S(1)}, u32[]{:S(2)}, u32[]{:S(2)}) %collective-permute-start.20) | collective-permute-done | bytes 786464 | tf_op jit(solution)/shard_map/ppermute | solution.py:26
  82.4 0.7 own_sum.3
  83.1 1.6 collective-permute-start.24
  84.9 0.7 hidden.2.mine.refs_6_.refs_9_
  85.7 3.2 %collective-permute-start.22 = (bf16[2,128,1536]{2,1,0:T(8,128)(2,1)S(1)}, bf16[2,128,1536]{2,1,0:T(8,128)(2,1)S(1)}, u32[]{:S(2)}, u32[]{:S(2)}) collective-permute-start(bf16[2,128,1536]{2,1,0:T(8,128)(2,1)S(1)} %hidden.2.mine.refs_6_.refs_9_), channel_id=1, source_target_pairs={{0,6},{2,0},{4,2},{6,4},{1,7},{3,1},{5,3},{7,5},{8,14},{10,8},{12,... | collective-permute-start | bytes 2359304 | tf_op jit(solution)/shard_map/ppermute | solution.py:26
  88.9 12.8 %collective-permute-done.24.other = bf16[2,128,1536]{2,1,0:T(8,128)(2,1)S(1)} collective-permute-done((bf16[2,128,1536]{2,1,0:T(8,128)(2,1)S(1)}, bf16[2,128,1536]{2,1,0:T(8,128)(2,1)S(1)}, u32[]{:S(2)}, u32[]{:S(2)}) %collective-permute-start.24) | collective-permute-done | bytes 786464 | tf_op jit(solution)/shard_map/ppermute | solution.py:26
  101.8 0.7 hidden.3.mine.refs_6_.refs_9_
  102.6 3.2 %collective-permute-start.27 = (bf16[2,128,1536]{2,1,0:T(8,128)(2,1)S(1)}, bf16[2,128,1536]{2,1,0:T(8,128)(2,1)S(1)}, u32[]{:S(2)}, u32[]{:S(2)}) collective-permute-start(bf16[2,128,1536]{2,1,0:T(8,128)(2,1)S(1)} %hidden.3.mine.refs_6_.refs_9_), channel_id=1, source_target_pairs={{0,6},{2,0},{4,2},{6,4},{1,7},{3,1},{5,3},{7,5},{8,14},{10,8},{12,... | collective-permute-start | bytes 2359304 | tf_op jit(solution)/shard_map/ppermute | solution.py:26
  105.9 3.2 %collective-permute-start.25 = (bf16[128,1536]{1,0:T(8,128)(2,1)S(1)}, bf16[128,1536]{1,0:T(8,128)(2,1)S(1)}, u32[]{:S(2)}, u32[]{:S(2)}) collective-permute-start(bf16[128,1536]{1,0:T(8,128)(2,1)S(1)} %get-tuple-element.151), channel_id=1, source_target_pairs={{0,6},{2,0},{4,2},{6,4},{1,7},{3,1},{5,3},{7,5},{8,14},{10,8},{12,... | collective-permute-start | bytes 1179656 | tf_op jit(solution)/shard_map/ppermute | solution.py:26
  109.2 2.2 %input_three.2 = (f32[3,128,384]{2,1,0:T(8,128)S(1)}, f32[3,128,384]{2,1,0:T(8,128)S(1)}) custom-call(bf16[2,128,1536]{2,1,0:T(8,128)(2,1)S(1)} %hidden.2.mine.refs_6_.refs_9_, bf16[2,128,1536]{2,1,0:T(8,128)(2,1)S(1)} %collective-permute-done.22.above.refs_7_.refs_10_, bf16[2,128,1536]{2,1,0:T(8,128)(2,1)S(1)} %collective-permute-done.23.below.refs_8_.refs_11_, ...), custom_call_target="tpu_custom_call" | custom-call | flops 115000000 | bytes 369000 | tf_op jit(solution)/shard_map/input_three/pallas_call | solution.py:50
  111.4 3.5 %grads_a.1 = (f32[768,1536]{1,0:T(8,128)S(1)}, f32[1536,768]{1,0:T(8,128)S(1)}) custom-call(bf16[512,768]{1,0:T(8,128)(2,1)S(1)} %get-tuple-element.159.refs_0_.refs_1_.refs_2_, bf16[512,768]{1,0:T(8,128)(2,1)S(1)} %get-tuple-element.159.refs_0_.refs_1_.refs_2_, bf16[512,768]{1,0:T(8,128)(2,1)S(1)} %get-tuple-element.159.refs_0_.refs_1_.refs_2_, ...), custom_call_target="tpu_custom_call" | custom-call | flops 115000000 | bytes 369000 | tf_op jit(solution)/shard_map/grads_a/pallas_call | solution.py:50
  114.9 2.2 %copy-done = f32[768,1536]{1,0:T(8,128)} copy-done((f32[768,1536]{1,0:T(8,128)}, f32[768,1536]{1,0:T(8,128)S(1)}, u32[]{:S(2)}) %copy-start) | copy-done | bytes 4718616
  117.1 7.2 %collective-permute-done.28.below.refs_8_.refs_11_ = bf16[2,128,1536]{2,1,0:T(8,128)(2,1)S(1)} collective-permute-done((bf16[2,128,1536]{2,1,0:T(8,128)(2,1)S(1)}, bf16[2,128,1536]{2,1,0:T(8,128)(2,1)S(1)}, u32[]{:S(2)}, u32[]{:S(2)}) %collective-permute-start.28) | collective-permute-done | bytes 786464 | tf_op jit(solution)/shard_map/ppermute | solution.py:26
  124.4 3.3 %collective-permute-start.32 = (bf16[128,1536]{1,0:T(8,128)(2,1)S(1)}, bf16[128,1536]{1,0:T(8,128)(2,1)S(1)}, u32[]{:S(2)}, u32[]{:S(2)}) collective-permute-start(bf16[128,1536]{1,0:T(8,128)(2,1)S(1)} %get-tuple-element.168), channel_id=1, source_target_pairs={{0,6},{2,0},{4,2},{6,4},{1,7},{3,1},{5,3},{7,5},{8,14},{10,8},{12,... | collective-permute-start | bytes 1179656 | tf_op jit(solution)/shard_map/ppermute | solution.py:26
  127.7 2.2 %input_three.3 = (f32[3,128,384]{2,1,0:T(8,128)S(1)}, f32[3,128,384]{2,1,0:T(8,128)S(1)}) custom-call(bf16[2,128,1536]{2,1,0:T(8,128)(2,1)S(1)} %hidden.3.mine.refs_6_.refs_9_, bf16[2,128,1536]{2,1,0:T(8,128)(2,1)S(1)} %collective-permute-done.27.above.refs_7_.refs_10_, bf16[2,128,1536]{2,1,0:T(8,128)(2,1)S(1)} %collective-permute-done.28.below.refs_8_.refs_11_, ...), custom_call_target="tpu_custom_call" | custom-call | flops 115000000 | bytes 369000 | tf_op jit(solution)/shard_map/input_three/pallas_call | solution.py:50
  129.9 3.8 %grads_b.1 = (f32[768,1536]{1,0:T(8,128)S(1)}, f32[1536,768]{1,0:T(8,128)S(1)}) custom-call(bf16[512,768]{1,0:T(8,128)(2,1)S(1)} %get-tuple-element.157.refs_0_.refs_1_.refs_2_, bf16[512,768]{1,0:T(8,128)(2,1)S(1)} %get-tuple-element.157.refs_0_.refs_1_.refs_2_, bf16[512,768]{1,0:T(8,128)(2,1)S(1)} %get-tuple-element.157.refs_0_.refs_1_.refs_2_, ...), custom_call_target="tpu_custom_call" | custom-call | flops 115000000 | bytes 369000 | tf_op jit(solution)/shard_map/grads_b/pallas_call | solution.py:50
  133.8 0.9 input_last.2
  134.8 0.5 collective-permute-start.30
  135.6 0.7 collective-permute-done.29.refs_0_
  137.2 1.5 collective-permute-done.33.grad.refs_8_
  138.7 0.9 input_last.3
  139.7 1.8 %collective-permute-start.35 = (bf16[4,32,384]{2,1,0:T(8,128)(2,1)S(1)}, bf16[4,32,384]{2,1,0:T(8,128)(2,1)S(1)}, u32[]{:S(2)}, u32[]{:S(2)}) collective-permute-start(bf16[4,32,384]{2,1,0:T(8,128)(2,1)S(1)} %get-tuple-element.187), channel_id=1, source_target_pairs={{0,32},{32,64},{64,96},{96,0},{1,33},{33,65},{65,97},{97,1},{2,34}... | collective-permute-start | bytes 294920 | tf_op jit(solution)/shard_map/ppermute | solution.py:26
  141.5 2.4 %collective-permute-start.36 = (bf16[4,32,384]{2,1,0:T(8,128)(2,1)S(1)}, bf16[4,32,384]{2,1,0:T(8,128)(2,1)S(1)}, u32[]{:S(2)}, u32[]{:S(2)}) collective-permute-start(bf16[4,32,384]{2,1,0:T(8,128)(2,1)S(1)} %get-tuple-element.188), channel_id=1, source_target_pairs={{0,64},{32,96},{64,0},{96,32},{1,65},{33,97},{65,1},{97,33},{2,66}... | collective-permute-start | bytes 294920 | tf_op jit(solution)/shard_map/ppermute | solution.py:26
  143.9 1.1 collective-permute-start.37
  145.0 3.1 %grads_last.1 = (bf16[384,3072]{1,0:T(8,128)(2,1)}, bf16[3072,384]{1,0:T(8,128)(2,1)}, bf16[384,1536]{1,0:T(8,128)(2,1)S(1)}, bf16[1536,384]{1,0:T(8,128)(2,1)S(1)}) custom-call(s32[1]{0:T(128)} %bitcast.2._.core.refs_0_, bf16[512,768]{1,0:T(8,128)(2,1)S(1)} %get-tuple-element.159.refs_0_.refs_1_.refs_2_, ...), custom_call_target="tpu_custom_call" | custom-call | flops 115000000 | bytes 369000 | tf_op jit(solution)/shard_map/grads_last/pallas_call | solution.py:50
  148.1 1.0 collective-permute-done.36.refs_2_
  149.3 0.5 collective-permute-start.43
  149.8 4.5 %collective-permute-start.38 = (bf16[4,32,384]{2,1,0:T(8,128)(2,1)S(1)}, bf16[4,32,384]{2,1,0:T(8,128)(2,1)S(1)}, u32[]{:S(2)}, u32[]{:S(2)}) collective-permute-start(bf16[4,32,384]{2,1,0:T(8,128)(2,1)S(1)} %get-tuple-element.203), channel_id=1, source_target_pairs={{0,80},{16,64},{32,112},{48,96},{64,16},{80,0},{96,48},{112,32},{1... | collective-permute-start | bytes 294920 | tf_op jit(solution)/shard_map/ppermute | solution.py:515
  154.3 1.1 collective-permute-start.39
  155.4 4.5 %collective-permute-start.40 = (bf16[4,32,384]{2,1,0:T(8,128)(2,1)S(1)}, bf16[4,32,384]{2,1,0:T(8,128)(2,1)S(1)}, u32[]{:S(2)}, u32[]{:S(2)}) collective-permute-start(bf16[4,32,384]{2,1,0:T(8,128)(2,1)S(1)} %get-tuple-element.205), channel_id=1, source_target_pairs={{0,112},{16,96},{32,16},{48,0},{64,48},{80,32},{96,80},{112,64},{1... | collective-permute-start | bytes 294920 | tf_op jit(solution)/shard_map/ppermute | solution.py:515
  159.9 0.8 collective-permute-start.41
  160.8 1.6 place.1
  162.4 1.2 collective-permute-done.39.refs_5_
  163.6 2.5 %collective-permute-done.41.refs_7_ = bf16[4,32,384]{2,1,0:T(8,128)(2,1)S(1)} collective-permute-done((bf16[4,32,384]{2,1,0:T(8,128)(2,1)S(1)}, bf16[4,32,384]{2,1,0:T(8,128)(2,1)S(1)}, u32[]{:S(2)}, u32[]{:S(2)}) %collective-permute-start.41) | collective-permute-done | bytes 98336 | tf_op jit(solution)/shard_map/ppermute | solution.py:515
  166.1 0.7 finish.1
  (61 shorter events, 3.6 us)
Async XLA Ops:
  1.7 11.8 %collective-permute-start.2 = (bf16[4,32,768]{2,1,0:T(8,128)(2,1)S(1)}, bf16[4,32,768]{2,1,0:T(8,128)(2,1)S(1)}, u32[]{:S(2)}, u32[]{:S(2)}) collective-permute-start(bf16[4,32,768]{2,1,0:T(8,128)(2,1)S(1)} %fusion.refs_0_), channel_id=1, source_target_pairs={{0,32},{32,64},{64,96},{96,0},{1,33},{33,65},{65,97},{97,1},{2,34}... | collective-permute-start | bytes 589832 | tf_op jit(solution)/shard_map/ppermute | solution.py:26
  3.4 11.7 %collective-permute-start.1 = (bf16[4,32,768]{2,1,0:T(8,128)(2,1)S(1)}, bf16[4,32,768]{2,1,0:T(8,128)(2,1)S(1)}, u32[]{:S(2)}, u32[]{:S(2)}) collective-permute-start(bf16[4,32,768]{2,1,0:T(8,128)(2,1)S(1)} %fusion.refs_0_), channel_id=1, source_target_pairs={{0,64},{32,96},{64,0},{96,32},{1,65},{33,97},{65,1},{97,33},{2,66}... | collective-permute-start | bytes 589832 | tf_op jit(solution)/shard_map/ppermute | solution.py:26
  6.3 8.8 %collective-permute-start = (bf16[4,32,768]{2,1,0:T(8,128)(2,1)S(1)}, bf16[4,32,768]{2,1,0:T(8,128)(2,1)S(1)}, u32[]{:S(2)}, u32[]{:S(2)}) collective-permute-start(bf16[4,32,768]{2,1,0:T(8,128)(2,1)S(1)} %fusion.refs_0_), channel_id=1, source_target_pairs={{0,96},{32,0},{64,32},{96,64},{1,97},{33,1},{65,33},{97,65},{2,98}... | collective-permute-start | bytes 589832 | tf_op jit(solution)/shard_map/ppermute | solution.py:26
  7.7 7.5 %collective-permute-start.4 = (bf16[4,32,768]{2,1,0:T(8,128)(2,1)S(1)}, bf16[4,32,768]{2,1,0:T(8,128)(2,1)S(1)}, u32[]{:S(2)}, u32[]{:S(2)}) collective-permute-start(bf16[4,32,768]{2,1,0:T(8,128)(2,1)S(1)} %fusion.refs_0_), channel_id=1, source_target_pairs={{0,16},{16,0},{1,17},{17,1},{2,18},{18,2},{3,19},{19,3},{4,20},{20... | collective-permute-start | bytes 589832 | tf_op jit(solution)/shard_map/ppermute | solution.py:26
  13.5 7.6 %copy-start.2 = (bf16[384,3072]{1,0:T(8,128)(2,1)S(1)}, bf16[384,3072]{1,0:T(8,128)(2,1)}, u32[]{:S(2)}) copy-start(bf16[384,3072]{1,0:T(8,128)(2,1)} %wi.2) | copy-start | bytes 7077892
  13.5 7.6 %copy-start.3 = (bf16[3072,384]{1,0:T(8,128)(2,1)S(1)}, bf16[3072,384]{1,0:T(8,128)(2,1)}, u32[]{:S(2)}) copy-start(bf16[3072,384]{1,0:T(8,128)(2,1)} %wo.2) | copy-start | bytes 7077892
  13.5 7.6 %collective-permute-start.8 = (bf16[2,4,384,384]{3,2,1,0:T(8,128)(2,1)}, bf16[2,4,384,384]{3,2,1,0:T(8,128)(2,1)S(1)}, u32[]{:S(2)}, u32[]{:S(2)}) collective-permute-start(bf16[2,4,384,384]{3,2,1,0:T(8,128)(2,1)} %pack.1), channel_id=1, source_target_pairs={{0,1},{1,0},{2,3},{3,2},{4,5},{5,4},{6,7},{7,6},{8,9},{9,8},{10,11... | collective-permute-start | bytes 7077896 | tf_op jit(solution)/shard_map/ppermute | solution.py:26
  15.2 4.2 %collective-permute-start.9 = (bf16[4,32,768]{2,1,0:T(8,128)(2,1)S(1)}, bf16[4,32,768]{2,1,0:T(8,128)(2,1)S(1)}, u32[]{:S(2)}, u32[]{:S(2)}) collective-permute-start(bf16[4,32,768]{2,1,0:T(8,128)(2,1)S(1)} %collective-permute-done.4.refs_0_), channel_id=1, source_target_pairs={{0,1},{1,0},{2,3},{3,2},{4,5},{5,4},{6,7},{7,6},{8,9},{9,8},{10,11... | collective-permute-start | bytes 589832 | tf_op jit(solution)/shard_map/ppermute | solution.py:26
  15.3 6.3 %collective-permute-start.3 = (bf16[512,768]{1,0:T(8,128)(2,1)S(1)}, bf16[512,768]{1,0:T(8,128)(2,1)S(1)}, u32[]{:S(2)}, u32[]{:S(2)}) collective-permute-start(bf16[512,768]{1,0:T(8,128)(2,1)S(1)} %join_a.1.own), channel_id=1, source_target_pairs={{0,1},{1,0},{2,3},{3,2},{4,5},{5,4},{6,7},{7,6},{8,9},{9,8},{10,11... | collective-permute-start | bytes 2359304 | tf_op jit(solution)/shard_map/ppermute | solution.py:26
  15.8 11.5 %collective-permute-start.7 = (bf16[4,32,768]{2,1,0:T(8,128)(2,1)S(1)}, bf16[4,32,768]{2,1,0:T(8,128)(2,1)S(1)}, u32[]{:S(2)}, u32[]{:S(2)}) collective-permute-start(bf16[4,32,768]{2,1,0:T(8,128)(2,1)S(1)} %collective-permute-done.4.refs_0_), channel_id=1, source_target_pairs={{0,32},{32,64},{64,96},{96,0},{1,33},{33,65},{65,97},{97,1},{2,34}... | collective-permute-start | bytes 589832 | tf_op jit(solution)/shard_map/ppermute | solution.py:26
  17.1 11.5 %collective-permute-start.6 = (bf16[4,32,768]{2,1,0:T(8,128)(2,1)S(1)}, bf16[4,32,768]{2,1,0:T(8,128)(2,1)S(1)}, u32[]{:S(2)}, u32[]{:S(2)}) collective-permute-start(bf16[4,32,768]{2,1,0:T(8,128)(2,1)S(1)} %collective-permute-done.4.refs_0_), channel_id=1, source_target_pairs={{0,64},{32,96},{64,0},{96,32},{1,65},{33,97},{65,1},{97,33},{2,66}... | collective-permute-start | bytes 589832 | tf_op jit(solution)/shard_map/ppermute | solution.py:26
  19.5 9.3 %collective-permute-start.5 = (bf16[4,32,768]{2,1,0:T(8,128)(2,1)S(1)}, bf16[4,32,768]{2,1,0:T(8,128)(2,1)S(1)}, u32[]{:S(2)}, u32[]{:S(2)}) collective-permute-start(bf16[4,32,768]{2,1,0:T(8,128)(2,1)S(1)} %collective-permute-done.4.refs_0_), channel_id=1, source_target_pairs={{0,96},{32,0},{64,32},{96,64},{1,97},{33,1},{65,33},{97,65},{2,98}... | collective-permute-start | bytes 589832 | tf_op jit(solution)/shard_map/ppermute | solution.py:26
  23.2 16.8 %collective-permute-start.14 = (bf16[128,1536]{1,0:T(8,128)(2,1)S(1)}, bf16[128,1536]{1,0:T(8,128)(2,1)S(1)}, u32[]{:S(2)}, u32[]{:S(2)}) collective-permute-start(bf16[128,1536]{1,0:T(8,128)(2,1)S(1)} %get-tuple-element.126), channel_id=1, source_target_pairs={{0,6},{2,0},{4,2},{6,4},{1,7},{3,1},{5,3},{7,5},{8,14},{10,8},{12,... | collective-permute-start | bytes 1179656 | tf_op jit(solution)/shard_map/ppermute | solution.py:26
  27.3 12.8 %collective-permute-start.13 = (bf16[128,1536]{1,0:T(8,128)(2,1)S(1)}, bf16[128,1536]{1,0:T(8,128)(2,1)S(1)}, u32[]{:S(2)}, u32[]{:S(2)}) collective-permute-start(bf16[128,1536]{1,0:T(8,128)(2,1)S(1)} %get-tuple-element.116), channel_id=1, source_target_pairs={{0,2},{2,4},{4,6},{6,0},{1,3},{3,5},{5,7},{7,1},{8,10},{10,12},{12... | collective-permute-start | bytes 1179656 | tf_op jit(solution)/shard_map/ppermute | solution.py:26
  28.8 1.4 collective-permute-start.10
  28.8 1.7 %collective-permute-start.11 = (bf16[4,32,768]{2,1,0:T(8,128)(2,1)S(1)}, bf16[4,32,768]{2,1,0:T(8,128)(2,1)S(1)}, u32[]{:S(2)}, u32[]{:S(2)}) collective-permute-start(bf16[4,32,768]{2,1,0:T(8,128)(2,1)S(1)} %collective-permute-done.6.refs_2_), channel_id=1, source_target_pairs={{0,1},{1,0},{2,3},{3,2},{4,5},{5,4},{6,7},{7,6},{8,9},{9,8},{10,11... | collective-permute-start | bytes 589832 | tf_op jit(solution)/shard_map/ppermute | solution.py:26
  29.3 1.5 collective-permute-start.12
  32.4 15.2 %collective-permute-start.18 = (bf16[128,1536]{1,0:T(8,128)(2,1)S(1)}, bf16[128,1536]{1,0:T(8,128)(2,1)S(1)}, u32[]{:S(2)}, u32[]{:S(2)}) collective-permute-start(bf16[128,1536]{1,0:T(8,128)(2,1)S(1)} %get-tuple-element.134), channel_id=1, source_target_pairs={{0,6},{2,0},{4,2},{6,4},{1,7},{3,1},{5,3},{7,5},{8,14},{10,8},{12,... | collective-permute-start | bytes 1179656 | tf_op jit(solution)/shard_map/ppermute | solution.py:26
  36.5 13.2 %collective-permute-start.17 = (bf16[128,1536]{1,0:T(8,128)(2,1)S(1)}, bf16[128,1536]{1,0:T(8,128)(2,1)S(1)}, u32[]{:S(2)}, u32[]{:S(2)}) collective-permute-start(bf16[128,1536]{1,0:T(8,128)(2,1)S(1)} %get-tuple-element.122), channel_id=1, source_target_pairs={{0,2},{2,4},{4,6},{6,0},{1,3},{3,5},{5,7},{7,1},{8,10},{10,12},{12... | collective-permute-start | bytes 1179656 | tf_op jit(solution)/shard_map/ppermute | solution.py:26
  40.7 25.9 %collective-permute-start.15 = (bf16[2,128,1536]{2,1,0:T(8,128)(2,1)S(1)}, bf16[2,128,1536]{2,1,0:T(8,128)(2,1)S(1)}, u32[]{:S(2)}, u32[]{:S(2)}) collective-permute-start(bf16[2,128,1536]{2,1,0:T(8,128)(2,1)S(1)} %get-tuple-element.129), channel_id=1, source_target_pairs={{0,2},{2,4},{4,6},{6,0},{1,3},{3,5},{5,7},{7,1},{8,10},{10,12},{12... | collective-permute-start | bytes 2359304 | tf_op jit(solution)/shard_map/ppermute | solution.py:26
  40.8 25.8 %collective-permute-start.16 = (bf16[2,128,1536]{2,1,0:T(8,128)(2,1)S(1)}, bf16[2,128,1536]{2,1,0:T(8,128)(2,1)S(1)}, u32[]{:S(2)}, u32[]{:S(2)}) collective-permute-start(bf16[2,128,1536]{2,1,0:T(8,128)(2,1)S(1)} %get-tuple-element.130), channel_id=1, source_target_pairs={{0,6},{2,0},{4,2},{6,4},{1,7},{3,1},{5,3},{7,5},{8,14},{10,8},{12,... | collective-permute-start | bytes 2359304 | tf_op jit(solution)/shard_map/ppermute | solution.py:26
  50.4 32.0 %collective-permute-start.20 = (bf16[2,128,1536]{2,1,0:T(8,128)(2,1)S(1)}, bf16[2,128,1536]{2,1,0:T(8,128)(2,1)S(1)}, u32[]{:S(2)}, u32[]{:S(2)}) collective-permute-start(bf16[2,128,1536]{2,1,0:T(8,128)(2,1)S(1)} %get-tuple-element.137), channel_id=1, source_target_pairs={{0,2},{2,4},{4,6},{6,0},{1,3},{3,5},{5,7},{7,1},{8,10},{10,12},{12... | collective-permute-start | bytes 2359304 | tf_op jit(solution)/shard_map/ppermute | solution.py:26
  50.6 31.8 %collective-permute-start.21 = (bf16[2,128,1536]{2,1,0:T(8,128)(2,1)S(1)}, bf16[2,128,1536]{2,1,0:T(8,128)(2,1)S(1)}, u32[]{:S(2)}, u32[]{:S(2)}) collective-permute-start(bf16[2,128,1536]{2,1,0:T(8,128)(2,1)S(1)} %get-tuple-element.138), channel_id=1, source_target_pairs={{0,6},{2,0},{4,2},{6,4},{1,7},{3,1},{5,3},{7,5},{8,14},{10,8},{12,... | collective-permute-start | bytes 2359304 | tf_op jit(solution)/shard_map/ppermute | solution.py:26
  67.3 17.6 %collective-permute-start.19 = (bf16[2,128,1536]{2,1,0:T(8,128)(2,1)S(1)}, bf16[2,128,1536]{2,1,0:T(8,128)(2,1)S(1)}, u32[]{:S(2)}, u32[]{:S(2)}) collective-permute-start(bf16[2,128,1536]{2,1,0:T(8,128)(2,1)S(1)} %get-tuple-element.142), channel_id=1, source_target_pairs={{0,8},{8,0},{1,9},{9,1},{2,10},{10,2},{3,11},{11,3},{4,12},{12,4},... | collective-permute-start | bytes 2359304 | tf_op jit(solution)/shard_map/ppermute | solution.py:26
  83.1 18.6 %collective-permute-start.24 = (bf16[2,128,1536]{2,1,0:T(8,128)(2,1)S(1)}, bf16[2,128,1536]{2,1,0:T(8,128)(2,1)S(1)}, u32[]{:S(2)}, u32[]{:S(2)}) collective-permute-start(bf16[2,128,1536]{2,1,0:T(8,128)(2,1)S(1)} %get-tuple-element.145), channel_id=1, source_target_pairs={{0,8},{8,0},{1,9},{9,1},{2,10},{10,2},{3,11},{11,3},{4,12},{12,4},... | collective-permute-start | bytes 2359304 | tf_op jit(solution)/shard_map/ppermute | solution.py:26
  85.6 20.2 %collective-permute-start.23 = (bf16[2,128,1536]{2,1,0:T(8,128)(2,1)S(1)}, bf16[2,128,1536]{2,1,0:T(8,128)(2,1)S(1)}, u32[]{:S(2)}, u32[]{:S(2)}) collective-permute-start(bf16[2,128,1536]{2,1,0:T(8,128)(2,1)S(1)} %hidden.2.mine.refs_6_.refs_9_), channel_id=1, source_target_pairs={{0,2},{2,4},{4,6},{6,0},{1,3},{3,5},{5,7},{7,1},{8,10},{10,12},{12... | collective-permute-start | bytes 2359304 | tf_op jit(solution)/shard_map/ppermute | solution.py:26
  85.7 20.1 %collective-permute-start.22 = (bf16[2,128,1536]{2,1,0:T(8,128)(2,1)S(1)}, bf16[2,128,1536]{2,1,0:T(8,128)(2,1)S(1)}, u32[]{:S(2)}, u32[]{:S(2)}) collective-permute-start(bf16[2,128,1536]{2,1,0:T(8,128)(2,1)S(1)} %hidden.2.mine.refs_6_.refs_9_), channel_id=1, source_target_pairs={{0,6},{2,0},{4,2},{6,4},{1,7},{3,1},{5,3},{7,5},{8,14},{10,8},{12,... | collective-permute-start | bytes 2359304 | tf_op jit(solution)/shard_map/ppermute | solution.py:26
  102.5 21.8 %collective-permute-start.28 = (bf16[2,128,1536]{2,1,0:T(8,128)(2,1)S(1)}, bf16[2,128,1536]{2,1,0:T(8,128)(2,1)S(1)}, u32[]{:S(2)}, u32[]{:S(2)}) collective-permute-start(bf16[2,128,1536]{2,1,0:T(8,128)(2,1)S(1)} %hidden.3.mine.refs_6_.refs_9_), channel_id=1, source_target_pairs={{0,2},{2,4},{4,6},{6,0},{1,3},{3,5},{5,7},{7,1},{8,10},{10,12},{12... | collective-permute-start | bytes 2359304 | tf_op jit(solution)/shard_map/ppermute | solution.py:26
  102.6 21.7 %collective-permute-start.27 = (bf16[2,128,1536]{2,1,0:T(8,128)(2,1)S(1)}, bf16[2,128,1536]{2,1,0:T(8,128)(2,1)S(1)}, u32[]{:S(2)}, u32[]{:S(2)}) collective-permute-start(bf16[2,128,1536]{2,1,0:T(8,128)(2,1)S(1)} %hidden.3.mine.refs_6_.refs_9_), channel_id=1, source_target_pairs={{0,6},{2,0},{4,2},{6,4},{1,7},{3,1},{5,3},{7,5},{8,14},{10,8},{12,... | collective-permute-start | bytes 2359304 | tf_op jit(solution)/shard_map/ppermute | solution.py:26
  105.9 27.9 %collective-permute-start.26 = (bf16[128,1536]{1,0:T(8,128)(2,1)S(1)}, bf16[128,1536]{1,0:T(8,128)(2,1)S(1)}, u32[]{:S(2)}, u32[]{:S(2)}) collective-permute-start(bf16[128,1536]{1,0:T(8,128)(2,1)S(1)} %get-tuple-element.156), channel_id=1, source_target_pairs={{0,2},{2,4},{4,6},{6,0},{1,3},{3,5},{5,7},{7,1},{8,10},{10,12},{12... | collective-permute-start | bytes 1179656 | tf_op jit(solution)/shard_map/ppermute | solution.py:26
  105.9 27.8 %collective-permute-start.25 = (bf16[128,1536]{1,0:T(8,128)(2,1)S(1)}, bf16[128,1536]{1,0:T(8,128)(2,1)S(1)}, u32[]{:S(2)}, u32[]{:S(2)}) collective-permute-start(bf16[128,1536]{1,0:T(8,128)(2,1)S(1)} %get-tuple-element.151), channel_id=1, source_target_pairs={{0,6},{2,0},{4,2},{6,4},{1,7},{3,1},{5,3},{7,5},{8,14},{10,8},{12,... | collective-permute-start | bytes 1179656 | tf_op jit(solution)/shard_map/ppermute | solution.py:26
  114.9 2.2 %copy-start = (f32[768,1536]{1,0:T(8,128)}, f32[768,1536]{1,0:T(8,128)S(1)}, u32[]{:S(2)}) copy-start(f32[768,1536]{1,0:T(8,128)S(1)} %get-tuple-element.164.refs_12_) | copy-start | bytes 14155780
  124.3 14.4 %collective-permute-start.33 = (bf16[128,1536]{1,0:T(8,128)(2,1)S(1)}, bf16[128,1536]{1,0:T(8,128)(2,1)S(1)}, u32[]{:S(2)}, u32[]{:S(2)}) collective-permute-start(bf16[128,1536]{1,0:T(8,128)(2,1)S(1)} %get-tuple-element.184), channel_id=1, source_target_pairs={{0,2},{2,4},{4,6},{6,0},{1,3},{3,5},{5,7},{7,1},{8,10},{10,12},{12... | collective-permute-start | bytes 1179656 | tf_op jit(solution)/shard_map/ppermute | solution.py:26
  124.4 5.5 %copy-start.1 = (f32[768,1536]{1,0:T(8,128)S(1)}, f32[768,1536]{1,0:T(8,128)}, u32[]{:S(2)}) copy-start(f32[768,1536]{1,0:T(8,128)} %copy-done) | copy-start | bytes 14155780
  124.4 14.3 %collective-permute-start.32 = (bf16[128,1536]{1,0:T(8,128)(2,1)S(1)}, bf16[128,1536]{1,0:T(8,128)(2,1)S(1)}, u32[]{:S(2)}, u32[]{:S(2)}) collective-permute-start(bf16[128,1536]{1,0:T(8,128)(2,1)S(1)} %get-tuple-element.168), channel_id=1, source_target_pairs={{0,6},{2,0},{4,2},{6,4},{1,7},{3,1},{5,3},{7,5},{8,14},{10,8},{12,... | collective-permute-start | bytes 1179656 | tf_op jit(solution)/shard_map/ppermute | solution.py:26
  134.7 1.6 collective-permute-start.29
  134.8 1.9 %collective-permute-start.30 = (f32[512,128]{1,0:T(8,128)S(1)}, f32[512,128]{1,0:T(8,128)S(1)}, u32[]{:S(2)}, u32[]{:S(2)}) collective-permute-start(f32[512,128]{1,0:T(8,128)S(1)} %get-tuple-element.181), channel_id=1, source_target_pairs={{0,1},{1,0},{2,3},{3,2},{4,5},{5,4},{6,7},{7,6},{8,9},{9,8},{10,11... | collective-permute-start | bytes 786440 | tf_op jit(solution)/shard_map/ppermute | solution.py:26
  135.3 1.8 %collective-permute-start.31 = (f32[512,128]{1,0:T(8,128)S(1)}, f32[512,128]{1,0:T(8,128)S(1)}, u32[]{:S(2)}, u32[]{:S(2)}) collective-permute-start(f32[512,128]{1,0:T(8,128)S(1)} %get-tuple-element.182), channel_id=1, source_target_pairs={{0,1},{1,0},{2,3},{3,2},{4,5},{5,4},{6,7},{7,6},{8,9},{9,8},{10,11... | collective-permute-start | bytes 786440 | tf_op jit(solution)/shard_map/ppermute | solution.py:26
  139.6 9.5 %collective-permute-start.34 = (f32[512,384]{1,0:T(8,128)S(1)}, f32[512,384]{1,0:T(8,128)S(1)}, u32[]{:S(2)}, u32[]{:S(2)}) collective-permute-start(f32[512,384]{1,0:T(8,128)S(1)} %get-tuple-element.186), channel_id=1, source_target_pairs={{0,1},{1,0},{2,3},{3,2},{4,5},{5,4},{6,7},{7,6},{8,9},{9,8},{10,11... | collective-permute-start | bytes 2359304 | tf_op jit(solution)/shard_map/ppermute | solution.py:26
  139.7 8.4 %collective-permute-start.35 = (bf16[4,32,384]{2,1,0:T(8,128)(2,1)S(1)}, bf16[4,32,384]{2,1,0:T(8,128)(2,1)S(1)}, u32[]{:S(2)}, u32[]{:S(2)}) collective-permute-start(bf16[4,32,384]{2,1,0:T(8,128)(2,1)S(1)} %get-tuple-element.187), channel_id=1, source_target_pairs={{0,32},{32,64},{64,96},{96,0},{1,33},{33,65},{65,97},{97,1},{2,34}... | collective-permute-start | bytes 294920 | tf_op jit(solution)/shard_map/ppermute | solution.py:26
  141.5 7.6 %collective-permute-start.36 = (bf16[4,32,384]{2,1,0:T(8,128)(2,1)S(1)}, bf16[4,32,384]{2,1,0:T(8,128)(2,1)S(1)}, u32[]{:S(2)}, u32[]{:S(2)}) collective-permute-start(bf16[4,32,384]{2,1,0:T(8,128)(2,1)S(1)} %get-tuple-element.188), channel_id=1, source_target_pairs={{0,64},{32,96},{64,0},{96,32},{1,65},{33,97},{65,1},{97,33},{2,66}... | collective-permute-start | bytes 294920 | tf_op jit(solution)/shard_map/ppermute | solution.py:26
  143.9 5.2 %collective-permute-start.37 = (bf16[4,32,384]{2,1,0:T(8,128)(2,1)S(1)}, bf16[4,32,384]{2,1,0:T(8,128)(2,1)S(1)}, u32[]{:S(2)}, u32[]{:S(2)}) collective-permute-start(bf16[4,32,384]{2,1,0:T(8,128)(2,1)S(1)} %get-tuple-element.189), channel_id=1, source_target_pairs={{0,96},{32,0},{64,32},{96,64},{1,97},{33,1},{65,33},{97,65},{2,98}... | collective-permute-start | bytes 294920 | tf_op jit(solution)/shard_map/ppermute | solution.py:26
  149.2 10.7 %collective-permute-start.42 = (bf16[384,1536]{1,0:T(8,128)(2,1)S(1)}, bf16[384,1536]{1,0:T(8,128)(2,1)S(1)}, u32[]{:S(2)}, u32[]{:S(2)}) collective-permute-start(bf16[384,1536]{1,0:T(8,128)(2,1)S(1)} %get-tuple-element.209), channel_id=1, source_target_pairs={{0,1},{1,0},{2,3},{3,2},{4,5},{5,4},{6,7},{7,6},{8,9},{9,8},{10,11... | collective-permute-start | bytes 3538952 | tf_op jit(solution)/shard_map/ppermute | solution.py:26
  149.3 11.5 %collective-permute-start.43 = (bf16[1536,384]{1,0:T(8,128)(2,1)S(1)}, bf16[1536,384]{1,0:T(8,128)(2,1)S(1)}, u32[]{:S(2)}, u32[]{:S(2)}) collective-permute-start(bf16[1536,384]{1,0:T(8,128)(2,1)S(1)} %get-tuple-element.210), channel_id=1, source_target_pairs={{0,1},{1,0},{2,3},{3,2},{4,5},{5,4},{6,7},{7,6},{8,9},{9,8},{10,11... | collective-permute-start | bytes 3538952 | tf_op jit(solution)/shard_map/ppermute | solution.py:26
  149.8 12.6 %collective-permute-start.38 = (bf16[4,32,384]{2,1,0:T(8,128)(2,1)S(1)}, bf16[4,32,384]{2,1,0:T(8,128)(2,1)S(1)}, u32[]{:S(2)}, u32[]{:S(2)}) collective-permute-start(bf16[4,32,384]{2,1,0:T(8,128)(2,1)S(1)} %get-tuple-element.203), channel_id=1, source_target_pairs={{0,80},{16,64},{32,112},{48,96},{64,16},{80,0},{96,48},{112,32},{1... | collective-permute-start | bytes 294920 | tf_op jit(solution)/shard_map/ppermute | solution.py:515
  154.3 9.3 %collective-permute-start.39 = (bf16[4,32,384]{2,1,0:T(8,128)(2,1)S(1)}, bf16[4,32,384]{2,1,0:T(8,128)(2,1)S(1)}, u32[]{:S(2)}, u32[]{:S(2)}) collective-permute-start(bf16[4,32,384]{2,1,0:T(8,128)(2,1)S(1)} %get-tuple-element.204), channel_id=1, source_target_pairs={{0,48},{16,32},{32,80},{48,64},{64,112},{80,96},{96,16},{112,0},{1... | collective-permute-start | bytes 294920 | tf_op jit(solution)/shard_map/ppermute | solution.py:515
  155.4 8.2 %collective-permute-start.40 = (bf16[4,32,384]{2,1,0:T(8,128)(2,1)S(1)}, bf16[4,32,384]{2,1,0:T(8,128)(2,1)S(1)}, u32[]{:S(2)}, u32[]{:S(2)}) collective-permute-start(bf16[4,32,384]{2,1,0:T(8,128)(2,1)S(1)} %get-tuple-element.205), channel_id=1, source_target_pairs={{0,112},{16,96},{32,16},{48,0},{64,48},{80,32},{96,80},{112,64},{1... | collective-permute-start | bytes 294920 | tf_op jit(solution)/shard_map/ppermute | solution.py:515
  159.9 6.1 %collective-permute-start.41 = (bf16[4,32,384]{2,1,0:T(8,128)(2,1)S(1)}, bf16[4,32,384]{2,1,0:T(8,128)(2,1)S(1)}, u32[]{:S(2)}, u32[]{:S(2)}) collective-permute-start(bf16[4,32,384]{2,1,0:T(8,128)(2,1)S(1)} %get-tuple-element.206), channel_id=1, source_target_pairs={{0,16},{16,0},{32,48},{48,32},{64,80},{80,64},{96,112},{112,96},{1... | collective-permute-start | bytes 294920 | tf_op jit(solution)/shard_map/ppermute | solution.py:515
